TPU v7x, 32 devices: a whole 2x2x4 slice. The times are simulated.
32 devices in a mesh: pair: 2 (over core), group: 2 (over x), rep: 8 (over z, y).
Axes of the slice: x: 2, y: 2, z: 4, core: 2. Of those that a mesh axis runs over, the one named last changes fastest.
Arguments:
- states: float32 [2, 2048, 4, 84, 84], P('pair', ('group', 'rep')), may hold values from 0 to 1
- actions: int32 [2, 2048], P('pair', ('group', 'rep')), may hold values from 0 to 17
- proj_lower: int32 [2048, 51], P(('group', 'rep')), may hold values from 0 to 49, as said below
- proj_upper: int32 [2048, 51], P(('group', 'rep')), may hold values from 1 to 50, as said below
- proj_weight: float32 [2048, 51], P(('group', 'rep')), may hold values from 0 to 1
- first_kernel: float32 [2, 32, 4, 8, 8], P('pair'), may hold values from -0.375 to 0.375
- first_bias: float32 [2, 32], P('pair'), may hold values from -3 to 3
- second_kernel: float32 [2, 64, 32, 4, 4], P('pair'), may hold values from -0.25 to 0.25
- second_bias: float32 [2, 64], P('pair'), may hold values from -3 to 3
- third_kernel: float32 [2, 64, 64, 3, 3], P('pair'), may hold values from -0.25 to 0.25
- third_bias: float32 [2, 64], P('pair'), may hold values from -3 to 3
- hidden_mean: float32 [2, 2, 3136, 512], P('pair'), may hold values from -0.109375 to 0.109375
- hidden_sigma: float32 [2, 2, 3136, 512], P('pair'), may hold values from -0.109375 to 0.109375
- hidden_bias_mean: float32 [2, 2, 512], P('pair'), may hold values from -3 to 3
- hidden_bias_sigma: float32 [2, 2, 512], P('pair'), may hold values from -3 to 3
- head_mean: float32 [2, 512, 969], P('pair'), may hold values from -0.25 to 0.25
- head_sigma: float32 [2, 512, 969], P('pair'), may hold values from -0.25 to 0.25
- head_bias_mean: float32 [2, 969], P('pair'), may hold values from -3 to 3
- head_bias_sigma: float32 [2, 969], P('pair'), may hold values from -3 to 3
- hidden_noise_in: float32 [2, 2, 3136], P('pair'), may hold values from -4 to 4
- hidden_noise_out: float32 [2, 2, 512], P('pair'), may hold values from -4 to 4
- head_noise_in: float32 [2, 2, 512], P('pair'), may hold values from -4 to 4
- head_noise_out: float32 [2, 969], P('pair'), may hold values from -4 to 4
Outputs:
- loss_value: float32 [], replicated
- states_grad: float32 [2048, 4, 84, 84], P(('group', 'rep'), 'pair')
- first_kernel_grad: float32 [32, 4, 8, 8], replicated
- first_bias_grad: float32 [32], replicated
- second_kernel_grad: float32 [64, 32, 4, 4], replicated
- second_bias_grad: float32 [64], replicated
- third_kernel_grad: float32 [64, 64, 3, 3], replicated
- third_bias_grad: float32 [64], replicated
- hidden_mean_grad: float32 [2, 3136, 512], P(None, ('pair', 'group'))
- hidden_sigma_grad: float32 [2, 3136, 512], P(None, ('pair', 'group'))
- hidden_bias_mean_grad: float32 [2, 512], replicated
- hidden_bias_sigma_grad: float32 [2, 512], replicated
- head_mean_grad: float32 [512, 969], P(('pair', 'group'))
- head_sigma_grad: float32 [512, 969], P(('pair', 'group'))
- head_bias_mean_grad: float32 [969], replicated
- head_bias_sigma_grad: float32 [969], replicated
Inputs may be any that keep to these rules, and one draw needn't show every extreme that they name: proj_lower does not fall along the atoms of a transition. proj_upper = proj_lower + 1.
All inputs are finite; a program needn't handle non-finite values.
Results may differ from a plain program's by a relative error of at most 0.0003.
Values sent between devices are 32-bit elements; how exact they have to be, the bound alone decides.
A program may use at most 256 MiB of HBM per device.

v0:
```python
import jax
import jax.numpy as jnp
from jax import lax
from jax.sharding import PartitionSpec as P

ATOMS = 51
ACTIONS = 18


HIGHEST = lax.Precision.HIGHEST


def passed_along(value, axis, by):
    count = lax.axis_size(axis)
    pairs = [(i, i + by) for i in range(count) if 0 <= i + by < count]
    return lax.ppermute(value, axis, pairs)


def smooth(values):
    return values * jax.nn.sigmoid(values)


def conv_layer(inputs, kernel, offset, stride):
    output = lax.conv_general_dilated(
        inputs,
        kernel,
        (stride, stride),
        "VALID",
        dimension_numbers=("NCHW", "OIHW", "NCHW"),
        precision=HIGHEST,
    )
    return smooth(output + offset[None, :, None, None])


def network(weights, noises, frames, chosen):
    torso_out = conv_layer(frames, weights[0], weights[1], 4)
    torso_out = conv_layer(torso_out, weights[2], weights[3], 2)
    torso_out = conv_layer(torso_out, weights[4], weights[5], 1)
    features = torso_out.reshape(torso_out.shape[0], -1)
    hidden_in, hidden_out, head_in, head_out = noises
    hidden_w = weights[6] + weights[7] * (hidden_in[:, :, None] * hidden_out[:, None, :])
    hidden_b = weights[8] + weights[9] * hidden_out
    hidden = smooth(
        jnp.einsum("bf,sfh->sbh", features, hidden_w, precision=HIGHEST) + hidden_b[:, None, :]
    )
    column = jnp.arange(head_out.shape[0])
    head_noise = jnp.where(column[None, :] < ATOMS, head_in[0][:, None], head_in[1][:, None])
    head_w = weights[10] + weights[11] * head_noise * head_out[None, :]
    head_b = weights[12] + weights[13] * head_out
    value_part = jnp.dot(hidden[0], head_w[:, :ATOMS], precision=HIGHEST) + head_b[:ATOMS]
    advantage = (jnp.dot(hidden[1], head_w[:, ATOMS:], precision=HIGHEST) + head_b[ATOMS:]).reshape(
        -1, ACTIONS, ATOMS
    )
    logits = value_part[:, None, :] + advantage - jnp.mean(advantage, axis=1, keepdims=True)
    action_hot = (chosen[:, None] == jnp.arange(ACTIONS)[None, :]).astype(jnp.float32)
    picked = jnp.sum(action_hot[:, :, None] * logits, axis=1)
    return jax.nn.log_softmax(picked, axis=-1)


def project(probabilities, lower_idx, upper_idx, upper_share):
    atom_index = jnp.arange(ATOMS)
    lower_hot = (lower_idx[:, :, None] == atom_index[None, None, :]).astype(jnp.float32)
    upper_hot = (upper_idx[:, :, None] == atom_index[None, None, :]).astype(jnp.float32)
    lower_mass = jnp.einsum(
        "bi,bij->bj", probabilities * (1.0 - upper_share), lower_hot, precision=HIGHEST
    )
    upper_mass = jnp.einsum("bi,bij->bj", probabilities * upper_share, upper_hot, precision=HIGHEST)
    return lower_mass + upper_mass


def local(
    states,
    actions,
    proj_lower,
    proj_upper,
    proj_weight,
    first_kernel,
    first_bias,
    second_kernel,
    second_bias,
    third_kernel,
    third_bias,
    hidden_mean,
    hidden_sigma,
    hidden_bias_mean,
    hidden_bias_sigma,
    head_mean,
    head_sigma,
    head_bias_mean,
    head_bias_sigma,
    hidden_noise_in,
    hidden_noise_out,
    head_noise_in,
    head_noise_out,
):
    stacked = (
        first_kernel,
        first_bias,
        second_kernel,
        second_bias,
        third_kernel,
        third_bias,
        hidden_mean,
        hidden_sigma,
        hidden_bias_mean,
        hidden_bias_sigma,
        head_mean,
        head_sigma,
        head_bias_mean,
        head_bias_sigma,
    )
    weights = tuple((array_item[0] for array_item in stacked))
    noises = tuple(
        (
            array_item[0]
            for array_item in (hidden_noise_in, hidden_noise_out, head_noise_in, head_noise_out)
        )
    )
    chosen = actions[0]

    def forward(weight_set, frames):
        return network(weight_set, noises, frames, chosen)

    log_probs, pullback = jax.vjp(forward, weights, states[0])
    own_dist = project(jnp.exp(log_probs), proj_lower, proj_upper, proj_weight)
    target_dist = passed_along(own_dist, "pair", -1)
    partner_logp = passed_along(log_probs, "pair", 1)
    batch_rows = log_probs.shape[0]
    local_loss = -jnp.sum(own_dist * partner_logp) / batch_rows
    weight_grads, frame_grads = pullback(-target_dist / batch_rows)
    half_frames = frame_grads.shape[1] // 2
    moved = passed_along(frame_grads[:, half_frames:], "pair", 1)
    states_grad = frame_grads[:, :half_frames] + moved
    summed = (
        lax.psum_scatter(weight_grads[6], ("pair", "group"), scatter_dimension=1, tiled=True),
        lax.psum_scatter(weight_grads[7], ("pair", "group"), scatter_dimension=1, tiled=True),
        lax.psum_scatter(
            weight_grads[10][None], ("pair", "group"), scatter_dimension=1, tiled=True
        ),
        lax.psum_scatter(
            weight_grads[11][None], ("pair", "group"), scatter_dimension=1, tiled=True
        ),
    )
    summed = lax.psum((summed[0], summed[1], summed[2], summed[3]), "rep")
    hidden_mean_grad = summed[0]
    hidden_sigma_grad = summed[1]
    head_mean_grad = summed[2][0]
    head_sigma_grad = summed[3][0]
    small = lax.psum(
        (
            weight_grads[0],
            weight_grads[1],
            weight_grads[2],
            weight_grads[3],
            weight_grads[4],
            weight_grads[5],
            weight_grads[8],
            weight_grads[9],
            weight_grads[12],
            weight_grads[13],
            local_loss,
        ),
        ("pair", "group", "rep"),
    )
    return (
        small[10],
        states_grad,
        small[0],
        small[1],
        small[2],
        small[3],
        small[4],
        small[5],
        hidden_mean_grad,
        hidden_sigma_grad,
        small[6],
        small[7],
        head_mean_grad,
        head_sigma_grad,
        small[8],
        small[9],
    )


def solution(mesh):
    placed = (
        P("pair", ("group", "rep"), None, None, None),
        P("pair", ("group", "rep")),
        P(("group", "rep"), None),
        P(("group", "rep"), None),
        P(("group", "rep"), None),
        P("pair", None, None, None, None),
        P("pair", None),
        P("pair", None, None, None, None),
        P("pair", None),
        P("pair", None, None, None, None),
        P("pair", None),
        P("pair", None, None, None),
        P("pair", None, None, None),
        P("pair", None, None),
        P("pair", None, None),
        P("pair", None, None),
        P("pair", None, None),
        P("pair", None),
        P("pair", None),
        P("pair", None, None),
        P("pair", None, None),
        P("pair", None, None),
        P("pair", None),
    )
    return jax.shard_map(
        local,
        mesh=mesh,
        in_specs=placed,
        out_specs=(
            P(),
            P(("group", "rep"), "pair", None, None),
            P(),
            P(),
            P(),
            P(),
            P(),
            P(),
            P(None, ("pair", "group"), None),
            P(None, ("pair", "group"), None),
            P(),
            P(),
            P(("pair", "group"), None),
            P(("pair", "group"), None),
            P(),
            P(),
        ),
        check_vma=False,
    )
```

profile of v0, /device:TPU:0, one launch (start us, length us, event | category | flops | bytes accessed | tf_op | source)
XLA Modules:
  0.0 1245.9 jit_solution(5060965615084797832)
XLA Ops:
  8.0 0.0 reduce-scatter.11.cloned.1.call-start
  8.1 0.8 multiply_add_fusion.2
  8.8 0.1 slice.39
  8.9 0.8 fusion.77
  9.7 0.7 fusion.66
  10.4 42.4 %fusion.2 = f32[128,32,20,20]{0,1,3,2:T(8,128)S(1)} fusion(f32[1,128,4,84,84]{1,2,4,3,0:T(4,128)} %param.23, f32[32,4,8,8]{0,3,2,1:T(8,128)} %bitcast.115), kind=kOutput, calls=%fused_computation.4 | convolution fusion | flops 5033164800 | bytes 21037056 | tf_op jit(solution)/shard_map/jvp()/conv_general_dilated | solution.py:24
  52.9 12.2 fusion.57
  65.1 9.5 fusion.31
  74.6 0.9 copy.80
  75.6 1.3 reshape.167
  77.0 2.6 fusion.22
  79.6 16.5 %fusion.50 = (f32[2,128,512]{2,1,0:T(8,128)S(1)}, f32[2,128,512]{2,1,0:T(8,128)}) fusion(f32[2,512]{1,0:T(2,128)S(1)} %fusion.67, f32[128,3136,1]{0,1,2:T(8,128)S(1)} %copy-done.4, f32[1,2,3136,512]{3,2,1,0:T(8,128)} %param.34, f32[1,2,3136,512]{3,2,1,0:T(8,128)} %param.35, f32[2,512]{1,0:T(2,128)S(1)} %bitcast.121, f32[2,3136]{1,0:T(2,128)S(1)} %bitcast.119), kind=kOutput, calls=%fused_computation.66 | convolution fusion | flops 4942790656 | bytes 28377600 | tf_op jit(solution)/shard_map/jvp(bf,sfh->sbh)/dot_general | solution.py:44
  96.2 0.4 convolution_add_fusion
  96.6 2.4 fusion.32
  99.0 1.1 reshape.166
  100.1 0.1 multiply_reduce_fusion.2
  100.3 2.4 collective-permute-start
  102.7 0.5 select_reduce_fusion
  103.1 0.3 collective-permute-done
  103.5 0.6 multiply_reduce_fusion.3
  104.1 1.3 collective-permute-start.1
  105.4 1.8 collective-permute-done.1
  107.3 0.3 fusion.54
  107.6 1.5 fusion.64
  109.1 1.1 add_any.42
  110.1 1.7 fusion.55
  111.8 2.3 fusion.23
  114.2 0.0 reduce-scatter.9.cloned.1.call-start
  114.2 0.7 reduce-scatter.9.cloned.1.call-update
  114.9 0.2 reduce-scatter.5.cloned.1.call-start
  115.2 0.4 convolution_bitcast_fusion.1
  115.6 1.4 fusion.43
  117.0 0.9 fusion.75
  117.9 12.7 %convolution_bitcast_fusion = f32[2,3136,512]{2,1,0:T(8,128)} fusion(f32[128,3136,1]{0,1,2:T(8,128)S(1)} %copy-done.5, f32[2,128,512]{2,1,0:T(8,128)S(1)} %get-tuple-element.100), kind=kOutput, calls=%fused_computation.16 | convolution fusion | flops 4932501504 | bytes 14974976 | tf_op jit(solution)/shard_map/transpose(jvp(bf,sfh->sbh))/dot_general | solution.py:44
  130.6 0.0 reduce-scatter.7.cloned.1.call-start
  130.7 22.7 %multiply_multiply_fusion = (f32[2,3136,512]{2,1,0:T(8,128)}, f32[3136,2,512]{2,0,1:T(8,128)}) fusion(f32[2,3136,512]{2,1,0:T(8,128)} %convolution_bitcast_fusion, f32[2,512]{1,0:T(2,128)S(1)} %bitcast.122, f32[2,3136]{1,0:T(2,128)S(1)} %bitcast.120, f32[1,2,3136,512]{3,2,1,0:T(8,128)} %param.35, f32[1,2,3136,512]{3,2,1,0:T(8,128)} %param.34), kind=kLoop, calls=%fused_computation | loop fusion | flops 12845056 | bytes 64254464 | tf_op jit(solution)/shard_map/transpose(jvp())/mul | solution.py:41
  153.4 0.0 all-reduce.12.cloned.1.call-start
  153.5 33.3 %copy.81 = f32[3136,2,512]{2,1,0:T(2,128)S(1)} copy(f32[3136,2,512]{2,0,1:T(8,128)} %get-tuple-element.109) | data formatting | bytes 25690112 | tf_op jit(solution)/shard_map/transpose(jvp(bf,sfh->sbh))/dot_general | solution.py:44
  186.9 11.5 fusion.80
  198.4 11.9 fusion.79
  210.3 56.6 %fusion.78 = (f32[32]{0:T(128)S(1)}, f32[128,32,20,20]{0,1,3,2:T(8,128)S(1)}) fusion(f32[128,32,20,20]{0,1,3,2:T(8,128)S(1)} %bitcast.114, f32[32]{0:T(128)S(1)} %bitcast.142, f32[128,64,9,9]{0,1,3,2:T(8,128)S(1)} %get-tuple-element.119, f32[64,32,4,4]{0,3,2,1:T(4,128)S(1)} %bitcast.137), kind=kOutput, calls=%fused_computation.108 | convolution fusion | flops 4094885888 | bytes 15892736 | tf_op jit(solution)/shard_map/transpose(jvp())/conv_general_dilated | solution.py:24
  267.0 540.6 %fusion.59 = f32[128,4,84,84]{0,1,3,2:T(4,128)S(1)} fusion(f32[128,32,20,20]{0,1,3,2:T(8,128)S(1)} %get-tuple-element.117, f32[32,4,8,8]{0,3,2,1:T(8,128)S(1)} %bitcast.116), kind=kOutput, calls=%fused_computation.78 | convolution fusion | flops 5033164800 | bytes 21037056 | tf_op jit(solution)/shard_map/transpose(jvp())/conv_general_dilated | solution.py:24
  807.6 6.4 slice.47
  814.0 0.9 copy-done.3
  814.9 5.0 collective-permute-start.2
  819.9 12.6 %fusion.68 = f32[64,64,3,3]{0,1,3,2:T(8,128)} fusion(f32[128,64,7,7]{0,1,3,2:T(8,128)S(1)} %get-tuple-element.121, f32[128,64,9,9]{0,1,3,2:T(8,128)S(1)} %copy-done.34, f32[64]{0:T(128)S(1)} %bitcast.140), kind=kOutput, calls=%fused_computation.103 | convolution fusion | flops 2777849856 | bytes 4407552 | tf_op jit(solution)/shard_map/transpose(jvp())/conv_general_dilated | solution.py:24
  832.5 18.0 %fusion.71 = f32[64,32,4,4]{0,1,3,2:T(8,128)} fusion(f32[128,64,9,9]{0,1,3,2:T(8,128)S(1)} %get-tuple-element.119, f32[128,32,20,20]{0,1,3,2:T(8,128)S(1)} %bitcast.114, f32[32]{0:T(128)S(1)} %bitcast.143), kind=kOutput, calls=%fused_computation.104 | convolution fusion | flops 4085055488 | bytes 9339008 | tf_op jit(solution)/shard_map/transpose(jvp())/conv_general_dilated | solution.py:24
  850.5 0.3 all-reduce.14.cloned.1.call-start
  850.8 0.0 reduce-scatter.11.cloned.1.call-done
  850.9 0.2 all-reduce.14.cloned.1.call-update
  851.8 0.1 reduce_sum.136
  851.9 0.1 fusion.74
  852.0 61.0 %fusion = f32[32,4,8,8]{0,1,3,2:T(4,128)S(1)} fusion(f32[128,32,20,20]{0,1,3,2:T(8,128)} %copy-done.2, f32[1,128,4,84,84]{1,2,4,3,0:T(4,128)} %param.23), kind=kOutput, calls=%fused_computation.2 | convolution fusion | flops 5033164800 | bytes 21037056 | tf_op jit(solution)/shard_map/transpose(jvp())/conv_general_dilated | solution.py:24
  913.0 44.3 %all-reduce.6 = (f32[]{:T(128)}, f32[32,4,8,8]{0,1,3,2:T(4,128)S(1)}, f32[32]{0:T(128)}, f32[64]{0:T(128)}, f32[64]{0:T(128)}, /*index=5*/f32[2,512]{1,0:T(2,128...) all-reduce(f32[]{:T(128)S(6)} %div.39, ...), channel_id=1, replica_groups=mesh['pair'=2,'group'=2,'rep'=8] {'pair','group','rep'}, use_global_device_ids=true, to_apply=%region_5.6 | all-reduce | flops 12339 | bytes 98712 | tf_op jit(solution)/shard_map/psum | solution.py:149
  957.3 0.7 copy.87
  958.0 21.8 %all-reduce.12.cloned.1.call-done = (f32[64,32,4,4]{0,1,3,2:T(8,128)}, f32[64,64,3,3]{0,1,3,2:T(8,128)}) async-done(((f32[64,32,4,4]{0,1,3,2:T(8,128)}, f32[64,64,3,3]{0,1,3,2:T(8,128)}), (f32[64,32,4,4]{0,1,3,2:T(8,128)}, f32[64,64,3,3]{0,1,3,2:T(8,128)})) %all-reduce.12.cloned.1.call-update) | async-done | bytes 278544 | tf_op jit(solution)/shard_map/psum | solution.py:149
  979.8 1.8 copy.88
  981.6 1.8 copy.89
  983.4 13.1 %slice_add_fusion = f32[128,2,84,84]{0,1,3,2:T(2,128)} fusion(f32[128,2,84,84]{0,1,3,2:T(2,128)} %collective-permute-done.2, f32[128,4,84,84]{0,1,3,2:T(4,128)} %copy-done.3), kind=kLoop, calls=%fused_computation.17 | loop fusion | flops 1806336 | bytes 21676032 | tf_op jit(solution)/shard_map/add | solution.py:133
  996.5 234.7 %all-reduce.14.cloned.1.call-done = (f32[2,784,512]{2,1,0:T(8,128)}, f32[2,784,512]{2,1,0:T(8,128)}, f32[128,969]{0,1:T(8,128)}, f32[128,969]{0,1:T(8,128)}) async-done(((f32[2,784,512]{2,1,0:T(8,128)}, f32[2,784,512]{2,1,0:T(8,128)}, f32[128,969]{0,1:T(8,128)}, f32[128,969]{0,1:T(8,128)}), (f32[2,784,512]{2,1,0:T(8,128)}, f32[2,784,512]{2,1,0:T(8,128)}, f32[128,969]{0,1:T(8,128)}, ...) | async-done | bytes 7414800 | tf_op jit(solution)/shard_map/psum | solution.py:144
  1231.2 4.1 copy.130
  1235.3 1.7 copy.131
  1237.0 0.8 copy.132
  1237.8 0.8 copy.133
  (99 shorter events, 0.6 us)
Async XLA Ops:
  8.0 57.1 %copy-start = (f32[1,64,64,3,3]{2,1,4,3,0:T(8,128)S(1)}, f32[1,64,64,3,3]{2,1,4,3,0:T(8,128)}, u32[]{:S(2)}) copy-start(f32[1,64,64,3,3]{2,1,4,3,0:T(8,128)} %param.32) | copy-start | bytes 442372
  8.0 842.8 %reduce-scatter.11.cloned.1.call-start = ((), (), s32[]{:S(2)}) async-start(), calls=%async_computation.7 | async-start | bytes 2498560 | tf_op jit(solution)/shard_map/reduce_scatter | solution.py:140
  8.8 44.0 %copy-start.22 = (f32[969]{0:T(1024)}, f32[969]{0:T(1024)S(1)}, u32[]{:S(2)}) copy-start(f32[969]{0:T(1024)S(1)} %multiply_add_fusion.2) | copy-start | bytes 11632
  10.3 42.5 %copy-start.27 = (f32[1,64,32,4,4]{1,4,3,2,0:T(4,128)S(1)}, f32[1,64,32,4,4]{1,4,3,2,0:T(4,128)}, u32[]{:S(2)}) copy-start(f32[1,64,32,4,4]{1,4,3,2,0:T(4,128)} %param.30) | copy-start | bytes 393220
  10.3 42.5 %copy-start.31 = (f32[1,32]{1,0:T(1,128)S(1)}, f32[1,32]{1,0:T(1,128)}, u32[]{:S(2)}) copy-start(f32[1,32]{1,0:T(1,128)} %param.29) | copy-start | bytes 388
  52.8 12.3 copy-start.6
  52.8 12.3 copy-start.26
  52.9 12.3 copy-start.29
  65.1 9.5 copy-start.33
  74.6 2.3 copy-start.15
  74.6 2.3 copy-start.23
  74.6 2.3 copy-start.24
  74.6 2.3 copy-start.16
  76.9 2.7 copy-start.4
  76.9 2.7 copy-start.13
  79.6 16.5 %slice-start.2 = ((f32[969]{0:T(1024)}), f32[51]{0:T(128)S(1)}, s32[]{:S(2)}) async-start(f32[969]{0:T(1024)} %copy-done.22), calls=%async_computation.12 | async-start | bytes 1024 | tf_op jit(solution)/shard_map/jvp()/slice | solution.py:50
  96.1 4.1 copy-start.14
  96.1 6.5 copy-start.20
  96.2 6.5 copy-start.21
  100.3 3.2 collective-permute-start
  104.1 3.1 collective-permute-start.1
  114.2 2.9 copy-start.8
  114.2 736.6 %reduce-scatter.9.cloned.1.call-start = ((), (), s32[]{:S(2)}) async-start(), calls=%async_computation.6 | async-start | bytes 2498560 | tf_op jit(solution)/shard_map/reduce_scatter | solution.py:137
  114.9 735.9 %reduce-scatter.5.cloned.1.call-start = ((), (), s32[]{:S(2)}) async-start(), calls=%async_computation.4 | async-start | bytes 16056320 | tf_op jit(solution)/shard_map/reduce_scatter | solution.py:135
  115.2 2.8 copy-start.5
  130.6 720.2 %reduce-scatter.7.cloned.1.call-start = ((), (), s32[]{:S(2)}) async-start(), calls=%async_computation.5 | async-start | bytes 16056320 | tf_op jit(solution)/shard_map/reduce_scatter | solution.py:136
  153.4 826.3 %all-reduce.12.cloned.1.call-start = ((), (), s32[]{:S(2)}) async-start(), calls=%async_computation.8 | async-start | bytes 1114112 | tf_op jit(solution)/shard_map/psum | solution.py:149
  153.5 33.4 %copy-start.9 = (f32[128,64,7,7]{0,1,3,2:T(8,128)S(1)}, f32[128,64,7,7]{0,1,3,2:T(8,128)}, u32[]{:S(2)}) copy-start(f32[128,64,7,7]{0,1,3,2:T(8,128)} %get-tuple-element.113) | copy-start | bytes 4816900
  153.5 56.8 %slice-start = ((s8[6553600]{0:T(1024)(128)(4,1)}), s8[4194304]{0:T(1024)(128)(4,1)S(1)}, s32[]{:S(2)}) async-start(s8[6553600]{0:T(1024)(128)(4,1)} %bitcast.113), calls=%async_computation.10 | async-start | bytes 8388608
  186.8 11.5 copy-start.30
  186.9 11.5 copy-start.34
  186.9 23.4 %slice-start.1 = ((s8[6553600]{0:T(1024)(128)(4,1)}), s8[2359296]{0:T(1024)(128)(4,1)S(1)}, s32[]{:S(2)}) async-start(s8[6553600]{0:T(1024)(128)(4,1)} %bitcast.113), calls=%async_computation.11 | async-start | bytes 4718592
  198.4 11.9 copy-start.28
  198.4 11.9 copy-start.32
  210.3 56.6 %copy-start.10 = (f32[1,32,4,8,8]{1,4,3,2,0:T(8,128)S(1)}, f32[1,32,4,8,8]{1,4,3,2,0:T(8,128)}, u32[]{:S(2)}) copy-start(f32[1,32,4,8,8]{1,4,3,2,0:T(8,128)} %param.28) | copy-start | bytes 98308
  267.0 540.6 %copy-start.2 = (f32[128,32,20,20]{0,1,3,2:T(8,128)}, f32[128,32,20,20]{0,1,3,2:T(8,128)S(1)}, u32[]{:S(2)}) copy-start(f32[128,32,20,20]{0,1,3,2:T(8,128)S(1)} %get-tuple-element.117) | copy-start | bytes 19660804
  807.6 7.3 copy-start.3
  814.9 168.5 %collective-permute-start.2 = (f32[128,2,84,84]{0,1,3,2:T(2,128)}, f32[128,2,84,84]{0,1,3,2:T(2,128)}, u32[]{:S(2)}, u32[]{:S(2)}) collective-permute-start(f32[128,2,84,84]{0,1,3,2:T(2,128)} %slice.47), channel_id=1, source_target_pairs={{0,16},{1,17},{2,18},{3,19},{4,20},{5,21},{6,22},{7,23},{8,24},{9,... | collective-permute-start | bytes 21676040 | tf_op jit(solution)/shard_map/ppermute | solution.py:16
  850.5 380.7 %all-reduce.14.cloned.1.call-start = ((), (), s32[]{:S(2)}) async-start(), calls=%async_computation.9 | async-start | bytes 14843904 | tf_op jit(solution)/shard_map/psum | solution.py:144
  850.9 0.9 copy-start.18
  850.9 1.0 copy-start.19
  850.9 1.0 copy-start.17
  850.9 1.0 copy-start.25
  1231.2 4.1 copy-start.7
  1231.2 7.3 copy-start.1
  1235.3 1.7 copy-start.12
  1235.3 2.5 copy-start.11
Sparse Core Ops, SparseCore 0:
  114.3 32.8 reduce-scatter.10
  149.8 30.7 reduce-scatter.8
  183.4 100.7 reduce-scatter.4
  286.9 100.7 reduce-scatter.6
Sparse Core Ops, SparseCore 1:
  850.6 129.1 all-reduce.11
  984.8 246.3 all-reduce.13
where the time goes:
time: 1250 us
  matrix products  812 us (65%)
  waiting for transfers between devices  260 us (21%)
  local copies, waits for them, and re-layouts  57.8 us (5%)
  other arithmetic  46 us (4%)
  blocking collectives  44.3 us (4%)
  between operations  16.8 us (1%)
    conv_general_dilated x9, matrix products, conv_layer(): lax.conv_general_dilated(inputs, kernel, (stride, stride), 'VALID', dimen...  765 us
    psum x1, waiting for transfers between devices, local(): summed = lax.psum((summed[0], summed[1], summed[2], summed[3]), 'rep')  235 us
    psum x1, blocking collectives, local(): lax.psum((weight_grads[0], weight_grads[1], weight_grads[2], weight_grads...  44.3 us
    dot_general x3, matrix products, network(): jnp.einsum('bf,sfh->sbh', features, hidden_w, precision=HIGHEST)  40.7 us
    dot_general x1, local copies, waits for them, and re-layouts, network(): jnp.einsum('bf,sfh->sbh', features, hidden_w, precision=HIGHEST)  33.3 us
  transfers between devices with their start and end apart: 9, of which 4 were waited for; matrix products, arithmetic and copies ran while one was open for 65% of the time, Pallas kernels for 0%

commit v1 on v0

v1 whole, which is shorter than its diff:
```python
import jax
import jax.numpy as jnp
from jax import lax
from jax.experimental import pallas as pl
from jax.experimental.pallas import tpu as pltpu
from jax.sharding import PartitionSpec as P

BF = jnp.bfloat16
F32 = jnp.float32
NN=(((1,),(0,)),((),()))
NT=(((1,),(1,)),((),()))
TN=(((0,),(0,)),((),()))

def split(v):
    hi = v.astype(BF)
    return hi, (v - hi.astype(F32)).astype(BF)

def dot(a, b, dims=NN):
    return lax.dot_general(a, b, dims, preferred_element_type=F32)

def dot3(a, b, dims=NN):
    ah, al = a; bh, bl = b
    return dot(ah, bh, dims) + (dot(ah, bl, dims) + dot(al, bh, dims))

def silu(v):
    return v * jax.nn.sigmoid(v)

def fwd_weights(k1, k2, k3):
    a = jnp.transpose(k1, (0, 2, 3, 1)).reshape(32, 2, 4, 32)
    a = jnp.stack([jnp.pad(a, ((0, 0), (0, 0), (0, 0), (16 * w, 32 - 16 * w))) for w in range(3)])
    w1 = jnp.transpose(a, (2, 0, 1, 3, 4)).reshape(192, 256)
    w2 = jnp.transpose(k2.reshape(64, 32, 2, 2, 4), (2, 0, 3, 4, 1)).reshape(128, 256)
    a = jnp.transpose(k3, (2, 0, 3, 1)).reshape(3, 64, 192)
    a = jnp.stack([jnp.pad(a, ((0, 0), (0, 0), (64 * w, 64 - 64 * w))) for w in range(2)])
    w3 = jnp.transpose(a, (1, 0, 2, 3)).reshape(384, 256)
    return w1, w2, w3

def fwd_kernel(x_ref, w1_ref, w2_ref, w3_ref, b1_ref, b2_ref, b3_ref, pre1_ref, pre2_ref, pre3_ref, f_ref,
               xh, xl, ws1, top1, top2, acc3, h1h, h1l, h2h, h2l):
    j = pl.program_id(0)
    @pl.when(j == 0)
    def _():
        xh[:, 336:, :] = jnp.zeros((4, 16, 128), BF)
        xl[:, 336:, :] = jnp.zeros((4, 16, 128), BF)
        top1[...] = jnp.zeros_like(top1)
        top2[...] = jnp.zeros_like(top2)
        acc3[...] = jnp.zeros_like(acc3)
        hi, lo = split(w1_ref[...])
        ws1[0] = hi
        ws1[1] = lo
        h2h[:, 576:, :] = jnp.zeros((9, 64, 128), BF)
        h2l[:, 576:, :] = jnp.zeros((9, 64, 128), BF)
    v = x_ref[...]
    hi = v.astype(BF)
    xh[:, 0:336, :] = hi
    xl[:, 0:336, :] = (v - hi.astype(F32)).astype(BF)
    rh = jnp.concatenate([xh[:, 48 * i:48 * i + 64, :].reshape(256, 128) for i in range(7)], axis=1)
    rl = jnp.concatenate([xl[:, 48 * i:48 * i + 64, :].reshape(256, 128) for i in range(7)], axis=1)
    r = dot3((ws1[0], ws1[1]), (rh, rl))
    out = top1[...] + r[96:]
    top1[...] = r[:96]
    b1 = b1_ref[...]
    row = jnp.maximum(j - 1, 0)
    for i in range(7):
        n = 96 if i < 6 else 64
        p = out[:n, 128 * i:128 * i + 128] + b1[:n]
        pre1_ref[0, 96 * i:96 * i + n, :] = p
        hh, hl = split(silu(p))
        h1h[row, 96 * i:96 * i + n, :] = hh
        h1l[row, 96 * i:96 * i + n, :] = hl

    @pl.when(j == pl.num_programs(0) - 1)
    def _():
        w2 = split(w2_ref[...])
        b2 = b2_ref[...]
        def step2(y, carry):
            rh = jnp.concatenate([h1h[pl.ds(2 * y, 2), 64 * i:64 * i + 128, :].reshape(256, 128) for i in range(9)], axis=1)
            rl = jnp.concatenate([h1l[pl.ds(2 * y, 2), 64 * i:64 * i + 128, :].reshape(256, 128) for i in range(9)], axis=1)
            r = dot3(w2, (rh, rl))
            o = top2[...] + r[64:]
            top2[...] = r[:64]
            row = jnp.maximum(y - 1, 0)
            for i in range(9):
                p = o[:, 128 * i:128 * i + 128] + b2
                pre2_ref[row, 64 * i:64 * i + 64, :] = p
                hh, hl = split(silu(p))
                h2h[row, 64 * i:64 * i + 64, :] = hh
                h2l[row, 64 * i:64 * i + 64, :] = hl
            return carry
        lax.fori_loop(0, 10, step2, 0)
        w3 = split(w3_ref[...])
        b3 = b3_ref[...]
        def step3(y, carry):
            rh = jnp.concatenate([h2h[y, 128 * i:128 * i + 256, :] for i in range(4)], axis=1)
            rl = jnp.concatenate([h2l[y, 128 * i:128 * i + 256, :] for i in range(4)], axis=1)
            r = dot3(w3, (rh, rl))
            for ky in range(3):
                for i in range(4):
                    acc3[y - ky + 2, 128 * i:128 * i + 128, :] += r[128 * ky:128 * ky + 128, 128 * i:128 * i + 128]
            return carry
        lax.fori_loop(0, 9, step3, 0)
        for y in range(7):
            for x in range(7):
                p = acc3[y + 2, 64 * x:64 * x + 64, :] + b3
                pre3_ref[pl.ds(y * 7 + x, 64, stride=49), :] = p
                f_ref[pl.ds(y * 7 + x, 64, stride=49), :] = silu(p)

def forward(x, w1, w2, w3, b1, b2, b3):
    full = lambda *s: pl.BlockSpec(s, lambda j: (0,) * len(s))
    return pl.pallas_call(
        fwd_kernel,
        grid=(21,),
        in_specs=[pl.BlockSpec((4, 336, 128), lambda j: (j, 0, 0)), full(192, 256), full(128, 256), full(384, 256),
                  full(96, 128), full(64, 128), full(64, 128)],
        out_specs=[pl.BlockSpec((1, 640, 128), lambda j: (jnp.maximum(j - 1, 0), 0, 0)), full(9, 576, 128),
                   full(3136, 128), full(3136, 128)],
        out_shape=[jax.ShapeDtypeStruct((20, 640, 128), F32), jax.ShapeDtypeStruct((9, 576, 128), F32),
                   jax.ShapeDtypeStruct((3136, 128), F32), jax.ShapeDtypeStruct((3136, 128), F32)],
        scratch_shapes=[pltpu.VMEM((4, 352, 128), BF), pltpu.VMEM((4, 352, 128), BF), pltpu.VMEM((2, 192, 256), BF),
                        pltpu.VMEM((96, 896), F32), pltpu.VMEM((64, 1152), F32), pltpu.VMEM((11, 512, 128), F32),
                        pltpu.VMEM((20, 640, 128), BF), pltpu.VMEM((20, 640, 128), BF),
                        pltpu.VMEM((9, 640, 128), BF), pltpu.VMEM((9, 640, 128), BF)],
        compiler_params=pltpu.CompilerParams(vmem_limit_bytes=60 * 2**20),
    )(x, w1, w2, w3, b1, b2, b3)


def dsilu(v):
    s = jax.nn.sigmoid(v)
    return s * (1.0 + v * (1.0 - s))

def bwd_weights(k1, k2, k3):
    a = jnp.transpose(k1.reshape(32, 2, 2, 2, 4, 2, 4), (1, 4, 6, 2, 3, 5, 0))
    cols = []
    for q in range(4):
        parts = []
        for xb in range(3):
            o = xb - q + 1
            parts.append(a[:, :, :, :, ::-1, o, :] if 0 <= o <= 1 else jnp.zeros((2, 4, 4, 2, 2, 32), F32))
        cols.append(jnp.stack(parts, axis=2))
    w1 = jnp.stack(cols, axis=6).reshape(192, 256)
    a = jnp.transpose(k2.reshape(64, 32, 2, 2, 2, 2), (3, 5, 1, 2, 4, 0))[:, :, :, ::-1, ::-1]
    w2 = a.reshape(128, 256)
    cols = []
    for q in range(4):
        parts = []
        for w in range(2):
            kx = w + 2 - q
            parts.append(jnp.transpose(k3[:, :, :, kx], (2, 1, 0)) if 0 <= kx <= 2 else jnp.zeros((3, 64, 64), F32))
        cols.append(jnp.stack(parts, axis=1))
    w3 = jnp.stack(cols, axis=3).reshape(384, 256)
    return w1, w2, w3

def bwd_kernel(x_ref, pre1_ref, pre2_ref, pre3_ref, df_ref, w1_ref, w2_ref, w3_ref,
               lo_ref, up_ref, g1_ref, g2_ref, g3_ref, gb1_ref, gb2_ref, gb3_ref,
               xh, xl, ws1, d3f, d3h, d3l, d2h, d2l, d1h, d1l, h2h, h2l, acc2, a1, a2, a3):
    j = pl.program_id(0)
    @pl.when(j == 0)
    def _():
        xh[:, 336:, :] = jnp.zeros((4, 16, 128), BF)
        xl[:, 336:, :] = jnp.zeros((4, 16, 128), BF)
        hi, lo = split(w1_ref[...])
        ws1[0] = hi
        ws1[1] = lo
        for ref in (d3h, d3l, d2h, d2l, acc2, a1, a2, a3):
            ref[...] = jnp.zeros_like(ref)
        for ref in (d1h, d1l):
            ref[0] = jnp.zeros((704, 128), BF)
            ref[21] = jnp.zeros((704, 128), BF)
            ref[:, 0:32, :] = jnp.zeros((22, 32, 128), BF)
            ref[:, 672:704, :] = jnp.zeros((22, 32, 128), BF)
        d3f[...] = df_ref[...] * dsilu(pre3_ref[...])
        total = jnp.zeros((64, 128), F32)
        for y in range(7):
            for x in range(7):
                d = d3f[pl.ds(y * 7 + x, 64, stride=49), :]
                total = total + d
                hi, lo = split(d)
                d3h[y + 2, 64 * (x + 2):64 * (x + 3), :] = hi
                d3l[y + 2, 64 * (x + 2):64 * (x + 3), :] = lo
        gb3_ref[...] = jnp.sum(total, axis=1, keepdims=True)
        w3 = split(w3_ref[...])
        h2h[:, 576:, :] = jnp.zeros((9, 64, 128), BF)
        h2l[:, 576:, :] = jnp.zeros((9, 64, 128), BF)
        def split2(y, c):
            hi, lo = split(silu(pre2_ref[y]))
            h2h[y, 0:576, :] = hi
            h2l[y, 0:576, :] = lo
            return c
        lax.fori_loop(0, 9, split2, 0)
        def dgrad3(y, c):
            rh = jnp.concatenate([d3h[y + 2, 128 * i:128 * i + 256, :] for i in range(5)], axis=1)
            rl = jnp.concatenate([d3l[y + 2, 128 * i:128 * i + 256, :] for i in range(5)], axis=1)
            r = dot3(w3, (rh, rl))
            for ky in range(3):
                for i in range(5):
                    acc2[y + ky, 128 * i:128 * i + 128, :] += r[128 * ky:128 * ky + 128, 128 * i:128 * i + 128]
            return c
        lax.fori_loop(0, 7, dgrad3, 0)
        def wgrad3(y, c):
            def lhs(ref):
                return jnp.concatenate([jnp.concatenate([ref[y - ky + 2, 128 * (i + 1):128 * (i + 2), :] for i in range(4)], axis=1) for ky in range(3)], axis=0)
            def rhs(ref):
                return jnp.concatenate([ref[y, 128 * i:128 * i + 256, :] for i in range(4)], axis=1)
            a3[...] += dot3((lhs(d3h), lhs(d3l)), (rhs(h2h), rhs(h2l)), NT)
            return c
        lax.fori_loop(0, 9, wgrad3, 0)
        for ky in range(3):
            g3_ref[ky] = a3[128 * ky:128 * ky + 64, 0:192] + a3[128 * ky + 64:128 * ky + 128, 64:256]
        w2 = split(w2_ref[...])
        def step2(y, total):
            for x in range(9):
                d = acc2[y, 64 * x:64 * x + 64, :] * dsilu(pre2_ref[y, 64 * x:64 * x + 64, :])
                total = total + d
                hi, lo = split(d)
                d2h[y + 1, 64 * (x + 1):64 * (x + 2), :] = hi
                d2l[y + 1, 64 * (x + 1):64 * (x + 2), :] = lo
            return total
        total = lax.fori_loop(0, 9, step2, jnp.zeros((64, 128), F32))
        gb2_ref[...] = jnp.sum(total, axis=1, keepdims=True)
        def block2(y, total):
            rh = jnp.concatenate([d2h[pl.ds(y, 2), 64 * i:64 * i + 128, :].reshape(256, 128) for i in range(10)], axis=1)
            rl = jnp.concatenate([d2l[pl.ds(y, 2), 64 * i:64 * i + 128, :].reshape(256, 128) for i in range(10)], axis=1)
            r = dot3(w2, (rh, rl))
            h1h, h1l = [], []
            for py in range(2):
                rowh, rowl = [], []
                for i in range(10):
                    p = pre1_ref[2 * y + py, 64 * i:64 * i + 64, :]
                    s = jax.nn.sigmoid(p)
                    h = p * s
                    d = r[64 * py:64 * py + 64, 128 * i:128 * i + 128] * (s * (1.0 + p * (1.0 - s)))
                    total = total + d[0:32] + d[32:64]
                    hi, lo = split(d)
                    d1h[2 * y + py + 1, 64 * i + 32:64 * i + 96, :] = hi
                    d1l[2 * y + py + 1, 64 * i + 32:64 * i + 96, :] = lo
                    hi, lo = split(h)
                    rowh.append(hi)
                    rowl.append(lo)
                h1h.append(rowh)
                h1l.append(rowl)
            def lhs(ref):
                return jnp.concatenate([jnp.concatenate([ref[y + 1 - h, 64 * (i + 1):64 * (i + 2), :] for i in range(9)], axis=1) for h in range(2)], axis=0)
            def rhs(rows):
                return jnp.concatenate([jnp.concatenate([rows[0][i], rows[0][i + 1], rows[1][i], rows[1][i + 1]], axis=0) for i in range(9)], axis=1)
            a2[...] += dot3((lhs(d2h), lhs(d2l)), (rhs(h1h), rhs(h1l)), NT)
            return total
        total = lax.fori_loop(0, 10, block2, jnp.zeros((32, 128), F32))
        gb1_ref[...] = jnp.sum(total, axis=1, keepdims=True)
        g2_ref[...] = a2[...]
    v = x_ref[...]
    hi = v.astype(BF)
    xh[:, 0:336, :] = hi
    xl[:, 0:336, :] = (v - hi.astype(F32)).astype(BF)
    rh = jnp.concatenate([d1h[pl.ds(j, 2), 96 * i:96 * i + 128, :].reshape(256, 128) for i in range(7)], axis=1)
    rl = jnp.concatenate([d1l[pl.ds(j, 2), 96 * i:96 * i + 128, :].reshape(256, 128) for i in range(7)], axis=1)
    r = dot3((ws1[0], ws1[1]), (rh, rl))
    for ky in range(4):
        for i in range(7):
            lo_ref[ky, 24 * i:24 * i + 24, :] = r[24 * ky:24 * ky + 24, 128 * i:128 * i + 128]
            up_ref[ky, 24 * i:24 * i + 24, :] = r[96 + 24 * ky:96 + 24 * ky + 24, 128 * i:128 * i + 128]
    def lhs(ref):
        return jnp.concatenate([jnp.concatenate([ref[j + 1 - h, 96 * i + 32:96 * i + 128, :] for i in range(7)], axis=1) for h in range(2)], axis=0)
    def rhs(ref):
        return jnp.concatenate([ref[:, 48 * i:48 * i + 64, :].reshape(256, 128) for i in range(7)], axis=1)
    a1[...] += dot3((lhs(d1h), lhs(d1l)), (rhs(xh), rhs(xl)), NT)
    @pl.when(j == pl.num_programs(0) - 1)
    def _():
        for h in range(2):
            for ky in range(4):
                g = a1[96 * h:96 * h + 32, 64 * ky:64 * ky + 32]
                g = g + a1[96 * h + 32:96 * h + 64, 64 * ky + 16:64 * ky + 48]
                g = g + a1[96 * h + 64:96 * h + 96, 64 * ky + 32:64 * ky + 64]
                g1_ref[4 * h + ky] = g

def backward(x, pre1, pre2, pre3, df, w1, w2, w3):
    full = lambda *s: pl.BlockSpec(s, lambda j: (0,) * len(s))
    one = lambda *s: pl.BlockSpec(s, lambda j: (0,) * len(s), pipeline_mode=pl.Buffered(1))
    sds = lambda *s: jax.ShapeDtypeStruct(s, F32)
    half = pl.BlockSpec((4, 168, 128), lambda j: (j, 0, 0))
    return pl.pallas_call(
        bwd_kernel,
        grid=(21,),
        in_specs=[pl.BlockSpec((4, 336, 128), lambda j: (j, 0, 0)), one(20, 640, 128), one(9, 576, 128), one(3136, 128), one(3136, 128),
                  one(192, 256), one(128, 256), one(384, 256)],
        out_specs=[half, half, full(8, 32, 32), full(128, 256), full(3, 64, 192), full(32, 1), full(64, 1), full(64, 1)],
        out_shape=[sds(84, 168, 128), sds(84, 168, 128), sds(8, 32, 32), sds(128, 256), sds(3, 64, 192), sds(32, 1), sds(64, 1), sds(64, 1)],
        scratch_shapes=[pltpu.VMEM((4, 352, 128), BF), pltpu.VMEM((4, 352, 128), BF), pltpu.VMEM((2, 192, 256), BF),
                        pltpu.VMEM((3136, 128), F32), pltpu.VMEM((11, 768, 128), BF), pltpu.VMEM((11, 768, 128), BF),
                        pltpu.VMEM((11, 704, 128), BF), pltpu.VMEM((11, 704, 128), BF),
                        pltpu.VMEM((22, 704, 128), BF), pltpu.VMEM((22, 704, 128), BF),
                        pltpu.VMEM((9, 640, 128), BF), pltpu.VMEM((9, 640, 128), BF),
                        pltpu.VMEM((9, 640, 128), F32), pltpu.VMEM((192, 256), F32), pltpu.VMEM((128, 256), F32), pltpu.VMEM((384, 256), F32)],
        compiler_params=pltpu.CompilerParams(vmem_limit_bytes=60 * 2**20),
    )(x, pre1, pre2, pre3, df, w1, w2, w3)

def torso_grads(g1, g2, g3):
    k1 = jnp.transpose(g1.reshape(8, 32, 8, 4), (1, 3, 0, 2))
    k2 = jnp.transpose(g2.reshape(2, 64, 2, 4, 32), (1, 4, 0, 2, 3)).reshape(64, 32, 4, 4)
    k3 = jnp.transpose(g3.reshape(3, 64, 3, 64), (1, 3, 0, 2))
    return k1, k2, k3

ATOMS, ACTIONS, PAD = 51, 18, 56
STEPS = 7

def column(row, lanes):
    tall = jnp.transpose(jnp.broadcast_to(row, (128, row.shape[1])))
    return jnp.concatenate([tall] * (lanes // 128), axis=1)

def noisy(mean_ref, sigma_ref, nin_ref, nout_ref, s):
    return mean_ref[s] + sigma_ref[s] * (column(nin_ref[0, s:s + 1, :], 512) * nout_ref[s:s + 1, :])

def mask_of(chosen, a):
    return jnp.where(chosen == a, 1.0 - 1.0 / ACTIONS, -1.0 / ACTIONS)

def hid_kernel(f_ref, m_ref, s_ref, nin_ref, nout_ref, hb_ref, wo_ref, bo_ref, c_ref, pl_ref, pw_ref,
               h_ref, g_ref, logp_ref, dist_ref, acc):
    j = pl.program_id(0)
    @pl.when(j == 0)
    def _():
        acc[...] = jnp.zeros_like(acc)
    f = split(f_ref[...])
    for s in range(2):
        w = split(noisy(m_ref, s_ref, nin_ref, nout_ref, s))
        acc[:, 512 * s:512 * s + 512] += dot3(f, w, TN)
    @pl.when(j == pl.num_programs(0) - 1)
    def _():
        h = acc[...] + hb_ref[...]
        h_ref[...] = h
        g = silu(h)
        g_ref[...] = g
        gt = jnp.transpose(g)
        wo = wo_ref[...]
        v = dot3(split(wo[0]), split(gt[:512])) + bo_ref[0]
        a = dot3(split(wo[1:].reshape(ACTIONS * PAD, 512)), split(gt[512:]))
        chosen = c_ref[...]
        z = v
        for i in range(ACTIONS):
            z = z + mask_of(chosen, i) * (a[PAD * i:PAD * i + PAD] + bo_ref[i + 1])
        row = lax.broadcasted_iota(jnp.int32, (PAD, 128), 0)
        z = jnp.where(row < ATOMS, z, -1e30)
        top = jnp.max(z, axis=0, keepdims=True)
        e = jnp.exp(z - top)
        tot = jnp.sum(e, axis=0, keepdims=True)
        logp_ref[...] = (z - top) - jnp.log(tot)
        p = e / tot
        dist = jnp.zeros((PAD, 128), F32)
        for i in range(ATOMS):
            lower = pl_ref[i:i + 1, :]
            share = pw_ref[i:i + 1, :]
            pi = p[i:i + 1, :]
            dist = dist + jnp.where(row == lower, pi * (1.0 - share), 0.0) + jnp.where(row == lower + 1, pi * share, 0.0)
        dist_ref[...] = dist

def hidden(f, m, s, nin, nout, hb, wo, bo, c, plow, pw):
    full = lambda *t: pl.BlockSpec(t, lambda j: (0,) * len(t))
    sds = lambda *t: jax.ShapeDtypeStruct(t, F32)
    k = 3136 // STEPS
    wspec = pl.BlockSpec((2, k, 512), lambda j: (0, j, 0))
    return pl.pallas_call(
        hid_kernel, grid=(STEPS,),
        in_specs=[pl.BlockSpec((k, 128), lambda j: (j, 0)), wspec, wspec, pl.BlockSpec((1, 2, k), lambda j: (j, 0, 0)), full(2, 512), full(1, 1024),
                  full(19, PAD, 512), full(19, PAD, 128), full(1, 128), full(ATOMS, 128), full(ATOMS, 128)],
        out_specs=[full(128, 1024), full(128, 1024), full(PAD, 128), full(PAD, 128)],
        out_shape=[sds(128, 1024), sds(128, 1024), sds(PAD, 128), sds(PAD, 128)],
        scratch_shapes=[pltpu.VMEM((128, 1024), F32)],
        compiler_params=pltpu.CompilerParams(vmem_limit_bytes=60 * 2**20),
    )(f, m, s, nin, nout, hb, wo, bo, c, plow, pw)

def hid_bwd_kernel(t_ref, logp_ref, h_ref, m_ref, s_ref, nin_ref, nout_ref, wo_ref, c_ref,
                   df_ref, dp_ref, dz_ref, loss_ref, bo_ref, dth, dtl):
    j = pl.program_id(0)
    @pl.when(j == 0)
    def _():
        t = t_ref[...]
        logp = logp_ref[...]
        chosen = c_ref[...]
        row = lax.broadcasted_iota(jnp.int32, (PAD, 128), 0)
        d = (jnp.exp(logp) * jnp.sum(t, axis=0, keepdims=True) - t) * (1.0 / 128)
        loss = -jnp.sum(jnp.where(row < ATOMS, t * logp, 0.0), axis=1, keepdims=True) * (1.0 / 128)
        loss_ref[...] = jnp.sum(loss, axis=0, keepdims=True)
        dz_ref[...] = jnp.where(row == ATOMS, chosen.astype(F32), d)
        bo_ref[0] = jnp.sum(d, axis=1, keepdims=True)
        parts = []
        for i in range(ACTIONS):
            p = mask_of(chosen, i) * d
            bo_ref[i + 1] = jnp.sum(p, axis=1, keepdims=True)
            parts.append(p)
        da = jnp.concatenate(parts, axis=0)
        wo = wo_ref[...]
        g0 = dot3(split(d), split(wo[0]), TN)
        g1 = dot3(split(da), split(wo[1:].reshape(ACTIONS * PAD, 512)), TN)
        for s, g in enumerate((g0, g1)):
            dp = g * dsilu(h_ref[:, 512 * s:512 * s + 512])
            dp_ref[:, 512 * s:512 * s + 512] = dp
            hi, lo = split(jnp.transpose(dp))
            dth[s] = hi
            dtl[s] = lo
    out = None
    for s in range(2):
        w = split(noisy(m_ref, s_ref, nin_ref, nout_ref, s))
        r = dot3(w, (dth[s], dtl[s]))
        out = r if out is None else out + r
    df_ref[...] = out

def hidden_bwd(t, logp, h, m, s, nin, nout, wo, c):
    full = lambda *u: pl.BlockSpec(u, lambda j: (0,) * len(u))
    sds = lambda *u: jax.ShapeDtypeStruct(u, F32)
    k = 3136 // STEPS
    wspec = pl.BlockSpec((2, k, 512), lambda j: (0, j, 0))
    return pl.pallas_call(
        hid_bwd_kernel, grid=(STEPS,),
        in_specs=[full(PAD, 128), full(PAD, 128), full(128, 1024), wspec, wspec, pl.BlockSpec((1, 2, k), lambda j: (j, 0, 0)), full(2, 512),
                  full(19, PAD, 512), full(1, 128)],
        out_specs=[pl.BlockSpec((k, 128), lambda j: (j, 0)), full(128, 1024), full(PAD, 128), full(1, 1), full(19, PAD, 1)],
        out_shape=[sds(3136, 128), sds(128, 1024), sds(PAD, 128), sds(1, 1), sds(19, PAD, 1)],
        scratch_shapes=[pltpu.VMEM((2, 512, 128), BF), pltpu.VMEM((2, 512, 128), BF)],
        compiler_params=pltpu.CompilerParams(vmem_limit_bytes=60 * 2**20),
    )(t, logp, h, m, s, nin, nout, wo, c)

def online_only(value):
    other = lax.ppermute(value, "pair", [(0, 1)])
    return jnp.where(lax.axis_index("pair") == 0, value, other)

def exchange(parts):
    groups = lax.axis_size("group")
    p, g = lax.axis_index("pair"), lax.axis_index("group")
    got = []
    for k in range(groups):
        to = (g + k) % groups
        mine = parts(0, to)
        if k:
            mine = lax.ppermute(mine, ("pair", "group"), [(i, (i + k) % groups) for i in range(groups)])
        theirs = lax.ppermute(parts(1, to), ("pair", "group"), [(i, groups + (i + k) % groups) for i in range(groups)])
        got.append(jnp.where(p == 0, mine, theirs))
    return got

HIGH = lax.Precision.HIGH

def local(states, actions, proj_lower, proj_upper, proj_weight, first_kernel, first_bias, second_kernel, second_bias,
          third_kernel, third_bias, hidden_mean, hidden_sigma, hidden_bias_mean, hidden_bias_sigma, head_mean, head_sigma,
          head_bias_mean, head_bias_sigma, hidden_noise_in, hidden_noise_out, head_noise_in, head_noise_out):
    pair = lax.axis_index("pair")
    groups = lax.axis_size("group")
    shards = 2 * groups
    n_in, n_out, e_in, e_out = hidden_noise_in[0], hidden_noise_out[0], head_noise_in[0], head_noise_out[0]
    noise = online_only(jnp.concatenate([v.reshape(-1) for v in (n_in, n_out, e_in, e_out)]))
    on_in = noise[:6272].reshape(2, 3136)
    on_out = noise[6272:7296].reshape(2, 512)
    on_ein = noise[7296:8320].reshape(2, 512)
    on_eout = noise[8320:]
    shard = pair * groups + lax.axis_index("group")

    x = jnp.transpose(states[0], (2, 3, 1, 0)).reshape(84, 336, 128)
    k1, k2, k3 = first_kernel[0], second_kernel[0], third_kernel[0]
    spread = lambda b, n: jnp.broadcast_to(jnp.tile(b, n)[:, None], (b.shape[0] * n, 128))
    pre1, pre2, pre3, feats = forward(x, *fwd_weights(k1, k2, k3), spread(first_bias[0], 3), spread(second_bias[0], 1), spread(third_bias[0], 1))
    feat_q = 3136 // shards
    f_got = exchange(lambda p, g: lax.dynamic_slice_in_dim(feats, (p * groups + g) * feat_q, feat_q, axis=0))

    wide = lambda v: jnp.pad(v.reshape(19, ATOMS, -1), ((0, 0), (0, PAD - ATOMS), (0, 0)))
    e_rows = jnp.concatenate([e_in[0:1], jnp.broadcast_to(e_in[1:2], (ACTIONS, 512))])
    wo = wide(head_mean[0].T) + wide(head_sigma[0].T) * (e_rows[:, None, :] * wide(e_out[:, None]))
    bo = jnp.broadcast_to(wide((head_bias_mean[0] + head_bias_sigma[0] * e_out)[:, None]), (19, PAD, 128))
    hb = (hidden_bias_mean[0] + hidden_bias_sigma[0] * n_out).reshape(1, 1024)
    nin = jnp.transpose(n_in.reshape(2, STEPS, 3136 // STEPS), (1, 0, 2))
    h, hid, logp, dist = hidden(feats, hidden_mean[0], hidden_sigma[0], nin, n_out, hb, wo, bo, actions, proj_lower.T, proj_weight.T)
    hid_q = 512 // shards
    hid_got = exchange(lambda p, g: lax.dynamic_slice_in_dim(hid.reshape(128, 2, 512), (p * groups + g) * hid_q, hid_q, axis=2))
    target = lax.ppermute(dist, "pair", [(1, 0)])
    df, dpre, dz, loss, bo_sum = hidden_bwd(target, logp, h, hidden_mean[0], hidden_sigma[0], nin, n_out, wo, actions)
    d_got = exchange(lambda p, g: jnp.concatenate([dpre, dz.T, jnp.zeros((128, 72), F32)], axis=1))
    d_all = jnp.concatenate(d_got, axis=0)
    f_all = jnp.concatenate(f_got, axis=1)
    hid_all = jnp.concatenate(hid_got, axis=0)
    part_hidden = jnp.einsum("fb,bsh->sfh", f_all, d_all[:, :1024].reshape(-1, 2, 512), precision=HIGH)
    dz_all = d_all[:, 1024:1024 + ATOMS]
    picked = d_all[:, 1024 + ATOMS]
    mask = jnp.where(picked[None, :] == jnp.arange(ACTIONS, dtype=F32)[:, None], 1.0 - 1.0 / ACTIONS, -1.0 / ACTIONS)
    da = (mask[:, None, :] * dz_all.T[None]).reshape(ACTIONS * ATOMS, -1)
    part_head = jnp.concatenate([jnp.dot(dz_all.T, hid_all[:, 0], precision=HIGH), jnp.dot(da, hid_all[:, 1], precision=HIGH)], axis=0)
    part_hidden, part_head, df = lax.optimization_barrier((part_hidden, part_head, df))
    hidden_grad, head_grad = lax.psum((part_hidden, part_head), "rep")

    lo, up, g1, g2, g3, gb1, gb2, gb3 = backward(x, pre1, pre2, pre3, df, *bwd_weights(k1, k2, k3))
    moved = lax.ppermute(up, "pair", [(0, 1)])
    grad_rows = jnp.where(pair == 0, lo, moved)
    states_grad = jnp.transpose(grad_rows.reshape(84, 84, 2, 128), (3, 2, 0, 1))
    small = [g1, g2, g3, gb1, gb2, gb3, jnp.sum(dpre, axis=0), bo_sum[:, :ATOMS], loss]
    flat = lax.psum(jnp.concatenate([v.reshape(-1) for v in small]), ("pair", "group", "rep"))
    out, at = [], 0
    for v in small:
        out.append(flat[at:at + v.size].reshape(v.shape))
        at += v.size
    g1, g2, g3, gb1, gb2, gb3, hb_grad, bo_grad, loss = out
    gk1, gk2, gk3 = torso_grads(g1, g2, g3)
    hb_grad = hb_grad.reshape(2, 512)
    bo_grad = bo_grad.reshape(-1)

    in_q = lax.dynamic_slice_in_dim(on_in, shard * feat_q, feat_q, axis=1)
    hidden_sigma_grad = hidden_grad * (in_q[:, :, None] * on_out[:, None, :])
    e_q = lax.dynamic_slice_in_dim(on_ein, shard * hid_q, hid_q, axis=1)
    column_of = jnp.arange(on_eout.shape[0])[:, None]
    head_sigma_grad = head_grad * (jnp.where(column_of < ATOMS, e_q[0:1], e_q[1:2]) * on_eout[:, None])
    return (loss.reshape(()), states_grad, gk1, gb1.reshape(-1), gk2, gb2.reshape(-1), gk3, gb3.reshape(-1), hidden_grad, hidden_sigma_grad,
            hb_grad, hb_grad * on_out, head_grad.T, head_sigma_grad.T, bo_grad, bo_grad * on_eout)


def solution(mesh):
    placed = (
        P("pair", ("group", "rep"), None, None, None),
        P("pair", ("group", "rep")),
        P(("group", "rep"), None),
        P(("group", "rep"), None),
        P(("group", "rep"), None),
        P("pair", None, None, None, None),
        P("pair", None),
        P("pair", None, None, None, None),
        P("pair", None),
        P("pair", None, None, None, None),
        P("pair", None),
        P("pair", None, None, None),
        P("pair", None, None, None),
        P("pair", None, None),
        P("pair", None, None),
        P("pair", None, None),
        P("pair", None, None),
        P("pair", None),
        P("pair", None),
        P("pair", None, None),
        P("pair", None, None),
        P("pair", None, None),
        P("pair", None),
    )
    return jax.shard_map(
        local,
        mesh=mesh,
        in_specs=placed,
        out_specs=(
            P(),
            P(("group", "rep"), "pair", None, None),
            P(),
            P(),
            P(),
            P(),
            P(),
            P(),
            P(None, ("pair", "group"), None),
            P(None, ("pair", "group"), None),
            P(),
            P(),
            P(("pair", "group"), None),
            P(("pair", "group"), None),
            P(),
            P(),
        ),
        check_vma=False,
    )
```

time: 1250 us -> 528 us (0.42)
  matrix products: 812 us -> 5.82 us
  Pallas kernels: 0 us -> 117 us
  blocking collectives: 44.3 us -> 0 us
  starting transfers between devices: 9.3 us -> 31.1 us
  other arithmetic: 46 us -> 29.7 us
    conv_general_dilated x9 -> x0, matrix products: 765 us -> none  [conv_layer(): lax.conv_general_dilated(inputs, kernel, (stride, stride), 'VALID', dimen...]
    pallas_call x0 -> x4, Pallas kernels: none -> 117 us  [the longest x1 53.4 us: backward(): pl.pallas_call(bwd_kernel, grid=(21,), in_specs=[pl.BlockSpec((4, 336, 12...]
    psum x1 -> x0, blocking collectives: 44.3 us -> none  [local(): lax.psum((weight_grads[0], weight_grads[1], weight_grads[2], weight_grads...]
    dot_general x9 -> x3, matrix products: 47.3 us -> 5.82 us  [the longest x1 3.15 us: local(): jnp.einsum('fb,bsh->sfh', f_all, d_all[:, :1024].reshape(-1, 2, 512), pre...]
    dot_general x1 -> x0, local copies, waits for them, and re-layouts: 33.3 us -> none  [network(): jnp.einsum('bf,sfh->sbh', features, hidden_w, precision=HIGHEST)]
    ppermute x3 -> x12, starting transfers between devices: 8.67 us -> 31.1 us  [the longest x6 15.6 us: exchange(): lax.ppermute(parts(1, to), ('pair', 'group'), [(i, groups + (i + k) % gro...]
    mul x5 -> x4, other arithmetic: 22.8 us -> 5.26 us  [the longest x1 3.93 us: local(): hidden_sigma_grad = hidden_grad * (in_q[:, :, None] * on_out[:, None, :])]
    add x4 -> x2, other arithmetic: 16.5 us -> 3.37 us  [the longest x1 3.36 us: local(): wide(head_mean[0].T)]
  transfers between devices with their start and end apart: 9 -> 14, of which waited for: 4 -> 5; matrix products, arithmetic and copies ran while one was open for 65% -> 12% of each run, Pallas kernels for 0% -> 6%
where the time goes in v1:
time: 528 us; the launch traced here: 525 us
  waiting for transfers between devices  272 us (52%)
  Pallas kernels  117 us (22%)
  local copies, waits for them, and re-layouts  55.1 us (10%)
  starting transfers between devices  31.1 us (6%)
  other arithmetic  29.7 us (6%)
  between operations  14.9 us (3%)
  matrix products  5.82 us (1%)
    psum x1, waiting for transfers between devices, local(): hidden_grad, head_grad = lax.psum((part_hidden, part_head), 'rep')  140 us
    psum x1, waiting for transfers between devices, local(): lax.psum(jnp.concatenate([v.reshape(-1) for v in small]), ('pair', 'group...  123 us
    pallas_call x1, Pallas kernels, backward(): pl.pallas_call(bwd_kernel, grid=(21,), in_specs=[pl.BlockSpec((4, 336, 12...  53.4 us
    pallas_call x1, Pallas kernels, forward(): pl.pallas_call(fwd_kernel, grid=(21,), in_specs=[pl.BlockSpec((4, 336, 12...  32.2 us
    pallas_call x1, Pallas kernels, hidden(): pl.pallas_call(hid_kernel, grid=(STEPS,), in_specs=[pl.BlockSpec((k, 128)...  15.9 us
    ppermute x6, starting transfers between devices, exchange(): lax.ppermute(parts(1, to), ('pair', 'group'), [(i, groups + (i + k) % gro...  15.6 us
    pallas_call x1, Pallas kernels, hidden_bwd(): pl.pallas_call(hid_bwd_kernel, grid=(STEPS,), in_specs=[full(PAD, 128), f...  15.5 us
    unnamed x66, local copies, waits for them, and re-layouts  13.2 us
  transfers between devices with their start and end apart: 14, of which 5 were waited for; matrix products, arithmetic and copies ran while one was open for 12% of the time, Pallas kernels for 6%

profile of v1, /device:TPU:0, one launch (start us, length us, event | category | flops | bytes accessed | tf_op | source)
XLA Modules:
  0.0 525.3 jit_solution(16322787419663684840)
XLA Ops:
  8.0 1.0 copy.73
  9.0 1.1 copy.117
  11.0 1.1 copy.76
  12.2 1.0 copy.77
  13.7 0.9 reshape.223.w1_ref
  16.8 32.2 %shard_map.333 = (f32[20,640,128]{2,1,0:T(8,128)}, f32[9,576,128]{2,1,0:T(8,128)}, f32[3136,128]{1,0:T(8,128)}, f32[3136,128]{1,0:T(8,128)}) custom-call(f32[84,336,128]{2,1,0:T(8,128)} %bitcast.158, f32[192,256]{1,0:T(8,128)} %reshape.223.w1_ref, f32[128,256]{1,0:T(8,128)} %copy.78.w2_ref, f32[384,256]{1,0:T(8,128)} %bitcast.172, ...), custom_call_target="tpu_custom_call" | custom-call | tf_op jit(solution)/shard_map/pallas_call | solution.py:110
  49.0 1.0 constant_dynamic-slice_fusion.7
  50.0 3.1 collective-permute-start.4
  57.4 1.4 copy.115
  58.8 1.7 reshape.227
  60.6 3.0 copy.114
  63.6 3.0 reshape.228
  66.6 3.4 multiply_add_fusion.wo_ref
  69.9 1.0 broadcast_in_dim.87.bo_ref
  70.9 15.9 %shard_map.334 = (f32[128,1024]{1,0:T(8,128)}, f32[128,1024]{1,0:T(8,128)}, f32[56,128]{1,0:T(8,128)}, f32[56,128]{1,0:T(8,128)}) custom-call(f32[3136,128]{1,0:T(8,128)} %get-tuple-element.43.f_ref, f32[2,3136,512]{2,1,0:T(8,128)} %bitcast.160, f32[2,3136,512]{2,1,0:T(8,128)} %bitcast.162, f32[7,2,448]{2,1,0:T(2,128)} %bitcast.196, f32[2,512]{1,0:T(2,128)} %bitcast.199, ...), custom_call_target="tpu_custom_call" | custom-call | tf_op jit(solution)/shard_map/pallas_call | solution.py:359
  86.9 1.4 collective-permute-start
  88.3 1.5 reshape.230
  89.9 3.0 collective-permute-start.7
  93.9 0.8 dynamic-slice_select_fusion.1
  94.7 4.8 collective-permute-start.9
  99.5 2.1 collective-permute-start.8
  101.6 0.9 pad_maximum_fusion
  103.4 0.9 reshape.232.w2_ref
  104.6 1.2 reshape.233.w3_ref
  105.8 1.1 reshape.231.w1_ref
  107.6 15.5 %shard_map.335 = (f32[3136,128]{1,0:T(8,128)}, f32[128,1024]{1,0:T(8,128)}, f32[56,128]{1,0:T(8,128)}, f32[1,1]{1,0:T(1,128)}, f32[19,56,1]{2,1,0:T(8,128)}) custom-call(f32[56,128]{1,0:T(8,128)} %copy-done.17, f32[56,128]{1,0:T(8,128)} %get-tuple-element.45.logp_ref, f32[128,1024]{1,0:T(8,128)} %get-tuple-element.46.h_ref, f32[2,3136,512]{2,1,0:T(8,128)} %bitcast.161, ...), custom_call_target="tpu_custom_call" | custom-call | tf_op jit(solution)/shard_map/pallas_call | solution.py:410
  123.1 1.0 copy.80
  124.1 1.1 concatenate.28
  125.2 1.3 collective-permute-start.3
  126.6 3.9 collective-permute-start.2
  130.5 1.3 collective-permute-start.1
  131.9 0.9 broadcast_select_fusion.4
  132.8 0.9 fusion.5
  133.7 1.0 dynamic-slice_select_fusion
  134.7 2.0 collective-permute-start.6
  136.7 2.1 collective-permute-start.5
  139.0 3.7 collective-permute-done.2
  143.9 1.4 fusion.14
  145.4 1.2 fusion.13
  146.6 0.8 pad_maximum_fusion.2
  147.6 3.8 collective-permute-done.5
  151.4 1.0 broadcast_select_fusion.3
  152.5 3.1 convolution_bitcast_fusion
  155.6 53.4 %shard_map.336 = (f32[84,168,128]{2,1,0:T(8,128)}, f32[84,168,128]{2,1,0:T(8,128)}, f32[8,32,32]{2,1,0:T(8,128)}, f32[128,256]{1,0:T(8,128)}, f32[3,64,192]{2,1,...) custom-call(f32[84,336,128]{2,1,0:T(8,128)} %bitcast.159, ...), custom_call_target="tpu_custom_call" | custom-call | tf_op jit(solution)/shard_map/pallas_call | solution.py:280
  209.0 4.3 collective-permute-start.10
  213.7 1.0 reshape.234
  214.7 1.0 copy.101
  215.6 0.8 reduce.4
  216.5 0.9 reduce.5
  217.3 0.9 reduce.6
  218.2 1.1 reshape.236
  219.3 7.5 %concatenate.33 = f32[79978]{0:T(1024)} concatenate(f32[8192]{0:T(1024)S(1)} %reshape.234, f32[32768]{0:T(1024)S(1)} %bitcast.187, f32[36864]{0:T(1024)S(1)} %reshape.236, f32[32]{0:T(128)S(1)} %reduce.4, f32[64]{0:T(128)S(1)} %reduce.5, f32[64]{0:T(128)S(1)} %reduce.6, f32[1024]{0:T(1024)S(1)} %reduce_sum.9, f32[969]{0:T(1024)S(1)} %reshape.240, f32[1]{0:T(128)} %bitcast.74), dimensions={0} | concatenate | bytes 639824 | tf_op jit(solution)/shard_map/concatenate | solution.py:489
  227.7 1.6 collective-permute-start.11
  230.1 122.8 %all-reduce.17.cloned.1.call-done = f32[79978]{0:T(1024)} async-done(((f32[79978]{0:T(1024)}), f32[79978]{0:T(1024)}) %all-reduce.17.cloned.1.call-update) | async-done | bytes 319928 | tf_op jit(solution)/shard_map/psum | solution.py:489
  353.6 0.9 slice.140
  355.5 0.9 slice.138
  356.9 0.9 copy.93
  357.8 1.1 reshape_reshape.13
  358.9 1.2 copy.92
  363.0 140.0 %all-reduce.19.cloned.1.call-done = (f32[2,784,512]{2,1,0:T(8,128)}, f32[969,128]{1,0:T(8,128)}) async-done(((f32[2,784,512]{2,1,0:T(8,128)}, f32[969,128]{1,0:T(8,128)}), (f32[2,784,512]{2,1,0:T(8,128)}, f32[969,128]{1,0:T(8,128)})) %all-reduce.19.cloned.1.call-update) | async-done | bytes 3707408 | tf_op jit(solution)/shard_map/psum | solution.py:482
  503.0 2.1 multiply_bitcast_fusion
  505.1 3.9 multiply_multiply_fusion
  509.0 7.0 %broadcast_select_fusion = f32[84,168,128]{2,1,0:T(8,128)} fusion(f32[84,168,128]{2,1,0:T(8,128)} %get-tuple-element.60, f32[84,168,128]{2,1,0:T(8,128)} %collective-permute-done.10, pred[]{:T(512)S(6)} %eq.34), kind=kLoop, calls=%fused_computation | loop fusion | flops 1806336 | bytes 21676032 | tf_op jit(solution)/shard_map/jit(_where)/select_n | solution.py:486
  516.0 1.7 copy.123
  (151 shorter events, 20.5 us)
Async XLA Ops:
  7.2 345.7 %all-reduce.17.cloned.1.call-start = ((), (), s32[]{:S(2)}) async-start(), calls=%async_computation | async-start | bytes 647168 | tf_op jit(solution)/shard_map/psum | solution.py:489
  13.2 1.4 copy-start.25
  13.2 2.1 copy-start.26
  16.7 36.5 %copy-start.13 = (f32[1,2,512]{2,1,0:T(2,128)S(1)}, f32[1,2,512]{2,1,0:T(2,128)}, u32[]{:S(2)}) copy-start(f32[1,2,512]{2,1,0:T(2,128)} %param.42) | copy-start | bytes 12292
  16.7 36.5 %copy-start.23 = (f32[1,2,512]{2,1,0:T(2,128)S(1)}, f32[1,2,512]{2,1,0:T(2,128)}, u32[]{:S(2)}) copy-start(f32[1,2,512]{2,1,0:T(2,128)} %param.35) | copy-start | bytes 12292
  16.7 36.5 %copy-start.24 = (f32[1,2,512]{2,1,0:T(2,128)S(1)}, f32[1,2,512]{2,1,0:T(2,128)}, u32[]{:S(2)}) copy-start(f32[1,2,512]{2,1,0:T(2,128)} %param.36) | copy-start | bytes 12292
  16.7 37.6 %copy-start.21 = (f32[1,969]{1,0:T(1,128)S(1)}, f32[1,969]{1,0:T(1,128)}, u32[]{:S(2)}) copy-start(f32[1,969]{1,0:T(1,128)} %param.39) | copy-start | bytes 11632
  16.7 38.2 %copy-start.22 = (f32[1,969]{1,0:T(1,128)S(1)}, f32[1,969]{1,0:T(1,128)}, u32[]{:S(2)}) copy-start(f32[1,969]{1,0:T(1,128)} %param.40) | copy-start | bytes 11632
  16.7 38.9 %copy-start.15 = (f32[1,969]{1,0:T(1,128)S(1)}, f32[1,969]{1,0:T(1,128)}, u32[]{:S(2)}) copy-start(f32[1,969]{1,0:T(1,128)} %param.44) | copy-start | bytes 11632
  16.7 39.6 %copy-start.19 = (f32[1,2,512]{2,1,0:T(2,128)S(1)}, f32[1,2,512]{2,1,0:T(2,128)}, u32[]{:S(2)}) copy-start(f32[1,2,512]{2,1,0:T(2,128)} %param.43) | copy-start | bytes 12292
  16.8 39.9 %copy-start.11 = (f32[1,2,3136]{2,1,0:T(2,128)S(1)}, f32[1,2,3136]{2,1,0:T(2,128)}, u32[]{:S(2)}) copy-start(f32[1,2,3136]{2,1,0:T(2,128)} %param.41) | copy-start | bytes 75268
  16.8 40.6 %copy-start.4 = (f32[1,512,969]{1,0,2:T(1,128)S(1)}, f32[1,512,969]{1,0,2:T(1,128)}, u32[]{:S(2)}) copy-start(f32[1,512,969]{1,0,2:T(1,128)} %param.37) | copy-start | bytes 5953540
  50.0 83.7 %collective-permute-start.4 = (f32[784,128]{1,0:T(8,128)S(1)}, f32[784,128]{1,0:T(8,128)}, u32[]{:S(2)}, u32[]{:S(2)}) collective-permute-start(f32[784,128]{1,0:T(8,128)S(1)} %constant_dynamic-slice_fusion.7), channel_id=1, source_target_pairs={{0,16},{8,24},{1,17},{9,25},{2,18},{10,26},{3,19},{11,27},{4,20},{... | collective-permute-start | bytes 1204232 | tf_op jit(solution)/shard_map/ppermute | solution.py:433
  70.9 22.0 %copy-start.9 = (f32[1,32,4,8,8]{1,4,3,2,0:T(8,128)S(1)}, f32[1,32,4,8,8]{1,4,3,2,0:T(8,128)}, u32[]{:S(2)}) copy-start(f32[1,32,4,8,8]{1,4,3,2,0:T(8,128)} %param.27) | copy-start | bytes 98308
  86.9 6.5 %copy-start.6 = (f32[1,64,64,3,3]{2,1,4,3,0:T(8,128)S(1)}, f32[1,64,64,3,3]{2,1,4,3,0:T(8,128)}, u32[]{:S(2)}) copy-start(f32[1,64,64,3,3]{2,1,4,3,0:T(8,128)} %param.31) | copy-start | bytes 442372
  86.9 20.1 %collective-permute-start = (f32[56,128]{1,0:T(8,128)}, f32[56,128]{1,0:T(8,128)S(1)}, u32[]{:S(2)}, u32[]{:S(2)}) collective-permute-start(f32[56,128]{1,0:T(8,128)} %get-tuple-element.44), channel_id=1, source_target_pairs={{16,0},{17,1},{18,2},{19,3},{20,4},{21,5},{22,6},{23,7},{24,8},{25... | collective-permute-start | bytes 86024 | tf_op jit(solution)/shard_map/ppermute | solution.py:469
  89.9 4.0 collective-permute-start.7
  93.8 8.7 %copy-start.7 = (f32[1,64,32,4,4]{1,4,3,2,0:T(4,128)S(1)}, f32[1,64,32,4,4]{1,4,3,2,0:T(4,128)}, u32[]{:S(2)}) copy-start(f32[1,64,32,4,4]{1,4,3,2,0:T(4,128)} %param.29) | copy-start | bytes 393220
  94.7 35.8 %collective-permute-start.9 = (f32[128,2,128]{2,1,0:T(2,128)}, f32[128,2,128]{2,1,0:T(2,128)}, u32[]{:S(2)}, u32[]{:S(2)}) collective-permute-start(f32[128,2,128]{2,1,0:T(2,128)} %get-tuple-element.104), channel_id=1, source_target_pairs={{0,24},{8,16},{1,25},{9,17},{2,26},{10,18},{3,27},{11,19},{4,28},{... | collective-permute-start | bytes 393224 | tf_op jit(solution)/shard_map/ppermute | solution.py:433
  99.5 32.3 %collective-permute-start.8 = (f32[128,2,128]{2,1,0:T(2,128)S(1)}, f32[128,2,128]{2,1,0:T(2,128)}, u32[]{:S(2)}, u32[]{:S(2)}) collective-permute-start(f32[128,2,128]{2,1,0:T(2,128)S(1)} %get-tuple-element.105), channel_id=1, source_target_pairs={{0,8},{8,0},{1,9},{9,1},{2,10},{10,2},{3,11},{11,3},{4,12},{12,4},... | collective-permute-start | bytes 393224 | tf_op jit(solution)/shard_map/ppermute | solution.py:432
  107.0 0.6 copy-start.17
  123.1 10.6 %copy-start.1 = (f32[3136,128]{1,0:T(8,128)S(1)}, f32[3136,128]{1,0:T(8,128)}, u32[]{:S(2)}) copy-start(f32[3136,128]{1,0:T(8,128)} %get-tuple-element.43.f_ref) | copy-start | bytes 4816900
  125.2 13.7 %collective-permute-start.3 = (f32[128,1152]{1,0:T(8,128)S(1)}, f32[128,1152]{1,0:T(8,128)S(1)}, u32[]{:S(2)}, u32[]{:S(2)}) collective-permute-start(f32[128,1152]{1,0:T(8,128)S(1)} %concatenate.28), channel_id=1, source_target_pairs={{0,24},{8,16},{1,25},{9,17},{2,26},{10,18},{3,27},{11,19},{4,28},{... | collective-permute-start | bytes 1769480 | tf_op jit(solution)/shard_map/ppermute | solution.py:433
  126.6 16.1 %collective-permute-start.2 = (f32[128,1152]{1,0:T(8,128)S(1)}, f32[128,1152]{1,0:T(8,128)S(1)}, u32[]{:S(2)}, u32[]{:S(2)}) collective-permute-start(f32[128,1152]{1,0:T(8,128)S(1)} %concatenate.28), channel_id=1, source_target_pairs={{0,8},{8,0},{1,9},{9,1},{2,10},{10,2},{3,11},{11,3},{4,12},{12,4},... | collective-permute-start | bytes 1769480 | tf_op jit(solution)/shard_map/ppermute | solution.py:432
  130.5 8.4 %collective-permute-start.1 = (f32[128,1152]{1,0:T(8,128)S(1)}, f32[128,1152]{1,0:T(8,128)S(1)}, u32[]{:S(2)}, u32[]{:S(2)}) collective-permute-start(f32[128,1152]{1,0:T(8,128)S(1)} %concatenate.28), channel_id=1, source_target_pairs={{0,16},{8,24},{1,17},{9,25},{2,18},{10,26},{3,19},{11,27},{4,20},{... | collective-permute-start | bytes 1769480 | tf_op jit(solution)/shard_map/ppermute | solution.py:433
  134.7 12.9 %collective-permute-start.6 = (f32[784,128]{1,0:T(8,128)}, f32[784,128]{1,0:T(8,128)}, u32[]{:S(2)}, u32[]{:S(2)}) collective-permute-start(f32[784,128]{1,0:T(8,128)} %get-tuple-element.101), channel_id=1, source_target_pairs={{0,24},{8,16},{1,25},{9,17},{2,26},{10,18},{3,27},{11,19},{4,28},{... | collective-permute-start | bytes 1204232 | tf_op jit(solution)/shard_map/ppermute | solution.py:433
  136.7 14.7 %collective-permute-start.5 = (f32[784,128]{1,0:T(8,128)}, f32[784,128]{1,0:T(8,128)}, u32[]{:S(2)}, u32[]{:S(2)}) collective-permute-start(f32[784,128]{1,0:T(8,128)} %get-tuple-element.102), channel_id=1, source_target_pairs={{0,8},{8,0},{1,9},{9,1},{2,10},{10,2},{3,11},{11,3},{4,12},{12,4},... | collective-permute-start | bytes 1204232 | tf_op jit(solution)/shard_map/ppermute | solution.py:432
  143.0 0.7 copy-start.5
  155.6 57.7 %copy-start.2 = (f32[128,1024]{1,0:T(8,128)S(1)}, f32[128,1024]{1,0:T(8,128)}, u32[]{:S(2)}) copy-start(f32[128,1024]{1,0:T(8,128)} %get-tuple-element.47) | copy-start | bytes 1572868
  155.6 57.7 %copy-start.8 = (f32[19,56,1]{2,1,0:T(8,128)S(1)}, f32[19,56,1]{2,1,0:T(8,128)}, u32[]{:S(2)}) copy-start(f32[19,56,1]{2,1,0:T(8,128)} %get-tuple-element.58) | copy-start | bytes 12772
  209.0 300.0 %collective-permute-start.10 = (f32[84,168,128]{2,1,0:T(8,128)}, f32[84,168,128]{2,1,0:T(8,128)}, u32[]{:S(2)}, u32[]{:S(2)}) collective-permute-start(f32[84,168,128]{2,1,0:T(8,128)} %get-tuple-element.61), channel_id=1, source_target_pairs={{0,16},{1,17},{2,18},{3,19},{4,20},{5,21},{6,22},{7,23},{8,24},{9,... | collective-permute-start | bytes 21676040 | tf_op jit(solution)/shard_map/ppermute | solution.py:485
  226.8 0.8 copy-start.12
  226.8 0.9 copy-start.14
  226.8 0.9 copy-start.20
  226.8 0.9 copy-start.16
  226.8 276.2 %all-reduce.19.cloned.1.call-start = ((), (), s32[]{:S(2)}) async-start(), calls=%async_computation.1 | async-start | bytes 7421952 | tf_op jit(solution)/shard_map/psum | solution.py:482
  227.7 2.2 collective-permute-start.11
  352.9 4.9 slice-start
  353.6 6.4 %copy-start.18 = (f32[2,512]{1,0:T(2,128)}, f32[2,512]{1,0:T(2,128)S(1)}, u32[]{:S(2)}) copy-start(f32[2,512]{1,0:T(2,128)S(1)} %reshape.245) | copy-start | bytes 12292
  356.4 4.2 copy-start.10
  509.0 7.0 %copy-start = (f32[2,784,512]{2,1,0:T(8,128)S(1)}, f32[2,784,512]{2,1,0:T(8,128)}, u32[]{:S(2)}) copy-start(f32[2,784,512]{2,1,0:T(8,128)} %get-tuple-element.143) | copy-start | bytes 9633796
  516.0 1.7 copy-start.3
Sparse Core Ops, SparseCore 0:
  226.9 125.9 all-reduce.16
  357.6 145.3 all-reduce.18

commit v2 on v1

v2 whole, which is shorter than its diff:
```python
import functools
import jax
import jax.numpy as jnp
from jax import lax
from jax.experimental import pallas as pl
from jax.experimental.pallas import tpu as pltpu
from jax.sharding import PartitionSpec as P

BF = jnp.bfloat16
F32 = jnp.float32
NN=(((1,),(0,)),((),()))
NT=(((1,),(1,)),((),()))
TN=(((0,),(0,)),((),()))

def split(v):
    hi = v.astype(BF)
    return hi, (v - hi.astype(F32)).astype(BF)

def dot(a, b, dims=NN):
    return lax.dot_general(a, b, dims, preferred_element_type=F32)

def dot3(a, b, dims=NN):
    ah, al = a; bh, bl = b
    return dot(ah, bh, dims) + (dot(ah, bl, dims) + dot(al, bh, dims))

def silu(v):
    return v * jax.nn.sigmoid(v)

def fwd_weights(k1, k2, k3):
    a = jnp.transpose(k1, (0, 2, 3, 1)).reshape(32, 2, 4, 32)
    a = jnp.stack([jnp.pad(a, ((0, 0), (0, 0), (0, 0), (16 * w, 32 - 16 * w))) for w in range(3)])
    w1 = jnp.transpose(a, (2, 0, 1, 3, 4)).reshape(192, 256)
    w2 = jnp.transpose(k2.reshape(64, 32, 2, 2, 4), (2, 0, 3, 4, 1)).reshape(128, 256)
    a = jnp.transpose(k3, (2, 0, 3, 1)).reshape(3, 64, 192)
    a = jnp.stack([jnp.pad(a, ((0, 0), (0, 0), (64 * w, 64 - 64 * w))) for w in range(2)])
    w3 = jnp.transpose(a, (1, 0, 2, 3)).reshape(384, 256)
    return w1, w2, w3

def fwd_kernel(x_ref, w1_ref, w2_ref, w3_ref, b1_ref, b2_ref, b3_ref, pre1_ref, pre2_ref, pre3_ref, f_ref,
               xh, xl, ws1, top1, top2, acc3, h1h, h1l, h2h, h2l):
    j = pl.program_id(0)
    @pl.when(j == 0)
    def _():
        xh[:, 336:, :] = jnp.zeros((4, 16, 128), BF)
        xl[:, 336:, :] = jnp.zeros((4, 16, 128), BF)
        top1[...] = jnp.zeros_like(top1)
        top2[...] = jnp.zeros_like(top2)
        acc3[...] = jnp.zeros_like(acc3)
        hi, lo = split(w1_ref[...])
        ws1[0] = hi
        ws1[1] = lo
        h2h[:, 576:, :] = jnp.zeros((9, 64, 128), BF)
        h2l[:, 576:, :] = jnp.zeros((9, 64, 128), BF)
    v = x_ref[...]
    hi = v.astype(BF)
    xh[:, 0:336, :] = hi
    xl[:, 0:336, :] = (v - hi.astype(F32)).astype(BF)
    rh = jnp.concatenate([xh[:, 48 * i:48 * i + 64, :].reshape(256, 128) for i in range(7)], axis=1)
    rl = jnp.concatenate([xl[:, 48 * i:48 * i + 64, :].reshape(256, 128) for i in range(7)], axis=1)
    r = dot3((ws1[0], ws1[1]), (rh, rl))
    out = top1[...] + r[96:]
    top1[...] = r[:96]
    b1 = b1_ref[...]
    row = jnp.maximum(j - 1, 0)
    for i in range(7):
        n = 96 if i < 6 else 64
        p = out[:n, 128 * i:128 * i + 128] + b1[:n]
        pre1_ref[0, 96 * i:96 * i + n, :] = p
        hh, hl = split(silu(p))
        h1h[row, 96 * i:96 * i + n, :] = hh
        h1l[row, 96 * i:96 * i + n, :] = hl

    @pl.when(j == pl.num_programs(0) - 1)
    def _():
        w2 = split(w2_ref[...])
        b2 = b2_ref[...]
        def step2(y, carry):
            rh = jnp.concatenate([h1h[pl.ds(2 * y, 2), 64 * i:64 * i + 128, :].reshape(256, 128) for i in range(9)], axis=1)
            rl = jnp.concatenate([h1l[pl.ds(2 * y, 2), 64 * i:64 * i + 128, :].reshape(256, 128) for i in range(9)], axis=1)
            r = dot3(w2, (rh, rl))
            o = top2[...] + r[64:]
            top2[...] = r[:64]
            row = jnp.maximum(y - 1, 0)
            for i in range(9):
                p = o[:, 128 * i:128 * i + 128] + b2
                pre2_ref[row, 64 * i:64 * i + 64, :] = p
                hh, hl = split(silu(p))
                h2h[row, 64 * i:64 * i + 64, :] = hh
                h2l[row, 64 * i:64 * i + 64, :] = hl
            return carry
        lax.fori_loop(0, 10, step2, 0)
        w3 = split(w3_ref[...])
        b3 = b3_ref[...]
        def step3(y, carry):
            rh = jnp.concatenate([h2h[y, 128 * i:128 * i + 256, :] for i in range(4)], axis=1)
            rl = jnp.concatenate([h2l[y, 128 * i:128 * i + 256, :] for i in range(4)], axis=1)
            r = dot3(w3, (rh, rl))
            for ky in range(3):
                for i in range(4):
                    acc3[y - ky + 2, 128 * i:128 * i + 128, :] += r[128 * ky:128 * ky + 128, 128 * i:128 * i + 128]
            return carry
        lax.fori_loop(0, 9, step3, 0)
        for y in range(7):
            for x in range(7):
                p = acc3[y + 2, 64 * x:64 * x + 64, :] + b3
                pre3_ref[pl.ds(y * 7 + x, 64, stride=49), :] = p
                f_ref[pl.ds(y * 7 + x, 64, stride=49), :] = silu(p)

def forward(x, w1, w2, w3, b1, b2, b3):
    full = lambda *s: pl.BlockSpec(s, lambda j: (0,) * len(s))
    return pl.pallas_call(
        fwd_kernel,
        grid=(21,),
        in_specs=[pl.BlockSpec((4, 336, 128), lambda j: (j, 0, 0)), full(192, 256), full(128, 256), full(384, 256),
                  full(96, 128), full(64, 128), full(64, 128)],
        out_specs=[pl.BlockSpec((1, 640, 128), lambda j: (jnp.maximum(j - 1, 0), 0, 0)), full(9, 576, 128),
                   full(3136, 128), full(3136, 128)],
        out_shape=[jax.ShapeDtypeStruct((20, 640, 128), F32), jax.ShapeDtypeStruct((9, 576, 128), F32),
                   jax.ShapeDtypeStruct((3136, 128), F32), jax.ShapeDtypeStruct((3136, 128), F32)],
        scratch_shapes=[pltpu.VMEM((4, 352, 128), BF), pltpu.VMEM((4, 352, 128), BF), pltpu.VMEM((2, 192, 256), BF),
                        pltpu.VMEM((96, 896), F32), pltpu.VMEM((64, 1152), F32), pltpu.VMEM((11, 512, 128), F32),
                        pltpu.VMEM((20, 640, 128), BF), pltpu.VMEM((20, 640, 128), BF),
                        pltpu.VMEM((9, 640, 128), BF), pltpu.VMEM((9, 640, 128), BF)],
        compiler_params=pltpu.CompilerParams(vmem_limit_bytes=60 * 2**20),
    )(x, w1, w2, w3, b1, b2, b3)


MESH_ID = pl.DeviceIdType.MESH


def coords():
    r = lax.axis_index("rep")
    return lax.axis_index("pair"), lax.axis_index("group"), r // 2, r % 2


def at(p, g, z, y):
    return (p, g, z * 2 + y)


def flip(z, k):
    return (z, z + 1 - 2 * (z % 2), z + 2 - 4 * (z // 2), 3 - z)[k]


def line(p, g, z, y):
    return [at(q, g, flip(z, k), y) for k in range(4) for q in ((p, 1 - p) if k else (1 - p,))]


def plane(p, g, z, y):
    return [at(p, g, z, 1 - y), at(p, 1 - g, z, y), at(p, 1 - g, z, 1 - y)]


def greet(devices):
    barrier = pltpu.get_barrier_semaphore()
    for device in devices:
        pl.semaphore_signal(barrier, inc=1, device_id=device, device_id_type=MESH_ID)
    pl.semaphore_wait(barrier, len(devices))


def remote(src, dst, send, recv, device):
    return pltpu.make_async_remote_copy(src_ref=src, dst_ref=dst, send_sem=send, recv_sem=recv, device_id=device, device_id_type=MESH_ID)


class Scatter:
    def __init__(self, parts, src, dst, send, recv, own):
        self.parts, self.src, self.dst, self.send, self.recv, self.own = parts, src, dst, send, recv, own
        self.p, self.g, self.z, self.y = coords()

    def copies(self):
        for k in range(4):
            for q in range(2):
                for i in range(self.parts):
                    zd = flip(self.z, k)
                    if k == 0 and q == 0:
                        yield pltpu.make_async_copy(self.src(q, zd, i), self.dst(self.z, i), self.own.at[i]), True
                    else:
                        yield remote(self.src(q, zd, i), self.dst(self.z, i), self.send.at[k * 2 + q, i], self.recv.at[k, i], at(q, self.g, zd, self.y)), False

    def start(self):
        @pl.when(self.p == 0)
        def _():
            for copy, own in self.copies():
                copy.start()

    def arrived(self, k):
        for i in range(self.parts):
            zs = flip(self.z, k)
            wait = remote(self.src(0, zs, i), self.dst(zs, i), self.send.at[0, i], self.recv.at[k, i], at(1 - self.p, self.g, self.z, self.y)).wait_recv
            if k:
                wait()
            else:
                pl.when(self.p == 1)(wait)
                pl.when(self.p == 0)(pltpu.make_async_copy(self.src(0, zs, i), self.dst(zs, i), self.own.at[i]).wait)

    def sent(self):
        @pl.when(self.p == 0)
        def _():
            for copy, own in self.copies():
                if not own:
                    copy.wait_send()


def scatter_sems(parts):
    return [pltpu.SemaphoreType.DMA((8, parts)), pltpu.SemaphoreType.DMA((4, parts)), pltpu.SemaphoreType.DMA((parts,))]


def f_scatter(f_ref, f1_ref, sems):
    def src(q, zd, i):
        return f_ref.at[pl.ds(pl.multiple_of((2 * q + i) * 784 + jnp.minimum(200 * zd, 584), 8), 200)]
    return Scatter(2, src, lambda z, i: f1_ref.at[i, z], *sems)


def g_scatter(hid_ref, g1_ref, sems):
    return Scatter(1, lambda q, zd, i: hid_ref.at[q, zd], lambda z, i: g1_ref.at[z], *sems)


def d_scatter(msg_ref, d1_ref, sems):
    return Scatter(1, lambda q, zd, i: msg_ref.at[q], lambda z, i: d1_ref.at[z], *sems)


def spread_plane(p, g, z, y, src, dst, send, recv):
    places = [(g, y), (g, 1 - y), (1 - g, y), (1 - g, 1 - y)]
    out = [pltpu.make_async_copy(src(*places[0]), dst(0), send.at[0])]
    for m in range(1, 4):
        out.append(remote(src(*places[m]), dst(m), send.at[m], recv.at[m], at(p, places[m][0], z, places[m][1])))
    return out
ATOMS, ACTIONS, PAD = 51, 18, 56
STEPS = 7

def column(row, lanes):
    tall = jnp.transpose(jnp.broadcast_to(row, (128, row.shape[1])))
    return jnp.concatenate([tall] * (lanes // 128), axis=1)

def noisy(mean_ref, sigma_ref, nin_ref, nout_ref, s):
    return mean_ref[s] + sigma_ref[s] * (column(nin_ref[0, s:s + 1, :], 512) * nout_ref[s:s + 1, :])

def mask_of(chosen, a):
    return jnp.where(chosen == a, 1.0 - 1.0 / ACTIONS, -1.0 / ACTIONS)

def hid_kernel(net, f_ref, m_ref, s_ref, nin_ref, nout_ref, hb_ref, wo_ref, bo_ref, c_ref, pl_ref, pw_ref, *rest):
    if net:
        f_all, h_ref, g_ref, logp_ref, dist_ref, f1_ref, acc = rest[:7]
        wire = f_scatter(f_all, f1_ref, rest[7:])
    else:
        h_ref, g_ref, logp_ref, dist_ref, acc = rest
    j = pl.program_id(0)
    @pl.when(j == 0)
    def _():
        if net:
            greet(line(*coords()))
            wire.start()
        acc[...] = jnp.zeros_like(acc)
    f = split(f_ref[...])
    for s in range(2):
        w = split(noisy(m_ref, s_ref, nin_ref, nout_ref, s))
        acc[:, 512 * s:512 * s + 512] += dot3(f, w, TN)
    @pl.when(j == pl.num_programs(0) - 1)
    def _():
        h = acc[...] + hb_ref[...]
        h_ref[...] = h
        gt = jnp.transpose(silu(h))
        for s in range(2):
            for q in range(2):
                for gg in range(2):
                    for z in range(4):
                        at_row = 512 * s + 256 * q + 128 * gg + 32 * z
                        g_ref[q, z, gg, s] = gt[at_row:at_row + 32]
        wo = wo_ref[...]
        v = dot3(split(wo[0]), split(gt[:512])) + bo_ref[0]
        a = dot3(split(wo[1:].reshape(ACTIONS * PAD, 512)), split(gt[512:]))
        chosen = c_ref[...]
        z = v
        for i in range(ACTIONS):
            z = z + mask_of(chosen, i) * (a[PAD * i:PAD * i + PAD] + bo_ref[i + 1])
        row = lax.broadcasted_iota(jnp.int32, (PAD, 128), 0)
        z = jnp.where(row < ATOMS, z, -1e30)
        top = jnp.max(z, axis=0, keepdims=True)
        e = jnp.exp(z - top)
        tot = jnp.sum(e, axis=0, keepdims=True)
        logp_ref[...] = (z - top) - jnp.log(tot)
        p = e / tot
        dist = jnp.zeros((PAD, 128), F32)
        for i in range(ATOMS):
            lower = pl_ref[i:i + 1, :]
            share = pw_ref[i:i + 1, :]
            pi = p[i:i + 1, :]
            dist = dist + jnp.where(row == lower, pi * (1.0 - share), 0.0) + jnp.where(row == lower + 1, pi * share, 0.0)
        dist_ref[...] = dist
        if net:
            for k in range(4):
                wire.arrived(k)
            wire.sent()

ANY = pl.BlockSpec(memory_space=pl.ANY)

def hidden(net, f, m, s, nin, nout, hb, wo, bo, c, plow, pw):
    full = lambda *t: pl.BlockSpec(t, lambda j: (0,) * len(t))
    sds = lambda *t: jax.ShapeDtypeStruct(t, F32)
    k = 3136 // STEPS
    wspec = pl.BlockSpec((2, k, 512), lambda j: (0, j, 0))
    return pl.pallas_call(
        functools.partial(hid_kernel, net), grid=(STEPS,),
        in_specs=[pl.BlockSpec((k, 128), lambda j: (j, 0)), wspec, wspec, pl.BlockSpec((1, 2, k), lambda j: (j, 0, 0)), full(2, 512), full(1, 1024),
                  full(19, PAD, 512), full(19, PAD, 128), full(1, 128), full(ATOMS, 128), full(ATOMS, 128)] + [ANY] * net,
        out_specs=[full(128, 1024), full(2, 4, 2, 2, 32, 128), full(PAD, 128), full(PAD, 128)] + [ANY] * net,
        out_shape=[sds(128, 1024), sds(2, 4, 2, 2, 32, 128), sds(PAD, 128), sds(PAD, 128)] + [sds(2, 4, 200, 128)] * net,
        scratch_shapes=[pltpu.VMEM((128, 1024), F32)] + scatter_sems(2) * net,
        compiler_params=pltpu.CompilerParams(vmem_limit_bytes=60 * 2**20, **(dict(collective_id=1, has_side_effects=True) if net else {})),
    )(f, m, s, nin, nout, hb, wo, bo, c, plow, pw, *([f] * net))

def hid_bwd_kernel(net, t_ref, logp_ref, h_ref, m_ref, s_ref, nin_ref, nout_ref, wo_ref, c_ref, *rest):
    if net:
        f1_ref, hid_ref, df_ref, msg_ref, small_ref, f2_ref, g1_ref, dth, dtl, fs, fr = rest[:11]
        wire = g_scatter(hid_ref, g1_ref, rest[11:])
        p, g, z, y = coords()
        fan = spread_plane(p, g, z, y, lambda gd, yd: f1_ref.at[gd], lambda m: f2_ref.at[m], fs, fr)
    else:
        df_ref, msg_ref, small_ref, dth, dtl = rest
    j = pl.program_id(0)
    @pl.when(j == 0)
    def _():
        if net:
            greet(line(p, g, z, y) + plane(p, g, z, y))
            for copy in fan:
                copy.start()
            wire.start()
        t = t_ref[...]
        logp = logp_ref[...]
        chosen = c_ref[...]
        row = lax.broadcasted_iota(jnp.int32, (PAD, 128), 0)
        d = (jnp.exp(logp) * jnp.sum(t, axis=0, keepdims=True) - t) * (1.0 / 128)
        loss = -jnp.sum(jnp.where(row < ATOMS, t * logp, 0.0), axis=1, keepdims=True) * (1.0 / 128)
        dz = jnp.where(row == ATOMS, chosen.astype(F32), d)
        da = jnp.concatenate([mask_of(chosen, i) * d for i in range(ACTIONS)], axis=0)
        wo = wo_ref[...]
        d2, da2 = split(d), split(da)
        g0 = dot3(d2, split(wo[0]), TN)
        g1 = dot3(da2, split(wo[1:].reshape(ACTIONS * PAD, 512)), TN)
        small_ref[...] = jnp.zeros_like(small_ref)
        for s, grad in enumerate((g0, g1)):
            dp = grad * dsilu(h_ref[:, 512 * s:512 * s + 512])
            total = jnp.sum(dp, axis=0, keepdims=True)
            for c in range(4):
                msg_ref[c // 2, s, 128 * (c % 2):128 * (c % 2) + 128, :] = dp[:, 128 * c:128 * c + 128]
                small_ref[4 * s + c:4 * s + c + 1, :] = total[:, 128 * c:128 * c + 128]
            for ph in range(2):
                msg_ref[ph, s, 256:312, :] = dz
            hi, lo = split(jnp.transpose(dp))
            dth[s] = hi
            dtl[s] = lo
        ones = jnp.ones((8, 128), BF)
        every = jnp.concatenate([d, da, jnp.zeros((1152 - 19 * PAD, 128), F32)], axis=0)
        eh, el = split(every)
        rest_ = (every - eh.astype(F32)) - el.astype(F32)
        rows = dot(ones, eh, NT) + dot(ones, el, NT) + dot(ones, rest_.astype(BF), NT)
        for c in range(9):
            small_ref[8 + c:9 + c, :] = rows[0:1, 128 * c:128 * c + 128]
        small_ref[17:18, :] = jnp.broadcast_to(jnp.sum(loss, axis=0, keepdims=True), (1, 128))
    out = None
    for s in range(2):
        w = split(noisy(m_ref, s_ref, nin_ref, nout_ref, s))
        r = dot3(w, (dth[s], dtl[s]))
        out = r if out is None else out + r
    df_ref[...] = out
    if net:
        @pl.when(j == pl.num_programs(0) - 1)
        def _():
            fan[0].wait()
            for copy in fan[1:]:
                copy.wait()
            for k in range(4):
                wire.arrived(k)
            wire.sent()

def hidden_bwd(net, t, logp, h, m, s, nin, nout, wo, c, *wired):
    full = lambda *u: pl.BlockSpec(u, lambda j: (0,) * len(u))
    sds = lambda *u: jax.ShapeDtypeStruct(u, F32)
    k = 3136 // STEPS
    wspec = pl.BlockSpec((2, k, 512), lambda j: (0, j, 0))
    return pl.pallas_call(
        functools.partial(hid_bwd_kernel, net), grid=(STEPS,),
        in_specs=[full(PAD, 128), full(PAD, 128), full(128, 1024), wspec, wspec, pl.BlockSpec((1, 2, k), lambda j: (j, 0, 0)), full(2, 512),
                  full(19, PAD, 512), full(1, 128)] + [ANY, ANY] * net,
        out_specs=[pl.BlockSpec((k, 128), lambda j: (j, 0)), full(2, 2, 312, 128), full(24, 128)] + [ANY, ANY] * net,
        out_shape=[sds(3136, 128), sds(2, 2, 312, 128), sds(24, 128)] + [sds(4, 4, 200, 128), sds(4, 2, 2, 32, 128)] * net,
        scratch_shapes=[pltpu.VMEM((2, 512, 128), BF), pltpu.VMEM((2, 512, 128), BF)]
        + ([pltpu.SemaphoreType.DMA((4,)), pltpu.SemaphoreType.DMA((4,))] + scatter_sems(1)) * net,
        compiler_params=pltpu.CompilerParams(vmem_limit_bytes=60 * 2**20, **(dict(collective_id=2, has_side_effects=True) if net else {})),
    )(t, logp, h, m, s, nin, nout, wo, c, *wired)

def dsilu(v):
    s = jax.nn.sigmoid(v)
    return s * (1.0 + v * (1.0 - s))

def bwd_weights(k1, k2, k3):
    a = jnp.transpose(k1.reshape(32, 2, 2, 2, 4, 2, 4), (1, 4, 6, 2, 3, 5, 0))
    cols = []
    for q in range(4):
        parts = []
        for xb in range(3):
            o = xb - q + 1
            parts.append(a[:, :, :, :, ::-1, o, :] if 0 <= o <= 1 else jnp.zeros((2, 4, 4, 2, 2, 32), F32))
        cols.append(jnp.stack(parts, axis=2))
    w1 = jnp.stack(cols, axis=6).reshape(192, 256)
    a = jnp.transpose(k2.reshape(64, 32, 2, 2, 2, 2), (3, 5, 1, 2, 4, 0))[:, :, :, ::-1, ::-1]
    w2 = a.reshape(128, 256)
    cols = []
    for q in range(4):
        parts = []
        for w in range(2):
            kx = w + 2 - q
            parts.append(jnp.transpose(k3[:, :, :, kx], (2, 1, 0)) if 0 <= kx <= 2 else jnp.zeros((3, 64, 64), F32))
        cols.append(jnp.stack(parts, axis=1))
    w3 = jnp.stack(cols, axis=3).reshape(384, 256)
    return w1, w2, w3


def low_kernel(net, pre1_ref, pre2_ref, pre3_ref, df_ref, w2_ref, w3_ref, *rest):
    if net:
        msg_ref, g1_ref, d1h, d1l, small_ref, d1_ref, d2_ref, d3_ref, g2_ref = rest[:9]
        d3f, d3h, d3l, d2h, d2l, h2h, h2l, acc2, a2, a3 = rest[9:19]
        ps, pr, gs, gr, ss, sr = rest[19:25]
        wire = d_scatter(msg_ref, d1_ref, rest[25:])
        p, g, z, y = coords()
        greet(line(p, g, z, y) + plane(p, g, z, y))
        wire.start()
        def fan(k):
            zs = flip(z, k)
            return (spread_plane(p, g, z, y, lambda gd, yd: d1_ref.at[zs, yd], lambda m: d2_ref.at[m, zs], ps.at[k], pr.at[k])
                    + spread_plane(p, g, z, y, lambda gd, yd: g1_ref.at[zs, gd, yd], lambda m: g2_ref.at[m, zs], gs.at[k], gr.at[k]))
        def forward(k):
            wire.arrived(k)
            for copy in fan(k):
                copy.start()
    else:
        d1h, d1l, small_ref, d3f, d3h, d3l, d2h, d2l, h2h, h2l, acc2, a2, a3 = rest
    def upper():
        for ref in (d3h, d3l, d2h, d2l, acc2, a2, a3):
            ref[...] = jnp.zeros_like(ref)
        small_ref[...] = jnp.zeros_like(small_ref)
        for ref in (d1h, d1l):
            ref[0] = jnp.zeros((704, 128), BF)
            ref[21] = jnp.zeros((704, 128), BF)
            ref[:, 0:32, :] = jnp.zeros((22, 32, 128), BF)
            ref[:, 672:704, :] = jnp.zeros((22, 32, 128), BF)
        d3f[...] = df_ref[...] * dsilu(pre3_ref[...])
        total = jnp.zeros((64, 128), F32)
        for y in range(7):
            for x in range(7):
                d = d3f[pl.ds(y * 7 + x, 64, stride=49), :]
                total = total + d
                hi, lo = split(d)
                d3h[y + 2, 64 * (x + 2):64 * (x + 3), :] = hi
                d3l[y + 2, 64 * (x + 2):64 * (x + 3), :] = lo
        small_ref[640:641, 0:64] = jnp.sum(jnp.transpose(total), axis=0, keepdims=True)
        w3 = split(w3_ref[...])
        h2h[:, 576:, :] = jnp.zeros((9, 64, 128), BF)
        h2l[:, 576:, :] = jnp.zeros((9, 64, 128), BF)
        def split2(y, c):
            hi, lo = split(silu(pre2_ref[y]))
            h2h[y, 0:576, :] = hi
            h2l[y, 0:576, :] = lo
            return c
        lax.fori_loop(0, 9, split2, 0)
        def dgrad3(y, c):
            rh = jnp.concatenate([d3h[y + 2, 128 * i:128 * i + 256, :] for i in range(5)], axis=1)
            rl = jnp.concatenate([d3l[y + 2, 128 * i:128 * i + 256, :] for i in range(5)], axis=1)
            r = dot3(w3, (rh, rl))
            for ky in range(3):
                for i in range(5):
                    acc2[y + ky, 128 * i:128 * i + 128, :] += r[128 * ky:128 * ky + 128, 128 * i:128 * i + 128]
            return c
        lax.fori_loop(0, 7, dgrad3, 0)
        def wgrad3(y, c):
            def lhs(ref):
                return jnp.concatenate([jnp.concatenate([ref[y - ky + 2, 128 * (i + 1):128 * (i + 2), :] for i in range(4)], axis=1) for ky in range(3)], axis=0)
            def rhs(ref):
                return jnp.concatenate([ref[y, 128 * i:128 * i + 256, :] for i in range(4)], axis=1)
            a3[...] += dot3((lhs(d3h), lhs(d3l)), (rhs(h2h), rhs(h2l)), NT)
            return c
        lax.fori_loop(0, 9, wgrad3, 0)
        for ky in range(3):
            grad = a3[128 * ky:128 * ky + 64, 0:192] + a3[128 * ky + 64:128 * ky + 128, 64:256]
            small_ref[256 + 64 * ky:320 + 64 * ky, :] = grad[:, 0:128]
            small_ref[448 + 64 * ky:512 + 64 * ky, 0:64] = grad[:, 128:192]
        def step2(y, total):
            for x in range(9):
                d = acc2[y, 64 * x:64 * x + 64, :] * dsilu(pre2_ref[y, 64 * x:64 * x + 64, :])
                total = total + d
                hi, lo = split(d)
                d2h[y + 1, 64 * (x + 1):64 * (x + 2), :] = hi
                d2l[y + 1, 64 * (x + 1):64 * (x + 2), :] = lo
            return total
        total = lax.fori_loop(0, 9, step2, jnp.zeros((64, 128), F32))
        small_ref[641:642, 0:64] = jnp.sum(jnp.transpose(total), axis=0, keepdims=True)
    def block2(y, total):
        w2 = split(w2_ref[...])
        rh = jnp.concatenate([d2h[pl.ds(y, 2), 64 * i:64 * i + 128, :].reshape(256, 128) for i in range(10)], axis=1)
        rl = jnp.concatenate([d2l[pl.ds(y, 2), 64 * i:64 * i + 128, :].reshape(256, 128) for i in range(10)], axis=1)
        r = dot3(w2, (rh, rl))
        h1h, h1l = [], []
        for py in range(2):
            rowh, rowl = [], []
            for i in range(10):
                v = pre1_ref[2 * y + py, 64 * i:64 * i + 64, :]
                s = jax.nn.sigmoid(v)
                d = r[64 * py:64 * py + 64, 128 * i:128 * i + 128] * (s * (1.0 + v * (1.0 - s)))
                total = total + d[0:32] + d[32:64]
                hi, lo = split(d)
                d1h[2 * y + py + 1, 64 * i + 32:64 * i + 96, :] = hi
                d1l[2 * y + py + 1, 64 * i + 32:64 * i + 96, :] = lo
                hi, lo = split(v * s)
                rowh.append(hi)
                rowl.append(lo)
            h1h.append(rowh)
            h1l.append(rowl)
        def lhs(ref):
            return jnp.concatenate([jnp.concatenate([ref[y + 1 - h, 64 * (i + 1):64 * (i + 2), :] for i in range(9)], axis=1) for h in range(2)], axis=0)
        def rhs(rows):
            return jnp.concatenate([jnp.concatenate([rows[0][i], rows[0][i + 1], rows[1][i], rows[1][i + 1]], axis=0) for i in range(9)], axis=1)
        a2[...] += dot3((lhs(d2h), lhs(d2l)), (rhs(h1h), rhs(h1l)), NT)
        return total
    def lower():
        total = lax.fori_loop(0, 10, block2, jnp.zeros((32, 128), F32))
        small_ref[642:643, 0:32] = jnp.sum(jnp.transpose(total), axis=0, keepdims=True)
        small_ref[0:128, :] = a2[:, 0:128]
        small_ref[128:256, :] = a2[:, 128:256]
    if not net:
        upper()
        lower()
        return
    pl.when(p == 0)(upper)
    for k in range(4):
        forward(k)
    pl.when(p == 0)(lower)
    fans = [fan(k) for k in range(4)]
    swaps = []
    for m in range(4):
        for k in range(4):
            for copy in (fans[k][m], fans[k][4 + m]):
                if m:
                    copy.wait_recv()
                else:
                    copy.wait()
        swap = remote(d2_ref.at[m, :, pl.ds(0, 256)], d3_ref.at[m], ss.at[m], sr.at[m], at(1 - p, g, z, y))
        swap.start()
        swaps.append(swap)
    for m in range(1, 4):
        for k in range(4):
            fans[k][m].wait_send()
            fans[k][4 + m].wait_send()
    for swap in swaps:
        swap.wait()
    wire.sent()

def lower_backward(net, pre1, pre2, pre3, df, w2, w3, *wired):
    one = lambda *s: pl.BlockSpec(s, lambda j: (0,) * len(s), pipeline_mode=pl.Buffered(1))
    sds = lambda *s: jax.ShapeDtypeStruct(s, F32)
    bfs = lambda *s: jax.ShapeDtypeStruct(s, BF)
    vmb = lambda *s: pltpu.VMEM(s, BF)
    dma = pltpu.SemaphoreType.DMA
    return pl.pallas_call(
        functools.partial(low_kernel, net),
        grid=(1,),
        in_specs=[one(20, 640, 128), one(9, 576, 128), one(3136, 128), one(3136, 128), one(128, 256), one(384, 256)] + [ANY, ANY] * net,
        out_specs=[one(22, 704, 128), one(22, 704, 128), one(648, 128)] + [ANY] * (4 * net),
        out_shape=[bfs(22, 704, 128), bfs(22, 704, 128), sds(648, 128)]
        + [sds(4, 2, 312, 128), sds(4, 4, 312, 128), sds(4, 4, 256, 128), sds(4, 4, 32, 128)] * net,
        scratch_shapes=[pltpu.VMEM((3136, 128), F32), vmb(11, 768, 128), vmb(11, 768, 128), vmb(11, 704, 128), vmb(11, 704, 128),
                        vmb(9, 640, 128), vmb(9, 640, 128), pltpu.VMEM((9, 640, 128), F32), pltpu.VMEM((128, 256), F32), pltpu.VMEM((384, 256), F32)]
        + ([dma((4, 4)), dma((4, 4)), dma((4, 4)), dma((4, 4)), dma((4,)), dma((4,))] + scatter_sems(1)) * net,
        compiler_params=pltpu.CompilerParams(vmem_limit_bytes=60 * 2**20, **(dict(collective_id=3, has_side_effects=True) if net else {})),
    )(pre1, pre2, pre3, df, w2, w3, *wired)

def first_kernel_bwd(net, x_ref, dha_ref, dhb_ref, dla_ref, dlb_ref, w1_ref, *rest):
    if net:
        r_ref, q_ref, small_ref, sg_ref, ag_ref, ah_ref, xh, xl, ws1, a1, lob, upb, ls, us, ur, zs_, zr, ys, yr, own = rest
        p, g, z, y = coords()
        def along_z(k):
            to = at(p, g, flip(z, k), y)
            if k:
                return [remote(r_ref, ag_ref.at[y, z], zs_.at[k, 0], zr.at[k, 0], to), remote(q_ref, ah_ref.at[y, z], zs_.at[k, 1], zr.at[k, 1], to)]
            return [pltpu.make_async_copy(r_ref, ag_ref.at[y, z], own.at[0]), pltpu.make_async_copy(q_ref, ah_ref.at[y, z], own.at[1])]
        def along_y(k):
            zs = flip(z, k)
            a, b = (ag_ref.at[y, zs], ah_ref.at[y, zs]) if k else (r_ref, q_ref)
            to = at(p, g, z, 1 - y)
            return [remote(a, ag_ref.at[y, zs], ys.at[k, 0], yr.at[k, 0], to), remote(b, ah_ref.at[y, zs], ys.at[k, 1], yr.at[k, 1], to)]
        def states_out(j, slot):
            return (pltpu.make_async_copy(lob.at[slot], sg_ref.at[pl.ds(4 * j, 4)], ls.at[slot]),
                    remote(upb.at[slot], sg_ref.at[pl.ds(4 * j, 4)], us.at[slot], ur.at[j], at(1 - p, g, z, y)))
    else:
        small_ref, lo_ref, up_ref, xh, xl, ws1, a1 = rest
    j = pl.program_id(0)
    last = pl.num_programs(0) - 1
    @pl.when(j == 0)
    def _():
        if net:
            greet([at(q, g, flip(z, k), y) for k in range(1, 4) for q in (p,)] + [at(p, g, z, 1 - y), at(1 - p, g, z, y)])
            for k in (1, 2, 3, 0):
                for copy in along_z(k):
                    copy.start()
            for copy in along_y(0):
                copy.start()
        xh[:, 336:, :] = jnp.zeros((4, 16, 128), BF)
        xl[:, 336:, :] = jnp.zeros((4, 16, 128), BF)
        hi, lo = split(w1_ref[...])
        ws1[0] = hi
        ws1[1] = lo
        a1[...] = jnp.zeros_like(a1)
    def work():
        v = x_ref[...]
        hi = v.astype(BF)
        xh[:, 0:336, :] = hi
        xl[:, 0:336, :] = (v - hi.astype(F32)).astype(BF)
        def both(a, b):
            return jnp.concatenate([jnp.concatenate([a[0, 96 * i:96 * i + 128, :], b[0, 96 * i:96 * i + 128, :]], axis=0) for i in range(7)], axis=1)
        r = dot3((ws1[0], ws1[1]), (both(dha_ref, dhb_ref), both(dla_ref, dlb_ref)))
        if net:
            slot = j % 2
            @pl.when(j >= 2)
            def _():
                a, b = states_out(j - 2, slot)
                a.wait()
                b.wait_send()
            lo_to, up_to = lob.at[slot], upb.at[slot]
        else:
            lo_to, up_to = lo_ref, up_ref
        for ky in range(4):
            for i in range(7):
                lo_to[ky, 24 * i:24 * i + 24, :] = r[24 * ky:24 * ky + 24, 128 * i:128 * i + 128]
                up_to[ky, 24 * i:24 * i + 24, :] = r[96 + 24 * ky:96 + 24 * ky + 24, 128 * i:128 * i + 128]
        if net:
            for copy in states_out(j, slot):
                copy.start()
        def lhs(a, b):
            return jnp.concatenate([jnp.concatenate([ref[0, 96 * i + 32:96 * i + 128, :] for i in range(7)], axis=1) for ref in (b, a)], axis=0)
        def rhs(ref):
            return jnp.concatenate([ref[:, 48 * i:48 * i + 64, :].reshape(256, 128) for i in range(7)], axis=1)
        a1[...] += dot3((lhs(dha_ref, dhb_ref), lhs(dla_ref, dlb_ref)), (rhs(xh), rhs(xl)), NT)
    if net:
        pl.when(p == 0)(work)
        for k, step in ((1, 6), (2, 11), (3, 16)):
            @pl.when(j == step)
            def _():
                for copy in along_z(k):
                    copy.wait_recv()
                for copy in along_y(k):
                    copy.start()
    else:
        work()
    @pl.when(j == last)
    def _():
        for h in range(2):
            for ky in range(4):
                grad = a1[96 * h:96 * h + 32, 64 * ky:64 * ky + 32]
                grad = grad + a1[96 * h + 32:96 * h + 64, 64 * ky + 16:64 * ky + 48]
                grad = grad + a1[96 * h + 64:96 * h + 96, 64 * ky + 32:64 * ky + 64]
                small_ref[32 * h:32 * h + 32, 32 * ky:32 * ky + 32] = grad
        if net:
            @pl.when(p == 0)
            def _():
                for back in (1, 0):
                    a, b = states_out(j - back, (j - back) % 2)
                    a.wait()
                    b.wait_send()
            @pl.when(p == 1)
            def _():
                def arrive(i, c):
                    states_out(i, 0)[1].wait_recv()
                    return c
                lax.fori_loop(0, last + 1, arrive, 0)
            for k in range(4):
                for copy in along_z(k):
                    if k:
                        copy.wait_send()
                    else:
                        copy.wait()
                for copy in along_y(k):
                    copy.wait()

def first_backward(net, x, dh, dl, w1, *wired):
    full = lambda *s: pl.BlockSpec(s, lambda j: (0,) * len(s))
    sds = lambda *s: jax.ShapeDtypeStruct(s, F32)
    vmb = lambda *s: pltpu.VMEM(s, BF)
    dma = pltpu.SemaphoreType.DMA
    half = pl.BlockSpec((4, 168, 128), lambda j: (j, 0, 0))
    row = pl.BlockSpec((1, 704, 128), lambda j: (j, 0, 0))
    next_row = pl.BlockSpec((1, 704, 128), lambda j: (j + 1, 0, 0))
    return pl.pallas_call(
        functools.partial(first_kernel_bwd, net),
        grid=(21,),
        in_specs=[pl.BlockSpec((4, 336, 128), lambda j: (j, 0, 0)), row, next_row, row, next_row, full(192, 256)] + [ANY, ANY] * net,
        out_specs=[full(64, 128)] + ([ANY] * 3 if net else [half, half]),
        out_shape=[sds(64, 128)] + ([sds(84, 168, 128), sds(2, 4, 200, 512), sds(2, 4, 32, 1152)] if net else [sds(84, 168, 128), sds(84, 168, 128)]),
        scratch_shapes=[vmb(4, 352, 128), vmb(4, 352, 128), vmb(2, 192, 256), pltpu.VMEM((192, 256), F32)]
        + [pltpu.VMEM((2, 4, 168, 128), F32), pltpu.VMEM((2, 4, 168, 128), F32), dma((2,)), dma((2,)), dma((21,)),
           dma((4, 2)), dma((4, 2)), dma((4, 2)), dma((4, 2)), dma((2,))] * net,
        compiler_params=pltpu.CompilerParams(vmem_limit_bytes=60 * 2**20, **(dict(collective_id=4, has_side_effects=True) if net else {})),
    )(x, dh, dh, dl, dl, w1, *wired)

def wide_kernel(f_ref, d_ref, e_ref, g_ref, r_ref, q_ref, acc, acq):
    m = pl.program_id(0)
    p = lax.axis_index("pair")
    @pl.when(m == 0)
    def _():
        acc[...] = jnp.zeros_like(acc)
        acq[...] = jnp.zeros_like(acq)
    f = split(jnp.concatenate([f_ref[0, i] for i in range(4)], axis=1))
    def block(ref):
        return jnp.concatenate([jnp.concatenate([ref[0, i, 128 * c:128 * c + 128, :] for c in range(2)], axis=1) for i in range(4)], axis=0)
    acc[0] += dot3(f, split(block(d_ref)))
    acc[1] += dot3(f, split(block(e_ref)))
    dz = jnp.concatenate([d_ref[0, i, 256:312, :] for i in range(4)], axis=1)
    row = lax.broadcasted_iota(jnp.int32, (PAD, 512), 0)
    chosen = dz[ATOMS:ATOMS + 1].astype(jnp.int32)
    d = jnp.where(row < ATOMS, dz, 0.0)
    da = jnp.concatenate([d] + [mask_of(chosen, i) * d for i in range(ACTIONS)] + [jnp.zeros((1152 - 19 * PAD, 512), F32)], axis=0)
    g = split(jnp.concatenate([g_ref[0, i] for i in range(4)], axis=1))
    acq[...] += dot3(g, split(da), NT)
    @pl.when(m == 3)
    def _():
        r_ref[:, 0:256] = jnp.where(p == 0, acc[0], acc[1])
        r_ref[:, 256:512] = jnp.where(p == 0, acc[1], acc[0])
        q_ref[...] = acq[...]

def wide_grads(f2, d2, d3, g2):
    full = lambda *s: pl.BlockSpec(s, lambda j: (0,) * len(s))
    part = lambda n: pl.BlockSpec((1, 4, n, 128), lambda j: (j, 0, 0, 0))
    sds = lambda *s: jax.ShapeDtypeStruct(s, F32)
    return pl.pallas_call(
        wide_kernel, grid=(4,),
        in_specs=[part(200), part(312), part(256), part(32)],
        out_specs=[full(200, 512), full(32, 1152)],
        out_shape=[sds(200, 512), sds(32, 1152)],
        scratch_shapes=[pltpu.VMEM((2, 200, 256), F32), pltpu.VMEM((32, 1152), F32)],
        compiler_params=pltpu.CompilerParams(vmem_limit_bytes=60 * 2**20),
    )(f2, d2, d3, g2)

ROWS = 768

def sum_kernel(ag_ref, in_ref, out_ref, s0_ref, s1_ref, s2_ref, mean_ref, sigma_ref, tot_ref, pay, got, red, ss, sr, ts, tr, own):
    p, g = lax.axis_index("pair"), lax.axis_index("group")
    reps = lax.axis_size("rep")
    r = lax.axis_index("rep")
    me = (p * 2 + g) * reps + r
    chip = g * reps + r
    count = 4 * reps
    size = ROWS // count
    def spot(i):
        return (i // (2 * reps), (i // reps) % 2, i % reps)
    barrier = pltpu.get_barrier_semaphore()
    for k in range(1, count):
        pl.semaphore_signal(barrier, inc=1, device_id=spot((me + k) % count), device_id_type=MESH_ID)
    pl.semaphore_wait(barrier, count - 1)
    pay[0:24, :] = s0_ref[...]
    pay[24:672, :] = s1_ref[...]
    pay[672:736, :] = s2_ref[...]
    pay[736:, :] = jnp.zeros((ROWS - 736, 128), F32)
    def first(k):
        to = (me + k) % count
        src, dst = pay.at[pl.ds(pl.multiple_of(to * size, 8), size)], got.at[chip]
        return remote(src, dst, ss.at[k], sr.at[chip], spot(to)) if k else pltpu.make_async_copy(src, dst, own)
    @pl.when(p == 0)
    def _():
        for k in range(count):
            first(k).start()
    row_in = in_ref[...]
    for s in range(2):
        tall = column(in_ref[s:s + 1, :], 512) * out_ref[s:s + 1, :]
        for z, (start, n) in enumerate(((0, 200), (200, 200), (400, 184), (584, 200))):
            v = ag_ref[s, z, 0:n, :]
            mean_ref[s, start:start + n, :] = v
            sigma_ref[s, start:start + n, :] = v * tall[start:start + n]
    @pl.when(p == 0)
    def _():
        for k in range(1, count):
            first(k).wait_send()
        first(0).wait()
    for c in range(2 * reps):
        wait = remote(pay.at[pl.ds(0, size)], got.at[c], ss.at[0], sr.at[c], spot((me + 1) % count)).wait_recv
        pl.when(jnp.logical_or(p == 1, chip != c))(wait)
    red[...] = jnp.sum(got[...], axis=0)
    here = pl.ds(pl.multiple_of(me * size, 8), size)
    sends = [remote(red, tot_ref.at[here], ts.at[k], tr.at[me], spot((me + k) % count)) for k in range(1, count)]
    for copy in sends:
        copy.start()
    tot_ref[here, :] = red[...]
    for copy in sends:
        copy.wait_send()
    for k in range(1, count):
        who = (me + k) % count
        remote(red, tot_ref.at[pl.ds(pl.multiple_of(who * size, 8), size)], ts.at[k], tr.at[who], spot(who)).wait_recv()

def sum_all(ag, n_in, n_out, s0, s1, s2):
    vm = pl.BlockSpec(memory_space=pltpu.VMEM)
    sds = lambda *s: jax.ShapeDtypeStruct(s, F32)
    dma = pltpu.SemaphoreType.DMA
    return pl.pallas_call(
        sum_kernel,
        in_specs=[vm] * 6, out_specs=[vm] * 3,
        out_shape=[sds(2, 784, 512), sds(2, 784, 512), sds(ROWS, 128)],
        scratch_shapes=[pltpu.VMEM((ROWS, 128), F32), pltpu.VMEM((16, 24, 128), F32), pltpu.VMEM((24, 128), F32),
                        dma((32,)), dma((16,)), dma((32,)), dma((32,)), dma],
        compiler_params=pltpu.CompilerParams(vmem_limit_bytes=60 * 2**20, collective_id=5, has_side_effects=True),
    )(ag, n_in, n_out, s0, s1, s2)

def torso_grads(total):
    g1 = total[672:736].reshape(2, 32, 4, 8, 4)
    k1 = jnp.transpose(g1, (1, 4, 0, 2, 3)).reshape(32, 4, 8, 8)
    g2 = total[24:280].reshape(2, 2, 64, 4, 32)
    k2 = jnp.transpose(g2, (2, 4, 1, 0, 3)).reshape(64, 32, 4, 4)
    g3 = jnp.concatenate([total[280:472], total[472:664, 0:64]], axis=1).reshape(3, 64, 3, 64)
    k3 = jnp.transpose(g3, (1, 3, 0, 2))
    return k1, total[666, 0:32], k2, total[665, 0:64], k3, total[664, 0:64]

def online_only(value):
    other = lax.ppermute(value, "pair", [(0, 1)])
    return jnp.where(lax.axis_index("pair") == 0, value, other)

def exchange(parts):
    groups = lax.axis_size("group")
    p, g = lax.axis_index("pair"), lax.axis_index("group")
    got = []
    for k in range(groups):
        to = (g + k) % groups
        mine = parts(0, to)
        if k:
            mine = lax.ppermute(mine, ("pair", "group"), [(i, (i + k) % groups) for i in range(groups)])
        theirs = lax.ppermute(parts(1, to), ("pair", "group"), [(i, groups + (i + k) % groups) for i in range(groups)])
        got.append(jnp.where(p == 0, mine, theirs))
    return got

HIGH = lax.Precision.HIGH

def local(states, actions, proj_lower, proj_upper, proj_weight, first_kernel, first_bias, second_kernel, second_bias,
          third_kernel, third_bias, hidden_mean, hidden_sigma, hidden_bias_mean, hidden_bias_sigma, head_mean, head_sigma,
          head_bias_mean, head_bias_sigma, hidden_noise_in, hidden_noise_out, head_noise_in, head_noise_out):
    pair = lax.axis_index("pair")
    groups = lax.axis_size("group")
    shards = 2 * groups
    net = int(groups == 2 and lax.axis_size("rep") == 8)
    n_in, n_out, e_in, e_out = hidden_noise_in[0], hidden_noise_out[0], head_noise_in[0], head_noise_out[0]
    noise = online_only(jnp.concatenate([v.reshape(-1) for v in (n_in, n_out, e_in, e_out)]))
    on_in = noise[:6272].reshape(2, 3136)
    on_out = noise[6272:7296].reshape(2, 512)
    on_ein = noise[7296:8320].reshape(2, 512)
    on_eout = noise[8320:]
    shard = pair * groups + lax.axis_index("group")
    feat_q, hid_q = 3136 // shards, 512 // shards
    in_q = lax.dynamic_slice_in_dim(on_in, shard * feat_q, feat_q, axis=1)
    e_q = lax.dynamic_slice_in_dim(on_ein, shard * hid_q, hid_q, axis=1)

    x = jnp.transpose(states[0], (2, 3, 1, 0)).reshape(84, 336, 128)
    k1, k2, k3 = first_kernel[0], second_kernel[0], third_kernel[0]
    spread = lambda b, n: jnp.broadcast_to(jnp.tile(b, n)[:, None], (b.shape[0] * n, 128))
    pre1, pre2, pre3, feats = forward(x, *fwd_weights(k1, k2, k3), spread(first_bias[0], 3), spread(second_bias[0], 1), spread(third_bias[0], 1))

    wide = lambda v: jnp.pad(v.reshape(19, ATOMS, -1), ((0, 0), (0, PAD - ATOMS), (0, 0)))
    e_rows = jnp.concatenate([e_in[0:1], jnp.broadcast_to(e_in[1:2], (ACTIONS, 512))])
    wo = wide(head_mean[0].T) + wide(head_sigma[0].T) * (e_rows[:, None, :] * wide(e_out[:, None]))
    bo = jnp.broadcast_to(wide((head_bias_mean[0] + head_bias_sigma[0] * e_out)[:, None]), (19, PAD, 128))
    hb = (hidden_bias_mean[0] + hidden_bias_sigma[0] * n_out).reshape(1, 1024)
    nin = jnp.transpose(n_in.reshape(2, STEPS, 3136 // STEPS), (1, 0, 2))
    bw1, bw2, bw3 = bwd_weights(k1, k2, k3)
    h, hid, logp, dist, *f1 = hidden(net, feats, hidden_mean[0], hidden_sigma[0], nin, n_out, hb, wo, bo, actions, proj_lower.T, proj_weight.T)
    target = lax.ppermute(dist, "pair", [(1, 0)])
    df, msg, small_b, *f2g1 = hidden_bwd(net, target, logp, h, hidden_mean[0], hidden_sigma[0], nin, n_out, wo, actions, *f1, *([hid] * net))
    if net:
        f2, g1 = f2g1
        dh, dl, small_d, _, d2, d3, g2 = lower_backward(net, pre1, pre2, pre3, df, bw2, bw3, msg, g1)
        part_r, part_q = wide_grads(f2, d2, d3, g2)
        small_f, grad_rows, ag, ah = first_backward(net, x, dh, dl, bw1, part_r, part_q)
        hidden_grad, hidden_sigma_grad, total = sum_all(ag, in_q, on_out, small_b, small_d, small_f)
        value_part = jnp.transpose(ah[0].reshape(128, 1152)[:, :ATOMS])
        adv_part = jnp.transpose(ah[1].reshape(128, 1152)[:, PAD:19 * PAD].reshape(128, ACTIONS, PAD)[:, :, :ATOMS], (1, 2, 0)).reshape(ACTIONS * ATOMS, 128)
        head_grad = jnp.concatenate([value_part, adv_part], axis=0)
    else:
        f_got = exchange(lambda p, g: lax.dynamic_slice_in_dim(feats, (p * groups + g) * feat_q, feat_q, axis=0))
        hid = jnp.transpose(hid, (3, 0, 2, 1, 4, 5)).reshape(1024, 128).T
        hid_got = exchange(lambda p, g: lax.dynamic_slice_in_dim(hid.reshape(128, 2, 512), (p * groups + g) * hid_q, hid_q, axis=2))
        dpre = jnp.transpose(msg[:, :, :256].reshape(2, 2, 2, 128, 128), (3, 1, 0, 2, 4)).reshape(128, 1024)
        dz = msg[0, 0, 256:]
        d_all = jnp.concatenate(exchange(lambda p, g: jnp.concatenate([dpre, dz.T, jnp.zeros((128, 72), F32)], axis=1)), axis=0)
        f_all = jnp.concatenate(f_got, axis=1)
        hid_all = jnp.concatenate(hid_got, axis=0)
        part_hidden = jnp.einsum("fb,bsh->sfh", f_all, d_all[:, :1024].reshape(-1, 2, 512), precision=HIGH)
        dz_all = d_all[:, 1024:1024 + ATOMS]
        picked = d_all[:, 1024 + ATOMS]
        mask = jnp.where(picked[None, :] == jnp.arange(ACTIONS, dtype=F32)[:, None], 1.0 - 1.0 / ACTIONS, -1.0 / ACTIONS)
        da = (mask[:, None, :] * dz_all.T[None]).reshape(ACTIONS * ATOMS, -1)
        part_head = jnp.concatenate([jnp.dot(dz_all.T, hid_all[:, 0], precision=HIGH), jnp.dot(da, hid_all[:, 1], precision=HIGH)], axis=0)
        hidden_grad, head_grad = lax.psum((part_hidden, part_head), "rep")
        dh, dl, small_d = lower_backward(net, pre1, pre2, pre3, df, bw2, bw3)
        small_f, lo, up = first_backward(net, x, dh, dl, bw1)
        grad_rows = jnp.where(pair == 0, lo, lax.ppermute(up, "pair", [(0, 1)]))
        total = lax.psum(jnp.concatenate([small_b, small_d, small_f], axis=0), ("pair", "group", "rep"))
        hidden_sigma_grad = hidden_grad * (in_q[:, :, None] * on_out[:, None, :])
    states_grad = jnp.transpose(grad_rows.reshape(84, 84, 2, 128), (3, 2, 0, 1))
    gk1, gb1, gk2, gb2, gk3, gb3 = torso_grads(total)
    hb_grad = total[0:8].reshape(2, 512)
    bo_grad = total[8:17].reshape(-1)[:19 * PAD].reshape(19, PAD)[:, :ATOMS].reshape(-1)
    loss = total[17, 0]
    column_of = jnp.arange(on_eout.shape[0])[:, None]
    head_sigma_grad = head_grad * (jnp.where(column_of < ATOMS, e_q[0:1], e_q[1:2]) * on_eout[:, None])
    return (loss, states_grad, gk1, gb1, gk2, gb2, gk3, gb3, hidden_grad, hidden_sigma_grad,
            hb_grad, hb_grad * on_out, head_grad.T, head_sigma_grad.T, bo_grad, bo_grad * on_eout)


def solution(mesh):
    placed = (
        P("pair", ("group", "rep"), None, None, None),
        P("pair", ("group", "rep")),
        P(("group", "rep"), None),
        P(("group", "rep"), None),
        P(("group", "rep"), None),
        P("pair", None, None, None, None),
        P("pair", None),
        P("pair", None, None, None, None),
        P("pair", None),
        P("pair", None, None, None, None),
        P("pair", None),
        P("pair", None, None, None),
        P("pair", None, None, None),
        P("pair", None, None),
        P("pair", None, None),
        P("pair", None, None),
        P("pair", None, None),
        P("pair", None),
        P("pair", None),
        P("pair", None, None),
        P("pair", None, None),
        P("pair", None, None),
        P("pair", None),
    )
    return jax.shard_map(
        local,
        mesh=mesh,
        in_specs=placed,
        out_specs=(
            P(),
            P(("group", "rep"), "pair", None, None),
            P(),
            P(),
            P(),
            P(),
            P(),
            P(),
            P(None, ("pair", "group"), None),
            P(None, ("pair", "group"), None),
            P(),
            P(),
            P(("pair", "group"), None),
            P(("pair", "group"), None),
            P(),
            P(),
        ),
        check_vma=False,
    )
```

time: 528 us -> 312 us (0.59)
  waiting for transfers between devices: 272 us -> 0.01 us
  Pallas kernels: 117 us -> 245 us
  starting transfers between devices: 31.1 us -> 4.5 us
  other arithmetic: 29.7 us -> 9.2 us
  between operations: 14.9 us -> 1.23 us
  matrix products: 5.82 us -> 0 us
    psum x2 -> x0, waiting for transfers between devices: 263 us -> none  [the longest x1 140 us: local(): hidden_grad, head_grad = lax.psum((part_hidden, part_head), 'rep')]
    pallas_call x3 -> x6, Pallas kernels: 84.8 us -> 213 us  [the longest x1 69.3 us: first_backward(): pl.pallas_call(functools.partial(first_kernel_bwd, net), grid=(21,), in_s...]
    ppermute x10 -> x0, starting transfers between devices: 28.1 us -> none  [the longest x6 15.6 us: exchange(): lax.ppermute(parts(1, to), ('pair', 'group'), [(i, groups + (i + k) % gro...]
    select_n x8 -> x0, other arithmetic: 10.9 us -> none  [the longest x1 6.96 us: local(): grad_rows = jnp.where(pair == 0, lo, moved)]
    concatenate x2 -> x0, local copies, waits for them, and re-layouts: 8.62 us -> none  [the longest x1 7.48 us: local(): jnp.concatenate([v.reshape(-1) for v in small])]
    ppermute x10 -> x0, waiting for transfers between devices: 7.6 us -> none  [the longest x3 7.58 us: exchange(): lax.ppermute(mine, ('pair', 'group'), [(i, (i + k) % groups) for i in ran...]
    unnamed x66 -> x57, local copies, waits for them, and re-layouts: 13.2 us -> 19.6 us
    dot_general x3 -> x0, matrix products: 5.82 us -> none  [the longest x1 3.15 us: local(): jnp.einsum('fb,bsh->sfh', f_all, d_all[:, :1024].reshape(-1, 2, 512), pre...]
  transfers between devices with their start and end apart: 14 -> 2, of which waited for: 5 -> 0; matrix products, arithmetic and copies ran while one was open for 12% -> 3% of each run, Pallas kernels for 6% -> 53%
where the time goes in v2:
time: 312 us; the launch traced here: 311 us
  Pallas kernels  245 us (79%)
  local copies, waits for them, and re-layouts  51 us (16%)
  other arithmetic  9.2 us (3%)
  starting transfers between devices  4.5 us (1%)
    pallas_call x1, Pallas kernels, first_backward(): pl.pallas_call(functools.partial(first_kernel_bwd, net), grid=(21,), in_s...  69.3 us
    pallas_call x1, Pallas kernels, lower_backward(): pl.pallas_call(functools.partial(low_kernel, net), grid=(1,), in_specs=[o...  55.2 us
    pallas_call x1, Pallas kernels, forward(): pl.pallas_call(fwd_kernel, grid=(21,), in_specs=[pl.BlockSpec((4, 336, 12...  32.1 us
    pallas_call x1, Pallas kernels, hidden_bwd(): pl.pallas_call(functools.partial(hid_bwd_kernel, net), grid=(STEPS,), in_...  31 us
    pallas_call x1, Pallas kernels, sum_all(): pl.pallas_call(sum_kernel, in_specs=[vm] * 6, out_specs=[vm] * 3, out_sha...  24.8 us
    pallas_call x1, Pallas kernels, hidden(): pl.pallas_call(functools.partial(hid_kernel, net), grid=(STEPS,), in_spec...  24.3 us
    unnamed x57, local copies, waits for them, and re-layouts  19.6 us
    pallas_call x1, Pallas kernels, wide_grads(): pl.pallas_call(wide_kernel, grid=(4,), in_specs=[part(200), part(312), pa...  8.18 us
  transfers between devices with their start and end apart: 2, of which 0 were waited for; matrix products, arithmetic and copies ran while one was open for 3% of the time, Pallas kernels for 53%

profile of v2, /device:TPU:0, one launch (start us, length us, event | category | flops | bytes accessed | tf_op | source)
XLA Modules:
  0.0 310.8 jit_solution(3399688763644091482)
XLA Ops:
  0.6 1.0 copy.75
  1.8 0.3 copy.76
  2.1 0.9 reshape.182.w1_ref
  3.4 1.0 copy.79
  4.5 0.2 reshape.183
  4.7 0.8 copy.80.w2_ref
  5.6 0.5 broadcast.48
  6.1 0.7 reduce.9
  6.8 0.7 reduce.10
  7.6 0.7 reduce.11
  8.4 1.4 copy.114
  9.9 1.7 reshape.186
  11.6 3.0 copy.113
  14.6 3.0 reshape.187
  17.8 0.6 copy.118
  18.4 0.6 copy.104
  19.1 3.4 %multiply_add_fusion.wo_ref = f32[19,56,512]{2,1,0:T(8,128)} fusion(f32[19,51,512]{2,1,0:T(8,128)} %reshape.187, f32[19,51,512]{2,1,0:T(8,128)S(1)} %reshape.186, f32[19,56]{1,0:T(8,128)S(1)} %pad_bitcast_fusion.8, f32[19,512]{1,0:T(8,128)S(1)} %pad_maximum_fusion.6), kind=kLoop, calls=%fused_computation | loop fusion | flops 1634304 | bytes 6191264 | tf_op jit(solution)/shard_map/add | solution.py:860
  22.4 0.7 broadcast_in_dim.67.b1_ref
  23.1 0.7 broadcast_in_dim.69.b2_ref
  23.8 0.7 broadcast_in_dim.71.b3_ref
  24.5 32.1 %shard_map.333 = (f32[20,640,128]{2,1,0:T(8,128)}, f32[9,576,128]{2,1,0:T(8,128)}, f32[3136,128]{1,0:T(8,128)}, f32[3136,128]{1,0:T(8,128)}) custom-call(f32[84,336,128]{2,1,0:T(8,128)} %bitcast.157, f32[192,256]{1,0:T(8,128)} %reshape.182.w1_ref, f32[128,256]{1,0:T(8,128)} %copy.80.w2_ref, f32[384,256]{1,0:T(8,128)} %bitcast.169, ...), custom_call_target="tpu_custom_call" | custom-call | tf_op jit(solution)/shard_map/pallas_call | solution.py:111
  56.6 1.0 broadcast_in_dim.75.bo_ref
  57.6 24.3 %shard_map.334 = (f32[128,1024]{1,0:T(8,128)}, f32[2,4,2,2,32,128]{5,4,3,2,1,0:T(8,128)}, f32[56,128]{1,0:T(8,128)}, f32[56,128]{1,0:T(8,128)}, f32[2,4,200,128]{3,2,1,0:T(8,128)}) custom-call(f32[3136,128]{1,0:T(8,128)} %get-tuple-element.48.f_ref.rest_0_, f32[2,3136,512]{2,1,0:T(8,128)} %bitcast.159, f32[2,3136,512]{2,1,0:T(8,128)} %bitcast.161, ...), custom_call_target="tpu_custom_call" | custom-call | tf_op jit(solution)/shard_map/pallas_call | solution.py:300
  81.8 1.3 collective-permute-start
  83.3 3.2 %collective-permute-start.1 = (f32[9289]{0:T(1024)S(1)}, f32[9289]{0:T(1024)S(1)}, u32[]{:S(2)}, u32[]{:S(2)}) collective-permute-start(f32[9289]{0:T(1024)S(1)} %pad_maximum_fusion.7), channel_id=1, source_target_pairs={{0,16},{1,17},{2,18},{3,19},{4,20},{5,21},{6,22},{7,23},{8,24},{9,... | collective-permute-start | bytes 111476 | tf_op jit(solution)/shard_map/ppermute | solution.py:817
  87.1 0.3 pad_maximum_fusion.3
  87.4 0.9 pad_maximum_fusion.1
  88.3 0.3 copy.85
  88.6 1.2 reshape.189.w3_ref
  90.0 0.7 rev.6
  90.7 0.9 reshape.188.w2_ref
  91.6 1.1 reshape.190.w1_ref
  92.8 0.6 copy-done.11
  93.4 31.0 %shard_map.335 = (f32[3136,128]{1,0:T(8,128)}, f32[2,2,312,128]{3,2,1,0:T(8,128)}, f32[24,128]{1,0:T(8,128)}, f32[4,4,200,128]{3,2,1,0:T(8,128)}, f32[4,2,2,32,128]{4,3,2,1,0:T(8,128)}) custom-call(f32[56,128]{1,0:T(8,128)} %copy-done.11, f32[56,128]{1,0:T(8,128)} %get-tuple-element.50.logp_ref, f32[128,1024]{1,0:T(8,128)} %get-tuple-element.51.h_ref, ...), custom_call_target="tpu_custom_call" | custom-call | tf_op jit(solution)/shard_map/pallas_call | solution.py:379
  124.3 55.2 %shard_map.336 = (bf16[22,704,128]{2,1,0:T(8,128)(2,1)}, bf16[22,704,128]{2,1,0:T(8,128)(2,1)}, f32[648,128]{1,0:T(8,128)}, f32[4,2,312,128]{3,2,1,0:T(8,128)}, ...) custom-call(f32[20,640,128]{2,1,0:T(8,128)} %get-tuple-element.45.pre1_ref, ...), custom_call_target="tpu_custom_call" | custom-call | tf_op jit(solution)/shard_map/pallas_call | solution.py:561
  179.6 8.2 %shard_map.337 = (f32[200,512]{1,0:T(8,128)}, f32[32,1152]{1,0:T(8,128)}) custom-call(f32[4,4,200,128]{3,2,1,0:T(8,128)} %get-tuple-element.59.f_ref, f32[4,4,312,128]{3,2,1,0:T(8,128)} %get-tuple-element.60.d_ref, f32[4,4,256,128]{3,2,1,0:T(8,128)} %get-tuple-element.61.e_ref, f32[4,4,32,128]{3,2,1,0:T(8,128)} %get-tuple-element.62.g_ref), custom_call_target="tpu_custom_call" | custom-call | tf_op jit(solution)/shard_map/pallas_call | solution.py:730
  187.8 69.3 %shard_map.338 = (f32[64,128]{1,0:T(8,128)}, f32[84,168,128]{2,1,0:T(8,128)}, f32[2,4,200,512]{3,2,1,0:T(8,128)}, f32[2,4,32,1152]{3,2,1,0:T(8,128)}) custom-call(f32[84,336,128]{2,1,0:T(8,128)} %bitcast.158, bf16[22,704,128]{2,1,0:T(8,128)(2,1)} %get-tuple-element.57.dha_ref.dhb_ref, bf16[22,704,128]{2,1,0:T(8,128)(2,1)} %get-tuple-element.57.dha_ref.dhb_ref, ...), custom_call_target="tpu_custom_call" | custom-call | tf_op jit(solution)/shard_map/pallas_call | solution.py:689
  257.1 1.3 fusion.1
  258.4 0.2 slice.140
  258.6 0.2 copy.103
  259.2 0.6 reshape.192.out_ref
  259.8 0.7 constant_dynamic-slice_fusion.1.in_ref
  260.4 24.8 %shard_map.339 = (f32[2,784,512]{2,1,0:T(8,128)}, f32[2,784,512]{2,1,0:T(8,128)}, f32[768,128]{1,0:T(8,128)}) custom-call(f32[2,4,200,512]{3,2,1,0:T(8,128)} %get-tuple-element.65.ag_ref, f32[2,784]{1,0:T(2,128)} %constant_dynamic-slice_fusion.1.in_ref, f32[2,512]{1,0:T(2,128)} %reshape.192.out_ref, f32[24,128]{1,0:T(8,128)} %get-tuple-element.66.s0_ref, ...), custom_call_target="tpu_custom_call" | custom-call | tf_op jit(solution)/shard_map/pallas_call | solution.py:798
  285.2 0.7 slice_bitcast_fusion.4
  285.9 0.9 slice.116
  286.8 0.9 slice.117
  287.7 0.9 slice.114
  288.6 0.8 slice.112
  289.4 0.7 slice.119
  290.1 1.3 slice_bitcast_fusion.8
  291.3 1.2 slice.111
  292.5 1.2 slice_bitcast_fusion.10
  293.9 0.6 slice_multiply_fusion
  294.5 0.2 reshape.198
  294.7 0.7 copy.97
  295.5 0.2 reshape.196
  295.7 0.9 copy.96
  296.8 0.7 copy.91
  297.5 0.6 mul.74
  298.1 1.2 multiply_bitcast_fusion
  299.3 6.7 %copy.122 = f32[128,2,84,84]{0,1,3,2:T(2,128)} copy(f32[128,2,84,84]{0,1,3,2:T(2,128)} %bitcast.165) | data formatting | bytes 14450688
  306.0 1.7 copy.123
  307.7 1.4 copy-done
  309.1 1.7 copy.124
  (96 shorter events, 2.7 us)
Async XLA Ops:
  1.6 1.4 copy-start.3
  3.0 1.3 copy-start.4
  3.3 2.2 copy-start.21
  3.3 2.8 copy-start.9
  3.3 3.6 %copy-start.15 = (f32[1,969]{1,0:T(1,128)S(1)}, f32[1,969]{1,0:T(1,128)}, u32[]{:S(2)}) copy-start(f32[1,969]{1,0:T(1,128)} %param.39) | copy-start | bytes 11632
  3.3 4.3 %copy-start.16 = (f32[1,969]{1,0:T(1,128)S(1)}, f32[1,969]{1,0:T(1,128)}, u32[]{:S(2)}) copy-start(f32[1,969]{1,0:T(1,128)} %param.40) | copy-start | bytes 11632
  3.3 5.1 %copy-start.13 = (f32[1,2,512]{2,1,0:T(2,128)S(1)}, f32[1,2,512]{2,1,0:T(2,128)}, u32[]{:S(2)}) copy-start(f32[1,2,512]{2,1,0:T(2,128)} %param.43) | copy-start | bytes 12292
  3.3 5.1 %copy-start.2 = (f32[1,512,969]{1,0,2:T(1,128)S(1)}, f32[1,512,969]{1,0,2:T(1,128)}, u32[]{:S(2)}) copy-start(f32[1,512,969]{1,0,2:T(1,128)} %param.37) | copy-start | bytes 5953540
  14.6 3.1 copy-start.6
  14.6 3.8 %copy-start.7 = (f32[1,2,512]{2,1,0:T(2,128)S(1)}, f32[1,2,512]{2,1,0:T(2,128)}, u32[]{:S(2)}) copy-start(f32[1,2,512]{2,1,0:T(2,128)} %param.42) | copy-start | bytes 12292
  14.6 3.8 %copy-start.17 = (f32[1,2,512]{2,1,0:T(2,128)S(1)}, f32[1,2,512]{2,1,0:T(2,128)}, u32[]{:S(2)}) copy-start(f32[1,2,512]{2,1,0:T(2,128)} %param.35) | copy-start | bytes 12292
  14.6 3.8 %copy-start.18 = (f32[1,2,512]{2,1,0:T(2,128)S(1)}, f32[1,2,512]{2,1,0:T(2,128)}, u32[]{:S(2)}) copy-start(f32[1,2,512]{2,1,0:T(2,128)} %param.36) | copy-start | bytes 12292
  19.0 4.1 %copy-start.19 = (f32[1,64]{1,0:T(1,128)S(1)}, f32[1,64]{1,0:T(1,128)}, u32[]{:S(2)}) copy-start(f32[1,64]{1,0:T(1,128)} %param.30) | copy-start | bytes 772
  19.0 4.8 %copy-start.20 = (f32[1,64]{1,0:T(1,128)S(1)}, f32[1,64]{1,0:T(1,128)}, u32[]{:S(2)}) copy-start(f32[1,64]{1,0:T(1,128)} %param.32) | copy-start | bytes 772
  57.6 25.7 %copy-start.8 = (f32[1,2,512]{2,1,0:T(2,128)S(1)}, f32[1,2,512]{2,1,0:T(2,128)}, u32[]{:S(2)}) copy-start(f32[1,2,512]{2,1,0:T(2,128)} %param.42) | copy-start | bytes 12292
  57.6 28.9 %copy-start.5 = (f32[1,32,4,8,8]{1,4,3,2,0:T(8,128)S(1)}, f32[1,32,4,8,8]{1,4,3,2,0:T(8,128)}, u32[]{:S(2)}) copy-start(f32[1,32,4,8,8]{1,4,3,2,0:T(8,128)} %param.27) | copy-start | bytes 98308
  81.8 10.9 %collective-permute-start = (f32[56,128]{1,0:T(8,128)}, f32[56,128]{1,0:T(8,128)S(1)}, u32[]{:S(2)}, u32[]{:S(2)}) collective-permute-start(f32[56,128]{1,0:T(8,128)} %get-tuple-element.49), channel_id=1, source_target_pairs={{16,0},{17,1},{18,2},{19,3},{20,4},{21,5},{22,6},{23,7},{24,8},{25... | collective-permute-start | bytes 86024 | tf_op jit(solution)/shard_map/ppermute | solution.py:866
  83.3 175.8 %collective-permute-start.1 = (f32[9289]{0:T(1024)S(1)}, f32[9289]{0:T(1024)S(1)}, u32[]{:S(2)}, u32[]{:S(2)}) collective-permute-start(f32[9289]{0:T(1024)S(1)} %pad_maximum_fusion.7), channel_id=1, source_target_pairs={{0,16},{1,17},{2,18},{3,19},{4,20},{5,21},{6,22},{7,23},{8,24},{9,... | collective-permute-start | bytes 111476 | tf_op jit(solution)/shard_map/ppermute | solution.py:817
  92.8 0.6 copy-start.11
  287.7 9.8 %copy-start.10 = (f32[2,512]{1,0:T(2,128)S(1)}, f32[2,512]{1,0:T(2,128)}, u32[]{:S(2)}) copy-start(f32[2,512]{1,0:T(2,128)} %reshape.192.out_ref) | copy-start | bytes 12292
  293.9 5.5 %copy-start.14 = (f32[969]{0:T(1024)}, f32[969]{0:T(1024)S(1)}, u32[]{:S(2)}) copy-start(f32[969]{0:T(1024)S(1)} %reshape.205) | copy-start | bytes 11632
  297.5 8.5 %copy-start.12 = (f32[2,512]{1,0:T(2,128)}, f32[2,512]{1,0:T(2,128)S(1)}, u32[]{:S(2)}) copy-start(f32[2,512]{1,0:T(2,128)S(1)} %reshape.199) | copy-start | bytes 12292
  299.3 6.7 %copy-start.1 = (f32[2,784,512]{2,1,0:T(8,128)S(1)}, f32[2,784,512]{2,1,0:T(8,128)}, u32[]{:S(2)}) copy-start(f32[2,784,512]{2,1,0:T(8,128)} %get-tuple-element.162) | copy-start | bytes 9633796
  306.0 3.1 copy-start

commit v3 on v2

v3 whole, which is shorter than its diff:
```python
import functools
import jax
import jax.numpy as jnp
from jax import lax
from jax.experimental import pallas as pl
from jax.experimental.pallas import tpu as pltpu
from jax.sharding import PartitionSpec as P

BF = jnp.bfloat16
F32 = jnp.float32
NN=(((1,),(0,)),((),()))
NT=(((1,),(1,)),((),()))
TN=(((0,),(0,)),((),()))

def split(v):
    hi = v.astype(BF)
    return hi, (v - hi.astype(F32)).astype(BF)

def dot(a, b, dims=NN):
    return lax.dot_general(a, b, dims, preferred_element_type=F32)

def dot3(a, b, dims=NN):
    ah, al = a; bh, bl = b
    return dot(ah, bh, dims) + (dot(ah, bl, dims) + dot(al, bh, dims))

def silu(v):
    return v * jax.nn.sigmoid(v)

def prep_kernel(k1_ref, k2_ref, k3_ref, b1_ref, b2_ref, b3_ref, f1_ref, f2_ref, f3_ref, r1_ref, r2_ref, r3_ref, c1_ref, c2_ref, c3_ref,
                t1a, t1b, u1a, u1b, m2, m3, n2, n3):
    for ref in (t1a, t1b, u1a, u1b, m2, m3, n2, n3):
        ref[...] = jnp.zeros_like(ref)
    def put(ref, start, stride, v, lane):
        n = v.shape[0]
        pieces = [jnp.zeros((n, lane), F32)] * (lane > 0) + [v] + [jnp.zeros((n, 96 - lane), F32)] * (lane < 96)
        rows = pl.ds(start, n, stride=stride)
        ref[rows, :] = ref[rows, :] + jnp.concatenate(pieces, axis=1)
    for c in range(4):
        for ky in range(8):
            v = k1_ref[c, ky]
            h, kq = ky // 4, ky % 4
            for w in range(3):
                put((t1a, t1b)[h], kq * 64 + 16 * w + c, 4, v, 32 * w)
            base = (c // 2) * 96 + kq * 24 + c % 2
            for q in range(4):
                if q == 0:
                    put((u1b, u1a)[h], base, 2, v[4:8], 0)
                elif q == 3:
                    put((u1b, u1a)[h], base + 16, 2, v[0:4], 96)
                else:
                    put((u1b, u1a)[h], base + 8 * (q - 1), 2, v, 32 * q)
    for ky in range(4):
        for kx in range(4):
            v = k2_ref[:, ky, kx, :]
            h, py, wx, px = ky // 2, ky % 2, 1 - kx // 2, kx % 2
            m2[py * 128 + kx * 32:py * 128 + kx * 32 + 32, 64 * h:64 * h + 64] = v
            n2[(py * 2 + px) * 32:(py * 2 + px) * 32 + 32, 128 * (1 - h) + 64 * wx:128 * (1 - h) + 64 * wx + 64] = v
    for ky in range(3):
        for kx in range(3):
            v = k3_ref[ky, kx]
            vt = jnp.transpose(v)
            for w in range(2):
                m3[ky * 128 + w * 64:ky * 128 + w * 64 + 64, 64 * (w + kx):64 * (w + kx) + 64] = v
                q = w + 2 - kx
                n3[ky * 128 + w * 64:ky * 128 + w * 64 + 64, 64 * q:64 * q + 64] = vt
    w1 = jnp.concatenate([jnp.transpose(t1a[...])[0:96], jnp.transpose(t1b[...])[0:96]], axis=0)
    pairs = ((f1_ref, w1), (f2_ref, jnp.transpose(m2[...])), (f3_ref, m3[...]), (r1_ref, jnp.concatenate([u1a[...], u1b[...]], axis=1)), (r2_ref, n2[...]), (r3_ref, n3[...]))
    for ref, v in pairs:
        hi, lo = split(v)
        ref[0] = hi
        ref[1] = lo
    for ref, b_ref, n, times in ((c1_ref, b1_ref, 32, 3), (c2_ref, b2_ref, 64, 1), (c3_ref, b3_ref, 64, 1)):
        col = jnp.transpose(jnp.broadcast_to(b_ref[...], (128, n)))
        for i in range(times):
            ref[n * i:n * i + n, :] = col

def prepare(k1, k2, k3, b1, b2, b3):
    vm = pl.BlockSpec(memory_space=pltpu.VMEM)
    bfs = lambda *s: jax.ShapeDtypeStruct(s, BF)
    sds = lambda *s: jax.ShapeDtypeStruct(s, F32)
    f32 = lambda *s: pltpu.VMEM(s, F32)
    return pl.pallas_call(
        prep_kernel, in_specs=[vm] * 6, out_specs=[vm] * 9,
        out_shape=[bfs(2, 192, 256), bfs(2, 128, 256), bfs(2, 384, 256), bfs(2, 192, 256), bfs(2, 128, 256), bfs(2, 384, 256), sds(96, 128), sds(64, 128), sds(64, 128)],
        scratch_shapes=[f32(256, 128), f32(256, 128), f32(192, 128), f32(192, 128), f32(256, 128), f32(384, 256), f32(128, 256), f32(384, 256)],
        compiler_params=pltpu.CompilerParams(vmem_limit_bytes=60 * 2**20),
    )(jnp.transpose(k1, (1, 2, 3, 0)), jnp.transpose(k2, (1, 2, 3, 0)), jnp.transpose(k3, (2, 3, 0, 1)), b1, b2, b3)

def fwd_kernel(x_ref, w1_ref, w2_ref, w3_ref, b1_ref, b2_ref, b3_ref, pre1_ref, pre2_ref, pre3_ref, f_ref,
               xh, xl, top1, top2, acc3, h1h, h1l, h2h, h2l):
    j = pl.program_id(0)
    @pl.when(j == 0)
    def _():
        xh[:, 336:, :] = jnp.zeros((4, 16, 128), BF)
        xl[:, 336:, :] = jnp.zeros((4, 16, 128), BF)
        top1[...] = jnp.zeros_like(top1)
        top2[...] = jnp.zeros_like(top2)
        acc3[...] = jnp.zeros_like(acc3)
        h2h[:, 576:, :] = jnp.zeros((9, 64, 128), BF)
        h2l[:, 576:, :] = jnp.zeros((9, 64, 128), BF)
    v = x_ref[...]
    hi = v.astype(BF)
    xh[:, 0:336, :] = hi
    xl[:, 0:336, :] = (v - hi.astype(F32)).astype(BF)
    rh = jnp.concatenate([xh[:, 48 * i:48 * i + 64, :].reshape(256, 128) for i in range(7)], axis=1)
    rl = jnp.concatenate([xl[:, 48 * i:48 * i + 64, :].reshape(256, 128) for i in range(7)], axis=1)
    r = dot3((w1_ref[0], w1_ref[1]), (rh, rl))
    out = top1[...] + r[96:]
    top1[...] = r[:96]
    b1 = b1_ref[...]
    row = jnp.maximum(j - 1, 0)
    for i in range(7):
        n = 96 if i < 6 else 64
        p = out[:n, 128 * i:128 * i + 128] + b1[:n]
        pre1_ref[0, 96 * i:96 * i + n, :] = p
        hh, hl = split(silu(p))
        h1h[row, 96 * i:96 * i + n, :] = hh
        h1l[row, 96 * i:96 * i + n, :] = hl

    @pl.when(j == pl.num_programs(0) - 1)
    def _():
        w2 = (w2_ref[0], w2_ref[1])
        b2 = b2_ref[...]
        def step2(y, carry):
            rh = jnp.concatenate([h1h[pl.ds(2 * y, 2), 64 * i:64 * i + 128, :].reshape(256, 128) for i in range(9)], axis=1)
            rl = jnp.concatenate([h1l[pl.ds(2 * y, 2), 64 * i:64 * i + 128, :].reshape(256, 128) for i in range(9)], axis=1)
            r = dot3(w2, (rh, rl))
            o = top2[...] + r[64:]
            top2[...] = r[:64]
            row = jnp.maximum(y - 1, 0)
            for i in range(9):
                p = o[:, 128 * i:128 * i + 128] + b2
                pre2_ref[row, 64 * i:64 * i + 64, :] = p
                hh, hl = split(silu(p))
                h2h[row, 64 * i:64 * i + 64, :] = hh
                h2l[row, 64 * i:64 * i + 64, :] = hl
            return carry
        lax.fori_loop(0, 10, step2, 0)
        w3 = (w3_ref[0], w3_ref[1])
        b3 = b3_ref[...]
        def step3(y, carry):
            rh = jnp.concatenate([h2h[y, 128 * i:128 * i + 256, :] for i in range(4)], axis=1)
            rl = jnp.concatenate([h2l[y, 128 * i:128 * i + 256, :] for i in range(4)], axis=1)
            r = dot3(w3, (rh, rl))
            for ky in range(3):
                for i in range(4):
                    acc3[y - ky + 2, 128 * i:128 * i + 128, :] += r[128 * ky:128 * ky + 128, 128 * i:128 * i + 128]
            return carry
        lax.fori_loop(0, 9, step3, 0)
        for y in range(7):
            for x in range(7):
                p = acc3[y + 2, 64 * x:64 * x + 64, :] + b3
                pre3_ref[pl.ds(y * 7 + x, 64, stride=49), :] = p
                f_ref[pl.ds(y * 7 + x, 64, stride=49), :] = silu(p)

def forward(x, w1, w2, w3, b1, b2, b3):
    full = lambda *s: pl.BlockSpec(s, lambda j: (0,) * len(s))
    return pl.pallas_call(
        fwd_kernel,
        grid=(21,),
        in_specs=[pl.BlockSpec((4, 336, 128), lambda j: (j, 0, 0)), full(2, 192, 256), full(2, 128, 256), full(2, 384, 256),
                  full(96, 128), full(64, 128), full(64, 128)],
        out_specs=[pl.BlockSpec((1, 640, 128), lambda j: (jnp.maximum(j - 1, 0), 0, 0)), full(9, 576, 128),
                   full(3136, 128), full(3136, 128)],
        out_shape=[jax.ShapeDtypeStruct((20, 640, 128), F32), jax.ShapeDtypeStruct((9, 576, 128), F32),
                   jax.ShapeDtypeStruct((3136, 128), F32), jax.ShapeDtypeStruct((3136, 128), F32)],
        scratch_shapes=[pltpu.VMEM((4, 352, 128), BF), pltpu.VMEM((4, 352, 128), BF),
                        pltpu.VMEM((96, 896), F32), pltpu.VMEM((64, 1152), F32), pltpu.VMEM((11, 512, 128), F32),
                        pltpu.VMEM((20, 640, 128), BF), pltpu.VMEM((20, 640, 128), BF),
                        pltpu.VMEM((9, 640, 128), BF), pltpu.VMEM((9, 640, 128), BF)],
        compiler_params=pltpu.CompilerParams(vmem_limit_bytes=60 * 2**20),
    )(x, w1, w2, w3, b1, b2, b3)


MESH_ID = pl.DeviceIdType.MESH


def coords():
    r = lax.axis_index("rep")
    return lax.axis_index("pair"), lax.axis_index("group"), r // 2, r % 2


def at(p, g, z, y):
    return (p, g, z * 2 + y)


def flip(z, k):
    return (z, z + 1 - 2 * (z % 2), z + 2 - 4 * (z // 2), 3 - z)[k]


def line(p, g, z, y):
    return [at(q, g, flip(z, k), y) for k in range(4) for q in ((p, 1 - p) if k else (1 - p,))]


def plane(p, g, z, y):
    return [at(p, g, z, 1 - y), at(p, 1 - g, z, y), at(p, 1 - g, z, 1 - y)]


def greet(devices):
    barrier = pltpu.get_barrier_semaphore()
    for device in devices:
        pl.semaphore_signal(barrier, inc=1, device_id=device, device_id_type=MESH_ID)
    pl.semaphore_wait(barrier, len(devices))


def remote(src, dst, send, recv, device):
    return pltpu.make_async_remote_copy(src_ref=src, dst_ref=dst, send_sem=send, recv_sem=recv, device_id=device, device_id_type=MESH_ID)


class Scatter:
    def __init__(self, parts, src, dst, send, recv, own, cores=2):
        self.parts, self.src, self.dst, self.send, self.recv, self.own, self.cores = parts, src, dst, send, recv, own, cores
        self.p, self.g, self.z, self.y = coords()

    def copies(self):
        for k in range(4):
            for q in range(self.cores):
                for i in range(self.parts):
                    zd = flip(self.z, k)
                    if k == 0 and q == 0:
                        yield pltpu.make_async_copy(self.src(q, zd, i), self.dst(self.z, i), self.own.at[i]), True
                    else:
                        yield remote(self.src(q, zd, i), self.dst(self.z, i), self.send.at[k * 2 + q, i], self.recv.at[k, i], at(q, self.g, zd, self.y)), False

    def start(self):
        @pl.when(self.p == 0)
        def _():
            for copy, own in self.copies():
                copy.start()

    def arrived(self, k):
        if self.cores == 1:
            pl.when(self.p == 0)(lambda: self.landed(k))
        else:
            self.landed(k)

    def landed(self, k):
        for i in range(self.parts):
            zs = flip(self.z, k)
            wait = remote(self.src(0, zs, i), self.dst(zs, i), self.send.at[0, i], self.recv.at[k, i], at(1 - self.p, self.g, self.z, self.y)).wait_recv
            local = pltpu.make_async_copy(self.src(0, zs, i), self.dst(zs, i), self.own.at[i]).wait
            if k:
                wait()
            elif self.cores == 1:
                local()
            else:
                pl.when(self.p == 1)(wait)
                pl.when(self.p == 0)(local)

    def sent(self):
        @pl.when(self.p == 0)
        def _():
            for copy, own in self.copies():
                if not own:
                    copy.wait_send()


def scatter_sems(parts):
    return [pltpu.SemaphoreType.DMA((8, parts)), pltpu.SemaphoreType.DMA((4, parts)), pltpu.SemaphoreType.DMA((parts,))]


def f_scatter(f_ref, f1_ref, sems):
    def src(q, zd, i):
        return f_ref.at[pl.ds(pl.multiple_of((2 * q + i) * 784 + jnp.minimum(200 * zd, 584), 8), 200)]
    return Scatter(2, src, lambda z, i: f1_ref.at[i, z], *sems)


def g_scatter(hid_ref, g1_ref, sems):
    return Scatter(1, lambda q, zd, i: hid_ref.at[q, zd], lambda z, i: g1_ref.at[z], *sems)


def d_scatter(msg_ref, d1_ref, sems):
    return Scatter(1, lambda q, zd, i: msg_ref.at[q], lambda z, i: d1_ref.at[z], *sems)


def z_scatter(dz_ref, dz1_ref, sems):
    return Scatter(1, lambda q, zd, i: dz_ref, lambda z, i: dz1_ref.at[z], *sems, cores=1)


def spread_plane(p, g, z, y, src, dst, send, recv):
    places = [(g, y), (g, 1 - y), (1 - g, y), (1 - g, 1 - y)]
    out = [pltpu.make_async_copy(src(*places[0]), dst(0), send.at[0])]
    for m in range(1, 4):
        out.append(remote(src(*places[m]), dst(m), send.at[m], recv.at[m], at(p, places[m][0], z, places[m][1])))
    return out
ATOMS, ACTIONS, PAD = 51, 18, 56
OUTS, OUTP = 969, 976
STEPS = 7
ANY = pl.BlockSpec(memory_space=pl.ANY)
VMEM = pl.BlockSpec(memory_space=pltpu.VMEM)

def column(row, lanes):
    tall = jnp.transpose(jnp.broadcast_to(row, (128, row.shape[1])))
    return jnp.concatenate([tall] * (lanes // 128), axis=1)

def noisy(mean_ref, sigma_ref, nin_ref, nout_ref, s):
    return mean_ref[s] + sigma_ref[s] * (column(nin_ref[0, s:s + 1, :], 512) * nout_ref[s:s + 1, :])

def mask_of(chosen, a):
    return jnp.where(chosen == a, 1.0 - 1.0 / ACTIONS, -1.0 / ACTIONS)

def hid_kernel(net, f_ref, m_ref, s_ref, nin_ref, nout_ref, hb_ref, wo_ref, bo_ref, c_ref, pl_ref, pw_ref, *rest):
    if net:
        f_all, h_ref, g_ref, logp_ref, dist_ref, f1_ref, acc, adv = rest[:8]
        wire = f_scatter(f_all, f1_ref, rest[8:])
    else:
        h_ref, g_ref, logp_ref, dist_ref, acc, adv = rest
    j = pl.program_id(0)
    @pl.when(j == 0)
    def _():
        if net:
            greet(line(*coords()))
            wire.start()
        acc[...] = jnp.zeros_like(acc)
    f = split(f_ref[...])
    for s in range(2):
        w = split(noisy(m_ref, s_ref, nin_ref, nout_ref, s))
        acc[:, 512 * s:512 * s + 512] += dot3(f, w, TN)
    @pl.when(j == pl.num_programs(0) - 1)
    def _():
        h = acc[...] + hb_ref[...]
        h_ref[...] = h
        gt = jnp.transpose(silu(h))
        for s in range(2):
            for q in range(2):
                for gg in range(2):
                    for z in range(4):
                        at_row = 512 * s + 256 * q + 128 * gg + 32 * z
                        g_ref[q, z, gg, s] = gt[at_row:at_row + 32]
        both = dot3(split(wo_ref[...]), split(jnp.concatenate([gt[:512], gt[512:]], axis=1)))
        bias = column(bo_ref[...], 128)
        adv[...] = both[:, 128:] + bias
        z = both[0:PAD, 0:128] + bias[0:PAD]
        chosen = c_ref[...]
        for i in range(ACTIONS):
            z = z + mask_of(chosen, i) * adv[ATOMS * (i + 1):ATOMS * (i + 1) + PAD, :]
        row = lax.broadcasted_iota(jnp.int32, (PAD, 128), 0)
        z = jnp.where(row < ATOMS, z, -1e30)
        top = jnp.max(z, axis=0, keepdims=True)
        e = jnp.exp(z - top)
        tot = jnp.sum(e, axis=0, keepdims=True)
        logp_ref[...] = (z - top) - jnp.log(tot)
        p = e / tot
        dist = jnp.zeros((PAD, 128), F32)
        for i in range(ATOMS):
            lower = pl_ref[i:i + 1, :]
            share = pw_ref[i:i + 1, :]
            pi = p[i:i + 1, :]
            dist = dist + jnp.where(row == lower, pi * (1.0 - share), 0.0) + jnp.where(row == lower + 1, pi * share, 0.0)
        dist_ref[...] = dist
        if net:
            for k in range(4):
                wire.arrived(k)
            wire.sent()

def hidden(net, f, m, s, nin, nout, hb, wo, bo, c, plow, pw):
    full = lambda *t: pl.BlockSpec(t, lambda j: (0,) * len(t))
    sds = lambda *t: jax.ShapeDtypeStruct(t, F32)
    k = 3136 // STEPS
    wspec = pl.BlockSpec((2, k, 512), lambda j: (0, j, 0))
    return pl.pallas_call(
        functools.partial(hid_kernel, net), grid=(STEPS,),
        in_specs=[pl.BlockSpec((k, 128), lambda j: (j, 0)), wspec, wspec, pl.BlockSpec((1, 2, k), lambda j: (j, 0, 0)), full(2, 512), full(1, 1024),
                  full(OUTP, 512), full(1, OUTP), full(1, 128), full(ATOMS, 128), full(ATOMS, 128)] + [ANY] * net,
        out_specs=[full(128, 1024), full(2, 4, 2, 2, 32, 128), full(PAD, 128), full(PAD, 128)] + [ANY] * net,
        out_shape=[sds(128, 1024), sds(2, 4, 2, 2, 32, 128), sds(PAD, 128), sds(PAD, 128)] + [sds(2, 4, 200, 128)] * net,
        scratch_shapes=[pltpu.VMEM((128, 1024), F32), pltpu.VMEM((OUTP, 128), F32)] + scatter_sems(2) * net,
        compiler_params=pltpu.CompilerParams(vmem_limit_bytes=60 * 2**20, **(dict(collective_id=1, has_side_effects=True) if net else {})),
    )(f, m, s, nin, nout, hb, wo, bo, c, plow, pw, *([f] * net))

def hid_bwd_kernel(net, t_ref, logp_ref, h_ref, m_ref, s_ref, nin_ref, nout_ref, wo_ref, c_ref, *rest):
    if net:
        f1_ref, hid_ref, df_ref, small_ref, f2_ref, g1_ref, d1_ref, dz1_ref, dth, dtl, da, msg, dz_to, t_got, fs, fr, ts, tr = rest[:18]
        g_wire = g_scatter(hid_ref, g1_ref, rest[18:21])
        d_wire = d_scatter(msg, d1_ref, rest[21:24])
        z_wire = z_scatter(dz_to, dz1_ref, rest[24:27])
        wires = (g_wire, d_wire, z_wire)
        p, g, z, y = coords()
        fan = spread_plane(p, g, z, y, lambda gd, yd: f1_ref.at[gd], lambda m: f2_ref.at[m], fs, fr)
        target = remote(t_ref, t_got, ts, tr, at(1 - p, g, z, y))
    else:
        df_ref, small_ref, msg, dz_to, dth, dtl, da = rest
        t_got = t_ref
    j = pl.program_id(0)
    def begin():
        t = t_got[...]
        logp = logp_ref[...]
        chosen = c_ref[...]
        row = lax.broadcasted_iota(jnp.int32, (PAD, 128), 0)
        d = (jnp.exp(logp) * jnp.sum(t, axis=0, keepdims=True) - t) * (1.0 / 128)
        loss = -jnp.sum(jnp.where(row < ATOMS, t * logp, 0.0), axis=1, keepdims=True) * (1.0 / 128)
        dz_to[...] = jnp.where(row == ATOMS, chosen.astype(F32), d)
        da[...] = jnp.zeros_like(da)
        da[0:PAD, 0:128] = d
        for i in range(ACTIONS):
            da[ATOMS * (i + 1):ATOMS * (i + 1) + PAD, 128:256] = mask_of(chosen, i) * d
        every = da[...]
        eh, el = split(every)
        grads = dot3((eh, el), split(wo_ref[...]), TN)
        small_ref[...] = jnp.zeros_like(small_ref)
        for s in range(2):
            dp = grads[128 * s:128 * s + 128] * dsilu(h_ref[:, 512 * s:512 * s + 512])
            total = jnp.sum(dp, axis=0, keepdims=True)
            for c in range(4):
                msg[c // 2, s, 128 * (c % 2):128 * (c % 2) + 128, :] = dp[:, 128 * c:128 * c + 128]
                small_ref[4 * s + c:4 * s + c + 1, :] = total[:, 128 * c:128 * c + 128]
            hi, lo = split(jnp.transpose(dp))
            dth[s] = hi
            dtl[s] = lo
        if net:
            d_wire.start()
            z_wire.start()
        ones = jnp.ones((8, 256), BF)
        left = (every - eh.astype(F32)) - el.astype(F32)
        rows = dot(ones, eh, NT) + dot(ones, el, NT) + dot(ones, left.astype(BF), NT)
        for c in range(8):
            n = min(128, OUTP - 128 * c)
            small_ref[8 + c:9 + c, 0:n] = rows[0:1, 128 * c:128 * c + n]
        small_ref[16:17, :] = jnp.broadcast_to(jnp.sum(loss, axis=0, keepdims=True), (1, 128))
    def step():
        out = None
        for s in range(2):
            w = split(noisy(m_ref, s_ref, nin_ref, nout_ref, s))
            r = dot3(w, (dth[s], dtl[s]))
            out = r if out is None else out + r
        df_ref[...] = out
    if not net:
        pl.when(j == 0)(begin)
        step()
        return
    @pl.when(j == 0)
    def _():
        greet(line(p, g, z, y) + plane(p, g, z, y))
        pl.when(p == 1)(target.start)
        for copy in fan:
            copy.start()
        g_wire.start()
        @pl.when(p == 0)
        def _():
            target.wait_recv()
            begin()
    pl.when(p == 0)(step)
    @pl.when(j == pl.num_programs(0) - 1)
    def _():
        pl.when(p == 1)(target.wait_send)
        for copy in fan:
            copy.wait()
        for wire in wires:
            for k in range(4):
                wire.arrived(k)
            wire.sent()

def hidden_bwd(net, t, logp, h, m, s, nin, nout, wo, c, *wired):
    full = lambda *u: pl.BlockSpec(u, lambda j: (0,) * len(u))
    sds = lambda *u: jax.ShapeDtypeStruct(u, F32)
    dma = pltpu.SemaphoreType.DMA
    k = 3136 // STEPS
    wspec = pl.BlockSpec((2, k, 512), lambda j: (0, j, 0))
    return pl.pallas_call(
        functools.partial(hid_bwd_kernel, net), grid=(STEPS,),
        in_specs=[full(PAD, 128), full(PAD, 128), full(128, 1024), wspec, wspec, pl.BlockSpec((1, 2, k), lambda j: (j, 0, 0)), full(2, 512),
                  full(OUTP, 512), full(1, 128)] + [ANY, ANY] * net,
        out_specs=[pl.BlockSpec((k, 128), lambda j: (j, 0)), full(24, 128)] + ([ANY] * 4 if net else [full(2, 2, 256, 128), full(PAD, 128)]),
        out_shape=[sds(3136, 128), sds(24, 128)] + ([sds(4, 4, 200, 128), sds(4, 2, 2, 32, 128), sds(4, 2, 256, 128), sds(4, PAD, 128)] if net
                                                    else [sds(2, 2, 256, 128), sds(PAD, 128)]),
        scratch_shapes=[pltpu.VMEM((2, 512, 128), BF), pltpu.VMEM((2, 512, 128), BF), pltpu.VMEM((OUTP, 256), F32)]
        + ([pltpu.VMEM((2, 2, 256, 128), F32), pltpu.VMEM((PAD, 128), F32), pltpu.VMEM((PAD, 128), F32), dma((4,)), dma((4,)), dma, dma]
           + scatter_sems(1) * 3) * net,
        compiler_params=pltpu.CompilerParams(vmem_limit_bytes=60 * 2**20, **(dict(collective_id=2, has_side_effects=True) if net else {})),
    )(t, logp, h, m, s, nin, nout, wo, c, *wired)

def dsilu(v):
    s = jax.nn.sigmoid(v)
    return s * (1.0 + v * (1.0 - s))

def low_kernel(net, pre1_ref, pre2_ref, pre3_ref, df_ref, w2_ref, w3_ref, *rest):
    if net:
        d1_ref, g1_ref, dz1_ref, d1h, d1l, small_ref, d2_ref, d3_ref, g2_ref, dz2_ref = rest[:10]
        d3f, d3h, d3l, d2h, d2l, h2h, h2l, acc2, a2, a3 = rest[10:20]
        ps, pr, gs, gr, qs, qr, ss, sr, ts, tr = rest[20:]
        p, g, z, y = coords()
        greet(plane(p, g, z, y) + [at(1 - p, g, z, y)])
        fan_d = spread_plane(p, g, z, y, lambda gd, yd: d1_ref.at[:, yd], lambda m: d2_ref.at[m], ps, pr)
        fan_g = spread_plane(p, g, z, y, lambda gd, yd: g1_ref.at[:, gd, yd], lambda m: g2_ref.at[m], gs, gr)
        fan_z = spread_plane(p, g, z, y, lambda gd, yd: dz1_ref, lambda m: dz2_ref.at[m], qs, qr)
        swaps = [remote(d2_ref.at[m], d3_ref.at[m], ss.at[m], sr.at[m], at(1 - p, g, z, y)) for m in range(4)]
        hand = remote(dz2_ref, dz2_ref, ts, tr, at(1 - p, g, z, y))
        for copy in fan_d + fan_g:
            copy.start()
        @pl.when(p == 0)
        def _():
            for copy in fan_z:
                copy.start()
        fan_d[0].wait()
        swaps[0].start()
    else:
        d1h, d1l, small_ref, d3f, d3h, d3l, d2h, d2l, h2h, h2l, acc2, a2, a3 = rest
    def upper():
        for ref in (d3h, d3l, d2h, d2l, acc2, a2, a3):
            ref[...] = jnp.zeros_like(ref)
        small_ref[...] = jnp.zeros_like(small_ref)
        for ref in (d1h, d1l):
            ref[0] = jnp.zeros((704, 128), BF)
            ref[21] = jnp.zeros((704, 128), BF)
            ref[:, 0:32, :] = jnp.zeros((22, 32, 128), BF)
            ref[:, 672:704, :] = jnp.zeros((22, 32, 128), BF)
        d3f[...] = df_ref[...] * dsilu(pre3_ref[...])
        total = jnp.zeros((64, 128), F32)
        for y in range(7):
            for x in range(7):
                d = d3f[pl.ds(y * 7 + x, 64, stride=49), :]
                total = total + d
                hi, lo = split(d)
                d3h[y + 2, 64 * (x + 2):64 * (x + 3), :] = hi
                d3l[y + 2, 64 * (x + 2):64 * (x + 3), :] = lo
        small_ref[640:641, 0:64] = jnp.sum(jnp.transpose(total), axis=0, keepdims=True)
        w3 = (w3_ref[0], w3_ref[1])
        h2h[:, 576:, :] = jnp.zeros((9, 64, 128), BF)
        h2l[:, 576:, :] = jnp.zeros((9, 64, 128), BF)
        def split2(y, c):
            hi, lo = split(silu(pre2_ref[y]))
            h2h[y, 0:576, :] = hi
            h2l[y, 0:576, :] = lo
            return c
        lax.fori_loop(0, 9, split2, 0)
        def dgrad3(y, c):
            rh = jnp.concatenate([d3h[y + 2, 128 * i:128 * i + 256, :] for i in range(5)], axis=1)
            rl = jnp.concatenate([d3l[y + 2, 128 * i:128 * i + 256, :] for i in range(5)], axis=1)
            r = dot3(w3, (rh, rl))
            for ky in range(3):
                for i in range(5):
                    acc2[y + ky, 128 * i:128 * i + 128, :] += r[128 * ky:128 * ky + 128, 128 * i:128 * i + 128]
            return c
        lax.fori_loop(0, 7, dgrad3, 0)
        def wgrad3(y, c):
            def lhs(ref):
                return jnp.concatenate([jnp.concatenate([ref[y - ky + 2, 128 * (i + 1):128 * (i + 2), :] for i in range(4)], axis=1) for ky in range(3)], axis=0)
            def rhs(ref):
                return jnp.concatenate([ref[y, 128 * i:128 * i + 256, :] for i in range(4)], axis=1)
            a3[...] += dot3((lhs(d3h), lhs(d3l)), (rhs(h2h), rhs(h2l)), NT)
            return c
        lax.fori_loop(0, 9, wgrad3, 0)
        for ky in range(3):
            grad = a3[128 * ky:128 * ky + 64, 0:192] + a3[128 * ky + 64:128 * ky + 128, 64:256]
            small_ref[256 + 64 * ky:320 + 64 * ky, :] = grad[:, 0:128]
            small_ref[448 + 64 * ky:512 + 64 * ky, 0:64] = grad[:, 128:192]
        def step2(y, total):
            for x in range(9):
                d = acc2[y, 64 * x:64 * x + 64, :] * dsilu(pre2_ref[y, 64 * x:64 * x + 64, :])
                total = total + d
                hi, lo = split(d)
                d2h[y + 1, 64 * (x + 1):64 * (x + 2), :] = hi
                d2l[y + 1, 64 * (x + 1):64 * (x + 2), :] = lo
            return total
        total = lax.fori_loop(0, 9, step2, jnp.zeros((64, 128), F32))
        small_ref[641:642, 0:64] = jnp.sum(jnp.transpose(total), axis=0, keepdims=True)
    def block2(y, total):
        w2 = (w2_ref[0], w2_ref[1])
        rh = jnp.concatenate([d2h[pl.ds(y, 2), 64 * i:64 * i + 128, :].reshape(256, 128) for i in range(10)], axis=1)
        rl = jnp.concatenate([d2l[pl.ds(y, 2), 64 * i:64 * i + 128, :].reshape(256, 128) for i in range(10)], axis=1)
        r = dot3(w2, (rh, rl))
        h1h, h1l = [], []
        for py in range(2):
            rowh, rowl = [], []
            for i in range(10):
                v = pre1_ref[2 * y + py, 64 * i:64 * i + 64, :]
                s = jax.nn.sigmoid(v)
                d = r[64 * py:64 * py + 64, 128 * i:128 * i + 128] * (s * (1.0 + v * (1.0 - s)))
                total = total + d[0:32] + d[32:64]
                hi, lo = split(d)
                d1h[2 * y + py + 1, 64 * i + 32:64 * i + 96, :] = hi
                d1l[2 * y + py + 1, 64 * i + 32:64 * i + 96, :] = lo
                hi, lo = split(v * s)
                rowh.append(hi)
                rowl.append(lo)
            h1h.append(rowh)
            h1l.append(rowl)
        def lhs(ref):
            return jnp.concatenate([jnp.concatenate([ref[y + 1 - h, 64 * (i + 1):64 * (i + 2), :] for i in range(9)], axis=1) for h in range(2)], axis=0)
        def rhs(rows):
            return jnp.concatenate([jnp.concatenate([rows[0][i], rows[0][i + 1], rows[1][i], rows[1][i + 1]], axis=0) for i in range(9)], axis=1)
        a2[...] += dot3((lhs(d2h), lhs(d2l)), (rhs(h1h), rhs(h1l)), NT)
        return total
    def lower():
        total = lax.fori_loop(0, 10, block2, jnp.zeros((32, 128), F32))
        small_ref[642:643, 0:32] = jnp.sum(jnp.transpose(total), axis=0, keepdims=True)
        small_ref[0:128, :] = a2[:, 0:128]
        small_ref[128:256, :] = a2[:, 128:256]
    if not net:
        upper()
        lower()
        return
    @pl.when(p == 0)
    def _():
        upper()
        lower()
    for m in range(1, 4):
        fan_d[m].wait_recv()
        swaps[m].start()
    @pl.when(p == 0)
    def _():
        for copy in fan_z:
            copy.wait()
        hand.start()
        hand.wait_send()
    pl.when(p == 1)(hand.wait_recv)
    for copy in fan_g:
        copy.wait()
    for m in range(1, 4):
        fan_d[m].wait_send()
    for swap in swaps:
        swap.wait()

def lower_backward(net, pre1, pre2, pre3, df, w2, w3, *wired):
    one = lambda *s: pl.BlockSpec(s, lambda j: (0,) * len(s), pipeline_mode=pl.Buffered(1))
    sds = lambda *s: jax.ShapeDtypeStruct(s, F32)
    bfs = lambda *s: jax.ShapeDtypeStruct(s, BF)
    vmb = lambda *s: pltpu.VMEM(s, BF)
    dma = pltpu.SemaphoreType.DMA
    return pl.pallas_call(
        functools.partial(low_kernel, net),
        grid=(1,),
        in_specs=[one(20, 640, 128), one(9, 576, 128), one(3136, 128), one(3136, 128), one(2, 128, 256), one(2, 384, 256)] + [ANY] * (3 * net),
        out_specs=[one(22, 704, 128), one(22, 704, 128), one(648, 128)] + [ANY] * (4 * net),
        out_shape=[bfs(22, 704, 128), bfs(22, 704, 128), sds(648, 128)]
        + [sds(4, 4, 256, 128), sds(4, 4, 256, 128), sds(4, 4, 32, 128), sds(4, 4, PAD, 128)] * net,
        scratch_shapes=[pltpu.VMEM((3136, 128), F32), vmb(11, 768, 128), vmb(11, 768, 128), vmb(11, 704, 128), vmb(11, 704, 128),
                        vmb(9, 640, 128), vmb(9, 640, 128), pltpu.VMEM((9, 640, 128), F32), pltpu.VMEM((128, 256), F32), pltpu.VMEM((384, 256), F32)]
        + ([dma((4,))] * 8 + [dma, dma]) * net,
        compiler_params=pltpu.CompilerParams(vmem_limit_bytes=60 * 2**20, **(dict(collective_id=3, has_side_effects=True) if net else {})),
    )(pre1, pre2, pre3, df, w2, w3, *wired)

def first_kernel_bwd(net, x_ref, dha_ref, dhb_ref, dla_ref, dlb_ref, w1_ref, *rest):
    if net:
        r_ref, q_ref, s0_ref, s1_ref, tot_ref, sg_ref, ag_ref, ah_ref, xh, xl, a1, lob, upb, pay, got, red, tot, ls, us, ur, zs_, zr, ys, yr, own = rest[:25]
        as_, ar, bs, br, cs, cr, one_ = rest[25:]
        p, g, z, y = coords()
        reps = lax.axis_size("rep")
        chips = 2 * reps
        me = g * reps + lax.axis_index("rep")
        size = ROWS // chips
        def chip(i):
            return (0, i // reps, i % reps)
        def part(i):
            return pl.ds(pl.multiple_of(i * size, 8), size)
        def give(k):
            to = (me + k) % chips
            if k:
                return remote(pay.at[part(to)], got.at[me], as_.at[k], ar.at[k], chip(to))
            return pltpu.make_async_copy(pay.at[part(me)], got.at[me], one_)
        def given(k):
            who = (me + chips - k) % chips
            return remote(pay.at[part(me)], got.at[who], as_.at[k], ar.at[k], chip(who))
        def tell(k):
            return remote(red, tot.at[part(me)], bs.at[k], br.at[k], chip((me + k) % chips))
        def told(k):
            who = (me + chips - k) % chips
            return remote(red, tot.at[part(who)], bs.at[k], br.at[k], chip(who))
        hand = remote(tot, tot, cs, cr, at(1 - p, g, z, y))
        small_ref = pay.at[pl.ds(672, 64)]
        def rows_of(zz):
            return pl.ds(pl.multiple_of(32 * zz, 8), 32)
        def head_at(yy, zz):
            return ah_ref.at[pl.ds(yy, 1 + 7 * yy), rows_of(zz)]
        def along_z(k, yy):
            to = at(p, g, flip(z, k), y)
            a, b = (r_ref, ag_ref.at[yy, z]), (q_ref.at[pl.ds(yy, 1 + 7 * yy)], head_at(yy, z))
            if k:
                return [remote(*a, zs_.at[k, 0], zr.at[k, 0], to), remote(*b, zs_.at[k, 1], zr.at[k, 1], to)]
            return [pltpu.make_async_copy(*a, own.at[0]), pltpu.make_async_copy(*b, own.at[1])]
        def along_y(k, yy):
            zs = flip(z, k)
            a, b = (ag_ref.at[yy, zs], head_at(yy, zs)) if k else (r_ref, q_ref.at[pl.ds(yy, 1 + 7 * yy)])
            to = at(p, g, z, 1 - y)
            return [remote(a, ag_ref.at[yy, zs], ys.at[k, 0], yr.at[k, 0], to), remote(b, head_at(yy, zs), ys.at[k, 1], yr.at[k, 1], to)]
        def each(do, flipped=False):
            for yy in range(2):
                pl.when(y == (1 - yy if flipped else yy))(functools.partial(do, yy))
        def states_out(j, slot):
            return (pltpu.make_async_copy(lob.at[slot], sg_ref.at[pl.ds(4 * j, 4)], ls.at[slot]),
                    remote(upb.at[slot], sg_ref.at[pl.ds(4 * j, 4)], us.at[slot], ur.at[j], at(1 - p, g, z, y)))
    else:
        small_ref, lo_ref, up_ref, xh, xl, a1 = rest
    j = pl.program_id(0)
    last = pl.num_programs(0) - 1
    @pl.when(j == 0)
    def _():
        if net:
            pl.when(p == 0)(lambda: greet([chip((me + k) % chips) for k in range(1, chips)] + [at(1, g, z, y)]))
            pl.when(p == 1)(lambda: greet([at(1, g, flip(z, k), y) for k in range(1, 4)] + [at(1, g, z, 1 - y), at(0, g, z, y)]))
            pay[0:24, :] = s0_ref[...]
            pay[24:672, :] = s1_ref[...]
            pay[736:, :] = jnp.zeros((ROWS - 736, 128), F32)
            def begin(yy):
                for copy in along_z(1, yy) + along_y(0, yy) + along_z(2, yy) + along_z(3, yy) + along_z(0, yy):
                    copy.start()
            each(begin)
        xh[:, 336:, :] = jnp.zeros((4, 16, 128), BF)
        xl[:, 336:, :] = jnp.zeros((4, 16, 128), BF)
        a1[...] = jnp.zeros_like(a1)
    def work():
        v = x_ref[...]
        hi = v.astype(BF)
        xh[:, 0:336, :] = hi
        xl[:, 0:336, :] = (v - hi.astype(F32)).astype(BF)
        def both(a, b):
            return jnp.concatenate([jnp.concatenate([a[0, 96 * i:96 * i + 128, :], b[0, 96 * i:96 * i + 128, :]], axis=0) for i in range(7)], axis=1)
        r = dot3((w1_ref[0], w1_ref[1]), (both(dha_ref, dhb_ref), both(dla_ref, dlb_ref)))
        if net:
            slot = j % 2
            @pl.when(j >= 2)
            def _():
                a, b = states_out(j - 2, slot)
                a.wait()
                b.wait_send()
            lo_to, up_to = lob.at[slot], upb.at[slot]
        else:
            lo_to, up_to = lo_ref, up_ref
        for ky in range(4):
            for i in range(7):
                lo_to[ky, 24 * i:24 * i + 24, :] = r[24 * ky:24 * ky + 24, 128 * i:128 * i + 128]
                up_to[ky, 24 * i:24 * i + 24, :] = r[96 + 24 * ky:96 + 24 * ky + 24, 128 * i:128 * i + 128]
        if net:
            for copy in states_out(j, slot):
                copy.start()
        def lhs(a, b):
            return jnp.concatenate([jnp.concatenate([ref[0, 96 * i + 32:96 * i + 128, :] for i in range(7)], axis=1) for ref in (b, a)], axis=0)
        def rhs(ref):
            return jnp.concatenate([ref[:, 48 * i:48 * i + 64, :].reshape(256, 128) for i in range(7)], axis=1)
        a1[...] += dot3((lhs(dha_ref, dhb_ref), lhs(dla_ref, dlb_ref)), (rhs(xh), rhs(xl)), NT)
    if net:
        pl.when(p == 0)(work)
        def pass_on(k, yy):
            for copy in along_z(k, yy):
                copy.wait_recv()
            for copy in along_y(k, yy):
                copy.start()
        for k, step in ((1, 9), (2, 18)):
            pl.when(j == step)(lambda: each(functools.partial(pass_on, k)))
    else:
        work()
    @pl.when(j == last)
    def _():
        for h in range(2):
            for ky in range(4):
                grad = a1[96 * h:96 * h + 32, 64 * ky:64 * ky + 32]
                grad = grad + a1[96 * h + 32:96 * h + 64, 64 * ky + 16:64 * ky + 48]
                grad = grad + a1[96 * h + 64:96 * h + 96, 64 * ky + 32:64 * ky + 64]
                small_ref[32 * h:32 * h + 32, 32 * ky:32 * ky + 32] = grad
        if net:
            @pl.when(p == 0)
            def _():
                for k in range(chips):
                    give(k).start()
            each(functools.partial(pass_on, 3))
            @pl.when(p == 0)
            def _():
                give(0).wait()
                for k in range(1, chips):
                    given(k).wait_recv()
                red[...] = jnp.sum(got[...], axis=0)
                tot[part(me), :] = red[...]
                for k in range(1, chips):
                    tell(k).start()
                for k in range(1, chips):
                    told(k).wait_recv()
                hand.start()
                for k in range(1, chips):
                    give(k).wait_send()
                    tell(k).wait_send()
                hand.wait_send()
                for back in (1, 0):
                    a, b = states_out(j - back, (j - back) % 2)
                    a.wait()
                    b.wait_send()
            @pl.when(p == 1)
            def _():
                hand.wait_recv()
                def arrive(i, c):
                    states_out(i, 0)[1].wait_recv()
                    return c
                lax.fori_loop(0, last + 1, arrive, 0)
            tot_ref[...] = tot[...]
            def sent(yy):
                for k in range(4):
                    for copy in along_z(k, yy):
                        if k:
                            copy.wait_send()
                        else:
                            copy.wait()
                    for copy in along_y(k, yy):
                        copy.wait_send()
            each(sent)
            def came(yy):
                for k in range(4):
                    for copy in along_y(k, yy):
                        copy.wait_recv()
            each(came, flipped=True)

def first_backward(net, x, dh, dl, w1, *wired):
    full = lambda *s: pl.BlockSpec(s, lambda j: (0,) * len(s))
    sds = lambda *s: jax.ShapeDtypeStruct(s, F32)
    vmb = lambda *s: pltpu.VMEM(s, BF)
    dma = pltpu.SemaphoreType.DMA
    half = pl.BlockSpec((4, 168, 128), lambda j: (j, 0, 0))
    row = pl.BlockSpec((1, 704, 128), lambda j: (j, 0, 0))
    next_row = pl.BlockSpec((1, 704, 128), lambda j: (j + 1, 0, 0))
    return pl.pallas_call(
        functools.partial(first_kernel_bwd, net),
        grid=(21,),
        in_specs=[pl.BlockSpec((4, 336, 128), lambda j: (j, 0, 0)), row, next_row, row, next_row, full(2, 192, 256)] + [ANY, ANY, full(24, 128), full(648, 128)] * net,
        out_specs=[full(ROWS, 128)] + [ANY] * 3 if net else [full(64, 128), half, half],
        out_shape=[sds(ROWS, 128), sds(84, 168, 128), sds(2, 4, 200, 512), sds(9, 128, 128)] if net else [sds(64, 128), sds(84, 168, 128), sds(84, 168, 128)],
        scratch_shapes=[vmb(4, 352, 128), vmb(4, 352, 128), pltpu.VMEM((192, 256), F32)]
        + [pltpu.VMEM((2, 4, 168, 128), F32), pltpu.VMEM((2, 4, 168, 128), F32), pltpu.VMEM((ROWS, 128), F32), pltpu.VMEM((16, ROWS // 16, 128), F32),
           pltpu.VMEM((ROWS // 16, 128), F32), pltpu.VMEM((ROWS, 128), F32), dma((2,)), dma((2,)), dma((21,)),
           dma((4, 2)), dma((4, 2)), dma((4, 2)), dma((4, 2)), dma((2,)), dma((16,)), dma((16,)), dma((16,)), dma((16,)), dma, dma, dma] * net,
        compiler_params=pltpu.CompilerParams(vmem_limit_bytes=60 * 2**20, **(dict(collective_id=4, has_side_effects=True) if net else {})),
    )(x, dh, dh, dl, dl, w1, *wired)

ROWS = 768

def wide_kernel(f_ref, d_ref, e_ref, g_ref, z_ref, r_ref, q_ref, acc, acq, da):
    m = pl.program_id(0)
    p = lax.axis_index("pair")
    @pl.when(m == 0)
    def _():
        acc[...] = jnp.zeros_like(acc)
        acq[...] = jnp.zeros_like(acq)
        da[...] = jnp.zeros_like(da)
    f = split(jnp.concatenate([f_ref[0, i] for i in range(4)], axis=1))
    def block(ref):
        return jnp.concatenate([jnp.concatenate([ref[0, i, 128 * c:128 * c + 128, :] for c in range(2)], axis=1) for i in range(4)], axis=0)
    acc[0] += dot3(f, split(block(d_ref)))
    acc[1] += dot3(f, split(block(e_ref)))
    dz = jnp.concatenate([z_ref[0, i] for i in range(4)], axis=1)
    row = lax.broadcasted_iota(jnp.int32, (PAD, 512), 0)
    chosen = dz[ATOMS:ATOMS + 1].astype(jnp.int32)
    d = jnp.where(row < ATOMS, dz, 0.0)
    da[0:PAD, :] = d
    for i in range(ACTIONS):
        da[128 + ATOMS * i:128 + ATOMS * i + PAD, :] = mask_of(chosen, i) * d
    g = split(jnp.concatenate([g_ref[0, i] for i in range(4)], axis=1))
    acq[...] += dot3(g, split(da[...]), NT)
    @pl.when(m == 3)
    def _():
        r_ref[:, 0:256] = jnp.where(p == 0, acc[0], acc[1])
        r_ref[:, 256:512] = jnp.where(p == 0, acc[1], acc[0])
        for c in range(9):
            q_ref[c] = acq[:, 128 * c:128 * c + 128]

def wide_grads(f2, d2, d3, g2, z2):
    full = lambda *s: pl.BlockSpec(s, lambda j: (0,) * len(s))
    part = lambda n: pl.BlockSpec((1, 4, n, 128), lambda j: (j, 0, 0, 0))
    sds = lambda *s: jax.ShapeDtypeStruct(s, F32)
    return pl.pallas_call(
        wide_kernel, grid=(4,),
        in_specs=[part(200), part(256), part(256), part(32), part(PAD)],
        out_specs=[full(200, 512), full(9, 32, 128)],
        out_shape=[sds(200, 512), sds(9, 32, 128)],
        scratch_shapes=[pltpu.VMEM((2, 200, 256), F32), pltpu.VMEM((32, 1152), F32), pltpu.VMEM((1152, 512), F32)],
        compiler_params=pltpu.CompilerParams(vmem_limit_bytes=60 * 2**20),
    )(f2, d2, d3, g2, z2)

def torso_out(tot, k1_ref, k2_ref, k3_ref, b1_ref, b2_ref, b3_ref, t1, t2):
    t1[:, 0:64] = jnp.transpose(tot[672:736, :])
    t1[:, 64:128] = jnp.zeros((128, 64), F32)
    for ky in range(4):
        for c in range(4):
            v = t1[pl.ds(32 * ky + c, 8, stride=4), :]
            for h in range(2):
                k1_ref[c, 4 * h + ky] = v[:, 32 * h:32 * h + 32]
    for py in range(2):
        t2[...] = jnp.transpose(tot[24 + 128 * py:152 + 128 * py, :])
        for h in range(2):
            for kx in range(4):
                k2_ref[:, 2 * h + py, kx, :] = t2[32 * kx:32 * kx + 32, 64 * h:64 * h + 64]
    for ky in range(3):
        for kx in range(3):
            base = (280 if kx < 2 else 472) + 64 * ky
            k3_ref[ky, kx] = tot[base:base + 64, 64 * (kx % 2):64 * (kx % 2) + 64]
    b3_ref[...] = tot[664:665, 0:64]
    b2_ref[...] = tot[665:666, 0:64]
    b1_ref[...] = tot[666:667, 0:32]

def finish_kernel(ag_ref, ah_ref, tot_ref, in_ref, out_ref, ein_ref, eout_ref, mean_ref, sigma_ref, hm_ref, hs_ref, k1_ref, k2_ref, k3_ref, b1_ref, b2_ref, b3_ref,
                  hb_ref, hbs_ref, bo_ref, bos_ref, loss_ref, t1, t2):
    for s in range(2):
        tall = column(in_ref[s:s + 1, :], 512) * out_ref[s:s + 1, :]
        for z, (start, n) in enumerate(((0, 200), (200, 200), (400, 184), (584, 200))):
            v = ag_ref[s, z, 0:n, :]
            mean_ref[s, start:start + n, :] = v
            sigma_ref[s, start:start + n, :] = v * tall[start:start + n]
    noise = column(eout_ref[...], 128)
    for c in range(9):
        start = 0 if c == 0 else ATOMS + 128 * (c - 1)
        n = min(128, (ATOMS if c == 0 else OUTS) - start)
        v = jnp.transpose(ah_ref[c])[0:n]
        hm_ref[start:start + n, :] = v
        hs_ref[start:start + n, :] = v * (noise[start:start + n] * ein_ref[min(c, 1):min(c, 1) + 1, :])
    torso_out(tot_ref, k1_ref, k2_ref, k3_ref, b1_ref, b2_ref, b3_ref, t1, t2)
    for s in range(2):
        for c in range(4):
            v = tot_ref[4 * s + c:4 * s + c + 1, :]
            hb_ref[s:s + 1, 128 * c:128 * c + 128] = v
            hbs_ref[s:s + 1, 128 * c:128 * c + 128] = v * out_ref[s:s + 1, 128 * c:128 * c + 128]
    for c in range(8):
        n = min(128, OUTS - 128 * c)
        v = tot_ref[8 + c:9 + c, 0:n]
        bo_ref[:, 128 * c:128 * c + n] = v
        bos_ref[:, 128 * c:128 * c + n] = v * eout_ref[:, 128 * c:128 * c + n]
    loss_ref[...] = tot_ref[16:17, :]

def finish(ag, ah, tot, n_in, n_out, e_in, e_out):
    sds = lambda *s: jax.ShapeDtypeStruct(s, F32)
    return pl.pallas_call(
        finish_kernel, in_specs=[VMEM] * 7, out_specs=[VMEM] * 15,
        out_shape=[sds(2, 784, 512), sds(2, 784, 512), sds(OUTS, 128), sds(OUTS, 128), sds(4, 8, 8, 32), sds(32, 4, 4, 64), sds(3, 3, 64, 64), sds(1, 32), sds(1, 64), sds(1, 64),
                   sds(2, 512), sds(2, 512), sds(1, OUTS), sds(1, OUTS), sds(1, 128)],
        scratch_shapes=[pltpu.VMEM((128, 128), F32), pltpu.VMEM((128, 128), F32)],
        compiler_params=pltpu.CompilerParams(vmem_limit_bytes=60 * 2**20),
    )(ag, ah, tot, n_in, n_out, e_in, e_out)

def small_finish_kernel(tot_ref, k1_ref, k2_ref, k3_ref, b1_ref, b2_ref, b3_ref, t1, t2):
    torso_out(tot_ref, k1_ref, k2_ref, k3_ref, b1_ref, b2_ref, b3_ref, t1, t2)

def small_finish(tot):
    sds = lambda *s: jax.ShapeDtypeStruct(s, F32)
    return pl.pallas_call(
        small_finish_kernel, in_specs=[VMEM], out_specs=[VMEM] * 6,
        out_shape=[sds(4, 8, 8, 32), sds(32, 4, 4, 64), sds(3, 3, 64, 64), sds(1, 32), sds(1, 64), sds(1, 64)],
        scratch_shapes=[pltpu.VMEM((128, 128), F32), pltpu.VMEM((128, 128), F32)],
    )(tot)

def online_only(value):
    other = lax.ppermute(value, "pair", [(0, 1)])
    return jnp.where(lax.axis_index("pair") == 0, value, other)

def exchange(parts):
    groups = lax.axis_size("group")
    p, g = lax.axis_index("pair"), lax.axis_index("group")
    got = []
    for k in range(groups):
        to = (g + k) % groups
        mine = parts(0, to)
        if k:
            mine = lax.ppermute(mine, ("pair", "group"), [(i, (i + k) % groups) for i in range(groups)])
        theirs = lax.ppermute(parts(1, to), ("pair", "group"), [(i, groups + (i + k) % groups) for i in range(groups)])
        got.append(jnp.where(p == 0, mine, theirs))
    return got

HIGH = lax.Precision.HIGH

def local(states, actions, proj_lower, proj_upper, proj_weight, first_kernel, first_bias, second_kernel, second_bias,
          third_kernel, third_bias, hidden_mean, hidden_sigma, hidden_bias_mean, hidden_bias_sigma, head_mean, head_sigma,
          head_bias_mean, head_bias_sigma, hidden_noise_in, hidden_noise_out, head_noise_in, head_noise_out):
    pair = lax.axis_index("pair")
    groups = lax.axis_size("group")
    shards = 2 * groups
    net = int(groups == 2 and lax.axis_size("rep") == 8)
    n_in, n_out, e_in, e_out = hidden_noise_in[0], hidden_noise_out[0], head_noise_in[0], head_noise_out[0]
    noise = online_only(jnp.concatenate([v.reshape(-1) for v in (n_in, n_out, e_in, e_out)]))
    on_in = noise[:6272].reshape(2, 3136)
    on_out = noise[6272:7296].reshape(2, 512)
    on_ein = noise[7296:8320].reshape(2, 512)
    on_eout = noise[8320:]
    shard = pair * groups + lax.axis_index("group")
    feat_q, hid_q = 3136 // shards, 512 // shards
    in_q = lax.dynamic_slice_in_dim(on_in, shard * feat_q, feat_q, axis=1)
    e_q = lax.dynamic_slice_in_dim(on_ein, shard * hid_q, hid_q, axis=1)

    x = jnp.transpose(states[0], (2, 3, 1, 0)).reshape(84, 336, 128)
    fw1, fw2, fw3, bw1, bw2, bw3, c1, c2, c3 = prepare(first_kernel[0], second_kernel[0], third_kernel[0], first_bias, second_bias, third_bias)
    e_out = e_out[None]
    e_rows = jnp.where(jnp.arange(OUTS)[:, None] < ATOMS, e_in[0:1], e_in[1:2])
    wo = jnp.pad(head_mean[0].T + head_sigma[0].T * (e_rows * e_out.T), ((0, OUTP - OUTS), (0, 0)))
    bo = jnp.pad(head_bias_mean + head_bias_sigma * e_out, ((0, 0), (0, OUTP - OUTS)))
    hb = (hidden_bias_mean[0] + hidden_bias_sigma[0] * n_out).reshape(1, 1024)
    nin = jnp.transpose(n_in.reshape(2, STEPS, 3136 // STEPS), (1, 0, 2))
    pre1, pre2, pre3, feats = forward(x, fw1, fw2, fw3, c1, c2, c3)
    h, hid, logp, dist, *f1 = hidden(net, feats, hidden_mean[0], hidden_sigma[0], nin, n_out, hb, wo, bo, actions, proj_lower.T, proj_weight.T)
    back = (logp, h, hidden_mean[0], hidden_sigma[0], nin, n_out, wo, actions)
    if net:
        df, small_b, f2, g1, d1, dz1 = hidden_bwd(net, dist, *back, *f1, hid)
        dh, dl, small_d, d2, d3, g2, z2 = lower_backward(net, pre1, pre2, pre3, df, bw2, bw3, d1, g1, dz1)
        part_r, part_q = wide_grads(f2, d2, d3, g2, z2)
        total, grad_rows, ag, ah = first_backward(net, x, dh, dl, bw1, part_r, part_q, small_b, small_d)
        (hidden_grad, hidden_sigma_grad, head_t, head_sigma_t, gk1, gk2, gk3, gb1, gb2, gb3, hb_grad, hbs_grad, bo_grad, bos_grad,
         loss) = finish(ag, ah, total, in_q, on_out, e_q, on_eout[None])
    else:
        df, small_b, msg, dz = hidden_bwd(net, lax.ppermute(dist, "pair", [(1, 0)]), *back)
        f_got = exchange(lambda p, g: lax.dynamic_slice_in_dim(feats, (p * groups + g) * feat_q, feat_q, axis=0))
        hid = jnp.transpose(hid, (3, 0, 2, 1, 4, 5)).reshape(1024, 128).T
        hid_got = exchange(lambda p, g: lax.dynamic_slice_in_dim(hid.reshape(128, 2, 512), (p * groups + g) * hid_q, hid_q, axis=2))
        dpre = jnp.transpose(msg.reshape(2, 2, 2, 128, 128), (3, 1, 0, 2, 4)).reshape(128, 1024)
        d_all = jnp.concatenate(exchange(lambda p, g: jnp.concatenate([dpre, dz.T, jnp.zeros((128, 72), F32)], axis=1)), axis=0)
        f_all = jnp.concatenate(f_got, axis=1)
        hid_all = jnp.concatenate(hid_got, axis=0)
        part_hidden = jnp.einsum("fb,bsh->sfh", f_all, d_all[:, :1024].reshape(-1, 2, 512), precision=HIGH)
        dz_all = d_all[:, 1024:1024 + ATOMS]
        picked = d_all[:, 1024 + ATOMS]
        mask = jnp.where(picked[None, :] == jnp.arange(ACTIONS, dtype=F32)[:, None], 1.0 - 1.0 / ACTIONS, -1.0 / ACTIONS)
        da = (mask[:, None, :] * dz_all.T[None]).reshape(ACTIONS * ATOMS, -1)
        part_head = jnp.concatenate([jnp.dot(dz_all.T, hid_all[:, 0], precision=HIGH), jnp.dot(da, hid_all[:, 1], precision=HIGH)], axis=0)
        hidden_grad, head_t = lax.psum((part_hidden, part_head), "rep")
        dh, dl, small_d = lower_backward(net, pre1, pre2, pre3, df, bw2, bw3)
        small_f, lo, up = first_backward(net, x, dh, dl, bw1)
        grad_rows = jnp.where(pair == 0, lo, lax.ppermute(up, "pair", [(0, 1)]))
        total = lax.psum(jnp.concatenate([small_b, small_d, small_f], axis=0), ("pair", "group", "rep"))
        hidden_sigma_grad = hidden_grad * (in_q[:, :, None] * on_out[:, None, :])
        head_sigma_t = head_t * (jnp.where(jnp.arange(OUTS)[:, None] < ATOMS, e_q[0:1], e_q[1:2]) * on_eout[:, None])
        gk1, gk2, gk3, gb1, gb2, gb3 = small_finish(total)
        hb_grad = total[0:8].reshape(2, 512)
        bo_grad = total[8:16].reshape(1, -1)[:, :OUTS]
        hbs_grad, bos_grad = hb_grad * on_out, bo_grad * on_eout
        loss = total[16:17]
    states_grad = jnp.transpose(grad_rows.reshape(84, 84, 2, 128), (3, 2, 0, 1))
    return (loss[0, 0], states_grad, jnp.transpose(gk1, (3, 0, 1, 2)), gb1[0], jnp.transpose(gk2, (3, 0, 1, 2)), gb2[0], jnp.transpose(gk3, (2, 3, 0, 1)), gb3[0],
            hidden_grad, hidden_sigma_grad, hb_grad, hbs_grad, head_t.T, head_sigma_t.T, bo_grad[0], bos_grad[0])


def solution(mesh):
    placed = (
        P("pair", ("group", "rep"), None, None, None),
        P("pair", ("group", "rep")),
        P(("group", "rep"), None),
        P(("group", "rep"), None),
        P(("group", "rep"), None),
        P("pair", None, None, None, None),
        P("pair", None),
        P("pair", None, None, None, None),
        P("pair", None),
        P("pair", None, None, None, None),
        P("pair", None),
        P("pair", None, None, None),
        P("pair", None, None, None),
        P("pair", None, None),
        P("pair", None, None),
        P("pair", None, None),
        P("pair", None, None),
        P("pair", None),
        P("pair", None),
        P("pair", None, None),
        P("pair", None, None),
        P("pair", None, None),
        P("pair", None),
    )
    return jax.shard_map(
        local,
        mesh=mesh,
        in_specs=placed,
        out_specs=(
            P(),
            P(("group", "rep"), "pair", None, None),
            P(),
            P(),
            P(),
            P(),
            P(),
            P(),
            P(None, ("pair", "group"), None),
            P(None, ("pair", "group"), None),
            P(),
            P(),
            P(("pair", "group"), None),
            P(("pair", "group"), None),
            P(),
            P(),
        ),
        check_vma=False,
    )
```

time: 312 us -> 266 us (0.85)
  local copies, waits for them, and re-layouts: 51 us -> 15.4 us
  other arithmetic: 9.2 us -> 4 us
    pallas_call x2 -> x3, Pallas kernels: 32.9 us -> 17.4 us  [the longest x1 8.65 us: wide_grads(): pl.pallas_call(wide_kernel, grid=(4,), in_specs=[part(200), part(256), pa...]
    pallas_call x1, Pallas kernels: 31 us -> 42.5 us  [hidden_bwd(): pl.pallas_call(functools.partial(hid_bwd_kernel, net), grid=(STEPS,), in_...]
    reshape x16 -> x0, local copies, waits for them, and re-layouts: 11.3 us -> none  [the longest x2 4.78 us: local(): v.reshape(19, ATOMS, -1)]
    unnamed x57 -> x12, local copies, waits for them, and re-layouts: 19.6 us -> 8.52 us
    slice x13 -> x2, local copies, waits for them, and re-layouts: 7.07 us -> 1.35 us  [the longest x1 0.77 us: local(): e_rows = jnp.where(jnp.arange(OUTS)[:, None] < ATOMS, e_in[0:1], e_in[1:2])]
    broadcast_in_dim x8 -> x0, local copies, waits for them, and re-layouts: 3.17 us -> none  [the longest x4 2.14 us: local(): jnp.broadcast_to(jnp.tile(b, n)[:, None], (b.shape[0] * n, 128))]
    transpose x7 -> x0, local copies, waits for them, and re-layouts: 3.16 us -> none  [the longest x1 1 us: fwd_weights(): w3 = jnp.transpose(a, (1, 0, 2, 3)).reshape(384, 256)]
  transfers between devices with their start and end apart: 2 -> 1, of which waited for: 0 -> 0; matrix products, arithmetic and copies ran while one was open for 3% -> 3% of each run, Pallas kernels for 53% -> 89%
where the time goes in v3:
time: 266 us; the launch traced here: 264 us
  Pallas kernels  242 us (91%)
  local copies, waits for them, and re-layouts  15.4 us (6%)
  other arithmetic  4 us (2%)
    pallas_call x1, Pallas kernels, first_backward(): pl.pallas_call(functools.partial(first_kernel_bwd, net), grid=(21,), in_s...  72.3 us
    pallas_call x1, Pallas kernels, lower_backward(): pl.pallas_call(functools.partial(low_kernel, net), grid=(1,), in_specs=[o...  54.4 us
    pallas_call x1, Pallas kernels, hidden_bwd(): pl.pallas_call(functools.partial(hid_bwd_kernel, net), grid=(STEPS,), in_...  42.5 us
    pallas_call x1, Pallas kernels, forward(): pl.pallas_call(fwd_kernel, grid=(21,), in_specs=[pl.BlockSpec((4, 336, 12...  32.1 us
    pallas_call x1, Pallas kernels, hidden(): pl.pallas_call(functools.partial(hid_kernel, net), grid=(STEPS,), in_spec...  23.2 us
    pallas_call x1, Pallas kernels, wide_grads(): pl.pallas_call(wide_kernel, grid=(4,), in_specs=[part(200), part(256), pa...  8.65 us
    unnamed x12, local copies, waits for them, and re-layouts  8.52 us
    pallas_call x1, Pallas kernels, finish(): pl.pallas_call(finish_kernel, in_specs=[VMEM] * 7, out_specs=[VMEM] * 15,...  5.94 us
  transfers between devices with their start and end apart: 1, of which 0 were waited for; matrix products, arithmetic and copies ran while one was open for 3% of the time, Pallas kernels for 89%

profile of v3, /device:TPU:0, one launch (start us, length us, event | category | flops | bytes accessed | tf_op | source)
XLA Modules:
  0.0 264.4 jit_solution(4730763085983107821)
XLA Ops:
  0.6 0.8 reshape_squeeze.13
  1.5 0.7 copy.42
  2.2 0.7 copy.43
  2.9 0.7 pad_maximum_fusion
  3.5 2.3 collective-permute-start
  5.9 0.8 fusion.2
  6.7 0.7 add_bitcast_fusion
  7.4 0.0 copy-start.1
  7.4 0.0 copy-start.2
  7.4 0.0 copy-start.3
  7.4 0.0 copy-start
  7.4 2.5 fusion
  10.0 0.0 copy-done.1
  10.0 0.0 copy-done.2
  10.0 0.0 copy-done.3
  10.0 0.0 copy-done
  10.1 0.1 reshape_squeeze.12
  10.1 0.6 copy.47
  10.8 0.6 copy.41
  11.4 1.5 pad.8.wo_ref
  12.8 0.6 pad.9.bo_ref
  13.4 2.8 %shard_map.333 = (bf16[2,192,256]{2,1,0:T(8,128)(2,1)}, bf16[2,128,256]{2,1,0:T(8,128)(2,1)}, bf16[2,384,256]{2,1,0:T(8,128)(2,1)}, bf16[2,192,256]{2,1,0:T(8,12...) custom-call(f32[4,8,8,32]{3,2,1,0:T(8,128)} %bitcast.69, ...), custom_call_target="tpu_custom_call" | custom-call | tf_op jit(solution)/shard_map/pallas_call | solution.py:82
  16.3 32.1 %shard_map.334 = (f32[20,640,128]{2,1,0:T(8,128)}, f32[9,576,128]{2,1,0:T(8,128)}, f32[3136,128]{1,0:T(8,128)}, f32[3136,128]{1,0:T(8,128)}) custom-call(f32[84,336,128]{2,1,0:T(8,128)} %bitcast.58, bf16[2,192,256]{2,1,0:T(8,128)(2,1)} %get-tuple-element.68.w1_ref, bf16[2,128,256]{2,1,0:T(8,128)(2,1)} %get-tuple-element.69.w2_ref, ...), custom_call_target="tpu_custom_call" | custom-call | tf_op jit(solution)/shard_map/pallas_call | solution.py:158
  48.4 23.2 %shard_map.335 = (f32[128,1024]{1,0:T(8,128)}, f32[2,4,2,2,32,128]{5,4,3,2,1,0:T(8,128)}, f32[56,128]{1,0:T(8,128)}, f32[56,128]{1,0:T(8,128)}, f32[2,4,200,128]{3,2,1,0:T(8,128)}) custom-call(f32[3136,128]{1,0:T(8,128)} %get-tuple-element.77.f_ref.rest_0_, f32[2,3136,512]{2,1,0:T(8,128)} %bitcast.60, f32[2,3136,512]{2,1,0:T(8,128)} %bitcast.62, ...), custom_call_target="tpu_custom_call" | custom-call | tf_op jit(solution)/shard_map/pallas_call | solution.py:361
  71.6 42.5 %shard_map.336 = (f32[3136,128]{1,0:T(8,128)}, f32[24,128]{1,0:T(8,128)}, f32[4,4,200,128]{3,2,1,0:T(8,128)}, f32[4,2,2,32,128]{4,3,2,1,0:T(8,128)}, f32[4,2,256,128]{3,2,1,0:T(8,128)}, /*index=5*/f32[4,56,128]{2,1,0:T(8,128)}) custom-call(f32[56,128]{1,0:T(8,128)} %get-tuple-element.78.t_ref, f32[56,128]{1,0:T(8,128)} %get-tuple-element.79.logp_ref, ...), custom_call_target="tpu_custom_call" | custom-call | tf_op jit(solution)/shard_map/pallas_call | solution.py:459
  114.1 54.4 %shard_map.337 = (bf16[22,704,128]{2,1,0:T(8,128)(2,1)}, bf16[22,704,128]{2,1,0:T(8,128)(2,1)}, f32[648,128]{1,0:T(8,128)}, f32[4,4,256,128]{3,2,1,0:T(8,128)}, ...) custom-call(f32[20,640,128]{2,1,0:T(8,128)} %get-tuple-element.74.pre1_ref, ...), custom_call_target="tpu_custom_call" | custom-call | tf_op jit(solution)/shard_map/pallas_call | solution.py:620
  168.4 8.7 %shard_map.338 = (f32[200,512]{1,0:T(8,128)}, f32[9,32,128]{2,1,0:T(8,128)}) custom-call(f32[4,4,200,128]{3,2,1,0:T(8,128)} %get-tuple-element.92.f_ref, f32[4,4,256,128]{3,2,1,0:T(8,128)} %get-tuple-element.93.d_ref, f32[4,4,256,128]{3,2,1,0:T(8,128)} %get-tuple-element.94.e_ref, f32[4,4,32,128]{3,2,1,0:T(8,128)} %get-tuple-element.95.g_ref, ...), custom_call_target="tpu_custom_call" | custom-call | tf_op jit(solution)/shard_map/pallas_call | solution.py:856
  177.1 72.3 %shard_map.339 = (f32[768,128]{1,0:T(8,128)}, f32[84,168,128]{2,1,0:T(8,128)}, f32[2,4,200,512]{3,2,1,0:T(8,128)}, f32[9,128,128]{2,1,0:T(8,128)}) custom-call(f32[84,336,128]{2,1,0:T(8,128)} %bitcast.59, bf16[22,704,128]{2,1,0:T(8,128)(2,1)} %get-tuple-element.89.dha_ref.dhb_ref, bf16[22,704,128]{2,1,0:T(8,128)(2,1)} %get-tuple-element.89.dha_ref.dhb_ref, ...), custom_call_target="tpu_custom_call" | custom-call | tf_op jit(solution)/shard_map/pallas_call | solution.py:808
  249.4 0.0 collective-permute-done
  249.4 0.6 slice.33
  250.0 0.1 reshape.88
  250.1 0.6 reshape.89.out_ref
  250.7 0.6 constant_dynamic-slice_fusion.ein_ref
  251.3 0.7 constant_dynamic-slice_fusion.1.in_ref
  251.9 5.9 %shard_map.340 = (f32[2,784,512]{2,1,0:T(8,128)}, f32[2,784,512]{2,1,0:T(8,128)}, f32[969,128]{1,0:T(8,128)}, f32[969,128]{1,0:T(8,128)}, f32[4,8,8,32]{3,2,1,0:...) custom-call(f32[2,4,200,512]{3,2,1,0:T(8,128)} %get-tuple-element.10, ...), custom_call_target="tpu_custom_call" | custom-call | tf_op jit(solution)/shard_map/pallas_call | solution.py:916
  257.9 6.5 %copy.49 = f32[128,2,84,84]{0,1,3,2:T(2,128)} copy(f32[128,2,84,84]{0,1,3,2:T(2,128)} %bitcast.64) | data formatting | bytes 14450688
  (6 shorter events, 0.0 us)
Async XLA Ops:
  3.5 245.8 %collective-permute-start = (f32[9289]{0:T(1024)S(1)}, f32[9289]{0:T(1024)S(1)}, u32[]{:S(2)}, u32[]{:S(2)}) collective-permute-start(f32[9289]{0:T(1024)S(1)} %pad_maximum_fusion), channel_id=1, source_target_pairs={{0,16},{1,17},{2,18},{3,19},{4,20},{5,21},{6,22},{7,23},{8,24},{9,... | collective-permute-start | bytes 111476 | tf_op jit(solution)/shard_map/ppermute | solution.py:936
  7.4 2.6 copy-start.1
  7.4 2.6 copy-start.2
  7.4 2.6 copy-start.3
  7.4 2.6 copy-start

commit v4 on v3

--- a/solution.py
+++ b/solution.py
@@ -86,88 +86,98 @@
         compiler_params=pltpu.CompilerParams(vmem_limit_bytes=60 * 2**20),
     )(jnp.transpose(k1, (1, 2, 3, 0)), jnp.transpose(k2, (1, 2, 3, 0)), jnp.transpose(k3, (2, 3, 0, 1)), b1, b2, b3)
 
-def fwd_kernel(x_ref, w1_ref, w2_ref, w3_ref, b1_ref, b2_ref, b3_ref, pre1_ref, pre2_ref, pre3_ref, f_ref,
-               xh, xl, top1, top2, acc3, h1h, h1l, h2h, h2l):
-    j = pl.program_id(0)
-    @pl.when(j == 0)
-    def _():
-        xh[:, 336:, :] = jnp.zeros((4, 16, 128), BF)
-        xl[:, 336:, :] = jnp.zeros((4, 16, 128), BF)
-        top1[...] = jnp.zeros_like(top1)
-        top2[...] = jnp.zeros_like(top2)
-        acc3[...] = jnp.zeros_like(acc3)
-        h2h[:, 576:, :] = jnp.zeros((9, 64, 128), BF)
-        h2l[:, 576:, :] = jnp.zeros((9, 64, 128), BF)
-    v = x_ref[...]
-    hi = v.astype(BF)
-    xh[:, 0:336, :] = hi
-    xl[:, 0:336, :] = (v - hi.astype(F32)).astype(BF)
-    rh = jnp.concatenate([xh[:, 48 * i:48 * i + 64, :].reshape(256, 128) for i in range(7)], axis=1)
-    rl = jnp.concatenate([xl[:, 48 * i:48 * i + 64, :].reshape(256, 128) for i in range(7)], axis=1)
-    r = dot3((w1_ref[0], w1_ref[1]), (rh, rl))
-    out = top1[...] + r[96:]
-    top1[...] = r[:96]
-    b1 = b1_ref[...]
-    row = jnp.maximum(j - 1, 0)
-    for i in range(7):
-        n = 96 if i < 6 else 64
-        p = out[:n, 128 * i:128 * i + 128] + b1[:n]
-        pre1_ref[0, 96 * i:96 * i + n, :] = p
-        hh, hl = split(silu(p))
-        h1h[row, 96 * i:96 * i + n, :] = hh
-        h1l[row, 96 * i:96 * i + n, :] = hl
-
-    @pl.when(j == pl.num_programs(0) - 1)
-    def _():
-        w2 = (w2_ref[0], w2_ref[1])
-        b2 = b2_ref[...]
-        def step2(y, carry):
-            rh = jnp.concatenate([h1h[pl.ds(2 * y, 2), 64 * i:64 * i + 128, :].reshape(256, 128) for i in range(9)], axis=1)
-            rl = jnp.concatenate([h1l[pl.ds(2 * y, 2), 64 * i:64 * i + 128, :].reshape(256, 128) for i in range(9)], axis=1)
-            r = dot3(w2, (rh, rl))
-            o = top2[...] + r[64:]
-            top2[...] = r[:64]
-            row = jnp.maximum(y - 1, 0)
-            for i in range(9):
-                p = o[:, 128 * i:128 * i + 128] + b2
-                pre2_ref[row, 64 * i:64 * i + 64, :] = p
-                hh, hl = split(silu(p))
-                h2h[row, 64 * i:64 * i + 64, :] = hh
-                h2l[row, 64 * i:64 * i + 64, :] = hl
-            return carry
-        lax.fori_loop(0, 10, step2, 0)
-        w3 = (w3_ref[0], w3_ref[1])
-        b3 = b3_ref[...]
-        def step3(y, carry):
-            rh = jnp.concatenate([h2h[y, 128 * i:128 * i + 256, :] for i in range(4)], axis=1)
-            rl = jnp.concatenate([h2l[y, 128 * i:128 * i + 256, :] for i in range(4)], axis=1)
-            r = dot3(w3, (rh, rl))
-            for ky in range(3):
-                for i in range(4):
-                    acc3[y - ky + 2, 128 * i:128 * i + 128, :] += r[128 * ky:128 * ky + 128, 128 * i:128 * i + 128]
-            return carry
-        lax.fori_loop(0, 9, step3, 0)
-        for y in range(7):
-            for x in range(7):
-                p = acc3[y + 2, 64 * x:64 * x + 64, :] + b3
-                pre3_ref[pl.ds(y * 7 + x, 64, stride=49), :] = p
-                f_ref[pl.ds(y * 7 + x, 64, stride=49), :] = silu(p)
+def fwd_kernel(x_ref, w1_ref, w2_ref, w3_ref, b1_ref, b2_ref, b3_ref, pre1_hbm, pre2_hbm, pre3_ref, f_ref,
+               xs, pre1_ref, pre2_ref, xh, xl, top1, top2, acc3, h1h, h1l, h2h, h2l, x_sem, sem1, sem2):
+    def x_in(j):
+        return pltpu.make_async_copy(x_ref.at[pl.ds(4 * j, 4)], xs.at[pl.ds(4 * j, 4)], x_sem.at[j])
+    def row_out(row):
+        return pltpu.make_async_copy(pre1_ref.at[row], pre1_hbm.at[row], sem1.at[row])
+    for j in range(21):
+        x_in(j).start()
+    xh[:, 336:, :] = jnp.zeros((4, 16, 128), BF)
+    xl[:, 336:, :] = jnp.zeros((4, 16, 128), BF)
+    top1[...] = jnp.zeros_like(top1)
+    top2[...] = jnp.zeros_like(top2)
+    acc3[...] = jnp.zeros_like(acc3)
+    h2h[:, 576:, :] = jnp.zeros((9, 64, 128), BF)
+    h2l[:, 576:, :] = jnp.zeros((9, 64, 128), BF)
+    def step1(j, carry):
+        x_in(j).wait()
+        v = xs[pl.ds(4 * j, 4)]
+        hi = v.astype(BF)
+        xh[:, 0:336, :] = hi
+        xl[:, 0:336, :] = (v - hi.astype(F32)).astype(BF)
+        rh = jnp.concatenate([xh[:, 48 * i:48 * i + 64, :].reshape(256, 128) for i in range(7)], axis=1)
+        rl = jnp.concatenate([xl[:, 48 * i:48 * i + 64, :].reshape(256, 128) for i in range(7)], axis=1)
+        r = dot3((w1_ref[0], w1_ref[1]), (rh, rl))
+        out = top1[...] + r[96:]
+        top1[...] = r[:96]
+        b1 = b1_ref[...]
+        row = jnp.maximum(j - 1, 0)
+        for i in range(7):
+            n = 96 if i < 6 else 64
+            p = out[:n, 128 * i:128 * i + 128] + b1[:n]
+            pre1_ref[row, 96 * i:96 * i + n, :] = p
+            hh, hl = split(silu(p))
+            h1h[row, 96 * i:96 * i + n, :] = hh
+            h1l[row, 96 * i:96 * i + n, :] = hl
+        pl.when(j >= 1)(lambda: row_out(row).start())
+        return carry
+    lax.fori_loop(0, 21, step1, 0)
+    w2 = (w2_ref[0], w2_ref[1])
+    b2 = b2_ref[...]
+    def step2(y, carry):
+        rh = jnp.concatenate([h1h[pl.ds(2 * y, 2), 64 * i:64 * i + 128, :].reshape(256, 128) for i in range(9)], axis=1)
+        rl = jnp.concatenate([h1l[pl.ds(2 * y, 2), 64 * i:64 * i + 128, :].reshape(256, 128) for i in range(9)], axis=1)
+        r = dot3(w2, (rh, rl))
+        o = top2[...] + r[64:]
+        top2[...] = r[:64]
+        row = jnp.maximum(y - 1, 0)
+        for i in range(9):
+            p = o[:, 128 * i:128 * i + 128] + b2
+            pre2_ref[row, 64 * i:64 * i + 64, :] = p
+            hh, hl = split(silu(p))
+            h2h[row, 64 * i:64 * i + 64, :] = hh
+            h2l[row, 64 * i:64 * i + 64, :] = hl
+        return carry
+    lax.fori_loop(0, 10, step2, 0)
+    pre2_out = pltpu.make_async_copy(pre2_ref, pre2_hbm, sem2)
+    pre2_out.start()
+    w3 = (w3_ref[0], w3_ref[1])
+    b3 = b3_ref[...]
+    def step3(y, carry):
+        rh = jnp.concatenate([h2h[y, 128 * i:128 * i + 256, :] for i in range(4)], axis=1)
+        rl = jnp.concatenate([h2l[y, 128 * i:128 * i + 256, :] for i in range(4)], axis=1)
+        r = dot3(w3, (rh, rl))
+        for ky in range(3):
+            for i in range(4):
+                acc3[y - ky + 2, 128 * i:128 * i + 128, :] += r[128 * ky:128 * ky + 128, 128 * i:128 * i + 128]
+        return carry
+    lax.fori_loop(0, 9, step3, 0)
+    for y in range(7):
+        for x in range(7):
+            p = acc3[y + 2, 64 * x:64 * x + 64, :] + b3
+            pre3_ref[pl.ds(y * 7 + x, 64, stride=49), :] = p
+            f_ref[pl.ds(y * 7 + x, 64, stride=49), :] = silu(p)
+    pre2_out.wait()
+    for row in range(20):
+        row_out(row).wait()
 
 def forward(x, w1, w2, w3, b1, b2, b3):
-    full = lambda *s: pl.BlockSpec(s, lambda j: (0,) * len(s))
+    vm = pl.BlockSpec(memory_space=pltpu.VMEM)
+    hbm = pl.BlockSpec(memory_space=pl.ANY)
+    sds = lambda *s: jax.ShapeDtypeStruct(s, F32)
+    f32 = lambda *s: pltpu.VMEM(s, F32)
+    bf = lambda *s: pltpu.VMEM(s, BF)
+    dma = pltpu.SemaphoreType.DMA
     return pl.pallas_call(
         fwd_kernel,
-        grid=(21,),
-        in_specs=[pl.BlockSpec((4, 336, 128), lambda j: (j, 0, 0)), full(2, 192, 256), full(2, 128, 256), full(2, 384, 256),
-                  full(96, 128), full(64, 128), full(64, 128)],
-        out_specs=[pl.BlockSpec((1, 640, 128), lambda j: (jnp.maximum(j - 1, 0), 0, 0)), full(9, 576, 128),
-                   full(3136, 128), full(3136, 128)],
-        out_shape=[jax.ShapeDtypeStruct((20, 640, 128), F32), jax.ShapeDtypeStruct((9, 576, 128), F32),
-                   jax.ShapeDtypeStruct((3136, 128), F32), jax.ShapeDtypeStruct((3136, 128), F32)],
-        scratch_shapes=[pltpu.VMEM((4, 352, 128), BF), pltpu.VMEM((4, 352, 128), BF),
-                        pltpu.VMEM((96, 896), F32), pltpu.VMEM((64, 1152), F32), pltpu.VMEM((11, 512, 128), F32),
-                        pltpu.VMEM((20, 640, 128), BF), pltpu.VMEM((20, 640, 128), BF),
-                        pltpu.VMEM((9, 640, 128), BF), pltpu.VMEM((9, 640, 128), BF)],
+        in_specs=[hbm] + [vm] * 6,
+        out_specs=[hbm, hbm, vm, vm],
+        out_shape=[sds(20, 640, 128), sds(9, 576, 128), sds(3136, 128), sds(3136, 128)],
+        scratch_shapes=[f32(84, 336, 128), f32(20, 640, 128), f32(9, 576, 128), bf(4, 352, 128), bf(4, 352, 128),
+                        f32(96, 896), f32(64, 1152), f32(11, 512, 128), bf(20, 640, 128), bf(20, 640, 128), bf(9, 640, 128), bf(9, 640, 128),
+                        dma((21,)), dma((20,)), dma],
         compiler_params=pltpu.CompilerParams(vmem_limit_bytes=60 * 2**20),
     )(x, w1, w2, w3, b1, b2, b3)
 
@@ -259,18 +269,81 @@
     return [pltpu.SemaphoreType.DMA((8, parts)), pltpu.SemaphoreType.DMA((4, parts)), pltpu.SemaphoreType.DMA((parts,))]
 
 
-def f_scatter(f_ref, f1_ref, sems):
+FIRST = 104
+
+
+def f_scatter(f_ref, f1_ref, half, sems):
+    start, rows = (0, FIRST) if half == 0 else (FIRST, 200 - FIRST)
     def src(q, zd, i):
-        return f_ref.at[pl.ds(pl.multiple_of((2 * q + i) * 784 + jnp.minimum(200 * zd, 584), 8), 200)]
+        return f_ref.at[pl.ds(pl.multiple_of((2 * q + i) * 784 + jnp.minimum(200 * zd, 584) + start, 8), rows)]
     return Scatter(2, src, lambda z, i: f1_ref.at[i, z], *sems)
+
+
+def f_fan(f1_ref, f2_ref, send, recv):
+    return spread_plane(*coords(), lambda gd, yd: f1_ref.at[gd], lambda m: f2_ref.at[m], send, recv)
+
+
+class Line:
+    def __init__(self, parts, own, slot, send, recv):
+        self.parts, self.own, self.slot, self.send, self.recv = parts, own, slot, send, recv
+        self.p, self.g, self.z, self.y = coords()
+
+    def block(self, t, way):
+        return jnp.maximum(self.z - t, 0) if way == 0 else jnp.minimum(self.z + t, 3)
+
+    def there(self, t, way):
+        return self.z >= t if way == 0 else self.z + t <= 3
+
+    def copies(self, t, way):
+        to = at(self.p, self.g, jnp.minimum(self.z + 1, 3) if way == 0 else jnp.maximum(self.z - 1, 0), self.y)
+        zz = self.block(t, way)
+        return [remote(self.own(i) if t == 0 else self.slot(zz, i), self.slot(zz, i), self.send.at[t, way, i], self.recv.at[t, way, i], to) for i in range(self.parts)]
+
+    def goes(self, t, way):
+        return jnp.logical_and(self.there(t, way), self.z <= 2 if way == 0 else self.z >= 1)
+
+    def start(self, t):
+        for way in range(2):
+            def go():
+                for copy in self.copies(t, way):
+                    copy.start()
+            pl.when(self.goes(t, way))(go)
+
+    def arrive(self, t, then):
+        for way in range(2):
+            def come():
+                zz = self.block(t, way)
+                for i in range(self.parts):
+                    remote(self.slot(zz, i), self.slot(zz, i), self.send.at[t - 1, way, i], self.recv.at[t - 1, way, i], at(1 - self.p, self.g, self.z, self.y)).wait_recv()
+                if t < 3:
+                    def go():
+                        for copy in self.copies(t, way):
+                            copy.start()
+                    pl.when(self.goes(t, way))(go)
+                then(2 * t - 1 + way, zz)
+            pl.when(self.there(t, way))(come)
+
+    def each(self, do):
+        do(0, self.z)
+        for t in range(1, 4):
+            for way in range(2):
+                pl.when(self.there(t, way))(lambda: do(2 * t - 1 + way, self.block(t, way)))
+
+    def sent(self):
+        for t in range(3):
+            for way in range(2):
+                def done():
+                    for copy in self.copies(t, way):
+                        copy.wait_send()
+                pl.when(self.goes(t, way))(done)
+
+
+def line_sems(parts):
+    return [pltpu.SemaphoreType.DMA((3, 2, parts)), pltpu.SemaphoreType.DMA((3, 2, parts))]
 
 
 def g_scatter(hid_ref, g1_ref, sems):
     return Scatter(1, lambda q, zd, i: hid_ref.at[q, zd], lambda z, i: g1_ref.at[z], *sems)
-
-
-def d_scatter(msg_ref, d1_ref, sems):
-    return Scatter(1, lambda q, zd, i: msg_ref.at[q], lambda z, i: d1_ref.at[z], *sems)
 
 
 def z_scatter(dz_ref, dz1_ref, sems):
@@ -301,17 +374,28 @@
 
 def hid_kernel(net, f_ref, m_ref, s_ref, nin_ref, nout_ref, hb_ref, wo_ref, bo_ref, c_ref, pl_ref, pw_ref, *rest):
     if net:
-        f_all, h_ref, g_ref, logp_ref, dist_ref, f1_ref, acc, adv = rest[:8]
-        wire = f_scatter(f_all, f1_ref, rest[8:])
+        f_all, h_ref, g_ref, logp_ref, dist_ref, f1a_ref, f1b_ref, f2_ref, acc, adv, fs, fr = rest[:12]
+        wires = f_scatter(f_all, f1a_ref, 0, rest[12:15]), f_scatter(f_all, f1b_ref, 1, rest[15:18])
+        fan = f_fan(f1a_ref, f2_ref, fs, fr)
+        p, g, z, y = coords()
     else:
         h_ref, g_ref, logp_ref, dist_ref, acc, adv = rest
     j = pl.program_id(0)
     @pl.when(j == 0)
     def _():
         if net:
-            greet(line(*coords()))
-            wire.start()
+            greet(line(p, g, z, y) + plane(p, g, z, y))
+            wires[0].start()
         acc[...] = jnp.zeros_like(acc)
+    if net:
+        @pl.when(j == 4)
+        def _():
+            wires[0].sent()
+            wires[1].start()
+            for k in range(4):
+                wires[0].arrived(k)
+            for copy in fan:
+                copy.start()
     f = split(f_ref[...])
     for s in range(2):
         w = split(noisy(m_ref, s_ref, nin_ref, nout_ref, s))
@@ -350,8 +434,10 @@
         dist_ref[...] = dist
         if net:
             for k in range(4):
-                wire.arrived(k)
-            wire.sent()
+                wires[1].arrived(k)
+            wires[1].sent()
+            for copy in fan:
+                copy.wait()
 
 def hidden(net, f, m, s, nin, nout, hb, wo, bo, c, plow, pw):
     full = lambda *t: pl.BlockSpec(t, lambda j: (0,) * len(t))
@@ -362,22 +448,48 @@
         functools.partial(hid_kernel, net), grid=(STEPS,),
         in_specs=[pl.BlockSpec((k, 128), lambda j: (j, 0)), wspec, wspec, pl.BlockSpec((1, 2, k), lambda j: (j, 0, 0)), full(2, 512), full(1, 1024),
                   full(OUTP, 512), full(1, OUTP), full(1, 128), full(ATOMS, 128), full(ATOMS, 128)] + [ANY] * net,
-        out_specs=[full(128, 1024), full(2, 4, 2, 2, 32, 128), full(PAD, 128), full(PAD, 128)] + [ANY] * net,
-        out_shape=[sds(128, 1024), sds(2, 4, 2, 2, 32, 128), sds(PAD, 128), sds(PAD, 128)] + [sds(2, 4, 200, 128)] * net,
-        scratch_shapes=[pltpu.VMEM((128, 1024), F32), pltpu.VMEM((OUTP, 128), F32)] + scatter_sems(2) * net,
+        out_specs=[full(128, 1024), full(2, 4, 2, 2, 32, 128), full(PAD, 128), full(PAD, 128)] + [ANY, ANY, ANY] * net,
+        out_shape=[sds(128, 1024), sds(2, 4, 2, 2, 32, 128), sds(PAD, 128), sds(PAD, 128)]
+        + [sds(2, 4, FIRST, 128), sds(2, 4, 200 - FIRST, 128), sds(4, 4, FIRST, 128)] * net,
+        scratch_shapes=[pltpu.VMEM((128, 1024), F32), pltpu.VMEM((OUTP, 128), F32)] + ([pltpu.SemaphoreType.DMA((4,))] * 2 + scatter_sems(2) * 2) * net,
         compiler_params=pltpu.CompilerParams(vmem_limit_bytes=60 * 2**20, **(dict(collective_id=1, has_side_effects=True) if net else {})),
     )(f, m, s, nin, nout, hb, wo, bo, c, plow, pw, *([f] * net))
 
 def hid_bwd_kernel(net, t_ref, logp_ref, h_ref, m_ref, s_ref, nin_ref, nout_ref, wo_ref, c_ref, *rest):
     if net:
-        f1_ref, hid_ref, df_ref, small_ref, f2_ref, g1_ref, d1_ref, dz1_ref, dth, dtl, da, msg, dz_to, t_got, fs, fr, ts, tr = rest[:18]
-        g_wire = g_scatter(hid_ref, g1_ref, rest[18:21])
-        d_wire = d_scatter(msg, d1_ref, rest[21:24])
-        z_wire = z_scatter(dz_to, dz1_ref, rest[24:27])
-        wires = (g_wire, d_wire, z_wire)
+        f1b_ref, hid_ref, df_ref, small_ref, f2b_ref, g1_ref, d1_ref, dz1_ref, g2_ref, d2_ref, dz2_ref, d3_ref = rest[:12]
+        dth, dtl, da, msg, dz_to, t_got = rest[12:18]
+        ds, dr, gs, gr, qs, qr, fs, fr, ts, tr, hs, hr, ss, sr, ps, pr, own = rest[18:35]
+        g_wire = g_scatter(hid_ref, g1_ref, rest[35:38])
+        z_wire = z_scatter(dz_to, dz1_ref, rest[38:41])
         p, g, z, y = coords()
-        fan = spread_plane(p, g, z, y, lambda gd, yd: f1_ref.at[gd], lambda m: f2_ref.at[m], fs, fr)
-        target = remote(t_ref, t_got, ts, tr, at(1 - p, g, z, y))
+        d_line = Line(1, lambda i: d1_ref.at[z], lambda zz, i: d1_ref.at[zz], rest[41], rest[42])
+        partner = at(1 - p, g, z, y)
+        target = remote(t_ref, t_got, ts, tr, partner)
+        hand = remote(dz2_ref, dz2_ref, hs, hr, partner)
+        give = remote(msg.at[1], d1_ref.at[z], ps, pr, partner)
+        keep = pltpu.make_async_copy(msg.at[0], d1_ref.at[z], own)
+        fan_f = f_fan(f1b_ref, f2b_ref, fs, fr)
+        fan_g = spread_plane(p, g, z, y, lambda gd, yd: g1_ref.at[:, gd, yd], lambda m: g2_ref.at[m], gs, gr)
+        fan_z = spread_plane(p, g, z, y, lambda gd, yd: dz1_ref, lambda m: dz2_ref.at[m], qs, qr)
+        def fan_d(place, zz):
+            return spread_plane(p, g, z, y, lambda gd, yd: d1_ref.at[zz, yd], lambda m: d2_ref.at[m, zz], ds.at[place], dr.at[place])
+        def swap(place, zz):
+            return remote(d2_ref.at[:, zz], d3_ref.at[:, zz], ss.at[place], sr.at[place], partner)
+        def forward(place, zz):
+            for copy in fan_d(place, zz):
+                copy.start()
+        def forward_small():
+            for k in range(4):
+                g_wire.arrived(k)
+            for copy in fan_g:
+                copy.start()
+            for k in range(4):
+                z_wire.arrived(k)
+            @pl.when(p == 0)
+            def _():
+                for copy in fan_z:
+                    copy.start()
     else:
         df_ref, small_ref, msg, dz_to, dth, dtl, da = rest
         t_got = t_ref
@@ -408,8 +520,10 @@
             dth[s] = hi
             dtl[s] = lo
         if net:
-            d_wire.start()
+            give.start()
+            keep.start()
             z_wire.start()
+            keep.wait()
         ones = jnp.ones((8, 256), BF)
         left = (every - eh.astype(F32)) - el.astype(F32)
         rows = dot(ones, eh, NT) + dot(ones, el, NT) + dot(ones, left.astype(BF), NT)
@@ -432,22 +546,49 @@
     def _():
         greet(line(p, g, z, y) + plane(p, g, z, y))
         pl.when(p == 1)(target.start)
-        for copy in fan:
+        for copy in fan_f:
             copy.start()
         g_wire.start()
         @pl.when(p == 0)
         def _():
             target.wait_recv()
             begin()
+        pl.when(p == 1)(give.wait_recv)
+        d_line.start(0)
+        forward(0, z)
     pl.when(p == 0)(step)
+    pl.when(j == 3)(forward_small)
     @pl.when(j == pl.num_programs(0) - 1)
     def _():
+        for t in range(1, 4):
+            d_line.arrive(t, forward)
         pl.when(p == 1)(target.wait_send)
-        for copy in fan:
+        @pl.when(p == 0)
+        def _():
+            for copy in fan_z:
+                copy.wait()
+            hand.start()
+        def landed(place, zz):
+            copies = fan_d(place, zz)
+            copies[0].wait()
+            for copy in copies[1:]:
+                copy.wait_recv()
+            swap(place, zz).start()
+        d_line.each(landed)
+        for copy in fan_f + fan_g:
             copy.wait()
-        for wire in wires:
-            for k in range(4):
-                wire.arrived(k)
+        def gone(place, zz):
+            for copy in fan_d(place, zz)[1:]:
+                copy.wait_send()
+            swap(place, zz).wait()
+        d_line.each(gone)
+        d_line.sent()
+        @pl.when(p == 0)
+        def _():
+            give.wait_send()
+            hand.wait_send()
+        pl.when(p == 1)(hand.wait_recv)
+        for wire in (g_wire, z_wire):
             wire.sent()
 
 def hidden_bwd(net, t, logp, h, m, s, nin, nout, wo, c, *wired):
@@ -460,12 +601,12 @@
         functools.partial(hid_bwd_kernel, net), grid=(STEPS,),
         in_specs=[full(PAD, 128), full(PAD, 128), full(128, 1024), wspec, wspec, pl.BlockSpec((1, 2, k), lambda j: (j, 0, 0)), full(2, 512),
                   full(OUTP, 512), full(1, 128)] + [ANY, ANY] * net,
-        out_specs=[pl.BlockSpec((k, 128), lambda j: (j, 0)), full(24, 128)] + ([ANY] * 4 if net else [full(2, 2, 256, 128), full(PAD, 128)]),
-        out_shape=[sds(3136, 128), sds(24, 128)] + ([sds(4, 4, 200, 128), sds(4, 2, 2, 32, 128), sds(4, 2, 256, 128), sds(4, PAD, 128)] if net
-                                                    else [sds(2, 2, 256, 128), sds(PAD, 128)]),
+        out_specs=[pl.BlockSpec((k, 128), lambda j: (j, 0)), full(24, 128)] + ([ANY] * 8 if net else [full(2, 2, 256, 128), full(PAD, 128)]),
+        out_shape=[sds(3136, 128), sds(24, 128)] + ([sds(4, 4, 200 - FIRST, 128), sds(4, 2, 2, 32, 128), sds(4, 2, 256, 128), sds(4, PAD, 128), sds(4, 4, 32, 128), sds(4, 4, 256, 128),
+                                                     sds(4, 4, PAD, 128), sds(4, 4, 256, 128)] if net else [sds(2, 2, 256, 128), sds(PAD, 128)]),
         scratch_shapes=[pltpu.VMEM((2, 512, 128), BF), pltpu.VMEM((2, 512, 128), BF), pltpu.VMEM((OUTP, 256), F32)]
-        + ([pltpu.VMEM((2, 2, 256, 128), F32), pltpu.VMEM((PAD, 128), F32), pltpu.VMEM((PAD, 128), F32), dma((4,)), dma((4,)), dma, dma]
-           + scatter_sems(1) * 3) * net,
+        + ([pltpu.VMEM((2, 2, 256, 128), F32), pltpu.VMEM((PAD, 128), F32), pltpu.VMEM((PAD, 128), F32), dma((7, 4)), dma((7, 4))] + [dma((4,))] * 6 + [dma] * 4 + [dma((7,)), dma((7,)), dma, dma, dma]
+           + scatter_sems(1) * 2 + line_sems(1)) * net,
         compiler_params=pltpu.CompilerParams(vmem_limit_bytes=60 * 2**20, **(dict(collective_id=2, has_side_effects=True) if net else {})),
     )(t, logp, h, m, s, nin, nout, wo, c, *wired)
 
@@ -473,32 +614,124 @@
     s = jax.nn.sigmoid(v)
     return s * (1.0 + v * (1.0 - s))
 
-def low_kernel(net, pre1_ref, pre2_ref, pre3_ref, df_ref, w2_ref, w3_ref, *rest):
+
+ROWS = 768
+
+def bwd_kernel(net, x_ref, pre1_hbm, pre2_ref, pre3_ref, df_ref, w1_ref, w2_ref, w3_ref, *rest):
     if net:
-        d1_ref, g1_ref, dz1_ref, d1h, d1l, small_ref, d2_ref, d3_ref, g2_ref, dz2_ref = rest[:10]
-        d3f, d3h, d3l, d2h, d2l, h2h, h2l, acc2, a2, a3 = rest[10:20]
-        ps, pr, gs, gr, qs, qr, ss, sr, ts, tr = rest[20:]
+        r_ref, q_ref, s0_ref, tot_ref, sg_ref, ag_ref, ah_ref, bg_ref, bh_ref = rest[:9]
+        xs, pre1_ref, xh, xl, d3f, d3h, d3l, d2h, d2l, d1h, d1l, h2h, h2l, acc2, a1, a2, a3, pay, lob, upb, x_sem, sem1, ls, us = rest[9:33]
+        got, got1, red, tot, ur, zs_, zr, ys, yr, own, gs, gr, ws, wr, as_, ar, bs, br, es, er, cs, cr, one_ = rest[33:]
         p, g, z, y = coords()
-        greet(plane(p, g, z, y) + [at(1 - p, g, z, y)])
-        fan_d = spread_plane(p, g, z, y, lambda gd, yd: d1_ref.at[:, yd], lambda m: d2_ref.at[m], ps, pr)
-        fan_g = spread_plane(p, g, z, y, lambda gd, yd: g1_ref.at[:, gd, yd], lambda m: g2_ref.at[m], gs, gr)
-        fan_z = spread_plane(p, g, z, y, lambda gd, yd: dz1_ref, lambda m: dz2_ref.at[m], qs, qr)
-        swaps = [remote(d2_ref.at[m], d3_ref.at[m], ss.at[m], sr.at[m], at(1 - p, g, z, y)) for m in range(4)]
-        hand = remote(dz2_ref, dz2_ref, ts, tr, at(1 - p, g, z, y))
-        for copy in fan_d + fan_g:
-            copy.start()
-        @pl.when(p == 0)
-        def _():
-            for copy in fan_z:
+        reps = lax.axis_size("rep")
+        chips = 2 * reps
+        me = g * reps + lax.axis_index("rep")
+        size = ROWS // chips
+        def chip(i):
+            return (0, i // reps, i % reps)
+        def part(i):
+            return pl.ds(pl.multiple_of(i * size, 8), size)
+        def give(k):
+            to = (me + k) % chips
+            if k:
+                return remote(pay.at[part(to)], got.at[me], as_.at[k], ar.at[k], chip(to))
+            return pltpu.make_async_copy(pay.at[part(me)], got.at[me], one_)
+        def given(k):
+            who = (me + chips - k) % chips
+            return remote(pay.at[part(me)], got.at[who], as_.at[k], ar.at[k], chip(who))
+        def show(k):
+            return remote(pay.at[pl.ds(672, 64)], got1.at[me], es.at[k], er.at[k], chip((me + k) % chips))
+        def shown(k):
+            who = (me + chips - k) % chips
+            return remote(pay.at[pl.ds(672, 64)], got1.at[who], es.at[k], er.at[k], chip(who))
+        def tell(k):
+            return remote(red, tot.at[part(me)], bs.at[k], br.at[k], chip((me + k) % chips))
+        def told(k):
+            who = (me + chips - k) % chips
+            return remote(red, tot.at[part(who)], bs.at[k], br.at[k], chip(who))
+        hand = remote(tot, tot, cs, cr, at(1 - p, g, z, y))
+        def head_at(ref, yy, zz):
+            return ref.at[pl.ds(yy, 1 + 7 * yy), pl.ds(pl.multiple_of(32 * zz, 8), 32)]
+        def head_of(yy):
+            return q_ref.at[pl.ds(yy, 1 + 7 * yy)]
+        def slots(yy, zz):
+            return ag_ref.at[yy, zz], head_at(ah_ref, yy, zz), bg_ref.at[yy, zz], head_at(bh_ref, yy, zz)
+        def lines(yy):
+            mine = (r_ref, head_of(yy)) + slots(yy, z)[2:]
+            return Line(4, lambda i: mine[i], lambda zz, i: slots(yy, zz)[i], zs_, zr)
+        def keep(yy):
+            a, b, _, _ = slots(yy, z)
+            return [pltpu.make_async_copy(r_ref, a, own.at[0]), pltpu.make_async_copy(head_of(yy), b, own.at[1])]
+        def give_own(yy):
+            _, _, a, b = slots(yy, z)
+            return [remote(r_ref, a, gs.at[0], gr.at[0], at(1, g, z, y)), remote(head_of(yy), b, gs.at[1], gr.at[1], at(1, g, z, y))]
+        def along_y(place, zz, yy):
+            src = slots(yy, zz) if place else (r_ref, head_of(yy)) + slots(yy, z)[2:]
+            return [remote(src[i], slots(yy, zz)[i], ys.at[place, i], yr.at[place, i], at(p, g, z, 1 - y)) for i in range(4)]
+        def bring(place, zz, yy):
+            a, b, c, d = slots(yy, zz)
+            return [remote(c, a, ws.at[yy, place, 0], wr.at[yy, place, 0], at(0, g, z, y)), remote(d, b, ws.at[yy, place, 1], wr.at[yy, place, 1], at(0, g, z, y))]
+        def each(do, flipped=False):
+            for yy in range(2):
+                pl.when(y == (1 - yy if flipped else yy))(functools.partial(do, yy))
+        def states_out(j, slot):
+            return (pltpu.make_async_copy(lob.at[slot], sg_ref.at[pl.ds(4 * j, 4)], ls.at[slot]),
+                    remote(upb.at[slot], sg_ref.at[pl.ds(4 * j, 4)], us.at[slot], ur.at[j], at(1 - p, g, z, y)))
+        def gather(yy):
+            def then(place, zz):
+                for copy in along_y(place, zz, yy) + bring(place, zz, yy):
+                    copy.start()
+            for copy in give_own(yy):
+                copy.wait_recv()
+            lines(yy).start(0)
+            then(0, z)
+            for copy in keep(yy):
                 copy.start()
-        fan_d[0].wait()
-        swaps[0].start()
+            for t in range(1, 4):
+                lines(yy).arrive(t, then)
+        def second(yy):
+            def landed(place, zz):
+                for copy in along_y(place, zz, yy):
+                    copy.wait_recv()
+                for copy in bring(place, zz, yy):
+                    copy.start()
+            lines(yy).each(landed)
+        def finished(yy):
+            def gone(place, zz):
+                for copy in along_y(place, zz, yy) + bring(place, zz, yy):
+                    copy.wait_send()
+            for copy in keep(yy):
+                copy.wait()
+            lines(yy).sent()
+            lines(yy).each(gone)
+        def second_sent(yy):
+            def gone(place, zz):
+                for copy in bring(place, zz, yy):
+                    copy.wait_send()
+            lines(yy).each(gone)
+        def brought(yy):
+            def came(place, zz):
+                for copy in bring(place, zz, yy):
+                    copy.wait_recv()
+            lines(yy).each(came)
     else:
-        d1h, d1l, small_ref, d3f, d3h, d3l, d2h, d2l, h2h, h2l, acc2, a2, a3 = rest
+        tot_ref, lo_ref, up_ref, xs, pre1_ref, xh, xl, d3f, d3h, d3l, d2h, d2l, d1h, d1l, h2h, h2l, acc2, a1, a2, a3, pay, lob, upb, x_sem, sem1, ls, us = rest
+        def states_out(j, slot):
+            return (pltpu.make_async_copy(lob.at[slot], lo_ref.at[pl.ds(4 * j, 4)], ls.at[slot]),
+                    pltpu.make_async_copy(upb.at[slot], up_ref.at[pl.ds(4 * j, 4)], us.at[slot]))
+    small_ref = pay.at[pl.ds(24, 648)]
+    last = 20
+    def x_in(j):
+        return pltpu.make_async_copy(x_ref.at[pl.ds(4 * j, 4)], xs.at[pl.ds(4 * j, 4)], x_sem.at[j])
+    pre1_in = pltpu.make_async_copy(pre1_hbm, pre1_ref, sem1)
+    def fetch():
+        pre1_in.start()
+        for j in range(21):
+            x_in(j).start()
     def upper():
         for ref in (d3h, d3l, d2h, d2l, acc2, a2, a3):
             ref[...] = jnp.zeros_like(ref)
-        small_ref[...] = jnp.zeros_like(small_ref)
+        small_ref[...] = jnp.zeros((648, 128), F32)
         for ref in (d1h, d1l):
             ref[0] = jnp.zeros((704, 128), BF)
             ref[21] = jnp.zeros((704, 128), BF)
@@ -582,245 +815,158 @@
         a2[...] += dot3((lhs(d2h), lhs(d2l)), (rhs(h1h), rhs(h1l)), NT)
         return total
     def lower():
+        pre1_in.wait()
         total = lax.fori_loop(0, 10, block2, jnp.zeros((32, 128), F32))
         small_ref[642:643, 0:32] = jnp.sum(jnp.transpose(total), axis=0, keepdims=True)
         small_ref[0:128, :] = a2[:, 0:128]
         small_ref[128:256, :] = a2[:, 128:256]
-    if not net:
-        upper()
-        lower()
-        return
-    @pl.when(p == 0)
-    def _():
-        upper()
-        lower()
-    for m in range(1, 4):
-        fan_d[m].wait_recv()
-        swaps[m].start()
-    @pl.when(p == 0)
-    def _():
-        for copy in fan_z:
-            copy.wait()
-        hand.start()
-        hand.wait_send()
-    pl.when(p == 1)(hand.wait_recv)
-    for copy in fan_g:
-        copy.wait()
-    for m in range(1, 4):
-        fan_d[m].wait_send()
-    for swap in swaps:
-        swap.wait()
-
-def lower_backward(net, pre1, pre2, pre3, df, w2, w3, *wired):
-    one = lambda *s: pl.BlockSpec(s, lambda j: (0,) * len(s), pipeline_mode=pl.Buffered(1))
-    sds = lambda *s: jax.ShapeDtypeStruct(s, F32)
-    bfs = lambda *s: jax.ShapeDtypeStruct(s, BF)
-    vmb = lambda *s: pltpu.VMEM(s, BF)
-    dma = pltpu.SemaphoreType.DMA
-    return pl.pallas_call(
-        functools.partial(low_kernel, net),
-        grid=(1,),
-        in_specs=[one(20, 640, 128), one(9, 576, 128), one(3136, 128), one(3136, 128), one(2, 128, 256), one(2, 384, 256)] + [ANY] * (3 * net),
-        out_specs=[one(22, 704, 128), one(22, 704, 128), one(648, 128)] + [ANY] * (4 * net),
-        out_shape=[bfs(22, 704, 128), bfs(22, 704, 128), sds(648, 128)]
-        + [sds(4, 4, 256, 128), sds(4, 4, 256, 128), sds(4, 4, 32, 128), sds(4, 4, PAD, 128)] * net,
-        scratch_shapes=[pltpu.VMEM((3136, 128), F32), vmb(11, 768, 128), vmb(11, 768, 128), vmb(11, 704, 128), vmb(11, 704, 128),
-                        vmb(9, 640, 128), vmb(9, 640, 128), pltpu.VMEM((9, 640, 128), F32), pltpu.VMEM((128, 256), F32), pltpu.VMEM((384, 256), F32)]
-        + ([dma((4,))] * 8 + [dma, dma]) * net,
-        compiler_params=pltpu.CompilerParams(vmem_limit_bytes=60 * 2**20, **(dict(collective_id=3, has_side_effects=True) if net else {})),
-    )(pre1, pre2, pre3, df, w2, w3, *wired)
-
-def first_kernel_bwd(net, x_ref, dha_ref, dhb_ref, dla_ref, dlb_ref, w1_ref, *rest):
-    if net:
-        r_ref, q_ref, s0_ref, s1_ref, tot_ref, sg_ref, ag_ref, ah_ref, xh, xl, a1, lob, upb, pay, got, red, tot, ls, us, ur, zs_, zr, ys, yr, own = rest[:25]
-        as_, ar, bs, br, cs, cr, one_ = rest[25:]
-        p, g, z, y = coords()
-        reps = lax.axis_size("rep")
-        chips = 2 * reps
-        me = g * reps + lax.axis_index("rep")
-        size = ROWS // chips
-        def chip(i):
-            return (0, i // reps, i % reps)
-        def part(i):
-            return pl.ds(pl.multiple_of(i * size, 8), size)
-        def give(k):
-            to = (me + k) % chips
-            if k:
-                return remote(pay.at[part(to)], got.at[me], as_.at[k], ar.at[k], chip(to))
-            return pltpu.make_async_copy(pay.at[part(me)], got.at[me], one_)
-        def given(k):
-            who = (me + chips - k) % chips
-            return remote(pay.at[part(me)], got.at[who], as_.at[k], ar.at[k], chip(who))
-        def tell(k):
-            return remote(red, tot.at[part(me)], bs.at[k], br.at[k], chip((me + k) % chips))
-        def told(k):
-            who = (me + chips - k) % chips
-            return remote(red, tot.at[part(who)], bs.at[k], br.at[k], chip(who))
-        hand = remote(tot, tot, cs, cr, at(1 - p, g, z, y))
-        small_ref = pay.at[pl.ds(672, 64)]
-        def rows_of(zz):
-            return pl.ds(pl.multiple_of(32 * zz, 8), 32)
-        def head_at(yy, zz):
-            return ah_ref.at[pl.ds(yy, 1 + 7 * yy), rows_of(zz)]
-        def along_z(k, yy):
-            to = at(p, g, flip(z, k), y)
-            a, b = (r_ref, ag_ref.at[yy, z]), (q_ref.at[pl.ds(yy, 1 + 7 * yy)], head_at(yy, z))
-            if k:
-                return [remote(*a, zs_.at[k, 0], zr.at[k, 0], to), remote(*b, zs_.at[k, 1], zr.at[k, 1], to)]
-            return [pltpu.make_async_copy(*a, own.at[0]), pltpu.make_async_copy(*b, own.at[1])]
-        def along_y(k, yy):
-            zs = flip(z, k)
-            a, b = (ag_ref.at[yy, zs], head_at(yy, zs)) if k else (r_ref, q_ref.at[pl.ds(yy, 1 + 7 * yy)])
-            to = at(p, g, z, 1 - y)
-            return [remote(a, ag_ref.at[yy, zs], ys.at[k, 0], yr.at[k, 0], to), remote(b, head_at(yy, zs), ys.at[k, 1], yr.at[k, 1], to)]
-        def each(do, flipped=False):
-            for yy in range(2):
-                pl.when(y == (1 - yy if flipped else yy))(functools.partial(do, yy))
-        def states_out(j, slot):
-            return (pltpu.make_async_copy(lob.at[slot], sg_ref.at[pl.ds(4 * j, 4)], ls.at[slot]),
-                    remote(upb.at[slot], sg_ref.at[pl.ds(4 * j, 4)], us.at[slot], ur.at[j], at(1 - p, g, z, y)))
-    else:
-        small_ref, lo_ref, up_ref, xh, xl, a1 = rest
-    j = pl.program_id(0)
-    last = pl.num_programs(0) - 1
-    @pl.when(j == 0)
-    def _():
+    def states_gone(j, slot):
+        a, b = states_out(j, slot)
+        a.wait()
         if net:
-            pl.when(p == 0)(lambda: greet([chip((me + k) % chips) for k in range(1, chips)] + [at(1, g, z, y)]))
-            pl.when(p == 1)(lambda: greet([at(1, g, flip(z, k), y) for k in range(1, 4)] + [at(1, g, z, 1 - y), at(0, g, z, y)]))
-            pay[0:24, :] = s0_ref[...]
-            pay[24:672, :] = s1_ref[...]
-            pay[736:, :] = jnp.zeros((ROWS - 736, 128), F32)
-            def begin(yy):
-                for copy in along_z(1, yy) + along_y(0, yy) + along_z(2, yy) + along_z(3, yy) + along_z(0, yy):
-                    copy.start()
-            each(begin)
-        xh[:, 336:, :] = jnp.zeros((4, 16, 128), BF)
-        xl[:, 336:, :] = jnp.zeros((4, 16, 128), BF)
-        a1[...] = jnp.zeros_like(a1)
-    def work():
-        v = x_ref[...]
+            b.wait_send()
+        else:
+            b.wait()
+    def work(j, carry):
+        x_in(j).wait()
+        v = xs[pl.ds(4 * j, 4)]
         hi = v.astype(BF)
         xh[:, 0:336, :] = hi
         xl[:, 0:336, :] = (v - hi.astype(F32)).astype(BF)
-        def both(a, b):
-            return jnp.concatenate([jnp.concatenate([a[0, 96 * i:96 * i + 128, :], b[0, 96 * i:96 * i + 128, :]], axis=0) for i in range(7)], axis=1)
-        r = dot3((w1_ref[0], w1_ref[1]), (both(dha_ref, dhb_ref), both(dla_ref, dlb_ref)))
-        if net:
-            slot = j % 2
-            @pl.when(j >= 2)
-            def _():
-                a, b = states_out(j - 2, slot)
-                a.wait()
-                b.wait_send()
-            lo_to, up_to = lob.at[slot], upb.at[slot]
-        else:
-            lo_to, up_to = lo_ref, up_ref
+        def both(ref):
+            return jnp.concatenate([ref[pl.ds(j, 2), 96 * i:96 * i + 128, :].reshape(256, 128) for i in range(7)], axis=1)
+        r = dot3((w1_ref[0], w1_ref[1]), (both(d1h), both(d1l)))
+        slot = j % 2
+        pl.when(j >= 2)(lambda: states_gone(j - 2, slot))
+        lo_to, up_to = lob.at[slot], upb.at[slot]
         for ky in range(4):
             for i in range(7):
                 lo_to[ky, 24 * i:24 * i + 24, :] = r[24 * ky:24 * ky + 24, 128 * i:128 * i + 128]
                 up_to[ky, 24 * i:24 * i + 24, :] = r[96 + 24 * ky:96 + 24 * ky + 24, 128 * i:128 * i + 128]
-        if net:
-            for copy in states_out(j, slot):
-                copy.start()
-        def lhs(a, b):
-            return jnp.concatenate([jnp.concatenate([ref[0, 96 * i + 32:96 * i + 128, :] for i in range(7)], axis=1) for ref in (b, a)], axis=0)
+        for copy in states_out(j, slot):
+            copy.start()
+        def lhs(ref):
+            return jnp.concatenate([jnp.concatenate([ref[j + 1 - h, 96 * i + 32:96 * i + 128, :] for i in range(7)], axis=1) for h in range(2)], axis=0)
         def rhs(ref):
             return jnp.concatenate([ref[:, 48 * i:48 * i + 64, :].reshape(256, 128) for i in range(7)], axis=1)
-        a1[...] += dot3((lhs(dha_ref, dhb_ref), lhs(dla_ref, dlb_ref)), (rhs(xh), rhs(xl)), NT)
+        a1[...] += dot3((lhs(d1h), lhs(d1l)), (rhs(xh), rhs(xl)), NT)
+        return carry
     if net:
-        pl.when(p == 0)(work)
-        def pass_on(k, yy):
-            for copy in along_z(k, yy):
-                copy.wait_recv()
-            for copy in along_y(k, yy):
+        pl.when(p == 0)(fetch)
+        pl.when(p == 0)(lambda: greet([chip((me + k) % chips) for k in range(1, chips)] + [at(1, g, z, y)]))
+        pl.when(p == 1)(lambda: greet([at(1, g, flip(z, k), y) for k in range(1, 4)] + [at(1, g, z, 1 - y), at(0, g, z, y)]))
+        def begin(yy):
+            for copy in give_own(yy):
                 copy.start()
-        for k, step in ((1, 9), (2, 18)):
-            pl.when(j == step)(lambda: each(functools.partial(pass_on, k)))
+        pl.when(p == 0)(lambda: each(begin))
+        @pl.when(p == 1)
+        def _():
+            each(gather)
+            each(second, flipped=True)
+        pay[0:24, :] = s0_ref[...]
     else:
-        work()
-    @pl.when(j == last)
-    def _():
-        for h in range(2):
-            for ky in range(4):
-                grad = a1[96 * h:96 * h + 32, 64 * ky:64 * ky + 32]
-                grad = grad + a1[96 * h + 32:96 * h + 64, 64 * ky + 16:64 * ky + 48]
-                grad = grad + a1[96 * h + 64:96 * h + 96, 64 * ky + 32:64 * ky + 64]
-                small_ref[32 * h:32 * h + 32, 32 * ky:32 * ky + 32] = grad
-        if net:
-            @pl.when(p == 0)
-            def _():
-                for k in range(chips):
-                    give(k).start()
-            each(functools.partial(pass_on, 3))
-            @pl.when(p == 0)
-            def _():
-                give(0).wait()
-                for k in range(1, chips):
-                    given(k).wait_recv()
-                red[...] = jnp.sum(got[...], axis=0)
-                tot[part(me), :] = red[...]
-                for k in range(1, chips):
-                    tell(k).start()
-                for k in range(1, chips):
-                    told(k).wait_recv()
-                hand.start()
-                for k in range(1, chips):
-                    give(k).wait_send()
-                    tell(k).wait_send()
-                hand.wait_send()
-                for back in (1, 0):
-                    a, b = states_out(j - back, (j - back) % 2)
-                    a.wait()
-                    b.wait_send()
-            @pl.when(p == 1)
-            def _():
-                hand.wait_recv()
-                def arrive(i, c):
-                    states_out(i, 0)[1].wait_recv()
-                    return c
-                lax.fori_loop(0, last + 1, arrive, 0)
-            tot_ref[...] = tot[...]
-            def sent(yy):
-                for k in range(4):
-                    for copy in along_z(k, yy):
-                        if k:
-                            copy.wait_send()
-                        else:
-                            copy.wait()
-                    for copy in along_y(k, yy):
-                        copy.wait_send()
-            each(sent)
-            def came(yy):
-                for k in range(4):
-                    for copy in along_y(k, yy):
-                        copy.wait_recv()
-            each(came, flipped=True)
-
-def first_backward(net, x, dh, dl, w1, *wired):
-    full = lambda *s: pl.BlockSpec(s, lambda j: (0,) * len(s))
+        pay[0:24, :] = jnp.zeros((24, 128), F32)
+    pay[672:, :] = jnp.zeros((ROWS - 672, 128), F32)
+    xh[:, 336:, :] = jnp.zeros((4, 16, 128), BF)
+    xl[:, 336:, :] = jnp.zeros((4, 16, 128), BF)
+    a1[...] = jnp.zeros_like(a1)
+    if net:
+        pl.when(p == 0)(upper)
+        pl.when(p == 0)(lower)
+        @pl.when(p == 0)
+        def _():
+            for k in range(chips):
+                give(k).start()
+    else:
+        fetch()
+        upper()
+        lower()
+    if net:
+        @pl.when(p == 0)
+        def _():
+            lax.fori_loop(0, 7, work, 0)
+            give(0).wait()
+            for k in range(1, chips):
+                give(k).wait_send()
+            for k in range(1, chips):
+                given(k).wait_recv()
+            red[...] = jnp.sum(got[...], axis=0)
+            tot[part(me), :] = red[...]
+            for k in range(1, chips):
+                tell(k).start()
+            lax.fori_loop(7, 21, work, 0)
+    else:
+        lax.fori_loop(0, 21, work, 0)
+        for j in (last - 1, last):
+            states_gone(j, j % 2)
+    for h in range(2):
+        for ky in range(4):
+            grad = a1[96 * h:96 * h + 32, 64 * ky:64 * ky + 32]
+            grad = grad + a1[96 * h + 32:96 * h + 64, 64 * ky + 16:64 * ky + 48]
+            grad = grad + a1[96 * h + 64:96 * h + 96, 64 * ky + 32:64 * ky + 64]
+            pay[672 + 32 * h:704 + 32 * h, 32 * ky:32 * ky + 32] = grad
+    if net:
+        @pl.when(p == 0)
+        def _():
+            for k in range(1, chips):
+                show(k).start()
+            got1[me] = pay[672:736, :]
+        @pl.when(p == 0)
+        def _():
+            for k in range(1, chips):
+                told(k).wait_recv()
+            for k in range(1, chips):
+                shown(k).wait_recv()
+            tot[672:736, :] = jnp.sum(got1[...], axis=0)
+            hand.start()
+            for k in range(1, chips):
+                tell(k).wait_send()
+                show(k).wait_send()
+            hand.wait_send()
+            for j in (last - 1, last):
+                states_gone(j, j % 2)
+        @pl.when(p == 1)
+        def _():
+            hand.wait_recv()
+            def arrive(i, c):
+                states_out(i, 0)[1].wait_recv()
+                return c
+            lax.fori_loop(0, last + 1, arrive, 0)
+        tot_ref[...] = tot[...]
+        @pl.when(p == 0)
+        def _():
+            def given_own(yy):
+                for copy in give_own(yy):
+                    copy.wait_send()
+            each(given_own)
+            brought(0)
+            brought(1)
+        @pl.when(p == 1)
+        def _():
+            each(finished)
+            each(second_sent, flipped=True)
+    else:
+        tot_ref[...] = pay[...]
+
+def backward(net, x, pre1, pre2, pre3, df, w1, w2, w3, *wired):
     sds = lambda *s: jax.ShapeDtypeStruct(s, F32)
     vmb = lambda *s: pltpu.VMEM(s, BF)
+    f32 = lambda *s: pltpu.VMEM(s, F32)
     dma = pltpu.SemaphoreType.DMA
-    half = pl.BlockSpec((4, 168, 128), lambda j: (j, 0, 0))
-    row = pl.BlockSpec((1, 704, 128), lambda j: (j, 0, 0))
-    next_row = pl.BlockSpec((1, 704, 128), lambda j: (j + 1, 0, 0))
     return pl.pallas_call(
-        functools.partial(first_kernel_bwd, net),
-        grid=(21,),
-        in_specs=[pl.BlockSpec((4, 336, 128), lambda j: (j, 0, 0)), row, next_row, row, next_row, full(2, 192, 256)] + [ANY, ANY, full(24, 128), full(648, 128)] * net,
-        out_specs=[full(ROWS, 128)] + [ANY] * 3 if net else [full(64, 128), half, half],
-        out_shape=[sds(ROWS, 128), sds(84, 168, 128), sds(2, 4, 200, 512), sds(9, 128, 128)] if net else [sds(64, 128), sds(84, 168, 128), sds(84, 168, 128)],
-        scratch_shapes=[vmb(4, 352, 128), vmb(4, 352, 128), pltpu.VMEM((192, 256), F32)]
-        + [pltpu.VMEM((2, 4, 168, 128), F32), pltpu.VMEM((2, 4, 168, 128), F32), pltpu.VMEM((ROWS, 128), F32), pltpu.VMEM((16, ROWS // 16, 128), F32),
-           pltpu.VMEM((ROWS // 16, 128), F32), pltpu.VMEM((ROWS, 128), F32), dma((2,)), dma((2,)), dma((21,)),
-           dma((4, 2)), dma((4, 2)), dma((4, 2)), dma((4, 2)), dma((2,)), dma((16,)), dma((16,)), dma((16,)), dma((16,)), dma, dma, dma] * net,
-        compiler_params=pltpu.CompilerParams(vmem_limit_bytes=60 * 2**20, **(dict(collective_id=4, has_side_effects=True) if net else {})),
-    )(x, dh, dh, dl, dl, w1, *wired)
-
-ROWS = 768
-
-def wide_kernel(f_ref, d_ref, e_ref, g_ref, z_ref, r_ref, q_ref, acc, acq, da):
+        functools.partial(bwd_kernel, net),
+        in_specs=[ANY, ANY] + [VMEM] * 6 + [ANY, ANY, VMEM] * net,
+        out_specs=[VMEM] + [ANY] * (5 if net else 2),
+        out_shape=[sds(ROWS, 128)] + ([sds(84, 168, 128)] + [sds(2, 4, 200, 512), sds(9, 128, 128)] * 2 if net else [sds(84, 168, 128), sds(84, 168, 128)]),
+        scratch_shapes=[f32(84, 336, 128), f32(20, 640, 128), vmb(4, 352, 128), vmb(4, 352, 128), f32(3136, 128), vmb(11, 768, 128), vmb(11, 768, 128), vmb(11, 704, 128),
+                        vmb(11, 704, 128), vmb(22, 704, 128), vmb(22, 704, 128), vmb(9, 640, 128), vmb(9, 640, 128), f32(9, 640, 128), f32(192, 256), f32(128, 256),
+                        f32(384, 256), f32(ROWS, 128), f32(2, 4, 168, 128), f32(2, 4, 168, 128), dma((21,)), dma, dma((2,)), dma((2,))]
+        + ([f32(16, ROWS // 16, 128), f32(16, 64, 128), f32(ROWS // 16, 128), f32(ROWS, 128), dma((21,))]
+           + line_sems(4) + [dma((7, 4))] * 2 + [dma((2,))] * 3 + [dma((2, 7, 2))] * 2 + [dma((16,))] * 6 + [dma] * 3) * net,
+        compiler_params=pltpu.CompilerParams(vmem_limit_bytes=62 * 2**20, **(dict(collective_id=3, has_side_effects=True) if net else {})),
+    )(x, pre1, pre2, pre3, df, w1, w2, w3, *wired)
+
+def wide_kernel(fa_ref, fb_ref, d_ref, e_ref, g_ref, z_ref, r_ref, q_ref, acc, acq, da):
     m = pl.program_id(0)
     p = lax.axis_index("pair")
     @pl.when(m == 0)
@@ -828,7 +974,7 @@
         acc[...] = jnp.zeros_like(acc)
         acq[...] = jnp.zeros_like(acq)
         da[...] = jnp.zeros_like(da)
-    f = split(jnp.concatenate([f_ref[0, i] for i in range(4)], axis=1))
+    f = split(jnp.concatenate([jnp.concatenate([fa_ref[0, i], fb_ref[0, i]], axis=0) for i in range(4)], axis=1))
     def block(ref):
         return jnp.concatenate([jnp.concatenate([ref[0, i, 128 * c:128 * c + 128, :] for c in range(2)], axis=1) for i in range(4)], axis=0)
     acc[0] += dot3(f, split(block(d_ref)))
@@ -849,18 +995,18 @@
         for c in range(9):
             q_ref[c] = acq[:, 128 * c:128 * c + 128]
 
-def wide_grads(f2, d2, d3, g2, z2):
+def wide_grads(f2a, f2b, d2, d3, g2, z2):
     full = lambda *s: pl.BlockSpec(s, lambda j: (0,) * len(s))
     part = lambda n: pl.BlockSpec((1, 4, n, 128), lambda j: (j, 0, 0, 0))
     sds = lambda *s: jax.ShapeDtypeStruct(s, F32)
     return pl.pallas_call(
         wide_kernel, grid=(4,),
-        in_specs=[part(200), part(256), part(256), part(32), part(PAD)],
+        in_specs=[part(FIRST), part(200 - FIRST), part(256), part(256), part(32), part(PAD)],
         out_specs=[full(200, 512), full(9, 32, 128)],
         out_shape=[sds(200, 512), sds(9, 32, 128)],
         scratch_shapes=[pltpu.VMEM((2, 200, 256), F32), pltpu.VMEM((32, 1152), F32), pltpu.VMEM((1152, 512), F32)],
         compiler_params=pltpu.CompilerParams(vmem_limit_bytes=60 * 2**20),
-    )(f2, d2, d3, g2, z2)
+    )(f2a, f2b, d2, d3, g2, z2)
 
 def torso_out(tot, k1_ref, k2_ref, k3_ref, b1_ref, b2_ref, b3_ref, t1, t2):
     t1[:, 0:64] = jnp.transpose(tot[672:736, :])
@@ -978,13 +1124,12 @@
     hb = (hidden_bias_mean[0] + hidden_bias_sigma[0] * n_out).reshape(1, 1024)
     nin = jnp.transpose(n_in.reshape(2, STEPS, 3136 // STEPS), (1, 0, 2))
     pre1, pre2, pre3, feats = forward(x, fw1, fw2, fw3, c1, c2, c3)
-    h, hid, logp, dist, *f1 = hidden(net, feats, hidden_mean[0], hidden_sigma[0], nin, n_out, hb, wo, bo, actions, proj_lower.T, proj_weight.T)
+    h, hid, logp, dist, *f12 = hidden(net, feats, hidden_mean[0], hidden_sigma[0], nin, n_out, hb, wo, bo, actions, proj_lower.T, proj_weight.T)
     back = (logp, h, hidden_mean[0], hidden_sigma[0], nin, n_out, wo, actions)
     if net:
-        df, small_b, f2, g1, d1, dz1 = hidden_bwd(net, dist, *back, *f1, hid)
-        dh, dl, small_d, d2, d3, g2, z2 = lower_backward(net, pre1, pre2, pre3, df, bw2, bw3, d1, g1, dz1)
-        part_r, part_q = wide_grads(f2, d2, d3, g2, z2)
-        total, grad_rows, ag, ah = first_backward(net, x, dh, dl, bw1, part_r, part_q, small_b, small_d)
+        df, small_b, f2b, _, _, _, g2, d2, z2, d3 = hidden_bwd(net, dist, *back, f12[1], hid)
+        part_r, part_q = wide_grads(f12[2], f2b, d2, d3, g2, z2)
+        total, grad_rows, ag, ah, _, _ = backward(net, x, pre1, pre2, pre3, df, bw1, bw2, bw3, part_r, part_q, small_b)
         (hidden_grad, hidden_sigma_grad, head_t, head_sigma_t, gk1, gk2, gk3, gb1, gb2, gb3, hb_grad, hbs_grad, bo_grad, bos_grad,
          loss) = finish(ag, ah, total, in_q, on_out, e_q, on_eout[None])
     else:
@@ -1003,10 +1148,9 @@
         da = (mask[:, None, :] * dz_all.T[None]).reshape(ACTIONS * ATOMS, -1)
         part_head = jnp.concatenate([jnp.dot(dz_all.T, hid_all[:, 0], precision=HIGH), jnp.dot(da, hid_all[:, 1], precision=HIGH)], axis=0)
         hidden_grad, head_t = lax.psum((part_hidden, part_head), "rep")
-        dh, dl, small_d = lower_backward(net, pre1, pre2, pre3, df, bw2, bw3)
-        small_f, lo, up = first_backward(net, x, dh, dl, bw1)
+        small_d, lo, up = backward(net, x, pre1, pre2, pre3, df, bw1, bw2, bw3)
         grad_rows = jnp.where(pair == 0, lo, lax.ppermute(up, "pair", [(0, 1)]))
-        total = lax.psum(jnp.concatenate([small_b, small_d, small_f], axis=0), ("pair", "group", "rep"))
+        total = lax.psum(small_d + jnp.pad(small_b, ((0, ROWS - 24), (0, 0))), ("pair", "group", "rep"))
         hidden_sigma_grad = hidden_grad * (in_q[:, :, None] * on_out[:, None, :])
         head_sigma_t = head_t * (jnp.where(jnp.arange(OUTS)[:, None] < ATOMS, e_q[0:1], e_q[1:2]) * on_eout[:, None])
         gk1, gk2, gk3, gb1, gb2, gb3 = small_finish(total)

time: 266 us -> 222 us (0.83)
  Pallas kernels: 242 us -> 198 us
    pallas_call x4 -> x3, Pallas kernels: 167 us -> 110 us  [the longest x1 77 us: backward(): pl.pallas_call(functools.partial(bwd_kernel, net), in_specs=[ANY, ANY] +...]
    pallas_call x1, Pallas kernels: 23.2 us -> 30.5 us  [hidden(): pl.pallas_call(functools.partial(hid_kernel, net), grid=(STEPS,), in_spec...]
    pallas_call x1, Pallas kernels: 42.5 us -> 48.7 us  [hidden_bwd(): pl.pallas_call(functools.partial(hid_bwd_kernel, net), grid=(STEPS,), in_...]
  transfers between devices with their start and end apart: 1 -> 1, of which waited for: 0 -> 0; matrix products, arithmetic and copies ran while one was open for 3% -> 3% of each run, Pallas kernels for 89% -> 87%
where the time goes in v4:
time: 222 us; the launch traced here: 221 us
  Pallas kernels  198 us (89%)
  local copies, waits for them, and re-layouts  15.4 us (7%)
  other arithmetic  4 us (2%)
  starting transfers between devices  2.35 us (1%)
    pallas_call x1, Pallas kernels, backward(): pl.pallas_call(functools.partial(bwd_kernel, net), in_specs=[ANY, ANY] +...  77 us
    pallas_call x1, Pallas kernels, hidden_bwd(): pl.pallas_call(functools.partial(hid_bwd_kernel, net), grid=(STEPS,), in_...  48.7 us
    pallas_call x1, Pallas kernels, hidden(): pl.pallas_call(functools.partial(hid_kernel, net), grid=(STEPS,), in_spec...  30.5 us
    pallas_call x1, Pallas kernels, forward(): pl.pallas_call(fwd_kernel, in_specs=[hbm] + [vm] * 6, out_specs=[hbm, hbm...  24.7 us
    pallas_call x1, Pallas kernels, wide_grads(): pl.pallas_call(wide_kernel, grid=(4,), in_specs=[part(FIRST), part(200 -...  8.72 us
    unnamed x12, local copies, waits for them, and re-layouts  8.52 us
    pallas_call x1, Pallas kernels, finish(): pl.pallas_call(finish_kernel, in_specs=[VMEM] * 7, out_specs=[VMEM] * 15,...  5.94 us
  transfers between devices with their start and end apart: 1, of which 0 were waited for; matrix products, arithmetic and copies ran while one was open for 3% of the time, Pallas kernels for 87%

profile of v4, /device:TPU:0, one launch (start us, length us, event | category | flops | bytes accessed | tf_op | source)
XLA Modules:
  0.0 221.1 jit_solution(6251752218272963025)
XLA Ops:
  0.6 0.8 reshape_squeeze.13
  1.5 0.7 copy.42
  2.2 0.7 copy.43
  2.9 0.7 pad_maximum_fusion
  3.5 2.3 %collective-permute-start = (f32[9289]{0:T(1024)S(1)}, f32[9289]{0:T(1024)S(1)}, u32[]{:S(2)}, u32[]{:S(2)}) collective-permute-start(f32[9289]{0:T(1024)S(1)} %pad_maximum_fusion), channel_id=1, source_target_pairs={{0,16},{1,17},{2,18},{3,19},{4,20},{5,21},{6,22},{7,23},{8,24},{9,... | collective-permute-start | bytes 111476 | tf_op jit(solution)/shard_map/ppermute | solution.py:1082
  5.9 0.8 fusion.2
  6.7 0.7 add_bitcast_fusion
  7.4 0.0 copy-start.1
  7.4 0.0 copy-start.2
  7.4 0.0 copy-start.3
  7.4 0.0 copy-start
  7.4 2.5 %fusion = f32[969,512]{1,0:T(8,128)S(1)} fusion(f32[1,512,969]{1,0,2:T(1,128)} %param.38, f32[1,512,969]{1,0,2:T(1,128)} %param.37, f32[969]{0:T(1024)} %bitcast.74, f32[512]{0:T(512)S(1)} %bitcast.86, f32[512]{0:T(512)S(1)} %bitcast.85, pred[969]{0:T(1024)(128)(4,1)S(1)} %iota_compare_fusion), kind=kLoop, calls=%fused_computation.1 | loop fusion | flops 1984512 | bytes 5962477 | tf_op jit(solution)/shard_map/add | solution.py:1122
  10.0 0.0 copy-done.1
  10.0 0.0 copy-done.2
  10.0 0.0 copy-done.3
  10.0 0.0 copy-done
  10.1 0.1 reshape_squeeze.12
  10.1 0.6 copy.47
  10.8 0.6 copy.41
  11.4 1.5 pad.8.wo_ref
  12.8 0.6 pad.9.bo_ref
  13.4 2.8 %shard_map.333 = (bf16[2,192,256]{2,1,0:T(8,128)(2,1)}, bf16[2,128,256]{2,1,0:T(8,128)(2,1)}, bf16[2,384,256]{2,1,0:T(8,128)(2,1)}, bf16[2,192,256]{2,1,0:T(8,12...) custom-call(f32[4,8,8,32]{3,2,1,0:T(8,128)} %bitcast.69, ...), custom_call_target="tpu_custom_call" | custom-call | tf_op jit(solution)/shard_map/pallas_call | solution.py:82
  16.3 24.7 %shard_map.334 = (f32[20,640,128]{2,1,0:T(8,128)}, f32[9,576,128]{2,1,0:T(8,128)}, f32[3136,128]{1,0:T(8,128)}, f32[3136,128]{1,0:T(8,128)}) custom-call(f32[84,336,128]{2,1,0:T(8,128)} %bitcast.58, bf16[2,192,256]{2,1,0:T(8,128)(2,1)} %get-tuple-element.63.w1_ref, bf16[2,128,256]{2,1,0:T(8,128)(2,1)} %get-tuple-element.64.w2_ref, ...), custom_call_target="tpu_custom_call" | custom-call | tf_op jit(solution)/shard_map/pallas_call | solution.py:173
  41.0 30.5 %shard_map.335 = (f32[128,1024]{1,0:T(8,128)}, f32[2,4,2,2,32,128]{5,4,3,2,1,0:T(8,128)}, f32[56,128]{1,0:T(8,128)}, f32[56,128]{1,0:T(8,128)}, f32[2,4,104,128]...) custom-call(f32[3136,128]{1,0:T(8,128)} %get-tuple-element.72.f_ref.rest_0_, ...), custom_call_target="tpu_custom_call" | custom-call | tf_op jit(solution)/shard_map/pallas_call | solution.py:447
  71.5 48.7 %shard_map.336 = (f32[3136,128]{1,0:T(8,128)}, f32[24,128]{1,0:T(8,128)}, f32[4,4,96,128]{3,2,1,0:T(8,128)}, f32[4,2,2,32,128]{4,3,2,1,0:T(8,128)}, f32[4,2,256,...) custom-call(f32[56,128]{1,0:T(8,128)} %get-tuple-element.73.t_ref, ...), custom_call_target="tpu_custom_call" | custom-call | tf_op jit(solution)/shard_map/pallas_call | solution.py:600
  120.2 8.7 %shard_map.337 = (f32[200,512]{1,0:T(8,128)}, f32[9,32,128]{2,1,0:T(8,128)}) custom-call(f32[4,4,104,128]{3,2,1,0:T(8,128)} %get-tuple-element.82.fa_ref, f32[4,4,96,128]{3,2,1,0:T(8,128)} %get-tuple-element.83.fb_ref, f32[4,4,256,128]{3,2,1,0:T(8,128)} %get-tuple-element.84.d_ref, f32[4,4,256,128]{3,2,1,0:T(8,128)} %get-tuple-element.85.e_ref, ...), custom_call_target="tpu_custom_call" | custom-call | tf_op jit(solution)/shard_map/pallas_call | solution.py:1002
  129.0 77.0 %shard_map.338 = (f32[768,128]{1,0:T(8,128)}, f32[84,168,128]{2,1,0:T(8,128)}, f32[2,4,200,512]{3,2,1,0:T(8,128)}, f32[9,128,128]{2,1,0:T(8,128)}, f32[2,4,200,512]{3,2,1,0:T(8,128)}, /*index=5*/f32[9,128,128]{2,1,0:T(8,128)}) custom-call(f32[84,336,128]{2,1,0:T(8,128)} %bitcast.59, f32[20,640,128]{2,1,0:T(8,128)} %get-tuple-element.69.pre1_hbm, ...), custom_call_target="tpu_custom_call" | custom-call | tf_op jit(solution)/shard_map/pallas_call | solution.py:956
  206.0 0.0 collective-permute-done
  206.1 0.6 slice.33
  206.7 0.1 reshape.88
  206.8 0.6 reshape.89.out_ref
  207.4 0.6 constant_dynamic-slice_fusion.ein_ref
  207.9 0.7 constant_dynamic-slice_fusion.1.in_ref
  208.6 5.9 %shard_map.339 = (f32[2,784,512]{2,1,0:T(8,128)}, f32[2,784,512]{2,1,0:T(8,128)}, f32[969,128]{1,0:T(8,128)}, f32[969,128]{1,0:T(8,128)}, f32[4,8,8,32]{3,2,1,0:...) custom-call(f32[2,4,200,512]{3,2,1,0:T(8,128)} %get-tuple-element.91, ...), custom_call_target="tpu_custom_call" | custom-call | tf_op jit(solution)/shard_map/pallas_call | solution.py:1062
  214.6 6.5 %copy.49 = f32[128,2,84,84]{0,1,3,2:T(2,128)} copy(f32[128,2,84,84]{0,1,3,2:T(2,128)} %bitcast.64) | data formatting | bytes 14450688
  (6 shorter events, 0.0 us)
Async XLA Ops:
  3.5 202.5 %collective-permute-start = (f32[9289]{0:T(1024)S(1)}, f32[9289]{0:T(1024)S(1)}, u32[]{:S(2)}, u32[]{:S(2)}) collective-permute-start(f32[9289]{0:T(1024)S(1)} %pad_maximum_fusion), channel_id=1, source_target_pairs={{0,16},{1,17},{2,18},{3,19},{4,20},{5,21},{6,22},{7,23},{8,24},{9,... | collective-permute-start | bytes 111476 | tf_op jit(solution)/shard_map/ppermute | solution.py:1082
  7.4 2.6 %copy-start.1 = (f32[1,969]{1,0:T(1,128)S(1)}, f32[1,969]{1,0:T(1,128)}, u32[]{:S(2)}) copy-start(f32[1,969]{1,0:T(1,128)} %param.44) | copy-start | bytes 11632
  7.4 2.6 %copy-start.2 = (f32[1,969]{1,0:T(1,128)S(1)}, f32[1,969]{1,0:T(1,128)}, u32[]{:S(2)}) copy-start(f32[1,969]{1,0:T(1,128)} %param.39) | copy-start | bytes 11632
  7.4 2.6 %copy-start.3 = (f32[1,969]{1,0:T(1,128)S(1)}, f32[1,969]{1,0:T(1,128)}, u32[]{:S(2)}) copy-start(f32[1,969]{1,0:T(1,128)} %param.40) | copy-start | bytes 11632
  7.4 2.6 %copy-start = (f32[1,2,3136]{2,1,0:T(2,128)S(1)}, f32[1,2,3136]{2,1,0:T(2,128)}, u32[]{:S(2)}) copy-start(f32[1,2,3136]{2,1,0:T(2,128)} %param.41) | copy-start | bytes 75268

commit v5 on v4

--- a/solution.py
+++ b/solution.py
@@ -218,8 +218,8 @@
 
 
 class Scatter:
-    def __init__(self, parts, src, dst, send, recv, own, cores=2):
-        self.parts, self.src, self.dst, self.send, self.recv, self.own, self.cores = parts, src, dst, send, recv, own, cores
+    def __init__(self, parts, src, dst, send, recv, own, hold=None, cores=2):
+        self.parts, self.src, self.dst, self.send, self.recv, self.own, self.hold, self.cores = parts, src, dst, send, recv, own, hold, cores
         self.p, self.g, self.z, self.y = coords()
 
     def copies(self):
@@ -228,7 +228,7 @@
                 for i in range(self.parts):
                     zd = flip(self.z, k)
                     if k == 0 and q == 0:
-                        yield pltpu.make_async_copy(self.src(q, zd, i), self.dst(self.z, i), self.own.at[i]), True
+                        yield pltpu.make_async_copy(self.src(q, zd, i), self.dst(self.z, i) if self.hold is None else self.hold.at[i], self.own.at[i]), True
                     else:
                         yield remote(self.src(q, zd, i), self.dst(self.z, i), self.send.at[k * 2 + q, i], self.recv.at[k, i], at(q, self.g, zd, self.y)), False
 
@@ -248,7 +248,14 @@
         for i in range(self.parts):
             zs = flip(self.z, k)
             wait = remote(self.src(0, zs, i), self.dst(zs, i), self.send.at[0, i], self.recv.at[k, i], at(1 - self.p, self.g, self.z, self.y)).wait_recv
-            local = pltpu.make_async_copy(self.src(0, zs, i), self.dst(zs, i), self.own.at[i]).wait
+            def local():
+                if self.hold is None:
+                    pltpu.make_async_copy(self.src(0, zs, i), self.dst(zs, i), self.own.at[i]).wait()
+                else:
+                    pltpu.make_async_copy(self.src(0, zs, i), self.hold.at[i], self.own.at[i]).wait()
+                    out = pltpu.make_async_copy(self.hold.at[i], self.dst(zs, i), self.own.at[i])
+                    out.start()
+                    out.wait()
             if k:
                 wait()
             elif self.cores == 1:
@@ -265,8 +272,8 @@
                     copy.wait_send()
 
 
-def scatter_sems(parts):
-    return [pltpu.SemaphoreType.DMA((8, parts)), pltpu.SemaphoreType.DMA((4, parts)), pltpu.SemaphoreType.DMA((parts,))]
+def scatter_sems(parts, *hold):
+    return [pltpu.SemaphoreType.DMA((8, parts)), pltpu.SemaphoreType.DMA((4, parts)), pltpu.SemaphoreType.DMA((parts,))] + [pltpu.VMEM((parts,) + hold, F32)] * bool(hold)
 
 
 FIRST = 104
@@ -310,18 +317,15 @@
             pl.when(self.goes(t, way))(go)
 
     def arrive(self, t, then):
-        for way in range(2):
-            def come():
-                zz = self.block(t, way)
-                for i in range(self.parts):
+        for i in range(self.parts):
+            for way in range(2):
+                def come():
+                    zz = self.block(t, way)
                     remote(self.slot(zz, i), self.slot(zz, i), self.send.at[t - 1, way, i], self.recv.at[t - 1, way, i], at(1 - self.p, self.g, self.z, self.y)).wait_recv()
-                if t < 3:
-                    def go():
-                        for copy in self.copies(t, way):
-                            copy.start()
-                    pl.when(self.goes(t, way))(go)
-                then(2 * t - 1 + way, zz)
-            pl.when(self.there(t, way))(come)
+                    if t < 3:
+                        pl.when(self.goes(t, way))(self.copies(t, way)[i].start)
+                    then(2 * t - 1 + way, zz, i)
+                pl.when(self.there(t, way))(come)
 
     def each(self, do):
         do(0, self.z)
@@ -351,11 +355,8 @@
 
 
 def spread_plane(p, g, z, y, src, dst, send, recv):
-    places = [(g, y), (g, 1 - y), (1 - g, y), (1 - g, 1 - y)]
-    out = [pltpu.make_async_copy(src(*places[0]), dst(0), send.at[0])]
-    for m in range(1, 4):
-        out.append(remote(src(*places[m]), dst(m), send.at[m], recv.at[m], at(p, places[m][0], z, places[m][1])))
-    return out
+    places = [(g, 1 - y), (1 - g, y), (1 - g, 1 - y)]
+    return [remote(src(*to), dst(m), send.at[m], recv.at[m], at(p, to[0], z, to[1])) for m, to in enumerate(places)]
 ATOMS, ACTIONS, PAD = 51, 18, 56
 OUTS, OUTP = 969, 976
 STEPS = 7
@@ -375,7 +376,7 @@
 def hid_kernel(net, f_ref, m_ref, s_ref, nin_ref, nout_ref, hb_ref, wo_ref, bo_ref, c_ref, pl_ref, pw_ref, *rest):
     if net:
         f_all, h_ref, g_ref, logp_ref, dist_ref, f1a_ref, f1b_ref, f2_ref, acc, adv, fs, fr = rest[:12]
-        wires = f_scatter(f_all, f1a_ref, 0, rest[12:15]), f_scatter(f_all, f1b_ref, 1, rest[15:18])
+        wires = f_scatter(f_all, f1a_ref, 0, rest[12:16]), f_scatter(f_all, f1b_ref, 1, rest[16:20])
         fan = f_fan(f1a_ref, f2_ref, fs, fr)
         p, g, z, y = coords()
     else:
@@ -450,35 +451,46 @@
                   full(OUTP, 512), full(1, OUTP), full(1, 128), full(ATOMS, 128), full(ATOMS, 128)] + [ANY] * net,
         out_specs=[full(128, 1024), full(2, 4, 2, 2, 32, 128), full(PAD, 128), full(PAD, 128)] + [ANY, ANY, ANY] * net,
         out_shape=[sds(128, 1024), sds(2, 4, 2, 2, 32, 128), sds(PAD, 128), sds(PAD, 128)]
-        + [sds(2, 4, FIRST, 128), sds(2, 4, 200 - FIRST, 128), sds(4, 4, FIRST, 128)] * net,
-        scratch_shapes=[pltpu.VMEM((128, 1024), F32), pltpu.VMEM((OUTP, 128), F32)] + ([pltpu.SemaphoreType.DMA((4,))] * 2 + scatter_sems(2) * 2) * net,
+        + [sds(2, 4, FIRST, 128), sds(2, 4, 200 - FIRST, 128), sds(3, 4, FIRST, 128)] * net,
+        scratch_shapes=[pltpu.VMEM((128, 1024), F32), pltpu.VMEM((OUTP, 128), F32)] + ([pltpu.SemaphoreType.DMA((3,))] * 2 + scatter_sems(2, FIRST, 128) + scatter_sems(2, 200 - FIRST, 128)) * net,
         compiler_params=pltpu.CompilerParams(vmem_limit_bytes=60 * 2**20, **(dict(collective_id=1, has_side_effects=True) if net else {})),
     )(f, m, s, nin, nout, hb, wo, bo, c, plow, pw, *([f] * net))
 
 def hid_bwd_kernel(net, t_ref, logp_ref, h_ref, m_ref, s_ref, nin_ref, nout_ref, wo_ref, c_ref, *rest):
     if net:
+        noise, rest = list(zip(rest[2:6], rest[16:20])), rest[:2] + rest[6:16] + rest[20:]
         f1b_ref, hid_ref, df_ref, small_ref, f2b_ref, g1_ref, d1_ref, dz1_ref, g2_ref, d2_ref, dz2_ref, d3_ref = rest[:12]
         dth, dtl, da, msg, dz_to, t_got = rest[12:18]
         ds, dr, gs, gr, qs, qr, fs, fr, ts, tr, hs, hr, ss, sr, ps, pr, own = rest[18:35]
-        g_wire = g_scatter(hid_ref, g1_ref, rest[35:38])
-        z_wire = z_scatter(dz_to, dz1_ref, rest[38:41])
+        g_wire = g_scatter(hid_ref, g1_ref, rest[35:39])
+        z_wire = z_scatter(dz_to, dz1_ref, rest[39:42])
         p, g, z, y = coords()
-        d_line = Line(1, lambda i: d1_ref.at[z], lambda zz, i: d1_ref.at[zz], rest[41], rest[42])
+        d_line = Line(2, lambda i: d1_ref.at[z, i], lambda zz, i: d1_ref.at[zz, i], rest[42], rest[43])
         partner = at(1 - p, g, z, y)
         target = remote(t_ref, t_got, ts, tr, partner)
-        hand = remote(dz2_ref, dz2_ref, hs, hr, partner)
+        hands = [remote(dz2_ref, dz2_ref, hs.at[0], hr.at[0], partner), remote(dz1_ref, dz1_ref, hs.at[1], hr.at[1], partner)]
+        tells = [remote(src, dst, rest[44].at[i], rest[45].at[i], partner) for i, (src, dst) in enumerate(noise)]
         give = remote(msg.at[1], d1_ref.at[z], ps, pr, partner)
         keep = pltpu.make_async_copy(msg.at[0], d1_ref.at[z], own)
         fan_f = f_fan(f1b_ref, f2b_ref, fs, fr)
-        fan_g = spread_plane(p, g, z, y, lambda gd, yd: g1_ref.at[:, gd, yd], lambda m: g2_ref.at[m], gs, gr)
+        fan_g = spread_plane(p, g, z, y, lambda gd, yd: g1_ref.at[:, gd], lambda m: g2_ref.at[m], gs, gr)
         fan_z = spread_plane(p, g, z, y, lambda gd, yd: dz1_ref, lambda m: dz2_ref.at[m], qs, qr)
         def fan_d(place, zz):
             return spread_plane(p, g, z, y, lambda gd, yd: d1_ref.at[zz, yd], lambda m: d2_ref.at[m, zz], ds.at[place], dr.at[place])
+        def swap_own(place, zz):
+            return remote(d1_ref.at[zz, y], d3_ref.at[3, zz], ss.at[place, 0], sr.at[place, 0], partner)
         def swap(place, zz):
-            return remote(d2_ref.at[:, zz], d3_ref.at[:, zz], ss.at[place], sr.at[place], partner)
-        def forward(place, zz):
-            for copy in fan_d(place, zz):
-                copy.start()
+            return remote(d2_ref.at[:, zz], d3_ref.at[pl.ds(0, 3), zz], ss.at[place, 1], sr.at[place, 1], partner)
+        def forward(place, zz, s):
+            along_y, along_x, both = fan_d(place, zz)
+            @pl.when(y == s)
+            def _():
+                along_x.start()
+                swap_own(place, zz).start()
+            @pl.when(y != s)
+            def _():
+                both.start()
+                along_y.start()
         def forward_small():
             for k in range(4):
                 g_wire.arrived(k)
@@ -553,9 +565,12 @@
         def _():
             target.wait_recv()
             begin()
+            for copy in tells:
+                copy.start()
         pl.when(p == 1)(give.wait_recv)
         d_line.start(0)
-        forward(0, z)
+        for s in range(2):
+            forward(0, z, s)
     pl.when(p == 0)(step)
     pl.when(j == 3)(forward_small)
     @pl.when(j == pl.num_programs(0) - 1)
@@ -567,27 +582,31 @@
         def _():
             for copy in fan_z:
                 copy.wait()
-            hand.start()
+            for copy in hands:
+                copy.start()
         def landed(place, zz):
-            copies = fan_d(place, zz)
-            copies[0].wait()
-            for copy in copies[1:]:
+            for copy in fan_d(place, zz):
                 copy.wait_recv()
             swap(place, zz).start()
         d_line.each(landed)
         for copy in fan_f + fan_g:
             copy.wait()
         def gone(place, zz):
-            for copy in fan_d(place, zz)[1:]:
+            for copy in fan_d(place, zz):
                 copy.wait_send()
             swap(place, zz).wait()
+            swap_own(place, zz).wait()
         d_line.each(gone)
         d_line.sent()
         @pl.when(p == 0)
         def _():
             give.wait_send()
-            hand.wait_send()
-        pl.when(p == 1)(hand.wait_recv)
+            for copy in hands + tells:
+                copy.wait_send()
+        @pl.when(p == 1)
+        def _():
+            for copy in hands + tells:
+                copy.wait_recv()
         for wire in (g_wire, z_wire):
             wire.sent()
 
@@ -600,13 +619,13 @@
     return pl.pallas_call(
         functools.partial(hid_bwd_kernel, net), grid=(STEPS,),
         in_specs=[full(PAD, 128), full(PAD, 128), full(128, 1024), wspec, wspec, pl.BlockSpec((1, 2, k), lambda j: (j, 0, 0)), full(2, 512),
-                  full(OUTP, 512), full(1, 128)] + [ANY, ANY] * net,
-        out_specs=[pl.BlockSpec((k, 128), lambda j: (j, 0)), full(24, 128)] + ([ANY] * 8 if net else [full(2, 2, 256, 128), full(PAD, 128)]),
-        out_shape=[sds(3136, 128), sds(24, 128)] + ([sds(4, 4, 200 - FIRST, 128), sds(4, 2, 2, 32, 128), sds(4, 2, 256, 128), sds(4, PAD, 128), sds(4, 4, 32, 128), sds(4, 4, 256, 128),
-                                                     sds(4, 4, PAD, 128), sds(4, 4, 256, 128)] if net else [sds(2, 2, 256, 128), sds(PAD, 128)]),
+                  full(OUTP, 512), full(1, 128)] + [ANY] * (6 * net),
+        out_specs=[pl.BlockSpec((k, 128), lambda j: (j, 0)), full(24, 128)] + ([ANY] * 12 if net else [full(2, 2, 256, 128), full(PAD, 128)]),
+        out_shape=[sds(3136, 128), sds(24, 128)] + ([sds(3, 4, 200 - FIRST, 128), sds(4, 2, 2, 32, 128), sds(4, 2, 256, 128), sds(4, PAD, 128), sds(3, 4, 2, 32, 128), sds(3, 4, 256, 128),
+                                                     sds(3, 4, PAD, 128), sds(4, 4, 256, 128), sds(2, 3136), sds(2, 512), sds(2, 512), sds(1, OUTS)] if net else [sds(2, 2, 256, 128), sds(PAD, 128)]),
         scratch_shapes=[pltpu.VMEM((2, 512, 128), BF), pltpu.VMEM((2, 512, 128), BF), pltpu.VMEM((OUTP, 256), F32)]
-        + ([pltpu.VMEM((2, 2, 256, 128), F32), pltpu.VMEM((PAD, 128), F32), pltpu.VMEM((PAD, 128), F32), dma((7, 4)), dma((7, 4))] + [dma((4,))] * 6 + [dma] * 4 + [dma((7,)), dma((7,)), dma, dma, dma]
-           + scatter_sems(1) * 2 + line_sems(1)) * net,
+        + ([pltpu.VMEM((2, 2, 256, 128), F32), pltpu.VMEM((PAD, 128), F32), pltpu.VMEM((PAD, 128), F32), dma((7, 3)), dma((7, 3))] + [dma((3,))] * 6 + [dma, dma, dma((2,)), dma((2,)), dma((7, 2)), dma((7, 2)), dma, dma, dma]
+           + scatter_sems(1, 2, 2, 32, 128) + scatter_sems(1) + line_sems(2) + [dma((4,)), dma((4,))]) * net,
         compiler_params=pltpu.CompilerParams(vmem_limit_bytes=60 * 2**20, **(dict(collective_id=2, has_side_effects=True) if net else {})),
     )(t, logp, h, m, s, nin, nout, wo, c, *wired)
 
@@ -651,9 +670,9 @@
             return remote(red, tot.at[part(who)], bs.at[k], br.at[k], chip(who))
         hand = remote(tot, tot, cs, cr, at(1 - p, g, z, y))
         def head_at(ref, yy, zz):
-            return ref.at[pl.ds(yy, 1 + 7 * yy), pl.ds(pl.multiple_of(32 * zz, 8), 32)]
+            return ref.at[zz, pl.ds(5 * yy, 5 - yy)]
         def head_of(yy):
-            return q_ref.at[pl.ds(yy, 1 + 7 * yy)]
+            return q_ref.at[pl.ds(5 * yy, 5 - yy)]
         def slots(yy, zz):
             return ag_ref.at[yy, zz], head_at(ah_ref, yy, zz), bg_ref.at[yy, zz], head_at(bh_ref, yy, zz)
         def lines(yy):
@@ -678,13 +697,15 @@
             return (pltpu.make_async_copy(lob.at[slot], sg_ref.at[pl.ds(4 * j, 4)], ls.at[slot]),
                     remote(upb.at[slot], sg_ref.at[pl.ds(4 * j, 4)], us.at[slot], ur.at[j], at(1 - p, g, z, y)))
         def gather(yy):
-            def then(place, zz):
-                for copy in along_y(place, zz, yy) + bring(place, zz, yy):
-                    copy.start()
+            def then(place, zz, i):
+                along_y(place, zz, yy)[i].start()
+                if i >= 2:
+                    bring(place, zz, yy)[i - 2].start()
             for copy in give_own(yy):
                 copy.wait_recv()
             lines(yy).start(0)
-            then(0, z)
+            for i in range(4):
+                then(0, z, i)
             for copy in keep(yy):
                 copy.start()
             for t in range(1, 4):
@@ -827,12 +848,27 @@
             b.wait_send()
         else:
             b.wait()
-    def work(j, carry):
+    def wgrad1(j, carry):
         x_in(j).wait()
         v = xs[pl.ds(4 * j, 4)]
         hi = v.astype(BF)
         xh[:, 0:336, :] = hi
         xl[:, 0:336, :] = (v - hi.astype(F32)).astype(BF)
+        def lhs(ref):
+            return jnp.concatenate([jnp.concatenate([ref[j + 1 - h, 96 * i + 32:96 * i + 128, :] for i in range(7)], axis=1) for h in range(2)], axis=0)
+        def rhs(ref):
+            return jnp.concatenate([ref[:, 48 * i:48 * i + 64, :].reshape(256, 128) for i in range(7)], axis=1)
+        a1[...] += dot3((lhs(d1h), lhs(d1l)), (rhs(xh), rhs(xl)), NT)
+        return carry
+    def first_grad():
+        lax.fori_loop(0, 21, wgrad1, 0)
+        for h in range(2):
+            for ky in range(4):
+                grad = a1[96 * h:96 * h + 32, 64 * ky:64 * ky + 32]
+                grad = grad + a1[96 * h + 32:96 * h + 64, 64 * ky + 16:64 * ky + 48]
+                grad = grad + a1[96 * h + 64:96 * h + 96, 64 * ky + 32:64 * ky + 64]
+                pay[672 + 32 * h:704 + 32 * h, 32 * ky:32 * ky + 32] = grad
+    def dgrad1(j, carry):
         def both(ref):
             return jnp.concatenate([ref[pl.ds(j, 2), 96 * i:96 * i + 128, :].reshape(256, 128) for i in range(7)], axis=1)
         r = dot3((w1_ref[0], w1_ref[1]), (both(d1h), both(d1l)))
@@ -845,11 +881,6 @@
                 up_to[ky, 24 * i:24 * i + 24, :] = r[96 + 24 * ky:96 + 24 * ky + 24, 128 * i:128 * i + 128]
         for copy in states_out(j, slot):
             copy.start()
-        def lhs(ref):
-            return jnp.concatenate([jnp.concatenate([ref[j + 1 - h, 96 * i + 32:96 * i + 128, :] for i in range(7)], axis=1) for h in range(2)], axis=0)
-        def rhs(ref):
-            return jnp.concatenate([ref[:, 48 * i:48 * i + 64, :].reshape(256, 128) for i in range(7)], axis=1)
-        a1[...] += dot3((lhs(d1h), lhs(d1l)), (rhs(xh), rhs(xl)), NT)
         return carry
     if net:
         pl.when(p == 0)(fetch)
@@ -871,48 +902,25 @@
     xl[:, 336:, :] = jnp.zeros((4, 16, 128), BF)
     a1[...] = jnp.zeros_like(a1)
     if net:
-        pl.when(p == 0)(upper)
-        pl.when(p == 0)(lower)
         @pl.when(p == 0)
         def _():
+            upper()
+            lower()
+            first_grad()
             for k in range(chips):
                 give(k).start()
-    else:
-        fetch()
-        upper()
-        lower()
-    if net:
-        @pl.when(p == 0)
-        def _():
-            lax.fori_loop(0, 7, work, 0)
+            for k in range(1, chips):
+                show(k).start()
+            got1[me] = pay[672:736, :]
+            lax.fori_loop(0, 12, dgrad1, 0)
             give(0).wait()
-            for k in range(1, chips):
-                give(k).wait_send()
             for k in range(1, chips):
                 given(k).wait_recv()
             red[...] = jnp.sum(got[...], axis=0)
             tot[part(me), :] = red[...]
             for k in range(1, chips):
                 tell(k).start()
-            lax.fori_loop(7, 21, work, 0)
-    else:
-        lax.fori_loop(0, 21, work, 0)
-        for j in (last - 1, last):
-            states_gone(j, j % 2)
-    for h in range(2):
-        for ky in range(4):
-            grad = a1[96 * h:96 * h + 32, 64 * ky:64 * ky + 32]
-            grad = grad + a1[96 * h + 32:96 * h + 64, 64 * ky + 16:64 * ky + 48]
-            grad = grad + a1[96 * h + 64:96 * h + 96, 64 * ky + 32:64 * ky + 64]
-            pay[672 + 32 * h:704 + 32 * h, 32 * ky:32 * ky + 32] = grad
-    if net:
-        @pl.when(p == 0)
-        def _():
-            for k in range(1, chips):
-                show(k).start()
-            got1[me] = pay[672:736, :]
-        @pl.when(p == 0)
-        def _():
+            lax.fori_loop(12, 21, dgrad1, 0)
             for k in range(1, chips):
                 told(k).wait_recv()
             for k in range(1, chips):
@@ -920,11 +928,21 @@
             tot[672:736, :] = jnp.sum(got1[...], axis=0)
             hand.start()
             for k in range(1, chips):
+                give(k).wait_send()
                 tell(k).wait_send()
                 show(k).wait_send()
             hand.wait_send()
             for j in (last - 1, last):
                 states_gone(j, j % 2)
+    else:
+        fetch()
+        upper()
+        lower()
+        first_grad()
+        lax.fori_loop(0, 21, dgrad1, 0)
+        for j in (last - 1, last):
+            states_gone(j, j % 2)
+    if net:
         @pl.when(p == 1)
         def _():
             hand.wait_recv()
@@ -955,9 +973,9 @@
     dma = pltpu.SemaphoreType.DMA
     return pl.pallas_call(
         functools.partial(bwd_kernel, net),
-        in_specs=[ANY, ANY] + [VMEM] * 6 + [ANY, ANY, VMEM] * net,
+        in_specs=[ANY, ANY] + [VMEM] * 6 + [VMEM] * 3 * net,
         out_specs=[VMEM] + [ANY] * (5 if net else 2),
-        out_shape=[sds(ROWS, 128)] + ([sds(84, 168, 128)] + [sds(2, 4, 200, 512), sds(9, 128, 128)] * 2 if net else [sds(84, 168, 128), sds(84, 168, 128)]),
+        out_shape=[sds(ROWS, 128)] + ([sds(84, 168, 128)] + [sds(2, 4, 200, 512), sds(4, 9, 32, 128)] * 2 if net else [sds(84, 168, 128), sds(84, 168, 128)]),
         scratch_shapes=[f32(84, 336, 128), f32(20, 640, 128), vmb(4, 352, 128), vmb(4, 352, 128), f32(3136, 128), vmb(11, 768, 128), vmb(11, 768, 128), vmb(11, 704, 128),
                         vmb(11, 704, 128), vmb(22, 704, 128), vmb(22, 704, 128), vmb(9, 640, 128), vmb(9, 640, 128), f32(9, 640, 128), f32(192, 256), f32(128, 256),
                         f32(384, 256), f32(ROWS, 128), f32(2, 4, 168, 128), f32(2, 4, 168, 128), dma((21,)), dma, dma((2,)), dma((2,))]
@@ -966,47 +984,60 @@
         compiler_params=pltpu.CompilerParams(vmem_limit_bytes=62 * 2**20, **(dict(collective_id=3, has_side_effects=True) if net else {})),
     )(x, pre1, pre2, pre3, df, w1, w2, w3, *wired)
 
-def wide_kernel(fa_ref, fb_ref, d_ref, e_ref, g_ref, z_ref, r_ref, q_ref, acc, acq, da):
-    m = pl.program_id(0)
-    p = lax.axis_index("pair")
-    @pl.when(m == 0)
-    def _():
-        acc[...] = jnp.zeros_like(acc)
-        acq[...] = jnp.zeros_like(acq)
-        da[...] = jnp.zeros_like(da)
-    f = split(jnp.concatenate([jnp.concatenate([fa_ref[0, i], fb_ref[0, i]], axis=0) for i in range(4)], axis=1))
-    def block(ref):
-        return jnp.concatenate([jnp.concatenate([ref[0, i, 128 * c:128 * c + 128, :] for c in range(2)], axis=1) for i in range(4)], axis=0)
-    acc[0] += dot3(f, split(block(d_ref)))
-    acc[1] += dot3(f, split(block(e_ref)))
-    dz = jnp.concatenate([z_ref[0, i] for i in range(4)], axis=1)
-    row = lax.broadcasted_iota(jnp.int32, (PAD, 512), 0)
-    chosen = dz[ATOMS:ATOMS + 1].astype(jnp.int32)
-    d = jnp.where(row < ATOMS, dz, 0.0)
-    da[0:PAD, :] = d
-    for i in range(ACTIONS):
-        da[128 + ATOMS * i:128 + ATOMS * i + PAD, :] = mask_of(chosen, i) * d
-    g = split(jnp.concatenate([g_ref[0, i] for i in range(4)], axis=1))
-    acq[...] += dot3(g, split(da[...]), NT)
-    @pl.when(m == 3)
-    def _():
-        r_ref[:, 0:256] = jnp.where(p == 0, acc[0], acc[1])
-        r_ref[:, 256:512] = jnp.where(p == 0, acc[1], acc[0])
-        for c in range(9):
-            q_ref[c] = acq[:, 128 * c:128 * c + 128]
-
-def wide_grads(f2a, f2b, d2, d3, g2, z2):
-    full = lambda *s: pl.BlockSpec(s, lambda j: (0,) * len(s))
-    part = lambda n: pl.BlockSpec((1, 4, n, 128), lambda j: (j, 0, 0, 0))
+def wide_kernel(f1a, f1b, f2a, f2b, d1, d2, d3, g1, g2, z1, z2, r_ref, q_ref, fv, dv, ev, gv, zv, acc, acq, da, sem):
+    p, g = lax.axis_index("pair"), lax.axis_index("group")
+    y = lax.axis_index("rep") % 2
+    three, last = pl.ds(0, 3), 3
+    head, tail = pl.ds(0, FIRST), pl.ds(FIRST, 200 - FIRST)
+    pairs = [(f2a, fv.at[three, :, head]), (f1a.at[g], fv.at[last, :, head]), (f2b, fv.at[three, :, tail]), (f1b.at[g], fv.at[last, :, tail]),
+             (d2, dv.at[three]), (d1.at[:, y], dv.at[last]), (d3, ev), (g2, gv.at[three]), (g1.at[:, g], gv.at[last]), (z2, zv.at[three]), (z1, zv.at[last])]
+    copies = [pltpu.make_async_copy(a, b, sem.at[i]) for i, (a, b) in enumerate(pairs)]
+    for copy in copies:
+        copy.start()
+    acc[...] = jnp.zeros_like(acc)
+    acq[...] = jnp.zeros_like(acq)
+    da[...] = jnp.zeros_like(da)
+    for copy in copies:
+        copy.wait()
+    def block(ref, m):
+        return jnp.concatenate([jnp.concatenate([ref[m, i, 128 * c:128 * c + 128, :] for c in range(2)], axis=1) for i in range(4)], axis=0)
+    def step(m, carry):
+        f = split(jnp.concatenate([fv[m, i] for i in range(4)], axis=1))
+        acc[0] += dot3(f, split(block(dv, m)))
+        acc[1] += dot3(f, split(block(ev, m)))
+        dz = jnp.concatenate([zv[m, i] for i in range(4)], axis=1)
+        row = lax.broadcasted_iota(jnp.int32, (PAD, 512), 0)
+        chosen = dz[ATOMS:ATOMS + 1].astype(jnp.int32)
+        d = jnp.where(row < ATOMS, dz, 0.0)
+        da[0:PAD, :] = d
+        for i in range(ACTIONS):
+            da[128 + ATOMS * i:128 + ATOMS * i + PAD, :] = mask_of(chosen, i) * d
+        def units(s):
+            return split(jnp.concatenate([gv[m, i, s] for i in range(4)], axis=1))
+        @pl.when(y == 0)
+        def _():
+            acq[:, 0:128] += dot3(units(0), split(da[0:128, :]), NT)
+            acq[:, 128:640] += dot3(units(1), split(da[128:640, :]), NT)
+        @pl.when(y == 1)
+        def _():
+            acq[:, 640:1152] += dot3(units(1), split(da[640:1152, :]), NT)
+        return carry
+    lax.fori_loop(0, 4, step, 0)
+    r_ref[:, 0:256] = jnp.where(p == 0, acc[0], acc[1])
+    r_ref[:, 256:512] = jnp.where(p == 0, acc[1], acc[0])
+    for c in range(9):
+        q_ref[c] = acq[:, 128 * c:128 * c + 128]
+
+def wide_grads(*messages):
     sds = lambda *s: jax.ShapeDtypeStruct(s, F32)
+    f32 = lambda *s: pltpu.VMEM(s, F32)
     return pl.pallas_call(
-        wide_kernel, grid=(4,),
-        in_specs=[part(FIRST), part(200 - FIRST), part(256), part(256), part(32), part(PAD)],
-        out_specs=[full(200, 512), full(9, 32, 128)],
+        wide_kernel, in_specs=[ANY] * 11, out_specs=[VMEM] * 2,
         out_shape=[sds(200, 512), sds(9, 32, 128)],
-        scratch_shapes=[pltpu.VMEM((2, 200, 256), F32), pltpu.VMEM((32, 1152), F32), pltpu.VMEM((1152, 512), F32)],
+        scratch_shapes=[f32(4, 4, 200, 128), f32(4, 4, 256, 128), f32(4, 4, 256, 128), f32(4, 4, 2, 32, 128), f32(4, 4, PAD, 128),
+                        f32(2, 200, 256), f32(32, 1152), f32(1152, 512), pltpu.SemaphoreType.DMA((11,))],
         compiler_params=pltpu.CompilerParams(vmem_limit_bytes=60 * 2**20),
-    )(f2a, f2b, d2, d3, g2, z2)
+    )(*messages)
 
 def torso_out(tot, k1_ref, k2_ref, k3_ref, b1_ref, b2_ref, b3_ref, t1, t2):
     t1[:, 0:64] = jnp.transpose(tot[672:736, :])
@@ -1029,8 +1060,16 @@
     b2_ref[...] = tot[665:666, 0:64]
     b1_ref[...] = tot[666:667, 0:32]
 
-def finish_kernel(ag_ref, ah_ref, tot_ref, in_ref, out_ref, ein_ref, eout_ref, mean_ref, sigma_ref, hm_ref, hs_ref, k1_ref, k2_ref, k3_ref, b1_ref, b2_ref, b3_ref,
-                  hb_ref, hbs_ref, bo_ref, bos_ref, loss_ref, t1, t2):
+def finish_kernel(sg_ref, ag_ref, ah_ref, tot_ref, in_ref, out_ref, ein_ref, eout_ref, mean_ref, sigma_ref, hm_ref, hs_ref, k1_ref, k2_ref, k3_ref, b1_ref, b2_ref, b3_ref,
+                  hb_ref, hbs_ref, bo_ref, bos_ref, loss_ref, states_ref, t1, t2, sv, sem):
+    parts = [pl.ds(21 * i, 21) for i in range(4)]
+    reads = [pltpu.make_async_copy(sg_ref.at[part], sv.at[part], sem.at[0, i]) for i, part in enumerate(parts)]
+    moves = [pltpu.make_async_copy(sv.at[part], states_ref.at[part], sem.at[1, i]) for i, part in enumerate(parts)]
+    for copy in reads:
+        copy.start()
+    for i in range(4):
+        reads[i].wait()
+        moves[i].start()
     for s in range(2):
         tall = column(in_ref[s:s + 1, :], 512) * out_ref[s:s + 1, :]
         for z, (start, n) in enumerate(((0, 200), (200, 200), (400, 184), (584, 200))):
@@ -1041,7 +1080,7 @@
     for c in range(9):
         start = 0 if c == 0 else ATOMS + 128 * (c - 1)
         n = min(128, (ATOMS if c == 0 else OUTS) - start)
-        v = jnp.transpose(ah_ref[c])[0:n]
+        v = jnp.transpose(jnp.concatenate([ah_ref[z, c] for z in range(4)], axis=0))[0:n]
         hm_ref[start:start + n, :] = v
         hs_ref[start:start + n, :] = v * (noise[start:start + n] * ein_ref[min(c, 1):min(c, 1) + 1, :])
     torso_out(tot_ref, k1_ref, k2_ref, k3_ref, b1_ref, b2_ref, b3_ref, t1, t2)
@@ -1056,16 +1095,18 @@
         bo_ref[:, 128 * c:128 * c + n] = v
         bos_ref[:, 128 * c:128 * c + n] = v * eout_ref[:, 128 * c:128 * c + n]
     loss_ref[...] = tot_ref[16:17, :]
-
-def finish(ag, ah, tot, n_in, n_out, e_in, e_out):
+    for copy in moves:
+        copy.wait()
+
+def finish(sg, ag, ah, tot, n_in, n_out, e_in, e_out):
     sds = lambda *s: jax.ShapeDtypeStruct(s, F32)
     return pl.pallas_call(
-        finish_kernel, in_specs=[VMEM] * 7, out_specs=[VMEM] * 15,
+        finish_kernel, in_specs=[ANY] + [VMEM] * 7, out_specs=[VMEM] * 15 + [ANY],
         out_shape=[sds(2, 784, 512), sds(2, 784, 512), sds(OUTS, 128), sds(OUTS, 128), sds(4, 8, 8, 32), sds(32, 4, 4, 64), sds(3, 3, 64, 64), sds(1, 32), sds(1, 64), sds(1, 64),
-                   sds(2, 512), sds(2, 512), sds(1, OUTS), sds(1, OUTS), sds(1, 128)],
-        scratch_shapes=[pltpu.VMEM((128, 128), F32), pltpu.VMEM((128, 128), F32)],
+                   sds(2, 512), sds(2, 512), sds(1, OUTS), sds(1, OUTS), sds(1, 128), sds(84, 168, 128)],
+        scratch_shapes=[pltpu.VMEM((128, 128), F32), pltpu.VMEM((128, 128), F32), pltpu.VMEM((84, 168, 128), F32), pltpu.SemaphoreType.DMA((2, 4))],
         compiler_params=pltpu.CompilerParams(vmem_limit_bytes=60 * 2**20),
-    )(ag, ah, tot, n_in, n_out, e_in, e_out)
+    )(sg, ag, ah, tot, n_in, n_out, e_in, e_out)
 
 def small_finish_kernel(tot_ref, k1_ref, k2_ref, k3_ref, b1_ref, b2_ref, b3_ref, t1, t2):
     torso_out(tot_ref, k1_ref, k2_ref, k3_ref, b1_ref, b2_ref, b3_ref, t1, t2)
@@ -1077,10 +1118,6 @@
         out_shape=[sds(4, 8, 8, 32), sds(32, 4, 4, 64), sds(3, 3, 64, 64), sds(1, 32), sds(1, 64), sds(1, 64)],
         scratch_shapes=[pltpu.VMEM((128, 128), F32), pltpu.VMEM((128, 128), F32)],
     )(tot)
-
-def online_only(value):
-    other = lax.ppermute(value, "pair", [(0, 1)])
-    return jnp.where(lax.axis_index("pair") == 0, value, other)
 
 def exchange(parts):
     groups = lax.axis_size("group")
@@ -1105,15 +1142,12 @@
     shards = 2 * groups
     net = int(groups == 2 and lax.axis_size("rep") == 8)
     n_in, n_out, e_in, e_out = hidden_noise_in[0], hidden_noise_out[0], head_noise_in[0], head_noise_out[0]
-    noise = online_only(jnp.concatenate([v.reshape(-1) for v in (n_in, n_out, e_in, e_out)]))
-    on_in = noise[:6272].reshape(2, 3136)
-    on_out = noise[6272:7296].reshape(2, 512)
-    on_ein = noise[7296:8320].reshape(2, 512)
-    on_eout = noise[8320:]
+    own_noise = (n_in, n_out, e_in, e_out[None])
+    feat_q, hid_q = 3136 // shards, 512 // shards
     shard = pair * groups + lax.axis_index("group")
-    feat_q, hid_q = 3136 // shards, 512 // shards
-    in_q = lax.dynamic_slice_in_dim(on_in, shard * feat_q, feat_q, axis=1)
-    e_q = lax.dynamic_slice_in_dim(on_ein, shard * hid_q, hid_q, axis=1)
+    def of_shard(noise):
+        on_in, on_out, on_ein, on_eout = (jnp.where(pair == 0, mine, other) for mine, other in zip(own_noise, noise))
+        return (lax.dynamic_slice_in_dim(on_in, shard * feat_q, feat_q, axis=1), on_out, lax.dynamic_slice_in_dim(on_ein, shard * hid_q, hid_q, axis=1), on_eout)
 
     x = jnp.transpose(states[0], (2, 3, 1, 0)).reshape(84, 336, 128)
     fw1, fw2, fw3, bw1, bw2, bw3, c1, c2, c3 = prepare(first_kernel[0], second_kernel[0], third_kernel[0], first_bias, second_bias, third_bias)
@@ -1127,11 +1161,11 @@
     h, hid, logp, dist, *f12 = hidden(net, feats, hidden_mean[0], hidden_sigma[0], nin, n_out, hb, wo, bo, actions, proj_lower.T, proj_weight.T)
     back = (logp, h, hidden_mean[0], hidden_sigma[0], nin, n_out, wo, actions)
     if net:
-        df, small_b, f2b, _, _, _, g2, d2, z2, d3 = hidden_bwd(net, dist, *back, f12[1], hid)
-        part_r, part_q = wide_grads(f12[2], f2b, d2, d3, g2, z2)
+        df, small_b, f2b, g1, d1, z1, g2, d2, z2, d3, *noise = hidden_bwd(net, dist, *back, f12[1], hid, *own_noise)
+        part_r, part_q = wide_grads(f12[0], f12[1], f12[2], f2b, d1, d2, d3, g1, g2, z1, z2)
         total, grad_rows, ag, ah, _, _ = backward(net, x, pre1, pre2, pre3, df, bw1, bw2, bw3, part_r, part_q, small_b)
         (hidden_grad, hidden_sigma_grad, head_t, head_sigma_t, gk1, gk2, gk3, gb1, gb2, gb3, hb_grad, hbs_grad, bo_grad, bos_grad,
-         loss) = finish(ag, ah, total, in_q, on_out, e_q, on_eout[None])
+         loss, grad_rows) = finish(grad_rows, ag, ah, total, *of_shard(noise))
     else:
         df, small_b, msg, dz = hidden_bwd(net, lax.ppermute(dist, "pair", [(1, 0)]), *back)
         f_got = exchange(lambda p, g: lax.dynamic_slice_in_dim(feats, (p * groups + g) * feat_q, feat_q, axis=0))
@@ -1151,8 +1185,9 @@
         small_d, lo, up = backward(net, x, pre1, pre2, pre3, df, bw1, bw2, bw3)
         grad_rows = jnp.where(pair == 0, lo, lax.ppermute(up, "pair", [(0, 1)]))
         total = lax.psum(small_d + jnp.pad(small_b, ((0, ROWS - 24), (0, 0))), ("pair", "group", "rep"))
+        in_q, on_out, e_q, on_eout = of_shard(lax.ppermute(own_noise, "pair", [(0, 1)]))
         hidden_sigma_grad = hidden_grad * (in_q[:, :, None] * on_out[:, None, :])
-        head_sigma_t = head_t * (jnp.where(jnp.arange(OUTS)[:, None] < ATOMS, e_q[0:1], e_q[1:2]) * on_eout[:, None])
+        head_sigma_t = head_t * (jnp.where(jnp.arange(OUTS)[:, None] < ATOMS, e_q[0:1], e_q[1:2]) * on_eout.T)
         gk1, gk2, gk3, gb1, gb2, gb3 = small_finish(total)
         hb_grad = total[0:8].reshape(2, 512)
         bo_grad = total[8:16].reshape(1, -1)[:, :OUTS]

time: 222 us -> 209 us (0.941)
  local copies, waits for them, and re-layouts: 15.4 us -> 4.88 us
  other arithmetic: 4 us -> 7.8 us
  Pallas kernels: 198 us -> 195 us
  starting transfers between devices: 2.35 us -> 0 us
    pallas_call x1, Pallas kernels: 77 us -> 63.1 us  [backward(): pl.pallas_call(functools.partial(bwd_kernel, net), in_specs=[ANY, ANY] +...]
    unnamed x12 -> x9, local copies, waits for them, and re-layouts: 8.52 us -> 0.62 us
    pallas_call x2, Pallas kernels: 14.7 us -> 21.2 us  [the longest x1 11.5 us: finish(): pl.pallas_call(finish_kernel, in_specs=[ANY] + [VMEM] * 7, out_specs=[VME...]
    select_n x1 -> x4, other arithmetic: 0.01 us -> 3.83 us  [of_shard(): jnp.where(pair == 0, mine, other)]
    pallas_call x1, Pallas kernels: 48.7 us -> 51.4 us  [hidden_bwd(): pl.pallas_call(functools.partial(hid_bwd_kernel, net), grid=(STEPS,), in_...]
    ppermute x1 -> x0, starting transfers between devices: 2.35 us -> none  [online_only(): other = lax.ppermute(value, 'pair', [(0, 1)])]
  transfers between devices with their start and end apart: 1 -> 0, of which waited for: 0 -> 0; matrix products, arithmetic and copies ran while one was open for 3% -> 0% of each run, Pallas kernels for 87% -> 0%
where the time goes in v5:
time: 209 us; the launch traced here: 208 us
  Pallas kernels  195 us (93%)
  other arithmetic  7.8 us (4%)
  local copies, waits for them, and re-layouts  4.88 us (2%)
    pallas_call x1, Pallas kernels, backward(): pl.pallas_call(functools.partial(bwd_kernel, net), in_specs=[ANY, ANY] +...  63.1 us
    pallas_call x1, Pallas kernels, hidden_bwd(): pl.pallas_call(functools.partial(hid_bwd_kernel, net), grid=(STEPS,), in_...  51.4 us
    pallas_call x1, Pallas kernels, hidden(): pl.pallas_call(functools.partial(hid_kernel, net), grid=(STEPS,), in_spec...  31.5 us
    pallas_call x1, Pallas kernels, forward(): pl.pallas_call(fwd_kernel, in_specs=[hbm] + [vm] * 6, out_specs=[hbm, hbm...  24.7 us
    pallas_call x1, Pallas kernels, finish(): pl.pallas_call(finish_kernel, in_specs=[ANY] + [VMEM] * 7, out_specs=[VME...  11.5 us
    pallas_call x1, Pallas kernels, wide_grads(): pl.pallas_call(wide_kernel, in_specs=[ANY] * 11, out_specs=[VMEM] * 2, ou...  9.68 us

profile of v5, /device:TPU:0, one launch (start us, length us, event | category | flops | bytes accessed | tf_op | source)
XLA Modules:
  0.0 208.3 jit_solution(5664088194203546510)
XLA Ops:
  0.7 0.7 add_bitcast_fusion
  1.4 0.6 copy.41
  2.0 0.7 multiply_add_fusion
  2.7 0.6 pad.9.bo_ref
  3.3 0.8 fusion.1
  4.1 0.8 reshape_squeeze.3
  4.9 0.6 copy.45
  5.5 2.8 %shard_map.333 = (bf16[2,192,256]{2,1,0:T(8,128)(2,1)}, bf16[2,128,256]{2,1,0:T(8,128)(2,1)}, bf16[2,384,256]{2,1,0:T(8,128)(2,1)}, bf16[2,192,256]{2,1,0:T(8,12...) custom-call(f32[4,8,8,32]{3,2,1,0:T(8,128)} %bitcast.68, ...), custom_call_target="tpu_custom_call" | custom-call | tf_op jit(solution)/shard_map/pallas_call | solution.py:82
  8.4 2.5 %fusion = f32[969,512]{1,0:T(8,128)S(1)} fusion(f32[1,512,969]{1,0,2:T(1,128)} %param.38, f32[1,512,969]{1,0,2:T(1,128)} %param.37, f32[969]{0:T(1024)} %bitcast.72, f32[512]{0:T(512)S(1)} %bitcast.79, f32[512]{0:T(512)S(1)} %bitcast.78, pred[969]{0:T(1024)(128)(4,1)S(1)} %iota_compare_fusion), kind=kLoop, calls=%fused_computation.1 | loop fusion | flops 1984512 | bytes 5962477 | tf_op jit(solution)/shard_map/add | solution.py:1156
  10.9 1.4 pad.8.wo_ref
  12.3 24.7 %shard_map.334 = (f32[20,640,128]{2,1,0:T(8,128)}, f32[9,576,128]{2,1,0:T(8,128)}, f32[3136,128]{1,0:T(8,128)}, f32[3136,128]{1,0:T(8,128)}) custom-call(f32[84,336,128]{2,1,0:T(8,128)} %bitcast.56, bf16[2,192,256]{2,1,0:T(8,128)(2,1)} %get-tuple-element.72.w1_ref, bf16[2,128,256]{2,1,0:T(8,128)(2,1)} %get-tuple-element.73.w2_ref, ...), custom_call_target="tpu_custom_call" | custom-call | tf_op jit(solution)/shard_map/pallas_call | solution.py:173
  37.1 31.5 %shard_map.335 = (f32[128,1024]{1,0:T(8,128)}, f32[2,4,2,2,32,128]{5,4,3,2,1,0:T(8,128)}, f32[56,128]{1,0:T(8,128)}, f32[56,128]{1,0:T(8,128)}, f32[2,4,104,128]...) custom-call(f32[3136,128]{1,0:T(8,128)} %get-tuple-element.81.f_ref.rest_0_, ...), custom_call_target="tpu_custom_call" | custom-call | tf_op jit(solution)/shard_map/pallas_call | solution.py:448
  68.5 51.4 %shard_map.336 = (f32[3136,128]{1,0:T(8,128)}, f32[24,128]{1,0:T(8,128)}, f32[3,4,96,128]{3,2,1,0:T(8,128)}, f32[4,2,2,32,128]{4,3,2,1,0:T(8,128)}, f32[4,2,256,...) custom-call(f32[56,128]{1,0:T(8,128)} %get-tuple-element.82.t_ref, ...), custom_call_target="tpu_custom_call" | custom-call | tf_op jit(solution)/shard_map/pallas_call | solution.py:619
  120.0 0.0 copy-start
  120.0 0.0 copy-start.3
  120.0 0.0 copy-start.1
  120.0 0.0 copy-start.2
  120.0 9.7 %shard_map.337 = (f32[200,512]{1,0:T(8,128)}, f32[9,32,128]{2,1,0:T(8,128)}) custom-call(f32[2,4,104,128]{3,2,1,0:T(8,128)} %get-tuple-element.91.f1a, f32[2,4,96,128]{3,2,1,0:T(8,128)} %get-tuple-element.85.rest_0_.f1b, f32[3,4,104,128]{3,2,1,0:T(8,128)} %get-tuple-element.92.f2a, f32[3,4,96,128]{3,2,1,0:T(8,128)} %get-tuple-element.93.f2b, ...), custom_call_target="tpu_custom_call" | custom-call | tf_op jit(solution)/shard_map/pallas_call | solution.py:1034
  129.7 1.2 dynamic-slice_select_fusion.1.ein_ref
  130.9 0.0 copy-done
  130.9 0.0 copy-done.3
  130.9 0.6 broadcast_select_fusion.1.out_ref
  131.5 0.0 copy-done.1
  131.5 0.0 copy-done.2
  131.5 0.6 broadcast_select_fusion.eout_ref
  132.1 1.4 dynamic-slice_select_fusion.in_ref
  133.5 63.1 %shard_map.338 = (f32[768,128]{1,0:T(8,128)}, f32[84,168,128]{2,1,0:T(8,128)}, f32[2,4,200,512]{3,2,1,0:T(8,128)}, f32[4,9,32,128]{3,2,1,0:T(8,128)}, f32[2,4,20...) custom-call(f32[84,336,128]{2,1,0:T(8,128)} %bitcast.57, f32[20,640,128]{2,1,0:T(8,128)} %get-tuple-element.78.pre1_hbm, ...), custom_call_target="tpu_custom_call" | custom-call | tf_op jit(solution)/shard_map/pallas_call | solution.py:974
  196.6 11.5 %shard_map.339 = (f32[2,784,512]{2,1,0:T(8,128)}, f32[2,784,512]{2,1,0:T(8,128)}, f32[969,128]{1,0:T(8,128)}, f32[969,128]{1,0:T(8,128)}, f32[4,8,8,32]{3,2,1,0:...) custom-call(f32[84,168,128]{2,1,0:T(8,128)} %get-tuple-element.104.s, ...), custom_call_target="tpu_custom_call" | custom-call | tf_op jit(solution)/shard_map/pallas_call | solution.py:1103
  (1 shorter events, 0.0 us)
Async XLA Ops:
  120.0 11.0 %copy-start = (f32[1,2,512]{2,1,0:T(2,128)S(1)}, f32[1,2,512]{2,1,0:T(2,128)}, u32[]{:S(2)}) copy-start(f32[1,2,512]{2,1,0:T(2,128)} %param.42) | copy-start | bytes 12292
  120.0 11.0 %copy-start.3 = (f32[2,512]{1,0:T(2,128)S(1)}, f32[2,512]{1,0:T(2,128)}, u32[]{:S(2)}) copy-start(f32[2,512]{1,0:T(2,128)} %get-tuple-element.109) | copy-start | bytes 12292
  120.0 11.6 %copy-start.1 = (f32[1,969]{1,0:T(1,128)S(1)}, f32[1,969]{1,0:T(1,128)}, u32[]{:S(2)}) copy-start(f32[1,969]{1,0:T(1,128)} %rest_5_.1) | copy-start | bytes 11632
  120.0 11.5 %copy-start.2 = (f32[1,969]{1,0:T(1,128)S(1)}, f32[1,969]{1,0:T(1,128)}, u32[]{:S(2)}) copy-start(f32[1,969]{1,0:T(1,128)} %get-tuple-element.111) | copy-start | bytes 11632

commit v6 on v5

--- a/solution.py
+++ b/solution.py
@@ -276,11 +276,11 @@
     return [pltpu.SemaphoreType.DMA((8, parts)), pltpu.SemaphoreType.DMA((4, parts)), pltpu.SemaphoreType.DMA((parts,))] + [pltpu.VMEM((parts,) + hold, F32)] * bool(hold)
 
 
-FIRST = 104
-
-
-def f_scatter(f_ref, f1_ref, half, sems):
-    start, rows = (0, FIRST) if half == 0 else (FIRST, 200 - FIRST)
+PIECES = ((0, 72), (72, 72), (144, 56))
+
+
+def f_scatter(f_ref, f1_ref, piece, sems):
+    start, rows = PIECES[piece]
     def src(q, zd, i):
         return f_ref.at[pl.ds(pl.multiple_of((2 * q + i) * 784 + jnp.minimum(200 * zd, 584) + start, 8), rows)]
     return Scatter(2, src, lambda z, i: f1_ref.at[i, z], *sems)
@@ -373,12 +373,22 @@
 def mask_of(chosen, a):
     return jnp.where(chosen == a, 1.0 - 1.0 / ACTIONS, -1.0 / ACTIONS)
 
-def hid_kernel(net, f_ref, m_ref, s_ref, nin_ref, nout_ref, hb_ref, wo_ref, bo_ref, c_ref, pl_ref, pw_ref, *rest):
+def hid_kernel(net, f_ref, m_ref, s_ref, nin_ref, nout_ref, hm_ref, hs_ref, wo_ref, bm_ref, bs_ref, eout_ref, c_ref, pl_ref, pw_ref, *rest):
     if net:
-        f_all, h_ref, g_ref, logp_ref, dist_ref, f1a_ref, f1b_ref, f2_ref, acc, adv, fs, fr = rest[:12]
-        wires = f_scatter(f_all, f1a_ref, 0, rest[12:16]), f_scatter(f_all, f1b_ref, 1, rest[16:20])
-        fan = f_fan(f1a_ref, f2_ref, fs, fr)
+        f_all, h_ref, g_ref, logp_ref, dist_ref, t_ref = rest[:6]
+        f1_refs, f2_refs = rest[6:9], rest[9:11]
+        acc, adv, ts, tr, fs0, fr0, fs1, fr1 = rest[11:19]
+        wires = [f_scatter(f_all, f1_refs[i], i, rest[19 + 4 * i:23 + 4 * i]) for i in range(3)]
+        fans = [f_fan(f1_refs[0], f2_refs[0], fs0, fr0), f_fan(f1_refs[1], f2_refs[1], fs1, fr1)]
         p, g, z, y = coords()
+        target = remote(dist_ref, t_ref, ts, tr, at(1 - p, g, z, y))
+        def next_piece(i):
+            wires[i].sent()
+            wires[i + 1].start()
+            for k in range(4):
+                wires[i].arrived(k)
+            for copy in fans[i]:
+                copy.start()
     else:
         h_ref, g_ref, logp_ref, dist_ref, acc, adv = rest
     j = pl.program_id(0)
@@ -389,21 +399,16 @@
             wires[0].start()
         acc[...] = jnp.zeros_like(acc)
     if net:
-        @pl.when(j == 4)
-        def _():
-            wires[0].sent()
-            wires[1].start()
-            for k in range(4):
-                wires[0].arrived(k)
-            for copy in fan:
-                copy.start()
+        pl.when(j == 4)(lambda: next_piece(0))
+        pl.when(j == 6)(lambda: next_piece(1))
     f = split(f_ref[...])
     for s in range(2):
         w = split(noisy(m_ref, s_ref, nin_ref, nout_ref, s))
         acc[:, 512 * s:512 * s + 512] += dot3(f, w, TN)
     @pl.when(j == pl.num_programs(0) - 1)
     def _():
-        h = acc[...] + hb_ref[...]
+        hb = hm_ref[...] + hs_ref[...] * nout_ref[...]
+        h = jnp.concatenate([acc[:, 0:512] + hb[0:1], acc[:, 512:1024] + hb[1:2]], axis=1)
         h_ref[...] = h
         gt = jnp.transpose(silu(h))
         for s in range(2):
@@ -413,7 +418,7 @@
                         at_row = 512 * s + 256 * q + 128 * gg + 32 * z
                         g_ref[q, z, gg, s] = gt[at_row:at_row + 32]
         both = dot3(split(wo_ref[...]), split(jnp.concatenate([gt[:512], gt[512:]], axis=1)))
-        bias = column(bo_ref[...], 128)
+        bias = column(jnp.concatenate([bm_ref[...] + bs_ref[...] * eout_ref[...], jnp.zeros((1, OUTP - OUTS), F32)], axis=1), 128)
         adv[...] = both[:, 128:] + bias
         z = both[0:PAD, 0:128] + bias[0:PAD]
         chosen = c_ref[...]
@@ -425,51 +430,55 @@
         e = jnp.exp(z - top)
         tot = jnp.sum(e, axis=0, keepdims=True)
         logp_ref[...] = (z - top) - jnp.log(tot)
-        p = e / tot
+        prob = e / tot
         dist = jnp.zeros((PAD, 128), F32)
         for i in range(ATOMS):
             lower = pl_ref[i:i + 1, :]
             share = pw_ref[i:i + 1, :]
-            pi = p[i:i + 1, :]
+            pi = prob[i:i + 1, :]
             dist = dist + jnp.where(row == lower, pi * (1.0 - share), 0.0) + jnp.where(row == lower + 1, pi * share, 0.0)
         dist_ref[...] = dist
         if net:
+            pl.when(p == 1)(target.start)
             for k in range(4):
-                wires[1].arrived(k)
-            wires[1].sent()
-            for copy in fan:
+                wires[2].arrived(k)
+            wires[2].sent()
+            for copy in fans[0] + fans[1]:
                 copy.wait()
-
-def hidden(net, f, m, s, nin, nout, hb, wo, bo, c, plow, pw):
+            pl.when(p == 1)(target.wait_send)
+            pl.when(p == 0)(target.wait_recv)
+
+def hidden(net, f, m, s, nin, nout, hm, hs, wo, bm, bs, eout, c, plow, pw):
     full = lambda *t: pl.BlockSpec(t, lambda j: (0,) * len(t))
     sds = lambda *t: jax.ShapeDtypeStruct(t, F32)
     k = 3136 // STEPS
     wspec = pl.BlockSpec((2, k, 512), lambda j: (0, j, 0))
     return pl.pallas_call(
         functools.partial(hid_kernel, net), grid=(STEPS,),
-        in_specs=[pl.BlockSpec((k, 128), lambda j: (j, 0)), wspec, wspec, pl.BlockSpec((1, 2, k), lambda j: (j, 0, 0)), full(2, 512), full(1, 1024),
-                  full(OUTP, 512), full(1, OUTP), full(1, 128), full(ATOMS, 128), full(ATOMS, 128)] + [ANY] * net,
-        out_specs=[full(128, 1024), full(2, 4, 2, 2, 32, 128), full(PAD, 128), full(PAD, 128)] + [ANY, ANY, ANY] * net,
+        in_specs=[pl.BlockSpec((k, 128), lambda j: (j, 0)), wspec, wspec, pl.BlockSpec((1, 2, k), lambda j: (j, 0, 0)), full(2, 512), full(2, 512), full(2, 512),
+                  full(OUTP, 512), full(1, OUTS), full(1, OUTS), full(1, OUTS), full(1, 128), full(ATOMS, 128), full(ATOMS, 128)] + [ANY] * net,
+        out_specs=[full(128, 1024), full(2, 4, 2, 2, 32, 128), full(PAD, 128), full(PAD, 128)] + [ANY] * (6 * net),
         out_shape=[sds(128, 1024), sds(2, 4, 2, 2, 32, 128), sds(PAD, 128), sds(PAD, 128)]
-        + [sds(2, 4, FIRST, 128), sds(2, 4, 200 - FIRST, 128), sds(3, 4, FIRST, 128)] * net,
-        scratch_shapes=[pltpu.VMEM((128, 1024), F32), pltpu.VMEM((OUTP, 128), F32)] + ([pltpu.SemaphoreType.DMA((3,))] * 2 + scatter_sems(2, FIRST, 128) + scatter_sems(2, 200 - FIRST, 128)) * net,
+        + ([sds(PAD, 128)] + [sds(2, 4, n, 128) for _, n in PIECES] + [sds(3, 4, n, 128) for _, n in PIECES[:2]]) * net,
+        scratch_shapes=[pltpu.VMEM((128, 1024), F32), pltpu.VMEM((OUTP, 128), F32)]
+        + ([pltpu.SemaphoreType.DMA] * 2 + [pltpu.SemaphoreType.DMA((3,))] * 4 + sum([scatter_sems(2, n, 128) for _, n in PIECES], [])) * net,
         compiler_params=pltpu.CompilerParams(vmem_limit_bytes=60 * 2**20, **(dict(collective_id=1, has_side_effects=True) if net else {})),
-    )(f, m, s, nin, nout, hb, wo, bo, c, plow, pw, *([f] * net))
+    )(f, m, s, nin, nout, hm, hs, wo, bm, bs, eout, c, plow, pw, *([f] * net))
 
 def hid_bwd_kernel(net, t_ref, logp_ref, h_ref, m_ref, s_ref, nin_ref, nout_ref, wo_ref, c_ref, *rest):
     if net:
         noise, rest = list(zip(rest[2:6], rest[16:20])), rest[:2] + rest[6:16] + rest[20:]
         f1b_ref, hid_ref, df_ref, small_ref, f2b_ref, g1_ref, d1_ref, dz1_ref, g2_ref, d2_ref, dz2_ref, d3_ref = rest[:12]
-        dth, dtl, da, msg, dz_to, t_got = rest[12:18]
-        ds, dr, gs, gr, qs, qr, fs, fr, ts, tr, hs, hr, ss, sr, ps, pr, own = rest[18:35]
-        g_wire = g_scatter(hid_ref, g1_ref, rest[35:39])
-        z_wire = z_scatter(dz_to, dz1_ref, rest[39:42])
+        dth, dtl, da, msg, dz_to = rest[12:17]
+        ds, dr, gs, gr, qs, qr, fs, fr, hs, hr, ss, sr, ps, pr, own = rest[17:32]
+        g_wire = g_scatter(hid_ref, g1_ref, rest[32:36])
+        z_wire = z_scatter(dz_to, dz1_ref, rest[36:39])
         p, g, z, y = coords()
-        d_line = Line(2, lambda i: d1_ref.at[z, i], lambda zz, i: d1_ref.at[zz, i], rest[42], rest[43])
+        d_line = Line(2, lambda i: d1_ref.at[z, i], lambda zz, i: d1_ref.at[zz, i], rest[39], rest[40])
         partner = at(1 - p, g, z, y)
-        target = remote(t_ref, t_got, ts, tr, partner)
         hands = [remote(dz2_ref, dz2_ref, hs.at[0], hr.at[0], partner), remote(dz1_ref, dz1_ref, hs.at[1], hr.at[1], partner)]
-        tells = [remote(src, dst, rest[44].at[i], rest[45].at[i], partner) for i, (src, dst) in enumerate(noise)]
+        tells = [remote(src, dst, rest[41].at[i], rest[42].at[i], partner) for i, (src, dst) in enumerate(noise)]
+        own_tells = [pltpu.make_async_copy(src, dst, rest[43].at[i]) for i, (src, dst) in enumerate(noise)]
         give = remote(msg.at[1], d1_ref.at[z], ps, pr, partner)
         keep = pltpu.make_async_copy(msg.at[0], d1_ref.at[z], own)
         fan_f = f_fan(f1b_ref, f2b_ref, fs, fr)
@@ -504,10 +513,9 @@
                     copy.start()
     else:
         df_ref, small_ref, msg, dz_to, dth, dtl, da = rest
-        t_got = t_ref
     j = pl.program_id(0)
     def begin():
-        t = t_got[...]
+        t = t_ref[...]
         logp = logp_ref[...]
         chosen = c_ref[...]
         row = lax.broadcasted_iota(jnp.int32, (PAD, 128), 0)
@@ -557,15 +565,13 @@
     @pl.when(j == 0)
     def _():
         greet(line(p, g, z, y) + plane(p, g, z, y))
-        pl.when(p == 1)(target.start)
         for copy in fan_f:
             copy.start()
         g_wire.start()
         @pl.when(p == 0)
         def _():
-            target.wait_recv()
             begin()
-            for copy in tells:
+            for copy in tells + own_tells:
                 copy.start()
         pl.when(p == 1)(give.wait_recv)
         d_line.start(0)
@@ -577,7 +583,6 @@
     def _():
         for t in range(1, 4):
             d_line.arrive(t, forward)
-        pl.when(p == 1)(target.wait_send)
         @pl.when(p == 0)
         def _():
             for copy in fan_z:
@@ -603,6 +608,8 @@
             give.wait_send()
             for copy in hands + tells:
                 copy.wait_send()
+            for copy in own_tells:
+                copy.wait()
         @pl.when(p == 1)
         def _():
             for copy in hands + tells:
@@ -621,11 +628,11 @@
         in_specs=[full(PAD, 128), full(PAD, 128), full(128, 1024), wspec, wspec, pl.BlockSpec((1, 2, k), lambda j: (j, 0, 0)), full(2, 512),
                   full(OUTP, 512), full(1, 128)] + [ANY] * (6 * net),
         out_specs=[pl.BlockSpec((k, 128), lambda j: (j, 0)), full(24, 128)] + ([ANY] * 12 if net else [full(2, 2, 256, 128), full(PAD, 128)]),
-        out_shape=[sds(3136, 128), sds(24, 128)] + ([sds(3, 4, 200 - FIRST, 128), sds(4, 2, 2, 32, 128), sds(4, 2, 256, 128), sds(4, PAD, 128), sds(3, 4, 2, 32, 128), sds(3, 4, 256, 128),
+        out_shape=[sds(3136, 128), sds(24, 128)] + ([sds(3, 4, PIECES[2][1], 128), sds(4, 2, 2, 32, 128), sds(4, 2, 256, 128), sds(4, PAD, 128), sds(3, 4, 2, 32, 128), sds(3, 4, 256, 128),
                                                      sds(3, 4, PAD, 128), sds(4, 4, 256, 128), sds(2, 3136), sds(2, 512), sds(2, 512), sds(1, OUTS)] if net else [sds(2, 2, 256, 128), sds(PAD, 128)]),
         scratch_shapes=[pltpu.VMEM((2, 512, 128), BF), pltpu.VMEM((2, 512, 128), BF), pltpu.VMEM((OUTP, 256), F32)]
-        + ([pltpu.VMEM((2, 2, 256, 128), F32), pltpu.VMEM((PAD, 128), F32), pltpu.VMEM((PAD, 128), F32), dma((7, 3)), dma((7, 3))] + [dma((3,))] * 6 + [dma, dma, dma((2,)), dma((2,)), dma((7, 2)), dma((7, 2)), dma, dma, dma]
-           + scatter_sems(1, 2, 2, 32, 128) + scatter_sems(1) + line_sems(2) + [dma((4,)), dma((4,))]) * net,
+        + ([pltpu.VMEM((2, 2, 256, 128), F32), pltpu.VMEM((PAD, 128), F32), dma((7, 3)), dma((7, 3))] + [dma((3,))] * 6 + [dma((2,)), dma((2,)), dma((7, 2)), dma((7, 2)), dma, dma, dma]
+           + scatter_sems(1, 2, 2, 32, 128) + scatter_sems(1) + line_sems(2) + [dma((4,)), dma((4,)), dma((4,))]) * net,
         compiler_params=pltpu.CompilerParams(vmem_limit_bytes=60 * 2**20, **(dict(collective_id=2, has_side_effects=True) if net else {})),
     )(t, logp, h, m, s, nin, nout, wo, c, *wired)
 
@@ -984,24 +991,29 @@
         compiler_params=pltpu.CompilerParams(vmem_limit_bytes=62 * 2**20, **(dict(collective_id=3, has_side_effects=True) if net else {})),
     )(x, pre1, pre2, pre3, df, w1, w2, w3, *wired)
 
-def wide_kernel(f1a, f1b, f2a, f2b, d1, d2, d3, g1, g2, z1, z2, r_ref, q_ref, fv, dv, ev, gv, zv, acc, acq, da, sem):
+def wide_kernel(f1a, f1b, f1c, f2a, f2b, f2c, d1, d2, d3, g1, g2, z1, z2, r_ref, q_ref, fv, dv, ev, gv, zv, acc, acq, da, sem):
     p, g = lax.axis_index("pair"), lax.axis_index("group")
     y = lax.axis_index("rep") % 2
     three, last = pl.ds(0, 3), 3
-    head, tail = pl.ds(0, FIRST), pl.ds(FIRST, 200 - FIRST)
-    pairs = [(f2a, fv.at[three, :, head]), (f1a.at[g], fv.at[last, :, head]), (f2b, fv.at[three, :, tail]), (f1b.at[g], fv.at[last, :, tail]),
-             (d2, dv.at[three]), (d1.at[:, y], dv.at[last]), (d3, ev), (g2, gv.at[three]), (g1.at[:, g], gv.at[last]), (z2, zv.at[three]), (z1, zv.at[last])]
+    rows = [pl.ds(*piece) for piece in PIECES]
+    pairs = [(ref, fv.at[three, :, rows[i]]) for i, ref in enumerate((f2a, f2b, f2c))] + [(ref.at[g], fv.at[last, :, rows[i]]) for i, ref in enumerate((f1a, f1b, f1c))]
+    pairs += [(g2, gv.at[three]), (g1.at[:, g], gv.at[last]), (z2, zv.at[three]), (z1, zv.at[last])]
+    first = len(pairs)
+    for m in range(4):
+        pairs += [(d2.at[m] if m < 3 else d1.at[:, y], dv.at[m]), (d3.at[m], ev.at[m])]
     copies = [pltpu.make_async_copy(a, b, sem.at[i]) for i, (a, b) in enumerate(pairs)]
     for copy in copies:
         copy.start()
     acc[...] = jnp.zeros_like(acc)
     acq[...] = jnp.zeros_like(acq)
     da[...] = jnp.zeros_like(da)
-    for copy in copies:
+    for copy in copies[:first]:
         copy.wait()
     def block(ref, m):
         return jnp.concatenate([jnp.concatenate([ref[m, i, 128 * c:128 * c + 128, :] for c in range(2)], axis=1) for i in range(4)], axis=0)
-    def step(m, carry):
+    def step(m):
+        for copy in copies[first + 2 * m:first + 2 * m + 2]:
+            copy.wait()
         f = split(jnp.concatenate([fv[m, i] for i in range(4)], axis=1))
         acc[0] += dot3(f, split(block(dv, m)))
         acc[1] += dot3(f, split(block(ev, m)))
@@ -1021,8 +1033,8 @@
         @pl.when(y == 1)
         def _():
             acq[:, 640:1152] += dot3(units(1), split(da[640:1152, :]), NT)
-        return carry
-    lax.fori_loop(0, 4, step, 0)
+    for m in range(4):
+        step(m)
     r_ref[:, 0:256] = jnp.where(p == 0, acc[0], acc[1])
     r_ref[:, 256:512] = jnp.where(p == 0, acc[1], acc[0])
     for c in range(9):
@@ -1032,10 +1044,10 @@
     sds = lambda *s: jax.ShapeDtypeStruct(s, F32)
     f32 = lambda *s: pltpu.VMEM(s, F32)
     return pl.pallas_call(
-        wide_kernel, in_specs=[ANY] * 11, out_specs=[VMEM] * 2,
+        wide_kernel, in_specs=[ANY] * 13, out_specs=[VMEM] * 2,
         out_shape=[sds(200, 512), sds(9, 32, 128)],
         scratch_shapes=[f32(4, 4, 200, 128), f32(4, 4, 256, 128), f32(4, 4, 256, 128), f32(4, 4, 2, 32, 128), f32(4, 4, PAD, 128),
-                        f32(2, 200, 256), f32(32, 1152), f32(1152, 512), pltpu.SemaphoreType.DMA((11,))],
+                        f32(2, 200, 256), f32(32, 1152), f32(1152, 512), pltpu.SemaphoreType.DMA((18,))],
         compiler_params=pltpu.CompilerParams(vmem_limit_bytes=60 * 2**20),
     )(*messages)
 
@@ -1146,7 +1158,7 @@
     feat_q, hid_q = 3136 // shards, 512 // shards
     shard = pair * groups + lax.axis_index("group")
     def of_shard(noise):
-        on_in, on_out, on_ein, on_eout = (jnp.where(pair == 0, mine, other) for mine, other in zip(own_noise, noise))
+        on_in, on_out, on_ein, on_eout = noise
         return (lax.dynamic_slice_in_dim(on_in, shard * feat_q, feat_q, axis=1), on_out, lax.dynamic_slice_in_dim(on_ein, shard * hid_q, hid_q, axis=1), on_eout)
 
     x = jnp.transpose(states[0], (2, 3, 1, 0)).reshape(84, 336, 128)
@@ -1154,15 +1166,15 @@
     e_out = e_out[None]
     e_rows = jnp.where(jnp.arange(OUTS)[:, None] < ATOMS, e_in[0:1], e_in[1:2])
     wo = jnp.pad(head_mean[0].T + head_sigma[0].T * (e_rows * e_out.T), ((0, OUTP - OUTS), (0, 0)))
-    bo = jnp.pad(head_bias_mean + head_bias_sigma * e_out, ((0, 0), (0, OUTP - OUTS)))
-    hb = (hidden_bias_mean[0] + hidden_bias_sigma[0] * n_out).reshape(1, 1024)
     nin = jnp.transpose(n_in.reshape(2, STEPS, 3136 // STEPS), (1, 0, 2))
     pre1, pre2, pre3, feats = forward(x, fw1, fw2, fw3, c1, c2, c3)
-    h, hid, logp, dist, *f12 = hidden(net, feats, hidden_mean[0], hidden_sigma[0], nin, n_out, hb, wo, bo, actions, proj_lower.T, proj_weight.T)
+    h, hid, logp, dist, *f12 = hidden(net, feats, hidden_mean[0], hidden_sigma[0], nin, n_out, hidden_bias_mean[0], hidden_bias_sigma[0], wo, head_bias_mean, head_bias_sigma, e_out, actions, proj_lower.T, proj_weight.T)
     back = (logp, h, hidden_mean[0], hidden_sigma[0], nin, n_out, wo, actions)
     if net:
-        df, small_b, f2b, g1, d1, z1, g2, d2, z2, d3, *noise = hidden_bwd(net, dist, *back, f12[1], hid, *own_noise)
-        part_r, part_q = wide_grads(f12[0], f12[1], f12[2], f2b, d1, d2, d3, g1, g2, z1, z2)
+        target, *f12 = f12
+        f1, f2 = f12[:3], f12[3:]
+        df, small_b, f2c, g1, d1, z1, g2, d2, z2, d3, *noise = hidden_bwd(net, target, *back, f1[2], hid, *own_noise)
+        part_r, part_q = wide_grads(*f1, *f2, f2c, d1, d2, d3, g1, g2, z1, z2)
         total, grad_rows, ag, ah, _, _ = backward(net, x, pre1, pre2, pre3, df, bw1, bw2, bw3, part_r, part_q, small_b)
         (hidden_grad, hidden_sigma_grad, head_t, head_sigma_t, gk1, gk2, gk3, gb1, gb2, gb3, hb_grad, hbs_grad, bo_grad, bos_grad,
          loss, grad_rows) = finish(grad_rows, ag, ah, total, *of_shard(noise))
@@ -1185,7 +1197,7 @@
         small_d, lo, up = backward(net, x, pre1, pre2, pre3, df, bw1, bw2, bw3)
         grad_rows = jnp.where(pair == 0, lo, lax.ppermute(up, "pair", [(0, 1)]))
         total = lax.psum(small_d + jnp.pad(small_b, ((0, ROWS - 24), (0, 0))), ("pair", "group", "rep"))
-        in_q, on_out, e_q, on_eout = of_shard(lax.ppermute(own_noise, "pair", [(0, 1)]))
+        in_q, on_out, e_q, on_eout = of_shard([jnp.where(pair == 0, mine, lax.ppermute(mine, "pair", [(0, 1)])) for mine in own_noise])
         hidden_sigma_grad = hidden_grad * (in_q[:, :, None] * on_out[:, None, :])
         head_sigma_t = head_t * (jnp.where(jnp.arange(OUTS)[:, None] < ATOMS, e_q[0:1], e_q[1:2]) * on_eout.T)
         gk1, gk2, gk3, gb1, gb2, gb3 = small_finish(total)

time: 209 us -> 204 us (0.976)
  other arithmetic: 7.8 us -> 2.52 us
    pallas_call x1, Pallas kernels: 51.4 us -> 47.5 us  [hidden_bwd(): pl.pallas_call(functools.partial(hid_bwd_kernel, net), grid=(STEPS,), in_...]
    select_n x4 -> x0, other arithmetic: 3.83 us -> none  [of_shard(): jnp.where(pair == 0, mine, other)]
    pallas_call x1, Pallas kernels: 31.5 us -> 34.4 us  [hidden(): pl.pallas_call(functools.partial(hid_kernel, net), grid=(STEPS,), in_spec...]
    dynamic_slice x0 -> x2, local copies, waits for them, and re-layouts: none -> 2.65 us  [the longest x1 1.37 us: of_shard(): lax.dynamic_slice_in_dim(on_in, shard * feat_q, feat_q, axis=1)]
where the time goes in v6:
time: 204 us; the launch traced here: 203 us
  Pallas kernels  193 us (95%)
  local copies, waits for them, and re-layouts  6.31 us (3%)
  other arithmetic  2.52 us (1%)
    pallas_call x1, Pallas kernels, backward(): pl.pallas_call(functools.partial(bwd_kernel, net), in_specs=[ANY, ANY] +...  63.6 us
    pallas_call x1, Pallas kernels, hidden_bwd(): pl.pallas_call(functools.partial(hid_bwd_kernel, net), grid=(STEPS,), in_...  47.5 us
    pallas_call x1, Pallas kernels, hidden(): pl.pallas_call(functools.partial(hid_kernel, net), grid=(STEPS,), in_spec...  34.4 us
    pallas_call x1, Pallas kernels, forward(): pl.pallas_call(fwd_kernel, in_specs=[hbm] + [vm] * 6, out_specs=[hbm, hbm...  24.7 us
    pallas_call x1, Pallas kernels, finish(): pl.pallas_call(finish_kernel, in_specs=[ANY] + [VMEM] * 7, out_specs=[VME...  11.5 us
    pallas_call x1, Pallas kernels, wide_grads(): pl.pallas_call(wide_kernel, in_specs=[ANY] * 13, out_specs=[VMEM] * 2, ou...  8.81 us

profile of v6, /device:TPU:0, one launch (start us, length us, event | category | flops | bytes accessed | tf_op | source)
XLA Modules:
  0.0 203.0 jit_solution(4213414118045134282)
XLA Ops:
  0.7 0.8 fusion.1
  1.4 0.8 reshape_squeeze.3
  2.3 0.6 copy.44
  2.9 2.8 %shard_map.333 = (bf16[2,192,256]{2,1,0:T(8,128)(2,1)}, bf16[2,128,256]{2,1,0:T(8,128)(2,1)}, bf16[2,384,256]{2,1,0:T(8,128)(2,1)}, bf16[2,192,256]{2,1,0:T(8,12...) custom-call(f32[4,8,8,32]{3,2,1,0:T(8,128)} %bitcast.64, ...), custom_call_target="tpu_custom_call" | custom-call | tf_op jit(solution)/shard_map/pallas_call | solution.py:82
  5.7 2.5 %fusion = f32[969,512]{1,0:T(8,128)S(1)} fusion(f32[1,512,969]{1,0,2:T(1,128)} %param.38, f32[1,512,969]{1,0,2:T(1,128)} %param.37, f32[969]{0:T(1024)} %bitcast.69, f32[512]{0:T(512)S(1)} %bitcast.74, f32[512]{0:T(512)S(1)} %bitcast.73, pred[969]{0:T(1024)(128)(4,1)S(1)} %iota_compare_fusion), kind=kLoop, calls=%fused_computation.1 | loop fusion | flops 1984512 | bytes 5962477 | tf_op jit(solution)/shard_map/add | solution.py:1168
  8.2 1.4 pad.4.wo_ref
  9.7 24.7 %shard_map.334 = (f32[20,640,128]{2,1,0:T(8,128)}, f32[9,576,128]{2,1,0:T(8,128)}, f32[3136,128]{1,0:T(8,128)}, f32[3136,128]{1,0:T(8,128)}) custom-call(f32[84,336,128]{2,1,0:T(8,128)} %bitcast.54, bf16[2,192,256]{2,1,0:T(8,128)(2,1)} %get-tuple-element.74.w1_ref, bf16[2,128,256]{2,1,0:T(8,128)(2,1)} %get-tuple-element.75.w2_ref, ...), custom_call_target="tpu_custom_call" | custom-call | tf_op jit(solution)/shard_map/pallas_call | solution.py:173
  34.4 34.4 %shard_map.335 = (f32[128,1024]{1,0:T(8,128)}, f32[2,4,2,2,32,128]{5,4,3,2,1,0:T(8,128)}, f32[56,128]{1,0:T(8,128)}, f32[56,128]{1,0:T(8,128)}, f32[56,128]{1,0:...) custom-call(f32[3136,128]{1,0:T(8,128)} %get-tuple-element.83.f_ref., ...), custom_call_target="tpu_custom_call" | custom-call | tf_op jit(solution)/shard_map/pallas_call | solution.py:456
  68.8 47.5 %shard_map.336 = (f32[3136,128]{1,0:T(8,128)}, f32[24,128]{1,0:T(8,128)}, f32[3,4,56,128]{3,2,1,0:T(8,128)}, f32[4,2,2,32,128]{4,3,2,1,0:T(8,128)}, f32[4,2,256,...) custom-call(f32[56,128]{1,0:T(8,128)} %get-tuple-element.84.t_ref, ...), custom_call_target="tpu_custom_call" | custom-call | tf_op jit(solution)/shard_map/pallas_call | solution.py:626
  116.3 8.8 %shard_map.337 = (f32[200,512]{1,0:T(8,128)}, f32[9,32,128]{2,1,0:T(8,128)}) custom-call(f32[2,4,72,128]{3,2,1,0:T(8,128)} %get-tuple-element.93.f1a, f32[2,4,72,128]{3,2,1,0:T(8,128)} %get-tuple-element.94.f1b, f32[2,4,56,128]{3,2,1,0:T(8,128)} %get-tuple-element.87.rest_0_.f1c, f32[3,4,72,128]{3,2,1,0:T(8,128)} %get-tuple-element.95.f2a, ...), custom_call_target="tpu_custom_call" | custom-call | tf_op jit(solution)/shard_map/pallas_call | solution.py:1046
  125.1 1.3 constant_dynamic-slice_fusion.ein_ref
  126.4 1.4 constant_dynamic-slice_fusion.1.in_ref
  127.7 63.6 %shard_map.338 = (f32[768,128]{1,0:T(8,128)}, f32[84,168,128]{2,1,0:T(8,128)}, f32[2,4,200,512]{3,2,1,0:T(8,128)}, f32[4,9,32,128]{3,2,1,0:T(8,128)}, f32[2,4,20...) custom-call(f32[84,336,128]{2,1,0:T(8,128)} %bitcast.55, f32[20,640,128]{2,1,0:T(8,128)} %get-tuple-element.80.pre1_hbm, ...), custom_call_target="tpu_custom_call" | custom-call | tf_op jit(solution)/shard_map/pallas_call | solution.py:981
  191.4 11.5 %shard_map.339 = (f32[2,784,512]{2,1,0:T(8,128)}, f32[2,784,512]{2,1,0:T(8,128)}, f32[969,128]{1,0:T(8,128)}, f32[969,128]{1,0:T(8,128)}, f32[4,8,8,32]{3,2,1,0:...) custom-call(f32[84,168,128]{2,1,0:T(8,128)} %get-tuple-element.108.s, ...), custom_call_target="tpu_custom_call" | custom-call | tf_op jit(solution)/shard_map/pallas_call | solution.py:1115
  (1 shorter events, 0.0 us)

commit v7 on v6

--- a/solution.py
+++ b/solution.py
@@ -276,7 +276,7 @@
     return [pltpu.SemaphoreType.DMA((8, parts)), pltpu.SemaphoreType.DMA((4, parts)), pltpu.SemaphoreType.DMA((parts,))] + [pltpu.VMEM((parts,) + hold, F32)] * bool(hold)
 
 
-PIECES = ((0, 72), (72, 72), (144, 56))
+PIECES = ((0, 64), (64, 64), (128, 72))
 
 
 def f_scatter(f_ref, f1_ref, piece, sems):
@@ -399,8 +399,8 @@
             wires[0].start()
         acc[...] = jnp.zeros_like(acc)
     if net:
-        pl.when(j == 4)(lambda: next_piece(0))
-        pl.when(j == 6)(lambda: next_piece(1))
+        pl.when(j == 3)(lambda: next_piece(0))
+        pl.when(j == 5)(lambda: next_piece(1))
     f = split(f_ref[...])
     for s in range(2):
         w = split(noisy(m_ref, s_ref, nin_ref, nout_ref, s))
@@ -578,7 +578,7 @@
         for s in range(2):
             forward(0, z, s)
     pl.when(p == 0)(step)
-    pl.when(j == 3)(forward_small)
+    pl.when(j == 2)(forward_small)
     @pl.when(j == pl.num_programs(0) - 1)
     def _():
         for t in range(1, 4):

time: 204 us -> 203 us (level)
  no operation moved by 1% of the time
where the time goes in v7:
time: 203 us; the launch traced here: 202 us
  Pallas kernels  192 us (95%)
  local copies, waits for them, and re-layouts  6.31 us (3%)
  other arithmetic  2.52 us (1%)
    pallas_call x1, Pallas kernels, backward(): pl.pallas_call(functools.partial(bwd_kernel, net), in_specs=[ANY, ANY] +...  63.6 us
    pallas_call x1, Pallas kernels, hidden_bwd(): pl.pallas_call(functools.partial(hid_bwd_kernel, net), grid=(STEPS,), in_...  48.3 us
    pallas_call x1, Pallas kernels, hidden(): pl.pallas_call(functools.partial(hid_kernel, net), grid=(STEPS,), in_spec...  32.7 us
    pallas_call x1, Pallas kernels, forward(): pl.pallas_call(fwd_kernel, in_specs=[hbm] + [vm] * 6, out_specs=[hbm, hbm...  24.7 us
    pallas_call x1, Pallas kernels, finish(): pl.pallas_call(finish_kernel, in_specs=[ANY] + [VMEM] * 7, out_specs=[VME...  11.5 us
    pallas_call x1, Pallas kernels, wide_grads(): pl.pallas_call(wide_kernel, in_specs=[ANY] * 13, out_specs=[VMEM] * 2, ou...  8.81 us

profile of v7, /device:TPU:0, one launch (start us, length us, event | category | flops | bytes accessed | tf_op | source)
XLA Modules:
  0.0 202.1 jit_solution(15152985185733954882)
XLA Ops:
  0.7 0.8 fusion.1
  1.4 0.8 reshape_squeeze.3
  2.3 0.6 copy.44
  2.9 2.8 %shard_map.333 = (bf16[2,192,256]{2,1,0:T(8,128)(2,1)}, bf16[2,128,256]{2,1,0:T(8,128)(2,1)}, bf16[2,384,256]{2,1,0:T(8,128)(2,1)}, bf16[2,192,256]{2,1,0:T(8,12...) custom-call(f32[4,8,8,32]{3,2,1,0:T(8,128)} %bitcast.64, ...), custom_call_target="tpu_custom_call" | custom-call | tf_op jit(solution)/shard_map/pallas_call | solution.py:82
  5.7 2.5 %fusion = f32[969,512]{1,0:T(8,128)S(1)} fusion(f32[1,512,969]{1,0,2:T(1,128)} %param.38, f32[1,512,969]{1,0,2:T(1,128)} %param.37, f32[969]{0:T(1024)} %bitcast.69, f32[512]{0:T(512)S(1)} %bitcast.74, f32[512]{0:T(512)S(1)} %bitcast.73, pred[969]{0:T(1024)(128)(4,1)S(1)} %iota_compare_fusion), kind=kLoop, calls=%fused_computation.1 | loop fusion | flops 1984512 | bytes 5962477 | tf_op jit(solution)/shard_map/add | solution.py:1168
  8.2 1.4 pad.4.wo_ref
  9.7 24.7 %shard_map.334 = (f32[20,640,128]{2,1,0:T(8,128)}, f32[9,576,128]{2,1,0:T(8,128)}, f32[3136,128]{1,0:T(8,128)}, f32[3136,128]{1,0:T(8,128)}) custom-call(f32[84,336,128]{2,1,0:T(8,128)} %bitcast.54, bf16[2,192,256]{2,1,0:T(8,128)(2,1)} %get-tuple-element.74.w1_ref, bf16[2,128,256]{2,1,0:T(8,128)(2,1)} %get-tuple-element.75.w2_ref, ...), custom_call_target="tpu_custom_call" | custom-call | tf_op jit(solution)/shard_map/pallas_call | solution.py:173
  34.4 32.7 %shard_map.335 = (f32[128,1024]{1,0:T(8,128)}, f32[2,4,2,2,32,128]{5,4,3,2,1,0:T(8,128)}, f32[56,128]{1,0:T(8,128)}, f32[56,128]{1,0:T(8,128)}, f32[56,128]{1,0:...) custom-call(f32[3136,128]{1,0:T(8,128)} %get-tuple-element.83.f_ref., ...), custom_call_target="tpu_custom_call" | custom-call | tf_op jit(solution)/shard_map/pallas_call | solution.py:456
  67.1 48.3 %shard_map.336 = (f32[3136,128]{1,0:T(8,128)}, f32[24,128]{1,0:T(8,128)}, f32[3,4,72,128]{3,2,1,0:T(8,128)}, f32[4,2,2,32,128]{4,3,2,1,0:T(8,128)}, f32[4,2,256,...) custom-call(f32[56,128]{1,0:T(8,128)} %get-tuple-element.84.t_ref, ...), custom_call_target="tpu_custom_call" | custom-call | tf_op jit(solution)/shard_map/pallas_call | solution.py:626
  115.4 8.8 %shard_map.337 = (f32[200,512]{1,0:T(8,128)}, f32[9,32,128]{2,1,0:T(8,128)}) custom-call(f32[2,4,64,128]{3,2,1,0:T(8,128)} %get-tuple-element.93.f1a, f32[2,4,64,128]{3,2,1,0:T(8,128)} %get-tuple-element.94.f1b, f32[2,4,72,128]{3,2,1,0:T(8,128)} %get-tuple-element.87.rest_0_.f1c, f32[3,4,64,128]{3,2,1,0:T(8,128)} %get-tuple-element.95.f2a, ...), custom_call_target="tpu_custom_call" | custom-call | tf_op jit(solution)/shard_map/pallas_call | solution.py:1046
  124.2 1.3 constant_dynamic-slice_fusion.ein_ref
  125.5 1.4 constant_dynamic-slice_fusion.1.in_ref
  126.9 63.6 %shard_map.338 = (f32[768,128]{1,0:T(8,128)}, f32[84,168,128]{2,1,0:T(8,128)}, f32[2,4,200,512]{3,2,1,0:T(8,128)}, f32[4,9,32,128]{3,2,1,0:T(8,128)}, f32[2,4,20...) custom-call(f32[84,336,128]{2,1,0:T(8,128)} %bitcast.55, f32[20,640,128]{2,1,0:T(8,128)} %get-tuple-element.80.pre1_hbm, ...), custom_call_target="tpu_custom_call" | custom-call | tf_op jit(solution)/shard_map/pallas_call | solution.py:981
  190.4 11.5 %shard_map.339 = (f32[2,784,512]{2,1,0:T(8,128)}, f32[2,784,512]{2,1,0:T(8,128)}, f32[969,128]{1,0:T(8,128)}, f32[969,128]{1,0:T(8,128)}, f32[4,8,8,32]{3,2,1,0:...) custom-call(f32[84,168,128]{2,1,0:T(8,128)} %get-tuple-element.108.s, ...), custom_call_target="tpu_custom_call" | custom-call | tf_op jit(solution)/shard_map/pallas_call | solution.py:1115
  (1 shorter events, 0.0 us)

commit v8 on v6

--- a/solution.py
+++ b/solution.py
@@ -869,6 +869,10 @@
         return carry
     def first_grad():
         lax.fori_loop(0, 21, wgrad1, 0)
+        if net:
+            give(0).wait()
+            for k in range(1, chips):
+                give(k).wait_send()
         for h in range(2):
             for ky in range(4):
                 grad = a1[96 * h:96 * h + 32, 64 * ky:64 * ky + 32]
@@ -913,14 +917,13 @@
         def _():
             upper()
             lower()
-            first_grad()
             for k in range(chips):
                 give(k).start()
+            first_grad()
             for k in range(1, chips):
                 show(k).start()
             got1[me] = pay[672:736, :]
             lax.fori_loop(0, 12, dgrad1, 0)
-            give(0).wait()
             for k in range(1, chips):
                 given(k).wait_recv()
             red[...] = jnp.sum(got[...], axis=0)
@@ -935,7 +938,6 @@
             tot[672:736, :] = jnp.sum(got1[...], axis=0)
             hand.start()
             for k in range(1, chips):
-                give(k).wait_send()
                 tell(k).wait_send()
                 show(k).wait_send()
             hand.wait_send()

time: 204 us -> 203 us (level)
  no operation moved by 1% of the time
where the time goes in v8:
time: 203 us
  Pallas kernels  193 us (95%)
  local copies, waits for them, and re-layouts  6.31 us (3%)
  other arithmetic  2.52 us (1%)
    pallas_call x1, Pallas kernels, backward(): pl.pallas_call(functools.partial(bwd_kernel, net), in_specs=[ANY, ANY] +...  63.2 us
    pallas_call x1, Pallas kernels, hidden_bwd(): pl.pallas_call(functools.partial(hid_bwd_kernel, net), grid=(STEPS,), in_...  47.5 us
    pallas_call x1, Pallas kernels, hidden(): pl.pallas_call(functools.partial(hid_kernel, net), grid=(STEPS,), in_spec...  34.4 us
    pallas_call x1, Pallas kernels, forward(): pl.pallas_call(fwd_kernel, in_specs=[hbm] + [vm] * 6, out_specs=[hbm, hbm...  24.7 us
    pallas_call x1, Pallas kernels, finish(): pl.pallas_call(finish_kernel, in_specs=[ANY] + [VMEM] * 7, out_specs=[VME...  11.5 us
    pallas_call x1, Pallas kernels, wide_grads(): pl.pallas_call(wide_kernel, in_specs=[ANY] * 13, out_specs=[VMEM] * 2, ou...  8.81 us

profile of v8, /device:TPU:0, one launch (start us, length us, event | category | flops | bytes accessed | tf_op | source)
XLA Modules:
  0.0 202.6 jit_solution(13315762838602896990)
XLA Ops:
  0.7 0.8 fusion.1
  1.4 0.8 reshape_squeeze.3
  2.3 0.6 copy.44
  2.9 2.8 %shard_map.333 = (bf16[2,192,256]{2,1,0:T(8,128)(2,1)}, bf16[2,128,256]{2,1,0:T(8,128)(2,1)}, bf16[2,384,256]{2,1,0:T(8,128)(2,1)}, bf16[2,192,256]{2,1,0:T(8,12...) custom-call(f32[4,8,8,32]{3,2,1,0:T(8,128)} %bitcast.64, ...), custom_call_target="tpu_custom_call" | custom-call | tf_op jit(solution)/shard_map/pallas_call | solution.py:82
  5.7 2.5 %fusion = f32[969,512]{1,0:T(8,128)S(1)} fusion(f32[1,512,969]{1,0,2:T(1,128)} %param.38, f32[1,512,969]{1,0,2:T(1,128)} %param.37, f32[969]{0:T(1024)} %bitcast.69, f32[512]{0:T(512)S(1)} %bitcast.74, f32[512]{0:T(512)S(1)} %bitcast.73, pred[969]{0:T(1024)(128)(4,1)S(1)} %iota_compare_fusion), kind=kLoop, calls=%fused_computation.1 | loop fusion | flops 1984512 | bytes 5962477 | tf_op jit(solution)/shard_map/add | solution.py:1170
  8.2 1.4 pad.4.wo_ref
  9.7 24.7 %shard_map.334 = (f32[20,640,128]{2,1,0:T(8,128)}, f32[9,576,128]{2,1,0:T(8,128)}, f32[3136,128]{1,0:T(8,128)}, f32[3136,128]{1,0:T(8,128)}) custom-call(f32[84,336,128]{2,1,0:T(8,128)} %bitcast.54, bf16[2,192,256]{2,1,0:T(8,128)(2,1)} %get-tuple-element.74.w1_ref, bf16[2,128,256]{2,1,0:T(8,128)(2,1)} %get-tuple-element.75.w2_ref, ...), custom_call_target="tpu_custom_call" | custom-call | tf_op jit(solution)/shard_map/pallas_call | solution.py:173
  34.4 34.4 %shard_map.335 = (f32[128,1024]{1,0:T(8,128)}, f32[2,4,2,2,32,128]{5,4,3,2,1,0:T(8,128)}, f32[56,128]{1,0:T(8,128)}, f32[56,128]{1,0:T(8,128)}, f32[56,128]{1,0:...) custom-call(f32[3136,128]{1,0:T(8,128)} %get-tuple-element.83.f_ref., ...), custom_call_target="tpu_custom_call" | custom-call | tf_op jit(solution)/shard_map/pallas_call | solution.py:456
  68.8 47.5 %shard_map.336 = (f32[3136,128]{1,0:T(8,128)}, f32[24,128]{1,0:T(8,128)}, f32[3,4,56,128]{3,2,1,0:T(8,128)}, f32[4,2,2,32,128]{4,3,2,1,0:T(8,128)}, f32[4,2,256,...) custom-call(f32[56,128]{1,0:T(8,128)} %get-tuple-element.84.t_ref, ...), custom_call_target="tpu_custom_call" | custom-call | tf_op jit(solution)/shard_map/pallas_call | solution.py:626
  116.3 8.8 %shard_map.337 = (f32[200,512]{1,0:T(8,128)}, f32[9,32,128]{2,1,0:T(8,128)}) custom-call(f32[2,4,72,128]{3,2,1,0:T(8,128)} %get-tuple-element.93.f1a, f32[2,4,72,128]{3,2,1,0:T(8,128)} %get-tuple-element.94.f1b, f32[2,4,56,128]{3,2,1,0:T(8,128)} %get-tuple-element.87.rest_0_.f1c, f32[3,4,72,128]{3,2,1,0:T(8,128)} %get-tuple-element.95.f2a, ...), custom_call_target="tpu_custom_call" | custom-call | tf_op jit(solution)/shard_map/pallas_call | solution.py:1048
  125.1 1.3 constant_dynamic-slice_fusion.ein_ref
  126.4 1.4 constant_dynamic-slice_fusion.1.in_ref
  127.7 63.2 %shard_map.338 = (f32[768,128]{1,0:T(8,128)}, f32[84,168,128]{2,1,0:T(8,128)}, f32[2,4,200,512]{3,2,1,0:T(8,128)}, f32[4,9,32,128]{3,2,1,0:T(8,128)}, f32[2,4,20...) custom-call(f32[84,336,128]{2,1,0:T(8,128)} %bitcast.55, f32[20,640,128]{2,1,0:T(8,128)} %get-tuple-element.80.pre1_hbm, ...), custom_call_target="tpu_custom_call" | custom-call | tf_op jit(solution)/shard_map/pallas_call | solution.py:983
  190.9 11.5 %shard_map.339 = (f32[2,784,512]{2,1,0:T(8,128)}, f32[2,784,512]{2,1,0:T(8,128)}, f32[969,128]{1,0:T(8,128)}, f32[969,128]{1,0:T(8,128)}, f32[4,8,8,32]{3,2,1,0:...) custom-call(f32[84,168,128]{2,1,0:T(8,128)} %get-tuple-element.108.s, ...), custom_call_target="tpu_custom_call" | custom-call | tf_op jit(solution)/shard_map/pallas_call | solution.py:1117
  (1 shorter events, 0.0 us)
